TPU v7x, 128 devices: a whole 4x4x4 slice. The times are simulated.
128 devices in a mesh: tile: 32 (over z, y, core), rep: 4 (over x).
Axes of the slice: x: 4, y: 4, z: 4, core: 2. Of those that a mesh axis runs over, the one named last changes fastest.
Arguments:
- features: bfloat16 [4, 64, 64, 2048], P('rep', 'tile'), may hold values from -7 to 7
- head_grad: bfloat16 [4, 64, 64, 256], P('rep', 'tile'), may hold values from -6 to 6
- branch_weight: bfloat16 [29, 2048, 256], P(None, 'tile'), may hold values from -0.046875 to 0.046875
- proj_weight: bfloat16 [1280, 256], replicated, may hold values from -0.15625 to 0.15625
Outputs:
- head_out: bfloat16 [4, 64, 64, 256], P('rep', 'tile')
- grad_features: bfloat16 [4, 64, 64, 2048], P('rep', None, None, 'tile')
- grad_branch: float32 [29, 2048, 256], P(None, 'tile')
- grad_proj: float32 [1280, 256], replicated
All inputs are finite; a program needn't handle non-finite values.
Results may differ from a plain program's by a relative error of at most 0.01.
Values may be sent and summed in bfloat16 or wider, within the bound.
No kernel may reach another device: no remote copies, remote signals or barrier semaphores. Data moves between devices by JAX's collectives and lax.ppermute only.
A program may use at most 320 MiB of HBM per device.

v0:
```python
import jax
import jax.numpy as jnp
from jax import lax
from jax.sharding import PartitionSpec as P

reach_cells = 36


def tap_offsets():
    offsets = [(0, 0)]
    for dilation_index in range(3):
        spacing = 12 * (dilation_index + 1)
        for row_step in range(3):
            for col_step in range(3):
                offsets.append(((row_step - 1) * spacing, (col_step - 1) * spacing))
    return offsets


def tap_range(branch):
    if branch == 0:
        return (0, 1)
    return (1 + 9 * (branch - 1), 10 + 9 * (branch - 1))


def field_from(grads_map, weights, offsets, low, high):
    row_count, col_count, _ = grads_map.shape
    grad_pad = jnp.pad(grads_map, ((reach_cells, reach_cells), (reach_cells, reach_cells), (0, 0)))
    windows = []
    for tap_index in range(low, high):
        row_shift, col_shift = offsets[tap_index]
        row_start = reach_cells - row_shift
        col_start = reach_cells - col_shift
        windows.append(
            grad_pad[row_start : row_start + row_count, col_start : col_start + col_count, :]
        )
    joined = jnp.concatenate(windows, axis=2).reshape(row_count * col_count, -1)
    matrix = jnp.transpose(weights, (0, 2, 1)).reshape(-1, weights.shape[1])
    return jnp.dot(joined, matrix, preferred_element_type=jnp.float32).reshape(
        row_count, col_count, -1
    )


def local(features, head_grad, branch_weight, proj_weight):
    offsets = tap_offsets()
    owned = lax.all_to_all(features, "tile", split_axis=3, concat_axis=1, tiled=True)[0]
    all_rows, width, channels = owned.shape
    my_rows = features.shape[1]
    branch_width = proj_weight.shape[1]
    padded = jnp.pad(owned, ((reach_cells, reach_cells), (reach_cells, reach_cells), (0, 0)))
    pooled = jnp.mean(owned.astype(jnp.float32), axis=(0, 1))
    pool_part = jnp.dot(
        pooled, branch_weight[28].astype(jnp.float32), precision=lax.Precision.HIGHEST
    )

    def window_of(source, first_row, row_span, tap_index):
        row_shift, col_shift = offsets[tap_index]
        block = lax.dynamic_slice_in_dim(source, first_row + reach_cells + row_shift, row_span, 0)
        return block[:, reach_cells + col_shift : reach_cells + col_shift + width, :]

    def stacked_from(source, first_row, row_span, branch):
        low, high = tap_range(branch)
        joined = jnp.concatenate(
            [window_of(source, first_row, row_span, tap_index) for tap_index in range(low, high)],
            axis=2,
        )
        return joined.reshape(row_span * width, -1)

    pixel_span = lax.axis_size("tile") * (my_rows * width)
    first_row = jnp.int32(0) // width
    row_span = pixel_span // width
    columns = []
    for branch_branch in range(4):
        branch_low, branch_high = tap_range(branch_branch)
        columns.append(
            jnp.dot(
                stacked_from(padded, first_row, row_span, branch_branch),
                branch_weight[branch_low:branch_high].reshape(-1, branch_width),
                preferred_element_type=jnp.float32,
            )
        )
    columns.append(jnp.broadcast_to(pool_part, (pixel_span, branch_width)))
    pre = lax.psum_scatter(
        jnp.concatenate(columns, axis=1), "tile", scatter_dimension=0, tiled=True
    )
    act = jnp.maximum(pre, 0.0).astype(jnp.bfloat16)
    grad_rows = head_grad.reshape(-1, branch_width)
    head_out = (
        jnp.dot(act, proj_weight, preferred_element_type=jnp.float32)
        .astype(jnp.bfloat16)
        .reshape(head_grad.shape)
    )
    proj_part = lax.dot_general(
        act, grad_rows, (((0,), (0,)), ((), ())), preferred_element_type=jnp.float32
    )
    back = lax.dot_general(
        grad_rows, proj_weight, (((1,), (1,)), ((), ())), preferred_element_type=jnp.float32
    )
    grad_pre = jnp.where(pre > 0, back, 0.0).astype(jnp.bfloat16).reshape(my_rows, width, -1)
    pixel_total = all_rows * width
    every_grad = lax.all_gather(grad_pre, "tile", axis=0, tiled=True)
    flat_all = every_grad.reshape(all_rows * width, -1)
    weight_list = []
    interior = jnp.zeros((all_rows, width, channels), jnp.float32)
    for branch in range(4):
        low, high = tap_range(branch)
        grads = flat_all[:, branch * branch_width : (branch + 1) * branch_width]
        stacked = stacked_from(padded, 0, all_rows, branch)
        weight_list.append(
            lax.dot_general(
                stacked, grads, (((0,), (0,)), ((), ())), preferred_element_type=jnp.float32
            ).reshape(high - low, channels, branch_width)
        )
        grads_map = grads.reshape(all_rows, width, branch_width)
        interior = interior + field_from(grads_map, branch_weight[low:high], offsets, low, high)
    tap_grads = jnp.concatenate(weight_list, axis=0)
    pool_grad = jnp.sum(flat_all[:, 4 * branch_width :].astype(jnp.float32), axis=0)
    pool_field = (
        jnp.dot(pool_grad, branch_weight[28].astype(jnp.float32).T, precision=lax.Precision.HIGHEST)
        / pixel_total
    )
    grad_features = (interior + pool_field).astype(jnp.bfloat16)[None]
    local_grads = jnp.concatenate([tap_grads, jnp.outer(pooled, pool_grad)[None]], axis=0)
    grad_branch = lax.psum(local_grads, "rep")
    grad_proj = lax.psum(proj_part, ("tile", "rep"))
    return (head_out, grad_features, grad_branch, grad_proj)


def solution(mesh):
    placed = (
        P("rep", "tile", None, None),
        P("rep", "tile", None, None),
        P(None, "tile", None),
        P(),
    )
    return jax.shard_map(
        local,
        mesh=mesh,
        in_specs=placed,
        out_specs=(
            P("rep", "tile", None, None),
            P("rep", None, None, "tile"),
            P(None, "tile", None),
            P(),
        ),
        check_vma=False,
    )
```

profile of v0, /device:TPU:1, one launch (start us, length us, event | category | flops | bytes accessed | tf_op | source)
XLA Modules:
  0.0 570.5 jit_solution(9498575903480820093)
XLA Ops:
  7.2 2.5 copy.107
  11.2 9.6 %all-to-all-start = ((bf16[32,2,4096]{2,1,0:T(2,128)(2,1)}), bf16[32,2,4096]{2,1,0:T(2,128)(2,1)S(1)}, u32[]{:S(2)}, u32[]{:S(2)}) async-start(bf16[32,2,4096]{2,1,0:T(2,128)(2,1)} %reshape.312), calls=%async_computation | async-start | bytes 1048576 | tf_op jit(solution)/shard_map/all_to_all | solution.py:45
  22.2 10.2 %all-to-all-done = bf16[32,2,4096]{2,1,0:T(2,128)(2,1)S(1)} async-done(((bf16[32,2,4096]{2,1,0:T(2,128)(2,1)}), bf16[32,2,4096]{2,1,0:T(2,128)(2,1)S(1)}, u32[]{:S(2)}, u32[]{:S(2)}) %all-to-all-start) | async-done | bytes 524320 | tf_op jit(solution)/shard_map/all_to_all | solution.py:45
  37.5 3.2 pad_slice_fusion.1
  40.7 24.9 %pad_slice_fusion = (bf16[64,64,64]{2,1,0:T(8,128)(2,1)}, bf16[64,64,64]{2,1,0:T(8,128)(2,1)}, bf16[64,64,64]{2,1,0:T(8,128)(2,1)}, bf16[64,64,64]{2,1,0:T(8,128...) fusion(bf16[64,64,64]{2,1,0:T(8,128)(2,1)S(1)} %bitcast.174), kind=kLoop, calls=%fused_computation | loop fusion | bytes 10485760 | tf_op jit(solution)/shard_map/slice | solution.py:58
  66.5 3.5 reshape.281
  90.8 2.5 copy.146
  123.7 3.6 convolution_dynamic-update-slice_fusion.3
  135.0 4.1 convolution_dynamic-update-slice_fusion.2
  139.1 16.5 %convolution_dynamic-update-slice_fusion.1 = f32[4096,1280]{0,1:T(8,128)} fusion(f32[4096,1280]{0,1:T(8,128)} %convolution_dynamic-update-slice_fusion.2, bf16[4096,576]{0,1:T(8,128)(2,1)S(1)} %constant_dynamic-update-slice_fusion.9, bf16[576,256]{1,0:T(8,128)(2,1)S(1)} %bitcast.213), kind=kOutput, calls=%fused_computation.49 | convolution fusion | flops 1207959552 | bytes 9207808 | tf_op jit(solution)/shard_map/dot_general | solution.py:75
  155.6 3.9 convolution_dynamic-update-slice_fusion
  161.9 125.2 %reduce-scatter.2.cloned.1.call-done = f32[128,1280]{0,1:T(8,128)} async-done(((f32[4096,1280]{0,1:T(8,128)}), f32[128,1280]{0,1:T(8,128)}) %reduce-scatter.2.cloned.1.call-update) | async-done | bytes 655376 | tf_op jit(solution)/shard_map/reduce_scatter | solution.py:82
  295.2 53.3 %all-gather.2.cloned.1.call-done = bf16[64,64,1280]{2,1,0:T(8,128)(2,1)} async-done(((bf16[2,64,1280]{2,1,0:T(8,128)(2,1)}), bf16[64,64,1280]{2,1,0:T(8,128)(2,1)}) %all-gather.2.cloned.1.call-update) | async-done | bytes 10485776 | tf_op jit(solution)/shard_map/all_gather | solution.py:100
  350.6 2.7 fusion.41
  353.3 5.0 fusion.60
  365.3 2.5 fusion.11
  383.8 9.2 %copy-done.46 = bf16[64,64,2304]{2,1,0:T(8,128)(2,1)} copy-done((bf16[64,64,2304]{2,1,0:T(8,128)(2,1)}, bf16[64,64,2304]{2,1,0:T(8,128)(2,1)S(1)}, u32[]{:S(2)}) %copy-start.46) | copy-done | bytes 18874392
  400.7 10.3 %fusion.63 = f32[64,64,64]{2,1,0:T(8,128)S(1)} fusion(bf16[64,64,2304]{2,1,0:T(8,128)(2,1)} %copy-done.45, bf16[2304,64,1]{0,1,2:T(8,128)(2,1)S(1)} %copy-done.43), kind=kOutput, calls=%fused_computation.153 | convolution fusion | flops 1207959552 | bytes 20217856 | tf_op jit(solution)/shard_map/dot_general | solution.py:38
  411.0 10.3 %fusion.62 = f32[64,64,64]{2,1,0:T(8,128)S(1)} fusion(bf16[64,64,2304]{2,1,0:T(8,128)(2,1)} %fusion.16, bf16[2304,64,1]{0,1,2:T(8,128)(2,1)S(1)} %copy-done.42), kind=kOutput, calls=%fused_computation.152 | convolution fusion | flops 1207959552 | bytes 20217856 | tf_op jit(solution)/shard_map/dot_general | solution.py:38
  423.2 5.4 fusion.61
  428.6 2.5 fusion.31
  431.1 70.6 %all-reduce.9.cloned.1.call-done = f32[1280,256]{1,0:T(8,128)} async-done(((f32[1280,256]{1,0:T(8,128)}), f32[1280,256]{1,0:T(8,128)}) %all-reduce.9.cloned.1.call-update) | async-done | bytes 1310736 | tf_op jit(solution)/shard_map/psum | solution.py:124
  501.7 56.5 %all-reduce.7.cloned.1.call-done = f32[29,64,256]{2,1,0:T(8,128)} async-done(((f32[29,64,256]{2,1,0:T(8,128)}), f32[29,64,256]{2,1,0:T(8,128)}) %all-reduce.7.cloned.1.call-update) | async-done | bytes 1900560 | tf_op jit(solution)/shard_map/psum | solution.py:123
  558.2 3.0 copy.224
  (234 shorter events, 114.8 us)
Async XLA Ops:
  7.2 279.9 %copy-start = (bf16[1280,256]{1,0:T(8,128)(2,1)S(1)}, bf16[1280,256]{1,0:T(8,128)(2,1)}, u32[]{:S(2)}) copy-start(bf16[1280,256]{1,0:T(8,128)(2,1)} %param.7) | copy-start | bytes 1966084
  7.2 13.7 %copy-start.40 = (bf16[29,64,256]{2,1,0:T(8,128)(2,1)S(1)}, bf16[29,64,256]{2,1,0:T(8,128)(2,1)}, u32[]{:S(2)}) copy-start(bf16[29,64,256]{2,1,0:T(8,128)(2,1)} %param.6) | copy-start | bytes 2850820
  11.2 21.2 %all-to-all-start = ((bf16[32,2,4096]{2,1,0:T(2,128)(2,1)}), bf16[32,2,4096]{2,1,0:T(2,128)(2,1)S(1)}, u32[]{:S(2)}, u32[]{:S(2)}) async-start(bf16[32,2,4096]{2,1,0:T(2,128)(2,1)} %reshape.312), calls=%async_computation | async-start | bytes 1048576 | tf_op jit(solution)/shard_map/all_to_all | solution.py:45
  20.8 266.3 %reduce-scatter.2.cloned.1.call-start = ((), (), s32[]{:S(2)}) async-start(), calls=%async_computation.2 | async-start | bytes 21626880 | tf_op jit(solution)/shard_map/reduce_scatter | solution.py:82
  75.8 13.7 %copy-start.11 = (bf16[64,64,64]{2,1,0:T(8,128)(2,1)S(1)}, bf16[64,64,64]{2,1,0:T(8,128)(2,1)}, u32[]{:S(2)}) copy-start(bf16[64,64,64]{2,1,0:T(8,128)(2,1)} %get-tuple-element.11) | copy-start | bytes 1572868
  90.8 14.2 %copy-start.10 = (bf16[64,64,64]{2,1,0:T(8,128)(2,1)S(1)}, bf16[64,64,64]{2,1,0:T(8,128)(2,1)}, u32[]{:S(2)}) copy-start(bf16[64,64,64]{2,1,0:T(8,128)(2,1)} %get-tuple-element.18) | copy-start | bytes 1572868
  106.1 13.0 %copy-start.9 = (bf16[64,64,64]{2,1,0:T(8,128)(2,1)S(1)}, bf16[64,64,64]{2,1,0:T(8,128)(2,1)}, u32[]{:S(2)}) copy-start(bf16[64,64,64]{2,1,0:T(8,128)(2,1)} %get-tuple-element.25) | copy-start | bytes 1572868
  107.3 13.0 %copy-start.8 = (bf16[64,64,64]{2,1,0:T(8,128)(2,1)S(1)}, bf16[64,64,64]{2,1,0:T(8,128)(2,1)}, u32[]{:S(2)}) copy-start(bf16[64,64,64]{2,1,0:T(8,128)(2,1)} %get-tuple-element.26) | copy-start | bytes 1572868
  132.7 22.9 %copy-start.7 = (bf16[4096,576]{0,1:T(8,128)(2,1)}, bf16[4096,576]{0,1:T(8,128)(2,1)S(1)}, u32[]{:S(2)}) copy-start(bf16[4096,576]{0,1:T(8,128)(2,1)S(1)} %constant_dynamic-update-slice_fusion.18) | copy-start | bytes 14155780
  134.8 20.8 %copy-start.6 = (bf16[4096,576]{0,1:T(8,128)(2,1)}, bf16[4096,576]{0,1:T(8,128)(2,1)S(1)}, u32[]{:S(2)}) copy-start(bf16[4096,576]{0,1:T(8,128)(2,1)S(1)} %constant_dynamic-update-slice_fusion.9) | copy-start | bytes 14155780
  139.1 16.5 %copy-start.34 = (bf16[9,64,256]{2,1,0:T(8,128)(2,1)S(1)}, bf16[9,64,256]{2,1,0:T(8,128)(2,1)}, u32[]{:S(2)}) copy-start(bf16[9,64,256]{2,1,0:T(8,128)(2,1)} %get-tuple-element.37) | copy-start | bytes 884740
  161.8 125.3 %copy-start.44 = (bf16[1,2,64,256]{3,2,1,0:T(8,128)(2,1)S(1)}, bf16[1,2,64,256]{3,2,1,0:T(8,128)(2,1)}, u32[]{:S(2)}) copy-start(bf16[1,2,64,256]{3,2,1,0:T(8,128)(2,1)} %param.5) | copy-start | bytes 196612
  161.8 127.8 %copy-start.39 = (bf16[9,256,64]{1,2,0:T(8,128)(2,1)S(1)}, bf16[9,256,64]{1,2,0:T(8,128)(2,1)}, u32[]{:S(2)}) copy-start(bf16[9,256,64]{1,2,0:T(8,128)(2,1)} %get-tuple-element.32) | copy-start | bytes 884740
  161.8 128.9 %copy-start.38 = (bf16[9,256,64]{1,2,0:T(8,128)(2,1)S(1)}, bf16[9,256,64]{1,2,0:T(8,128)(2,1)}, u32[]{:S(2)}) copy-start(bf16[9,256,64]{1,2,0:T(8,128)(2,1)} %get-tuple-element.33) | copy-start | bytes 884740
  161.8 129.9 %copy-start.37 = (bf16[9,256,64]{1,2,0:T(8,128)(2,1)S(1)}, bf16[9,256,64]{1,2,0:T(8,128)(2,1)}, u32[]{:S(2)}) copy-start(bf16[9,256,64]{1,2,0:T(8,128)(2,1)} %get-tuple-element.34) | copy-start | bytes 884740
  161.8 186.6 %all-gather.2.cloned.1.call-start = ((), (), s32[]{:S(2)}) async-start(), calls=%async_computation.3 | async-start | bytes 10813440 | tf_op jit(solution)/shard_map/all_gather | solution.py:100
  289.5 212.2 %all-reduce.9.cloned.1.call-start = ((), (), s32[]{:S(2)}) async-start(), calls=%async_computation.5 | async-start | bytes 2621440 | tf_op jit(solution)/shard_map/psum | solution.py:124
  294.2 264.0 %all-reduce.7.cloned.1.call-start = ((), (), s32[]{:S(2)}) async-start(), calls=%async_computation.4 | async-start | bytes 3801088 | tf_op jit(solution)/shard_map/psum | solution.py:123
  361.2 14.3 %copy-start.45 = (bf16[64,64,2304]{2,1,0:T(8,128)(2,1)}, bf16[64,64,2304]{2,1,0:T(8,128)(2,1)S(1)}, u32[]{:S(2)}) copy-start(bf16[64,64,2304]{2,1,0:T(8,128)(2,1)S(1)} %fusion.24) | copy-start | bytes 56623108
  380.6 12.4 %slice-start = ((s8[10485760]{0:T(1024)(128)(4,1)}), s8[4194304]{0:T(1024)(128)(4,1)S(1)}, s32[]{:S(2)}) async-start(s8[10485760]{0:T(1024)(128)(4,1)} %bitcast.168), calls=%async_computation.6 | async-start | bytes 8388608
  400.7 20.7 %slice-start.9 = ((s8[18874368]{0:T(1024)(128)(4,1)}), s8[4194304]{0:T(1024)(128)(4,1)S(1)}, s32[]{:S(2)}) async-start(s8[18874368]{0:T(1024)(128)(4,1)} %bitcast.217), calls=%async_computation.15 | async-start | bytes 8388608
  400.7 20.7 %slice-start.10 = ((s8[18874368]{0:T(1024)(128)(4,1)}), s8[4194304]{0:T(1024)(128)(4,1)S(1)}, s32[]{:S(2)}) async-start(s8[18874368]{0:T(1024)(128)(4,1)} %bitcast.217), calls=%async_computation.16 | async-start | bytes 8388608
  400.7 20.7 %slice-start.11 = ((s8[18874368]{0:T(1024)(128)(4,1)}), s8[4194304]{0:T(1024)(128)(4,1)S(1)}, s32[]{:S(2)}) async-start(s8[18874368]{0:T(1024)(128)(4,1)} %bitcast.217), calls=%async_computation.17 | async-start | bytes 8388608
  428.6 135.1 %copy-start.1 = (bf16[1280,256]{1,0:T(8,128)(2,1)S(1)}, bf16[1280,256]{1,0:T(8,128)(2,1)}, u32[]{:S(2)}) copy-start(bf16[1280,256]{1,0:T(8,128)(2,1)} %param.7) | copy-start | bytes 1966084
  (42 other events, 238.5 us)
Sparse Core Ops, SparseCore 0:
  162.0 125.0 reduce-scatter.1
  290.2 58.2 all-gather.1
  354.6 147.0 all-reduce.8
  504.5 53.6 all-reduce.6
where the time goes:
time: 581 us; the launch traced here: 571 us
  waiting for transfers between devices  316 us (54%)
  local copies, waits for them, and re-layouts  155 us (27%)
  matrix products  71.6 us (12%)
  between operations  15.1 us (3%)
  starting transfers between devices  9.77 us (2%)
    reduce_scatter x1, waiting for transfers between devices, local(): lax.psum_scatter(jnp.concatenate(columns, axis=1), 'tile', scatter_dimens...  125 us
    psum x1, waiting for transfers between devices, local(): grad_proj = lax.psum(proj_part, ('tile', 'rep'))  70.6 us
    psum x1, waiting for transfers between devices, local(): grad_branch = lax.psum(local_grads, 'rep')  56.5 us
    unnamed x172, local copies, waits for them, and re-layouts  54.2 us
    all_gather x1, waiting for transfers between devices, local(): every_grad = lax.all_gather(grad_pre, 'tile', axis=0, tiled=True)  53.3 us
    concatenate x27, local copies, waits for them, and re-layouts, stacked_from(): jnp.concatenate([window_of(source, first_row, row_span, tap_index) for ta...  49.5 us
    dot_general x4, matrix products, field_from(): jnp.dot(joined, matrix, preferred_element_type=jnp.float32)  28.4 us
    dot_general x4, matrix products, local(): jnp.dot(stacked_from(padded, first_row, row_span, branch_branch), branch_...  28.1 us
  transfers between devices with their start and end apart: 5, of which 5 were waited for; matrix products, arithmetic and copies ran while one was open for 14% of the time, Pallas kernels for 0%

commit v1 on v0

v1 whole, which is shorter than its diff:
```python
import functools

import jax
import jax.numpy as jnp
from jax import lax
from jax.experimental import pallas as pl
from jax.experimental.pallas import tpu as pltpu
from jax.sharding import Mesh, PartitionSpec as P

GROUPS = 16
GP = 128
HALF = GROUPS * GP
COLS = 64
CH = 128
BR = 256
PAD = 9
SHIFTS = (0, -12, 12, -24, 24, -36, 36)
F32 = jnp.float32
BF = jnp.bfloat16
HIGH = lax.Precision.HIGHEST


def shift_slot(j, b):
    return SHIFTS.index((b - 1) * 12 * (j + 1))


def column_shift(value, amount):
    if amount == 0:
        return value
    n = value.shape[0]
    col = lax.broadcasted_iota(jnp.int32, value.shape, 0) & (COLS - 1)
    rolled = pltpu.roll(value, (-amount) % n, 0)
    return jnp.where((col + amount >= 0) & (col + amount < COLS), rolled, 0.0)


def join_weights(c, own, other, w):
    w[:, pl.ds(pl.multiple_of(c * 64, 64), 64), :] = own[...]
    w[:, pl.ds(pl.multiple_of((1 - c) * 64, 64), 64), :] = other[...]


def valid_steps(j, m, sign):
    steps = []
    for a in range(3):
        delta = 3 * (j + 1) * (a - 1)
        low = 4 * m + sign * delta
        if low + 3 >= 0 and low < GROUPS:
            steps.append((a, low))
    return steps


def forward_kernel(core_ref, x_ref, hg_ref, own, other, p_ref, colsum_ref, w, xs):
    join_weights(core_ref[0], own, other, w)
    xs[:, : PAD * GP, :] = jnp.zeros((7, PAD * GP, CH), BF)
    xs[:, PAD * GP + HALF :, :] = jnp.zeros((7, PAD * GP, CH), BF)
    total = jnp.zeros((1, CH), F32)
    for m in range(4):
        rows = pl.ds(m * 512, 512)
        chunk = x_ref[rows, :]
        wide = chunk.astype(F32)
        total = total + jnp.sum(wide, axis=0, keepdims=True)
        for slot, amount in enumerate(SHIFTS):
            xs[slot, pl.ds(PAD * GP + m * 512, 512), :] = column_shift(wide, amount).astype(BF)
    total8 = jnp.broadcast_to(total, (8, CH))
    colsum_ref[...] = total8
    pool = jnp.dot(total8, w[28].astype(F32), precision=HIGH, preferred_element_type=F32)
    hsum = jnp.broadcast_to(jnp.sum(hg_ref[...].astype(F32), axis=0, keepdims=True), (8, BR))
    extra = jnp.concatenate([pool, hsum, jnp.zeros((8, 512), F32)], axis=1)
    for s in range(GROUPS):
        p_ref[s, pl.ds(GP, 8), :] = extra
    for m in range(4):
        first = jnp.dot(x_ref[pl.ds(m * 512, 512), :], w[0], preferred_element_type=F32)
        for k in range(4):
            p_ref[4 * m + k, 0:GP, 0:BR] = first[k * GP : (k + 1) * GP]
        for j in range(3):
            steps = valid_steps(j, m, 1)
            left = jnp.concatenate(
                [xs[shift_slot(j, b), pl.ds((PAD + low) * GP, 512), :] for _, low in steps for b in range(3)], axis=1
            )
            start = 1 + 9 * j + 3 * steps[0][0]
            right = w[start : start + 3 * len(steps)].reshape(-1, BR)
            acc = jnp.dot(left, right, preferred_element_type=F32)
            for k in range(4):
                p_ref[4 * m + k, 0:GP, (j + 1) * BR : (j + 2) * BR] = acc[k * GP : (k + 1) * GP]


def turn_kernel(x_ref, xt_ref):
    for m in range(4):
        wide = x_ref[pl.ds(m * 512, 512), :].astype(F32)
        for slot, amount in enumerate(SHIFTS):
            xt_ref[slot, :, pl.ds(m * 512, 512)] = column_shift(wide, amount).T.astype(BF)


def middle_kernel(pre_ref, sums_ref, hg_ref, pw_ref, out_ref, gp_ref, gproj_ref, vec_ref):
    pre = pre_ref[0:GP, :]
    act = jnp.maximum(pre, 0.0).astype(BF)
    pool = sums_ref[:, 0:BR] * (1.0 / 4096.0)
    hsum = sums_ref[:, BR : 2 * BR]
    act4 = jnp.maximum(pool, 0.0).astype(BF)
    low = pw_ref[0:1024, :]
    high = pw_ref[1024:1280, :]
    const = jnp.dot(act4, high, preferred_element_type=F32)
    head = jnp.dot(act, low, preferred_element_type=F32) + const[0:1, :]
    out_ref[...] = head.astype(BF)
    hg = hg_ref[...]
    back = lax.dot_general(hg, low, (((1,), (1,)), ((), ())), preferred_element_type=F32)
    gp_ref[...] = jnp.where(pre > 0, back, 0.0).astype(BF)
    gproj_ref[...] = lax.dot_general(act, hg, (((0,), (0,)), ((), ())), preferred_element_type=F32).astype(BF)
    pool_grad = lax.dot_general(
        hsum, high.astype(F32), (((1,), (1,)), ((), ())), precision=HIGH, preferred_element_type=F32
    )
    vec_ref[:, 0:BR] = jnp.where(pool > 0, pool_grad, 0.0)
    vec_ref[:, BR : 2 * BR] = act4.astype(F32)
    vec_ref[:, 2 * BR : 3 * BR] = hsum


def backward_kernel(core_ref, xt_ref, g_ref, own, other, colsum_ref, vec_ref, dx_ref, dws_ref, dwo_ref, w, gpad, dw):
    c = core_ref[0]
    join_weights(c, own, other, w)
    gpad[0 : PAD * GP, :] = jnp.zeros((PAD * GP, 768), BF)
    gpad[PAD * GP + HALF :, :] = jnp.zeros((PAD * GP, 768), BF)
    gpad[PAD * GP : PAD * GP + HALF, :] = g_ref[:, BR:]
    dw[0] = jnp.dot(xt_ref[0], g_ref[:, 0:BR], preferred_element_type=F32)
    for j in range(3):
        cols = slice((j + 1) * BR, (j + 2) * BR)
        for a in range(3):
            delta = 3 * (j + 1) * (a - 1) * GP
            x_low, x_high = max(delta, 0), HALF + min(delta, 0)
            g_low, g_high = max(-delta, 0), HALF - max(delta, 0)
            left = jnp.concatenate([xt_ref[shift_slot(j, b), :, x_low:x_high] for b in range(3)], axis=0)
            part = jnp.dot(left, g_ref[g_low:g_high, cols], preferred_element_type=F32)
            start = 1 + 9 * j + 3 * a
            dw[start : start + 3] = part.reshape(3, CH, BR)
    pool_grad = vec_ref[:, 0:BR]
    dw[28] = lax.dot_general(
        colsum_ref[...], pool_grad, (((0,), (0,)), ((), ())), precision=HIGH, preferred_element_type=F32
    ) * (0.125 / 4096.0)
    field = lax.dot_general(
        pool_grad, w[28].astype(F32), (((1,), (1,)), ((), ())), precision=HIGH, preferred_element_type=F32
    )[0:1, :] * (1.0 / 4096.0)
    for m in range(4):
        rows = pl.ds(m * 512, 512)
        acc = field + lax.dot_general(
            g_ref[rows, 0:BR], w[0], (((1,), (1,)), ((), ())), preferred_element_type=F32
        )
        for j in range(3):
            steps = valid_steps(j, m, -1)
            left = jnp.concatenate([gpad[pl.ds((PAD + low) * GP, 512), j * BR : (j + 1) * BR] for _, low in steps], axis=1)
            right = jnp.concatenate(
                [w[1 + 9 * j + 3 * a : 4 + 9 * j + 3 * a].reshape(3 * CH, BR) for a, _ in steps], axis=1
            )
            spread = lax.dot_general(left, right, (((1,), (1,)), ((), ())), preferred_element_type=F32)
            for b in range(3):
                acc = acc + column_shift(spread[:, b * CH : (b + 1) * CH], -(b - 1) * 12 * (j + 1))
        low, high = acc[:, 0:64], acc[:, 64:128]
        dx_ref[0, rows, :] = jnp.where(c == 0, low, high).astype(BF)
        dx_ref[1, rows, :] = jnp.where(c == 0, high, low).astype(BF)
    dws_ref[...] = dw[:, pl.ds(pl.multiple_of(c * 64, 64), 64), :]
    dwo_ref[...] = dw[:, pl.ds(pl.multiple_of((1 - c) * 64, 64), 64), :].astype(BF)


def call(kernel, out_shape, scratch, flops, *args, scalar=False):
    specs = [pl.BlockSpec(memory_space=pltpu.VMEM) for _ in args]
    if scalar:
        specs[0] = pl.BlockSpec(memory_space=pltpu.SMEM)
    moved = sum(a.size * a.dtype.itemsize for a in jax.tree.leaves((args, out_shape)))
    return pl.pallas_call(
        kernel,
        out_shape=out_shape,
        in_specs=specs,
        out_specs=jax.tree.map(lambda _: pl.BlockSpec(memory_space=pltpu.VMEM), out_shape),
        scratch_shapes=scratch,
        compiler_params=pltpu.CompilerParams(vmem_limit_bytes=56 * 2**20),
        cost_estimate=pl.CostEstimate(flops=flops, bytes_accessed=moved, transcendentals=0),
    )(*args)


def swap(value):
    return lax.ppermute(value, "core", [(0, 1), (1, 0)])


def local(features, head_grad, branch_weight, proj_weight):
    shape = jax.ShapeDtypeStruct
    plane = ("z", "y")
    core = lax.axis_index("core").astype(jnp.int32).reshape(1)
    other = swap(branch_weight)
    grouped = features.reshape(GP, GROUPS, CH).transpose(1, 0, 2)
    x = lax.all_to_all(grouped, plane, split_axis=0, concat_axis=0, tiled=True).reshape(HALF, CH)
    hg = head_grad.reshape(GP, BR)
    sums, colsum = call(
        forward_kernel,
        (shape((GROUPS, GP + 8, 1024), F32), shape((8, CH), F32)),
        [pltpu.VMEM((29, CH, BR), BF), pltpu.VMEM((7, HALF + 2 * PAD * GP, CH), BF)],
        4 * 10**9,
        core, x, hg, branch_weight, other, scalar=True,
    )
    pre = lax.psum_scatter(sums, plane, scatter_dimension=0, tiled=True)[0]
    turned = call(turn_kernel, shape((7, CH, HALF), BF), [], 10**8, x)
    vectors = pre[GP:, 0:512]
    vectors = vectors + swap(vectors)
    head_out, gp, gproj, vec = call(
        middle_kernel,
        (shape((GP, BR), BF), shape((GP, 1024), BF), shape((1024, BR), BF), shape((8, 768), F32)),
        [], 2 * 10**8,
        pre, vectors, hg, proj_weight,
    )
    every = lax.all_gather(gp, plane, axis=0, tiled=True)
    part = lax.all_to_all(gproj.reshape(GROUPS, 64, BR), plane, split_axis=0, concat_axis=0, tiled=True)
    part = jnp.sum(part.astype(F32), axis=0)
    part = part + swap(part)
    part = part + lax.ppermute(part, "rep", [(0, 1), (1, 0), (2, 3), (3, 2)])
    part = part + lax.ppermute(part, "rep", [(0, 2), (2, 0), (1, 3), (3, 1)])
    spread = jnp.broadcast_to(part.astype(BF)[None], (GROUPS, 64, BR))
    spread = lax.all_to_all(spread, plane, split_axis=0, concat_axis=0, tiled=True).reshape(1024, BR)
    slabs = lax.all_gather(vec[0, BR:].reshape(2, BR), "rep", axis=0, tiled=False)
    last = jnp.einsum("sa,sb->ab", slabs[:, 0], slabs[:, 1], precision=HIGH)
    grad_proj = jnp.concatenate([spread.astype(F32), last], axis=0)
    dx, dws, dwo = call(
        backward_kernel,
        (shape((2, HALF, 64), BF), shape((29, 64, BR), F32), shape((29, 64, BR), BF)),
        [pltpu.VMEM((29, CH, BR), BF), pltpu.VMEM((HALF + 2 * PAD * GP, 768), BF), pltpu.VMEM((29, CH, BR), F32)],
        8 * 10**9,
        core, turned, every, branch_weight, other, colsum, vec, scalar=True,
    )
    mine, theirs = dx[0], swap(dx[1])
    first = jnp.where(core[0] == 0, mine, theirs).reshape(GROUPS, 1, 2, COLS, 64)
    second = jnp.where(core[0] == 0, theirs, mine).reshape(GROUPS, 1, 2, COLS, 64)
    grad_features = jnp.concatenate([first, second], axis=1).reshape(1, 64, COLS, 64)
    dw = (dws + swap(dwo).astype(F32)).astype(BF).reshape(4, 464, BR)
    dw = lax.all_to_all(dw, "rep", split_axis=0, concat_axis=0, tiled=True)
    dw = jnp.sum(dw.astype(F32), axis=0).astype(BF)
    grad_branch = lax.all_gather(dw, "rep", axis=0, tiled=True).astype(F32).reshape(29, 64, BR)
    return head_out.reshape(head_grad.shape), grad_features, grad_branch, grad_proj


def solution(mesh):
    fine = Mesh(mesh.devices.reshape(4, 4, 2, 4), ("z", "y", "core", "rep"))
    tile = ("z", "y", "core")
    return jax.shard_map(
        local,
        mesh=fine,
        in_specs=(P("rep", tile, None, None), P("rep", tile, None, None), P(None, tile, None), P()),
        out_specs=(P("rep", tile, None, None), P("rep", None, None, tile), P(None, tile, None), P()),
        check_vma=False,
    )
```

time: 581 us -> 249 us (0.43); the launches traced: 571 us -> 245 us
  waiting for transfers between devices: 316 us -> 123 us
  local copies, waits for them, and re-layouts: 155 us -> 8.5 us
  matrix products: 71.6 us -> 1.14 us
  blocking collectives: 0 us -> 35.5 us
  Pallas kernels: 0 us -> 28.9 us
  starting transfers between devices: 9.77 us -> 26 us
    psum x2 -> x0, waiting for transfers between devices: 127 us -> none  [the longest x1 70.6 us: local(): grad_proj = lax.psum(proj_part, ('tile', 'rep'))]
    reduce_scatter x1 -> x0, waiting for transfers between devices: 125 us -> none  [local(): lax.psum_scatter(jnp.concatenate(columns, axis=1), 'tile', scatter_dimens...]
    unnamed x4 -> x3, waiting for transfers between devices: 0.07 us -> 83.7 us
    dot_general x17 -> x1, matrix products: 71.6 us -> 1.14 us  [local(): last = jnp.einsum('sa,sb->ab', slabs[:, 0], slabs[:, 1], precision=HIGH)]
    concatenate x31 -> x1, local copies, waits for them, and re-layouts: 54.7 us -> 1.05 us  [local(): jnp.concatenate([first, second], axis=1).reshape(1, 64, COLS, 64)]
    unnamed x172 -> x11, local copies, waits for them, and re-layouts: 54.2 us -> 2.26 us
    all_gather x1, waiting for transfers between devices: 53.3 us -> 14.3 us  [local(): every = lax.all_gather(gp, plane, axis=0, tiled=True)]
    slice x3, local copies, waits for them, and re-layouts: 33.1 us -> 1.47 us  [the longest x1 0.73 us: local(): vec[0, BR:].reshape(2, BR)]
  transfers between devices with their start and end apart: 5 -> 12, of which waited for: 5 -> 6; matrix products, arithmetic and copies ran while one was open for 14% -> 5% of each run, Pallas kernels for 0% -> 7%
where the time goes in v1:
time: 249 us; the launch traced here: 245 us
  waiting for transfers between devices  123 us (49%)
  blocking collectives  35.5 us (14%)
  Pallas kernels  28.9 us (12%)
  starting transfers between devices  26 us (10%)
  between operations  14.1 us (6%)
  local copies, waits for them, and re-layouts  8.5 us (3%)
  other arithmetic  8.16 us (3%)
    unnamed x3, waiting for transfers between devices  83.7 us
    pallas_call x4, Pallas kernels, call(): pl.pallas_call(kernel, out_shape=out_shape, in_specs=specs, out_specs=jax...  28.9 us
    all_to_all x1, blocking collectives, local(): lax.all_to_all(gproj.reshape(GROUPS, 64, BR), plane, split_axis=0, concat...  15.5 us
    all_gather x1, waiting for transfers between devices, local(): every = lax.all_gather(gp, plane, axis=0, tiled=True)  14.3 us
    all_gather x1, blocking collectives, local(): lax.all_gather(dw, 'rep', axis=0, tiled=True).astype(F32)  12 us
    all_to_all x1, waiting for transfers between devices, local(): lax.all_to_all(grouped, plane, split_axis=0, concat_axis=0, tiled=True)  11 us
    all_to_all x1, waiting for transfers between devices, local(): dw = lax.all_to_all(dw, 'rep', split_axis=0, concat_axis=0, tiled=True)  9.76 us
    all_gather x1, blocking collectives, local(): lax.all_gather(vec[0, BR:].reshape(2, BR), 'rep', axis=0, tiled=False)  8.08 us
  transfers between devices with their start and end apart: 12, of which 6 were waited for; matrix products, arithmetic and copies ran while one was open for 5% of the time, Pallas kernels for 7%

profile of v1, /device:TPU:1, one launch (start us, length us, event | category | flops | bytes accessed | tf_op | source)
XLA Modules:
  0.0 245.2 jit_solution(12526117361220622035)
XLA Ops:
  7.2 1.5 collective-permute-start
  10.8 7.9 %all-to-all-start = ((bf16[16,128,128]{2,1,0:T(8,128)(2,1)}), bf16[16,128,128]{2,1,0:T(8,128)(2,1)S(1)}, u32[]{:S(2)}, u32[]{:S(2)}) async-start(bf16[16,128,128]{2,1,0:T(8,128)(2,1)} %bitcast.33), calls=%async_computation | async-start | bytes 1048576 | tf_op jit(solution)/shard_map/all_to_all | solution.py:187
  18.7 11.0 %all-to-all-done = bf16[16,128,128]{2,1,0:T(8,128)(2,1)S(1)} async-done(((bf16[16,128,128]{2,1,0:T(8,128)(2,1)}), bf16[16,128,128]{2,1,0:T(8,128)(2,1)S(1)}, u32[]{:S(2)}, u32[]{:S(2)}) %all-to-all-start) | async-done | bytes 524320 | tf_op jit(solution)/shard_map/all_to_all | solution.py:187
  30.8 9.4 %shard_map.75 = (f32[16,136,1024]{2,1,0:T(8,128)}, f32[8,128]{1,0:T(8,128)}) custom-call(s32[1]{0:T(128)} %bitcast.core_ref, bf16[2048,128]{1,0:T(8,128)(2,1)} %bitcast.38, bf16[128,256]{1,0:T(8,128)(2,1)} %bitcast.46, bf16[29,64,256]{2,1,0:T(8,128)(2,1)} %own.3, bf16[29,64,256]{2,1,0:T(8,128)(2,1)} %copy-done.4), custom_call_target="tpu_custom_call" | custom-call | flops 4000000000 | bytes 11407364 | tf_op jit(solution)/shard_map/pallas_call | solution.py:166
  40.3 83.7 %reduce-scatter.4.cloned.1.call-done = f32[1,136,1024]{2,1,0:T(8,128)} async-done(((f32[16,136,1024]{2,1,0:T(8,128)}), f32[1,136,1024]{2,1,0:T(8,128)}) %reduce-scatter.4.cloned.1.call-update) | async-done | bytes 557072
  124.7 1.7 collective-permute-start.1
  127.2 1.3 slice_add_fusion.sums_ref
  128.5 2.8 %shard_map.76 = (bf16[128,256]{1,0:T(8,128)(2,1)}, bf16[128,1024]{1,0:T(8,128)(2,1)}, bf16[1024,256]{1,0:T(8,128)(2,1)}, f32[8,768]{1,0:T(8,128)}) custom-call(f32[136,1024]{1,0:T(8,128)} %bitcast.43, f32[8,512]{1,0:T(8,128)} %slice_add_fusion.sums_ref, bf16[128,256]{1,0:T(8,128)(2,1)} %bitcast.47, bf16[1280,256]{1,0:T(8,128)(2,1)} %pw_ref.1), custom_call_target="tpu_custom_call" | custom-call | flops 200000000 | bytes 2170880 | tf_op jit(solution)/shard_map/pallas_call | solution.py:166
  131.4 15.5 %all_to_all.20 = bf16[16,64,256]{2,1,0:T(8,128)(2,1)S(1)} all-to-all(bf16[16,64,256]{2,1,0:T(8,128)(2,1)} %bitcast.45), channel_id=1, replica_groups=mesh['z'=4,'y'=4,'core'=2,'rep'=4] {'z','y'}, dimensions={0} | all-to-all | bytes 1048576 | tf_op jit(solution)/shard_map/all_to_all | solution.py:207
  146.9 3.3 %collective-permute-start.4 = (f32[64,256]{1,0:T(8,128)S(1)}, f32[64,256]{1,0:T(8,128)S(1)}, u32[]{:S(2)}, u32[]{:S(2)}) collective-permute-start(f32[64,256]{1,0:T(8,128)S(1)} %convert_reduce_fusion), channel_id=1, source_target_pairs={{0,4},{4,0},{1,5},{5,1},{2,6},{6,2},{3,7},{7,3},{8,12},{12,8},{9,1... | collective-permute-start | bytes 196616 | tf_op jit(solution)/shard_map/ppermute | solution.py:178
  150.2 3.8 %shard_map.77.xt_ref = bf16[7,128,2048]{2,1,0:T(8,128)(2,1)} custom-call(bf16[2048,128]{1,0:T(8,128)(2,1)} %bitcast.39), custom_call_target="tpu_custom_call" | custom-call | flops 100000000 | bytes 4194304 | tf_op jit(solution)/shard_map/pallas_call | solution.py:166
  154.0 1.2 collective-permute-start.5
  156.0 8.1 %all_gather.11 = f32[4,2,256]{2,1,0:T(2,128)S(1)} all-gather(f32[1,2,256]{2,1,0:T(2,128)S(1)} %all_gather_reshape_squeeze.3), channel_id=1, replica_groups=mesh['z'=4,'y'=4,'core'=2,'rep'=4] {'rep'}, dimensions={0}, use_global_device_ids=true | all-gather | bytes 10240 | tf_op jit(solution)/shard_map/all_gather | solution.py:214
  164.1 1.6 collective-permute-start.6
  165.7 3.1 %collective-permute-done.6 = f32[64,256]{1,0:T(8,128)S(1)} collective-permute-done((f32[64,256]{1,0:T(8,128)S(1)}, f32[64,256]{1,0:T(8,128)S(1)}, u32[]{:S(2)}, u32[]{:S(2)}) %collective-permute-start.6) | collective-permute-done | bytes 65568 | tf_op jit(solution)/shard_map/ppermute | solution.py:211
  169.7 3.8 %all-to-all-start.3 = ((bf16[16,64,256]{2,1,0:T(8,128)(2,1)}), bf16[16,64,256]{2,1,0:T(8,128)(2,1)S(1)}, u32[]{:S(2)}, u32[]{:S(2)}) async-start(bf16[16,64,256]{2,1,0:T(8,128)(2,1)} %broadcast_in_dim.2), calls=%async_computation.3 | async-start | bytes 1048576 | tf_op jit(solution)/shard_map/all_to_all | solution.py:213
  173.5 14.3 %all-gather.2.cloned.1.call-done.g_ref = bf16[2048,1024]{1,0:T(8,128)(2,1)} async-done(((bf16[128,1024]{1,0:T(8,128)(2,1)}), bf16[2048,1024]{1,0:T(8,128)(2,1)}) %all-gather.2.cloned.1.call-update) | async-done | bytes 4194320 | tf_op jit(solution)/shard_map/all_gather | solution.py:206
  187.8 12.8 %shard_map.78 = (bf16[2,2048,64]{2,1,0:T(8,128)(2,1)}, f32[29,64,256]{2,1,0:T(8,128)}, bf16[29,64,256]{2,1,0:T(8,128)(2,1)}) custom-call(s32[1]{0:T(128)} %bitcast.core_ref, bf16[7,128,2048]{2,1,0:T(8,128)(2,1)} %shard_map.77.xt_ref, bf16[2048,1024]{1,0:T(8,128)(2,1)} %all-gather.2.cloned.1.call-done.g_ref, bf16[29,64,256]{2,1,0:T(8,128)(2,1)} %own.3, ...), custom_call_target="tpu_custom_call" | custom-call | flops 8000000000 | bytes 13168644 | tf_op jit(solution)/shard_map/pallas_call | solution.py:166
  202.9 1.9 slice_bitcast_fusion
  204.8 2.4 add_convert_fusion
  207.2 4.1 %all-to-all-start.1 = ((bf16[4,464,256]{2,1,0:T(8,128)(2,1)}), bf16[4,464,256]{2,1,0:T(8,128)(2,1)S(1)}, u32[]{:S(2)}, u32[]{:S(2)}) async-start(bf16[4,464,256]{2,1,0:T(8,128)(2,1)} %bitcast.11), calls=%async_computation.1 | async-start | bytes 1900544 | tf_op jit(solution)/shard_map/all_to_all | solution.py:229
  214.9 9.8 %all-to-all-done.1 = bf16[4,464,256]{2,1,0:T(8,128)(2,1)S(1)} async-done(((bf16[4,464,256]{2,1,0:T(8,128)(2,1)}), bf16[4,464,256]{2,1,0:T(8,128)(2,1)S(1)}, u32[]{:S(2)}, u32[]{:S(2)}) %all-to-all-start.1) | async-done | bytes 950304 | tf_op jit(solution)/shard_map/all_to_all | solution.py:229
  224.9 12.0 %all_gather.10 = bf16[1856,256]{1,0:T(8,128)(2,1)S(1)} all-gather(bf16[464,256]{1,0:T(8,128)(2,1)S(1)} %reduce_sum.21), channel_id=1, replica_groups=mesh['z'=4,'y'=4,'core'=2,'rep'=4] {'rep'}, dimensions={0}, use_global_device_ids=true | all-gather | bytes 1187840 | tf_op jit(solution)/shard_map/all_gather | solution.py:231
  236.9 1.5 convert.3
  (41 shorter events, 12.6 us)
Async XLA Ops:
  7.2 22.5 %collective-permute-start = (bf16[29,64,256]{2,1,0:T(8,128)(2,1)}, bf16[29,64,256]{2,1,0:T(8,128)(2,1)S(1)}, u32[]{:S(2)}, u32[]{:S(2)}) collective-permute-start(bf16[29,64,256]{2,1,0:T(8,128)(2,1)} %own.3), channel_id=1, source_target_pairs={{0,4},{4,0},{1,5},{5,1},{2,6},{6,2},{3,7},{7,3},{8,12},{12,8},{9,1... | collective-permute-start | bytes 2850824 | tf_op jit(solution)/shard_map/ppermute | solution.py:178
  10.8 18.9 %all-to-all-start = ((bf16[16,128,128]{2,1,0:T(8,128)(2,1)}), bf16[16,128,128]{2,1,0:T(8,128)(2,1)S(1)}, u32[]{:S(2)}, u32[]{:S(2)}) async-start(bf16[16,128,128]{2,1,0:T(8,128)(2,1)} %bitcast.33), calls=%async_computation | async-start | bytes 1048576 | tf_op jit(solution)/shard_map/all_to_all | solution.py:187
  18.6 105.3 %reduce-scatter.4.cloned.1.call-start = ((), (), s32[]{:S(2)}) async-start(), calls=%async_computation.6 | async-start | bytes 9469952
  29.7 0.8 copy-start
  29.7 1.1 copy-start.4
  40.2 147.6 %all-gather.2.cloned.1.call-start = ((), (), s32[]{:S(2)}) async-start(), calls=%async_computation.5 | async-start | bytes 4456448 | tf_op jit(solution)/shard_map/all_gather | solution.py:206
  124.7 2.5 %collective-permute-start.1 = (f32[8,512]{1,0:T(8,128)S(1)}, f32[8,512]{1,0:T(8,128)S(1)}, u32[]{:S(2)}, u32[]{:S(2)}) collective-permute-start(f32[8,512]{1,0:T(8,128)S(1)} %slice.24), channel_id=1, source_target_pairs={{0,4},{4,0},{1,5},{5,1},{2,6},{6,2},{3,7},{7,3},{8,12},{12,8},{9,1... | collective-permute-start | bytes 49160 | tf_op jit(solution)/shard_map/ppermute | solution.py:178
  146.9 7.1 %collective-permute-start.4 = (f32[64,256]{1,0:T(8,128)S(1)}, f32[64,256]{1,0:T(8,128)S(1)}, u32[]{:S(2)}, u32[]{:S(2)}) collective-permute-start(f32[64,256]{1,0:T(8,128)S(1)} %convert_reduce_fusion), channel_id=1, source_target_pairs={{0,4},{4,0},{1,5},{5,1},{2,6},{6,2},{3,7},{7,3},{8,12},{12,8},{9,1... | collective-permute-start | bytes 196616 | tf_op jit(solution)/shard_map/ppermute | solution.py:178
  154.0 10.0 %collective-permute-start.5 = (f32[64,256]{1,0:T(8,128)S(1)}, f32[64,256]{1,0:T(8,128)S(1)}, u32[]{:S(2)}, u32[]{:S(2)}) collective-permute-start(f32[64,256]{1,0:T(8,128)S(1)} %add.19), channel_id=1, source_target_pairs={{0,1},{1,0},{2,3},{3,2},{4,5},{5,4},{6,7},{7,6},{8,9},{9,8},{10,11... | collective-permute-start | bytes 196616 | tf_op jit(solution)/shard_map/ppermute | solution.py:210
  164.1 4.7 %collective-permute-start.6 = (f32[64,256]{1,0:T(8,128)S(1)}, f32[64,256]{1,0:T(8,128)S(1)}, u32[]{:S(2)}, u32[]{:S(2)}) collective-permute-start(f32[64,256]{1,0:T(8,128)S(1)} %add.20), channel_id=1, source_target_pairs={{0,2},{2,0},{1,3},{3,1},{4,6},{6,4},{5,7},{7,5},{8,10},{10,8},{9,1... | collective-permute-start | bytes 196616 | tf_op jit(solution)/shard_map/ppermute | solution.py:211
  169.7 33.1 %all-to-all-start.3 = ((bf16[16,64,256]{2,1,0:T(8,128)(2,1)}), bf16[16,64,256]{2,1,0:T(8,128)(2,1)S(1)}, u32[]{:S(2)}, u32[]{:S(2)}) async-start(bf16[16,64,256]{2,1,0:T(8,128)(2,1)} %broadcast_in_dim.2), calls=%async_computation.3 | async-start | bytes 1048576 | tf_op jit(solution)/shard_map/all_to_all | solution.py:213
  200.7 4.1 %copy-start.1 = (f32[29,64,256]{2,1,0:T(8,128)S(1)}, f32[29,64,256]{2,1,0:T(8,128)}, u32[]{:S(2)}) copy-start(f32[29,64,256]{2,1,0:T(8,128)} %get-tuple-element.19) | copy-start | bytes 5701636
  200.7 4.1 %collective-permute-start.3 = (bf16[29,64,256]{2,1,0:T(8,128)(2,1)}, bf16[29,64,256]{2,1,0:T(8,128)(2,1)}, u32[]{:S(2)}, u32[]{:S(2)}) collective-permute-start(bf16[29,64,256]{2,1,0:T(8,128)(2,1)} %get-tuple-element.20), channel_id=1, source_target_pairs={{0,4},{4,0},{1,5},{5,1},{2,6},{6,2},{3,7},{7,3},{8,12},{12,8},{9,1... | collective-permute-start | bytes 2850824 | tf_op jit(solution)/shard_map/ppermute | solution.py:178
  204.8 7.7 %collective-permute-start.2 = (bf16[2048,64]{1,0:T(8,128)(2,1)}, bf16[2048,64]{1,0:T(8,128)(2,1)}, u32[]{:S(2)}, u32[]{:S(2)}) collective-permute-start(bf16[2048,64]{1,0:T(8,128)(2,1)} %slice_bitcast_fusion), channel_id=1, source_target_pairs={{0,4},{4,0},{1,5},{5,1},{2,6},{6,2},{3,7},{7,3},{8,12},{12,8},{9,1... | collective-permute-start | bytes 786440 | tf_op jit(solution)/shard_map/ppermute | solution.py:178
  207.2 4.1 %copy-start.3 = (f32[256,256]{1,0:T(8,128)S(1)}, f32[256,256]{1,0:T(8,128)}, u32[]{:S(2)}) copy-start(f32[256,256]{1,0:T(8,128)} %fusion) | copy-start | bytes 786436
  207.2 5.2 %copy-start.2 = (bf16[2,2048,64]{2,1,0:T(8,128)(2,1)S(1)}, bf16[2,2048,64]{2,1,0:T(8,128)(2,1)}, u32[]{:S(2)}) copy-start(bf16[2,2048,64]{2,1,0:T(8,128)(2,1)} %get-tuple-element.18) | copy-start | bytes 1572868
  207.2 17.4 %all-to-all-start.1 = ((bf16[4,464,256]{2,1,0:T(8,128)(2,1)}), bf16[4,464,256]{2,1,0:T(8,128)(2,1)S(1)}, u32[]{:S(2)}, u32[]{:S(2)}) async-start(bf16[4,464,256]{2,1,0:T(8,128)(2,1)} %bitcast.11), calls=%async_computation.1 | async-start | bytes 1900544 | tf_op jit(solution)/shard_map/all_to_all | solution.py:229
Sparse Core Ops, SparseCore 0:
  40.3 83.5 reduce-scatter.3
  131.5 56.2 all-gather.1

commit v2 on v1

v2 whole, which is shorter than its diff:
```python
import jax
import jax.numpy as jnp
from jax import lax
from jax.experimental import pallas as pl
from jax.experimental.pallas import tpu as pltpu
from jax.sharding import Mesh, PartitionSpec as P

GROUPS = 16
CH = 128
KCH = 512
BR = 256
HALF = 2048
PAD = 9
CUT = 15
SHIFTS = (0, -3, 3, -6, 6, -9, 9)
F32 = jnp.float32
BF = jnp.bfloat16
HIGH = lax.Precision.HIGHEST
ROWS_BY_COLS = (((1,), (1,)), ((), ()))
COLS_BY_COLS = (((0,), (0,)), ((), ()))


def shift_slot(j, b):
    return SHIFTS.index((b - 1) * 3 * (j + 1))


def column_shift(value, amount):
    if amount == 0:
        return value
    n = value.shape[0]
    col = lax.broadcasted_iota(jnp.int32, value.shape, 0) & 15
    rolled = pltpu.roll(value, (-amount) % n, 0)
    return jnp.where((col + amount >= 0) & (col + amount < 16), rolled, 0.0)


def wrap(value):
    return lax.rem(value + 8, 4)


def split_kernel(x_ref, hg_ref, first_ref, second_ref, wide):
    for t in range(GROUPS):
        wide[t] = x_ref[:, CH * t : CH * (t + 1)].astype(F32)
    for t in range(2):
        wide[GROUPS + t] = hg_ref[:, CH * t : CH * (t + 1)].astype(F32)
    for v in range(4):
        for t in range(GROUPS + 2):
            part = wide[t, pl.ds(v, 32, stride=4), :].astype(BF)
            if t < GROUPS:
                second_ref[t, 16 * v : 16 * (v + 1), :] = part[0:16]
                second_ref[t, 64 + 16 * v : 80 + 16 * v, :] = part[16:32]
                place = CH * (t % 4)
                first_ref[4 * (t // 4) + v, :, place : place + CH] = part
            else:
                place = KCH + CH * (t - GROUPS)
                for z in range(4):
                    first_ref[4 * z + v, :, place : place + CH] = part


def weight_copies(pos_ref, blocks, w, sem):
    y, c = pos_ref[1], pos_ref[2]
    places = [(0, 0, 29), (-1, 0, 29), (1, 0, 29), (2, 0, CUT), (2, CUT, 29)]
    copies = []
    for side in range(2):
        for k, (step, low, high) in enumerate(places):
            core = c if side == 0 else 1 - c
            start = pl.multiple_of(wrap(y + step) * CH + core * 64, 64)
            n = len(copies)
            copies.append(
                pltpu.make_async_copy(blocks[n], w.at[pl.ds(low, high - low), pl.ds(start, 64), :], sem.at[n])
            )
    return copies


def forward_kernel(pos_ref, x_ref, hg_ref, *refs):
    blocks, outs, (w, xs, total, sem) = refs[:10], refs[10:15], refs[15:]
    own_ref, plus_ref, minus_ref, plus_half, minus_half = outs
    copies = weight_copies(pos_ref, blocks, w, sem)
    for copy in copies:
        copy.start()
    wide = x_ref[:, 0:KCH].astype(F32)
    colsum = jnp.broadcast_to(jnp.sum(wide, axis=0, keepdims=True), (8, KCH))
    for slot, amount in enumerate(SHIFTS):
        if amount:
            xs[slot] = column_shift(wide, amount).astype(BF)
        else:
            xs[slot] = x_ref[:, 0:KCH]
    hsum = jnp.broadcast_to(jnp.sum(hg_ref[...].astype(F32), axis=0, keepdims=True), (8, BR))
    for copy in copies:
        copy.wait()
    pool = jnp.dot(colsum, w[28].astype(F32), precision=HIGH, preferred_element_type=F32)
    total[:, 0:BR] = jnp.dot(xs[0], w[0], preferred_element_type=F32)
    for j in range(3):
        cols = slice((j + 1) * BR, (j + 2) * BR)
        for a in (1, 0, 2):
            delta = 96 * (j + 1) * (a - 1)
            in_low, in_high = max(delta, 0), 512 + min(delta, 0)
            out_low, out_high = max(-delta, 0), 512 - max(delta, 0)
            left = jnp.concatenate([xs[shift_slot(j, b), in_low:in_high, :] for b in range(3)], axis=1)
            start = 1 + 9 * j + 3 * a
            part = jnp.dot(left, w[start : start + 3].reshape(3 * KCH, BR), preferred_element_type=F32)
            if a == 1:
                total[:, cols] = part
            else:
                total[out_low:out_high, cols] += part
    extra = jnp.concatenate([pool, hsum, jnp.zeros((8, 512), F32)], axis=1)
    z = pos_ref[0]

    def rows(step, low, size):
        return total[pl.ds(pl.multiple_of(wrap(z + step) * 128 + low, 64), size), :]

    own_ref[0:128, :] = rows(0, 0, 128)
    own_ref[128:136, :] = extra
    plus_ref[0:64, :] = rows(2, 0, 64)
    plus_ref[64:128, :] = rows(1, 64, 64)
    plus_ref[128:136, :] = extra
    minus_ref[0:64, :] = rows(2, 64, 64)
    minus_ref[64:72, :] = extra
    minus_ref[72:136, :] = rows(-1, 0, 64)
    plus_half[...] = rows(1, 0, 64)
    minus_half[0:64, :] = rows(-1, 64, 64)
    minus_half[64:72, :] = extra


def turn_kernel(x_ref, xt_ref, colsum_ref):
    total = jnp.zeros((1, CH), F32)
    for m in range(4):
        wide = x_ref[pl.ds(m * 512, 512), :].astype(F32)
        total = total + jnp.sum(wide, axis=0, keepdims=True)
        for slot, amount in enumerate(SHIFTS):
            xt_ref[slot, :, pl.ds(m * 512, 512)] = column_shift(wide, amount).T.astype(BF)
    colsum_ref[...] = jnp.broadcast_to(total, (8, CH))


def middle_kernel(pos_ref, own, from_low, from_high, half_a, half_b, x_ref, pw_ref, _, keep_ref, give_ref, pay_ref):
    top = own[0:64, :] + from_high[72:136, :] + half_a[...]
    bottom = own[64:136, :] + from_low[64:136, :] + half_b[...]
    pre = jnp.concatenate([top, bottom[0:64, :]], axis=0)
    act = jnp.maximum(pre, 0.0).astype(BF)
    low = pw_ref[0:1024, :]
    hg = x_ref[pl.ds(pl.multiple_of(pos_ref[0] * 128, 128), 128), KCH:]
    back = lax.dot_general(hg, low, ROWS_BY_COLS, preferred_element_type=F32)
    grads = jnp.where(pre > 0, back, 0.0)
    first = pos_ref[2] == 0
    keep_ref[0:8] = jnp.where(first, grads[:, 0:512], grads[:, 512:1024]).astype(BF).reshape(8, 16, 512)
    give_ref[0:8] = jnp.where(first, grads[:, 512:1024], grads[:, 0:512]).astype(BF).reshape(8, 16, 512)
    sums = jnp.concatenate([bottom[64:72, 0:512]] * 2, axis=0)
    one = sums.astype(BF).astype(F32)
    two = (sums - one).astype(BF).astype(F32)
    row = lax.broadcasted_iota(jnp.int32, sums.shape, 0)
    terms = jnp.where(row == 0, one, jnp.where(row == 1, two, jnp.where(row == 2, sums - one - two, 0.0))).astype(BF)
    keep_ref[8] = terms
    give_ref[8] = terms
    head = jnp.dot(act, low, preferred_element_type=F32).astype(BF)
    proj = lax.dot_general(act, hg, COLS_BY_COLS, preferred_element_type=F32).astype(BF)
    for t in range(GROUPS):
        pay_ref[t, 0:64, :] = proj[64 * t : 64 * (t + 1), :]
        pay_ref[t, 64:96, :] = head[32 * (t % 4) : 32 * (t % 4 + 1), :]


def pool_kernel(pos_ref, sums_ref, pw_ref, const_ref, grad_ref, outer_ref, whole):
    pool = sums_ref[:, 0:BR] * (1.0 / 4096.0)
    hsum = sums_ref[:, BR : 2 * BR]
    act = jnp.maximum(pool, 0.0).astype(BF)
    high = pw_ref[1024:1280, :]
    const_ref[...] = jnp.dot(act, high, preferred_element_type=F32)
    grad = lax.dot_general(hsum, high.astype(F32), ROWS_BY_COLS, precision=HIGH, preferred_element_type=F32)
    grad_ref[...] = jnp.where(pool > 0, grad, 0.0)
    whole[...] = 0.125 * lax.dot_general(
        act.astype(F32), hsum, COLS_BY_COLS, precision=HIGH, preferred_element_type=F32
    )
    chunk = pos_ref[0] * 4 + pos_ref[1]
    outer_ref[...] = whole[pl.ds(pl.multiple_of(chunk * 16, 16), 16), :]


def collect_kernel(pos_ref, pay_ref, const_ref, part_ref, head_ref, wide):
    total = pay_ref[0, 0:64, :].astype(F32)
    for t in range(1, GROUPS):
        total = total + pay_ref[t, 0:64, :].astype(F32)
    part_ref[...] = total
    for v in range(4):
        piece = pay_ref[4 * pos_ref[0] + v, 64:96, :].astype(F32) + const_ref[0:1, :]
        wide[0, pl.ds(v, 32, stride=4), :] = piece[:, 0:128]
        wide[1, pl.ds(v, 32, stride=4), :] = piece[:, 128:256]
    head_ref[:, 0:128] = wide[0].astype(BF)
    head_ref[:, 128:256] = wide[1].astype(BF)


def gather_copies(pos_ref, blocks, g, sem, pad):
    z, y, c = pos_ref[0], pos_ref[1], pos_ref[2]
    copies = []
    for side in range(2):
        half = c if side == 0 else 1 - c
        for place, far in enumerate((0, -1, 1, 2)):
            for k, step in enumerate((0, -1, 1, 2)):
                src = blocks[8 * side + 2 * place + k // 2].at[k % 2, side]
                v = wrap(y + jnp.where(half == 0, step, far))
                group = wrap(z + jnp.where(half == 0, far, step))
                cols = pl.ds(pl.multiple_of(512 * half, 512), 512)
                dst = g.at[pl.ds(2 * pad + 8 * group, 8), v, :, cols]
                copies.append(pltpu.make_async_copy(src, dst, sem.at[len(copies)]))
    return copies


def weight_grad_kernel(pos_ref, xt_ref, colsum_ref, grad_ref, *refs):
    blocks, (own_ref, other_ref), (g, dw, sem) = refs[:16], refs[-5:-3], refs[-3:]
    copies = gather_copies(pos_ref, blocks, g, sem, 0)
    for copy in copies:
        copy.start()
    for copy in copies:
        copy.wait()

    def grads(low, high, cols):
        return g[low // 64 : high // 64, :, :, cols].reshape(high - low, BR)

    dw[0] = jnp.dot(xt_ref[0], grads(0, HALF, slice(0, BR)), preferred_element_type=F32)
    for j in range(3):
        cols = slice((j + 1) * BR, (j + 2) * BR)
        for a in range(3):
            delta = 3 * (j + 1) * (a - 1) * 128
            x_low, x_high = max(delta, 0), HALF + min(delta, 0)
            g_low, g_high = max(-delta, 0), HALF - max(delta, 0)
            left = jnp.concatenate([xt_ref[shift_slot(j, b), :, x_low:x_high] for b in range(3)], axis=0)
            part = jnp.dot(left, grads(g_low, g_high, cols), preferred_element_type=F32)
            start = 1 + 9 * j + 3 * a
            dw[start : start + 3] = part.reshape(3, CH, BR)
    dw[28] = lax.dot_general(
        colsum_ref[...], grad_ref[...], COLS_BY_COLS, precision=HIGH, preferred_element_type=F32
    ) * (0.125 / 4096.0)
    c = pos_ref[2]
    own_ref[...] = dw[:, pl.ds(pl.multiple_of(c * 64, 64), 64), :].astype(BF)
    other_ref[...] = dw[:, pl.ds(pl.multiple_of((1 - c) * 64, 64), 64), :].astype(BF)


def field_grad_kernel(pos_ref, grad_ref, own, other, *refs):
    blocks, dx_ref, (g, w, whole, sem) = refs[:16], refs[-5], refs[-4:]
    copies = gather_copies(pos_ref, blocks, g, sem, PAD)
    for copy in copies:
        copy.start()
    c = pos_ref[2]
    w[:, pl.ds(pl.multiple_of(c * 64, 64), 64), :] = own[...]
    w[:, pl.ds(pl.multiple_of((1 - c) * 64, 64), 64), :] = other[...]
    g[0 : 2 * PAD] = jnp.zeros((2 * PAD, 4, 16, 1024), BF)
    g[2 * (PAD + GROUPS) :] = jnp.zeros((2 * PAD, 4, 16, 1024), BF)
    field = lax.dot_general(
        grad_ref[...], w[28].astype(F32), ROWS_BY_COLS, precision=HIGH, preferred_element_type=F32
    )[0:1, :] * (1.0 / 4096.0)
    for copy in copies:
        copy.wait()

    def grads(low, cols):
        return g[2 * (PAD + low) : 2 * (PAD + low + 4), :, :, cols].reshape(512, BR)

    for m in range(4):
        acc = field + lax.dot_general(
            grads(4 * m, slice(0, BR)), w[0], ROWS_BY_COLS, preferred_element_type=F32
        )
        for j in range(3):
            steps = []
            for a in range(3):
                low = 4 * m - 3 * (j + 1) * (a - 1)
                if low + 3 >= 0 and low < GROUPS:
                    steps.append((a, low))
            left = jnp.concatenate([grads(low, slice((j + 1) * BR, (j + 2) * BR)) for _, low in steps], axis=1)
            right = jnp.concatenate(
                [w[1 + 9 * j + 3 * a : 4 + 9 * j + 3 * a].reshape(3 * CH, BR) for a, _ in steps], axis=1
            )
            spread = lax.dot_general(left, right, ROWS_BY_COLS, preferred_element_type=F32)
            for b in range(3):
                acc = acc + column_shift(spread[:, b * CH : (b + 1) * CH], -(b - 1) * 3 * (j + 1))
        for row in range(8):
            for v in range(4):
                place = (4 * row + v) * 16
                whole[pl.ds(512 * m + 64 * row + v, 16, stride=4), :] = acc[place : place + 16, :]
    low, high = whole[:, 0:64], whole[:, 64:128]
    dx_ref[0] = jnp.where(c == 0, low, high).astype(BF)
    dx_ref[1] = jnp.where(c == 0, high, low).astype(BF)


def add_kernel(pos_ref, own, other, *outs):
    r = pos_ref[3]
    for k in range(4):
        rows = pl.ds(pl.multiple_of(wrap(r + k) * 464, 16), 464)
        outs[k][...] = (own[rows, :].astype(F32) + other[rows, :].astype(F32)).astype(BF)


def join_kernel(pos_ref, own, below, above, far_low, far_high, out_ref):
    r = pos_ref[3]

    def place(step, low, size):
        return pl.ds(pl.multiple_of(wrap(r + step) * 464 + low, 8), size)

    out_ref[place(0, 0, 464), :] = own[...].astype(F32)
    out_ref[place(-1, 0, 464), :] = below[...].astype(F32)
    out_ref[place(1, 0, 464), :] = above[...].astype(F32)
    out_ref[place(2, 0, 240), :] = far_low[...].astype(F32)
    out_ref[place(2, 240, 224), :] = far_high[...].astype(F32)


def call(kernel, out_shape, scratch, flops, *args, scalar=True, raw=0):
    specs = [pl.BlockSpec(memory_space=pltpu.VMEM) for _ in args]
    if scalar:
        specs[0] = pl.BlockSpec(memory_space=pltpu.SMEM)
    for k in range(raw):
        specs[len(args) - 1 - k] = pl.BlockSpec(memory_space=pl.ANY)
    moved = sum(a.size * a.dtype.itemsize for a in jax.tree.leaves((args, out_shape)))
    return pl.pallas_call(
        kernel,
        out_shape=out_shape,
        in_specs=specs,
        out_specs=jax.tree.map(lambda _: pl.BlockSpec(memory_space=pltpu.VMEM), out_shape),
        scratch_shapes=scratch,
        compiler_params=pltpu.CompilerParams(vmem_limit_bytes=60 * 2**20),
        cost_estimate=pl.CostEstimate(flops=flops, bytes_accessed=moved, transcendentals=0),
    )(*args)


def gate(values, after):
    anywhere = pl.BlockSpec(memory_space=pl.ANY)
    return pl.pallas_call(
        lambda *refs: None,
        out_shape=tuple(jax.ShapeDtypeStruct(v.shape, v.dtype) for v in values),
        in_specs=[anywhere] * (len(values) + len(after)),
        out_specs=(anywhere,) * len(values),
        input_output_aliases={k: k for k in range(len(values))},
        cost_estimate=pl.CostEstimate(flops=0, bytes_accessed=0, transcendentals=0),
    )(*values, *after)


def swap(value):
    return lax.ppermute(value, "core", [(0, 1), (1, 0)])


def send(value, axis, step):
    return lax.ppermute(value, axis, [(k, (k + step) % 4) for k in range(4)])


def pair(value, axis, bit):
    return lax.ppermute(value, axis, [(k, k ^ bit) for k in range(4)])


def cross(value, step, turn):
    pairs = []
    for z in range(4):
        for y in range(4):
            for c in range(2):
                along_y = (c == 0) != turn
                to = (z, (y + step) % 4) if along_y else ((z + step) % 4, y)
                pairs.append(((4 * z + y) * 2 + c, (4 * to[0] + to[1]) * 2 + c))
    return lax.ppermute(value, ("z", "y", "core"), pairs)


def local(features, head_grad, branch_weight, proj_weight):
    shape = jax.ShapeDtypeStruct
    plane = ("z", "y")
    pos = jnp.stack([lax.axis_index(n).astype(jnp.int32) for n in ("z", "y", "core", "rep")])

    def exchange(value):
        return lax.all_to_all(value, plane, split_axis=0, concat_axis=0, tiled=True)

    first, second = call(
        split_kernel,
        (shape((GROUPS, 32, KCH + BR), BF), shape((GROUPS, 128, CH), BF)),
        [pltpu.VMEM((GROUPS + 2, 128, CH), F32)], 10**6,
        features.reshape(128, 2048), head_grad.reshape(128, BR), scalar=False,
    )
    below, above = send(branch_weight, "y", 1), send(branch_weight, "y", -1)
    x = exchange(first).reshape(512, KCH + BR)
    below, above = gate((below, above), (x,))
    blocks = [branch_weight, below, above, send(below[0:CUT], "y", 1), send(above[CUT:29], "y", -1)]
    blocks = blocks + [swap(b) for b in blocks]
    own, plus, minus, plus_half, minus_half = call(
        forward_kernel,
        tuple(shape((n, 1024), F32) for n in (136, 136, 136, 64, 72)),
        [
            pltpu.VMEM((29, KCH, BR), BF), pltpu.VMEM((7, 512, KCH), BF), pltpu.VMEM((512, 1024), F32),
            pltpu.SemaphoreType.DMA((10,)),
        ],
        4 * 10**9, pos, x, head_grad.reshape(128, BR), *blocks, raw=10,
    )
    from_low, from_high = send(plus, "z", 1), send(minus, "z", -1)
    half_a = send(plus_half + from_low[0:64], "z", 1)
    half_b = send(minus_half + from_high[0:72], "z", -1)
    (second,) = gate((second,), (own,))
    turned, colsum = call(
        turn_kernel, (shape((7, CH, HALF), BF), shape((8, CH), F32)), [], 10**8,
        exchange(second).reshape(HALF, CH), scalar=False,
    )
    keep, give, pay = call(
        middle_kernel,
        (shape((9, 16, 512), BF), shape((9, 16, 512), BF), shape((GROUPS, 96, BR), BF)),
        [], 2 * 10**8, pos, own, from_low, from_high, half_a, half_b, x, proj_weight, turned, raw=1,
    )
    block = jnp.stack([keep, swap(give)])
    near = [block, cross(block, 1, False), cross(block, -1, False), cross(block, 2, False)]
    low = jnp.stack([near[0][:, 0:8], near[1][:, 0:8]])
    high = jnp.stack([near[2][:, 0:8], near[3][:, 0:8]])
    low_below, high_above = cross(low, 1, True), cross(high, -1, True)
    high_below, low_above = cross(high, 1, True), cross(low, -1, True)
    every = [
        low, high, low_below, high_below, low_above, high_above, cross(low_below, 1, True), cross(high_above, -1, True)
    ]
    every = every + [swap(piece) for piece in every]
    sums = jnp.sum(jnp.stack([piece[:, 8] for piece in near]).astype(F32), axis=(0, 1, 2))
    sums = jnp.broadcast_to(sums[None], (8, 512))
    sums = jnp.where(pos[2] == 0, sums, swap(sums))
    const, pool_grad, outer = call(
        pool_kernel, (shape((8, BR), F32), shape((8, BR), F32), shape((16, BR), F32)), [pltpu.VMEM((256, BR), F32)],
        10**7, pos, sums, proj_weight,
    )
    (pay,) = gate((pay,), (low, high))
    part, head_out = call(
        collect_kernel, (shape((64, BR), F32), shape((128, BR), BF)), [pltpu.VMEM((2, 128, 128), F32)],
        10**6, pos, exchange(pay), const,
    )
    part = jnp.concatenate([part + swap(part), outer], axis=0)
    part = part + pair(part, "rep", 1)
    part = part + pair(part, "rep", 2)
    part = exchange(jnp.broadcast_to(part.astype(BF)[None], (GROUPS, 80, BR))).astype(F32)
    grad_proj = jnp.concatenate([part[:, 0:64].reshape(1024, BR), part[:, 64:80].reshape(256, BR)], axis=0)
    dw, dw_other = call(
        weight_grad_kernel,
        (shape((29, 64, BR), BF), shape((29, 64, BR), BF)),
        [pltpu.VMEM((2 * GROUPS, 4, 16, 1024), BF), pltpu.VMEM((29, CH, BR), F32), pltpu.SemaphoreType.DMA((32,))],
        4 * 10**9, pos, turned, colsum, pool_grad, *every, raw=16,
    )
    quarters = call(
        add_kernel, (shape((464, BR), BF),) * 4, [], 10**6, pos, dw.reshape(1856, BR), swap(dw_other).reshape(1856, BR)
    )
    dx = call(
        field_grad_kernel,
        shape((2, HALF, 64), BF),
        [
            pltpu.VMEM((2 * (GROUPS + 2 * PAD), 4, 16, 1024), BF), pltpu.VMEM((29, CH, BR), BF),
            pltpu.VMEM((HALF, CH), F32), pltpu.SemaphoreType.DMA((32,)),
        ],
        4 * 10**9, pos, pool_grad, branch_weight, blocks[5], *every, quarters[0], raw=17,
    )
    terms = [quarters[0]] + [send(quarters[k], "rep", k) for k in (1, 3, 2)]
    dw = sum(term.astype(F32) for term in terms).astype(BF)
    below, above = send(dw, "rep", 1), send(dw, "rep", -1)
    far_low, far_high = send(below[0:240], "rep", 1), send(above[240:464], "rep", -1)
    grad_branch = call(
        join_kernel, shape((1856, BR), F32), [], 10**6, pos, dw, below, above, far_low, far_high
    ).reshape(29, 64, BR)
    mine, theirs = dx[0], swap(dx[1])
    even = jnp.where(pos[2] == 0, mine, theirs).reshape(GROUPS, 1, 2, 64, 64)
    odd = jnp.where(pos[2] == 0, theirs, mine).reshape(GROUPS, 1, 2, 64, 64)
    grad_features = jnp.concatenate([even, odd], axis=1).reshape(1, 64, 64, 64)
    return head_out.reshape(head_grad.shape), grad_features, grad_branch, grad_proj


def solution(mesh):
    fine = Mesh(mesh.devices.reshape(4, 4, 2, 4), ("z", "y", "core", "rep"))
    tile = ("z", "y", "core")
    return jax.shard_map(
        local,
        mesh=fine,
        in_specs=(P("rep", tile, None, None), P("rep", tile, None, None), P(None, tile, None), P()),
        out_specs=(P("rep", tile, None, None), P("rep", None, None, tile), P(None, tile, None), P()),
        check_vma=False,
    )
```

time: 249 us -> 234 us (0.940)
  waiting for transfers between devices: 123 us -> 45.3 us
  starting transfers between devices: 26 us -> 65.5 us
  Pallas kernels: 28.9 us -> 47.7 us
  between operations: 14.1 us -> 1.02 us
  blocking collectives: 35.5 us -> 47.3 us
  local copies, waits for them, and re-layouts: 8.5 us -> 19.6 us
  other arithmetic: 8.16 us -> 5.62 us
    unnamed x3 -> x0, waiting for transfers between devices: 83.7 us -> none
    ppermute x2 -> x26, waiting for transfers between devices: 3.12 us -> 40.4 us  [the longest x15 27.6 us: send(): return lax.ppermute(value, axis, [(k, (k + step) % 4) for k in range(4)])]
    ppermute x2 -> x26, starting transfers between devices: 2.82 us -> 34.7 us  [the longest x15 17.3 us: send(): return lax.ppermute(value, axis, [(k, (k + step) % 4) for k in range(4)])]
    all_to_all x1 -> x2, blocking collectives: 15.5 us -> 47.3 us  [exchange(): return lax.all_to_all(value, plane, split_axis=0, concat_axis=0, tiled=True)]
    all_to_all x3 -> x2, waiting for transfers between devices: 20.8 us -> 0.5 us  [exchange(): return lax.all_to_all(value, plane, split_axis=0, concat_axis=0, tiled=True)]
    all_gather x2 -> x0, blocking collectives: 20.1 us -> none  [the longest x1 12 us: local(): lax.all_gather(dw, 'rep', axis=0, tiled=True).astype(F32)]
    pallas_call x4 -> x10, Pallas kernels: 28.9 us -> 47.7 us  [call(): pl.pallas_call(kernel, out_shape=out_shape, in_specs=specs, out_specs=jax...]
    all_gather x1 -> x0, waiting for transfers between devices: 14.3 us -> none  [local(): every = lax.all_gather(gp, plane, axis=0, tiled=True)]
  transfers between devices with their start and end apart: 12 -> 46, of which waited for: 6 -> 16; matrix products, arithmetic and copies ran while one was open for 5% -> 7% of each run, Pallas kernels for 7% -> 13%
where the time goes in v2:
time: 234 us; the launch traced here: 232 us
  starting transfers between devices  65.5 us (28%)
  Pallas kernels  47.7 us (20%)
  blocking collectives  47.3 us (20%)
  waiting for transfers between devices  45.3 us (19%)
  local copies, waits for them, and re-layouts  19.6 us (8%)
  other arithmetic  5.62 us (2%)
    pallas_call x10, Pallas kernels, call(): pl.pallas_call(kernel, out_shape=out_shape, in_specs=specs, out_specs=jax...  47.7 us
    all_to_all x2, blocking collectives, exchange(): return lax.all_to_all(value, plane, split_axis=0, concat_axis=0, tiled=True)  47.3 us
    ppermute x15, waiting for transfers between devices, send(): return lax.ppermute(value, axis, [(k, (k + step) % 4) for k in range(4)])  27.6 us
    ppermute x18, starting transfers between devices, swap(): return lax.ppermute(value, 'core', [(0, 1), (1, 0)])  20.5 us
    ppermute x15, starting transfers between devices, send(): return lax.ppermute(value, axis, [(k, (k + step) % 4) for k in range(4)])  17.3 us
    ppermute x9, starting transfers between devices, cross(): return lax.ppermute(value, ('z', 'y', 'core'), pairs)  13.6 us
    all_to_all x2, starting transfers between devices, exchange(): return lax.all_to_all(value, plane, split_axis=0, concat_axis=0, tiled=True)  10.3 us
    ppermute x9, waiting for transfers between devices, cross(): return lax.ppermute(value, ('z', 'y', 'core'), pairs)  9.75 us
  transfers between devices with their start and end apart: 46, of which 16 were waited for; matrix products, arithmetic and copies ran while one was open for 7% of the time, Pallas kernels for 13%

profile of v2, /device:TPU:1, one launch (start us, length us, event | category | flops | bytes accessed | tf_op | source)
XLA Modules:
  0.0 232.0 jit_solution(5342703884848847329)
XLA Ops:
  0.6 3.6 %collective-permute-start.1 = (bf16[29,64,256]{2,1,0:T(8,128)(2,1)}, bf16[29,64,256]{2,1,0:T(8,128)(2,1)S(1)}, u32[]{:S(2)}, u32[]{:S(2)}) collective-permute-start(bf16[29,64,256]{2,1,0:T(8,128)(2,1)} %own.1), channel_id=1, source_target_pairs={{0,24},{8,0},{16,8},{24,16},{1,25},{9,1},{17,9},{25,17},{2,26},{10... | collective-permute-start | bytes 2850824 | tf_op jit(solution)/shard_map/ppermute | solution.py:334
  6.6 31.7 %all_to_all.20 = bf16[16,32,768]{2,1,0:T(8,128)(2,1)} all-to-all(bf16[16,32,768]{2,1,0:T(8,128)(2,1)} %get-tuple-element.29), channel_id=1, replica_groups=mesh['z'=4,'y'=4,'core'=2,'rep'=4] {'z','y'}, dimensions={0} | all-to-all | bytes 1572864 | tf_op jit(solution)/shard_map/all_to_all | solution.py:358
  45.0 2.9 %collective-permute-start.3 = (bf16[14,64,256]{2,1,0:T(8,128)(2,1)S(1)}, bf16[14,64,256]{2,1,0:T(8,128)(2,1)}, u32[]{:S(2)}, u32[]{:S(2)}) collective-permute-start(bf16[14,64,256]{2,1,0:T(8,128)(2,1)S(1)} %slice.55), channel_id=1, source_target_pairs={{0,24},{8,0},{16,8},{24,16},{1,25},{9,1},{17,9},{25,17},{2,26},{10... | collective-permute-start | bytes 1376264 | tf_op jit(solution)/shard_map/ppermute | solution.py:334
  47.9 4.2 %collective-permute-done.2.refs_3_ = bf16[15,64,256]{2,1,0:T(8,128)(2,1)S(1)} collective-permute-done((bf16[15,64,256]{2,1,0:T(8,128)(2,1)S(1)}, bf16[15,64,256]{2,1,0:T(8,128)(2,1)S(1)}, u32[]{:S(2)}, u32[]{:S(2)}) %collective-permute-start.2) | collective-permute-done | bytes 491552 | tf_op jit(solution)/shard_map/ppermute | solution.py:334
  52.1 3.5 %collective-permute-start.7 = (bf16[15,64,256]{2,1,0:T(8,128)(2,1)S(1)}, bf16[15,64,256]{2,1,0:T(8,128)(2,1)}, u32[]{:S(2)}, u32[]{:S(2)}) collective-permute-start(bf16[15,64,256]{2,1,0:T(8,128)(2,1)S(1)} %collective-permute-done.2.refs_3_), channel_id=1, source_target_pairs={{0,4},{4,0},{1,5},{5,1},{2,6},{6,2},{3,7},{7,3},{8,12},{12,8},{9,1... | collective-permute-start | bytes 1474568 | tf_op jit(solution)/shard_map/ppermute | solution.py:330
  61.3 9.3 %shard_map.77 = (f32[136,1024]{1,0:T(8,128)}, f32[136,1024]{1,0:T(8,128)}, f32[136,1024]{1,0:T(8,128)}, f32[64,1024]{1,0:T(8,128)}, f32[72,1024]{1,0:T(8,128)}) custom-call(s32[4]{0:T(128)} %pad_add_fusion.pos_ref, bf16[512,768]{1,0:T(8,128)(2,1)} %bitcast.46, bf16[128,256]{1,0:T(8,128)(2,1)} %bitcast.65, bf16[29,64,256]{2,1,0:T(8,128)(2,1)} %own.1, ...), custom_call_target="tpu_custom_call" | custom-call | flops 4000000000 | bytes 10682384 | tf_op jit(solution)/shard_map/pallas_call | solution.py:306
  72.2 6.6 %all-to-all-start.1 = ((bf16[16,128,128]{2,1,0:T(8,128)(2,1)}), bf16[16,128,128]{2,1,0:T(8,128)(2,1)S(1)}, u32[]{:S(2)}, u32[]{:S(2)}) async-start(bf16[16,128,128]{2,1,0:T(8,128)(2,1)} %shard_map.78), calls=%async_computation.1 | async-start | bytes 1048576 | tf_op jit(solution)/shard_map/all_to_all | solution.py:358
  78.8 10.2 %collective-permute-done.10.from_high = f32[136,1024]{1,0:T(8,128)S(1)} collective-permute-done((f32[136,1024]{1,0:T(8,128)}, f32[136,1024]{1,0:T(8,128)S(1)}, u32[]{:S(2)}, u32[]{:S(2)}) %collective-permute-start.10) | collective-permute-done | bytes 557088 | tf_op jit(solution)/shard_map/ppermute | solution.py:334
  92.3 4.1 %shard_map.79 = (bf16[7,128,2048]{2,1,0:T(8,128)(2,1)}, f32[8,128]{1,0:T(8,128)}) custom-call(bf16[2048,128]{1,0:T(8,128)(2,1)} %bitcast.49), custom_call_target="tpu_custom_call" | custom-call | flops 100000000 | bytes 4198400 | tf_op jit(solution)/shard_map/pallas_call | solution.py:306
  98.7 3.4 %shard_map.80 = (bf16[9,16,512]{2,1,0:T(8,128)(2,1)}, bf16[9,16,512]{2,1,0:T(8,128)(2,1)}, bf16[16,96,256]{2,1,0:T(8,128)(2,1)}) custom-call(s32[4]{0:T(128)} %pad_add_fusion.pos_ref, f32[136,1024]{1,0:T(8,128)} %get-tuple-element.32.refs_1_.own, f32[136,1024]{1,0:T(8,128)} %copy-done.6, f32[136,1024]{1,0:T(8,128)} %copy-done.5, f32[64,1024]{1,0:T(8,128)} %copy-done.16, ...), custom_call_target="tpu_custom_call" | custom-call | flops 200000000 | bytes 8421392 | tf_op jit(solution)/shard_map/pallas_call | solution.py:306
  102.1 3.1 %collective-permute-start.13 = (bf16[9,16,512]{2,1,0:T(8,128)(2,1)}, bf16[9,16,512]{2,1,0:T(8,128)(2,1)S(1)}, u32[]{:S(2)}, u32[]{:S(2)}) collective-permute-start(bf16[9,16,512]{2,1,0:T(8,128)(2,1)} %get-tuple-element.41), channel_id=1, source_target_pairs={{0,4},{4,0},{1,5},{5,1},{2,6},{6,2},{3,7},{7,3},{8,12},{12,8},{9,1... | collective-permute-start | bytes 442376 | tf_op jit(solution)/shard_map/ppermute | solution.py:330
  107.7 2.7 %collective-permute-start.15 = (bf16[2,9,16,512]{3,2,0,1:T(8,128)(2,1)S(1)}, bf16[2,9,16,512]{3,2,0,1:T(8,128)(2,1)S(1)}, u32[]{:S(2)}, u32[]{:S(2)}) collective-permute-start(bf16[2,9,16,512]{3,2,0,1:T(8,128)(2,1)S(1)} %pad_maximum_fusion.4), channel_id=1, source_target_pairs={{0,24},{4,100},{8,0},{12,108},{16,8},{20,116},{24,16},{28,124},{32... | collective-permute-start | bytes 884744 | tf_op jit(solution)/shard_map/ppermute | solution.py:349
  111.1 3.6 %collective-permute-done.14 = bf16[2,9,16,512]{3,2,0,1:T(8,128)(2,1)S(1)} collective-permute-done((bf16[2,9,16,512]{3,2,0,1:T(8,128)(2,1)S(1)}, bf16[2,9,16,512]{3,2,0,1:T(8,128)(2,1)S(1)}, u32[]{:S(2)}, u32[]{:S(2)}) %collective-permute-start.14) | collective-permute-done | bytes 294944 | tf_op jit(solution)/shard_map/ppermute | solution.py:349
  122.8 3.7 %all-to-all-start.2 = ((bf16[16,96,256]{2,1,0:T(8,128)(2,1)}), bf16[16,96,256]{2,1,0:T(8,128)(2,1)S(1)}, u32[]{:S(2)}, u32[]{:S(2)}) async-start(bf16[16,96,256]{2,1,0:T(8,128)(2,1)} %shard_map.81), calls=%async_computation.2 | async-start | bytes 1572864 | tf_op jit(solution)/shard_map/all_to_all | solution.py:358
  133.0 3.3 %collective-permute-done.21.refs_5_ = bf16[2,2,8,16,512]{4,3,2,1,0:T(8,128)(2,1)} collective-permute-done((bf16[2,2,8,16,512]{4,3,2,1,0:T(8,128)(2,1)}, bf16[2,2,8,16,512]{4,3,2,1,0:T(8,128)(2,1)}, u32[]{:S(2)}, u32[]{:S(2)}) %collective-permute-start.21) | collective-permute-done | bytes 524320 | tf_op jit(solution)/shard_map/ppermute | solution.py:349
  136.3 3.4 %collective-permute-start.23 = (bf16[2,2,8,16,512]{4,3,2,1,0:T(8,128)(2,1)}, bf16[2,2,8,16,512]{4,3,2,1,0:T(8,128)(2,1)}, u32[]{:S(2)}, u32[]{:S(2)}) collective-permute-start(bf16[2,2,8,16,512]{4,3,2,1,0:T(8,128)(2,1)} %collective-permute-done.21.refs_5_), channel_id=1, source_target_pairs={{0,96},{4,28},{8,104},{12,4},{16,112},{20,12},{24,120},{28,20},{32... | collective-permute-start | bytes 1572872 | tf_op jit(solution)/shard_map/ppermute | solution.py:349
  147.4 2.9 %collective-permute-done.22 = bf16[2,2,8,16,512]{4,3,1,2,0:T(8,128)(2,1)S(1)} collective-permute-done((bf16[2,2,8,16,512]{4,3,1,2,0:T(8,128)(2,1)S(1)}, bf16[2,2,8,16,512]{4,3,1,2,0:T(8,128)(2,1)S(1)}, u32[]{:S(2)}, u32[]{:S(2)}) %collective-permute-start.22) | collective-permute-done | bytes 524320 | tf_op jit(solution)/shard_map/ppermute | solution.py:349
  160.1 9.2 %shard_map.84 = (bf16[29,64,256]{2,1,0:T(8,128)(2,1)}, bf16[29,64,256]{2,1,0:T(8,128)(2,1)}) custom-call(s32[4]{0:T(128)} %pad_add_fusion.pos_ref, bf16[7,128,2048]{2,1,0:T(8,128)(2,1)} %get-tuple-element.38._.xt_ref, f32[8,128]{1,0:T(8,128)} %get-tuple-element.45.colsum_ref, f32[8,256]{1,0:T(8,128)} %get-tuple-element.44.grad_ref, ...), custom_call_target="tpu_custom_call" | custom-call | flops 4000000000 | bytes 13971472 | tf_op jit(solution)/shard_map/pallas_call | solution.py:306
  172.7 3.1 %collective-permute-done.43 = f32[80,256]{1,0:T(8,128)S(1)} collective-permute-done((f32[80,256]{1,0:T(8,128)S(1)}, f32[80,256]{1,0:T(8,128)S(1)}, u32[]{:S(2)}, u32[]{:S(2)}) %collective-permute-start.43) | collective-permute-done | bytes 81952 | tf_op jit(solution)/shard_map/ppermute | solution.py:338
  175.9 15.6 %all_to_all.21 = bf16[16,80,256]{2,1,0:T(8,128)(2,1)S(1)} all-to-all(bf16[16,80,256]{2,1,0:T(8,128)(2,1)S(1)} %broadcast_in_dim.5), channel_id=1, replica_groups=mesh['z'=4,'y'=4,'core'=2,'rep'=4] {'z','y'}, dimensions={0} | all-to-all | bytes 1310720 | tf_op jit(solution)/shard_map/all_to_all | solution.py:358
  199.1 9.9 %shard_map.86 = bf16[2,2048,64]{2,1,0:T(8,128)(2,1)} custom-call(s32[4]{0:T(128)} %pad_add_fusion.pos_ref, f32[8,256]{1,0:T(8,128)} %get-tuple-element.44.grad_ref, bf16[29,64,256]{2,1,0:T(8,128)(2,1)} %own.1, bf16[29,64,256]{2,1,0:T(8,128)(2,1)} %copy-done.23, bf16[2,2,8,16,512]{4,3,2,1,0:T(8,128)(2,1)} %copy.14.refs_1_.refs_0_, ...), custom_call_target="tpu_custom_call" | custom-call | flops 4000000000 | bytes 11059216 | tf_op jit(solution)/shard_map/pallas_call | solution.py:306
  210.1 3.2 %collective-permute-start.33 = (bf16[2048,64]{1,0:T(8,128)(2,1)S(1)}, bf16[2048,64]{1,0:T(8,128)(2,1)S(1)}, u32[]{:S(2)}, u32[]{:S(2)}) collective-permute-start(bf16[2048,64]{1,0:T(8,128)(2,1)S(1)} %slice_bitcast_fusion), channel_id=1, source_target_pairs={{0,4},{4,0},{1,5},{5,1},{2,6},{6,2},{3,7},{7,3},{8,12},{12,8},{9,1... | collective-permute-start | bytes 786440 | tf_op jit(solution)/shard_map/ppermute | solution.py:330
  216.2 5.8 %collective-permute-done.38.above = bf16[464,256]{1,0:T(8,128)(2,1)S(1)} collective-permute-done((bf16[464,256]{1,0:T(8,128)(2,1)S(1)}, bf16[464,256]{1,0:T(8,128)(2,1)S(1)}, u32[]{:S(2)}, u32[]{:S(2)}) %collective-permute-start.38) | collective-permute-done | bytes 237600 | tf_op jit(solution)/shard_map/ppermute | solution.py:334
  225.8 2.9 %collective-permute-done.39.far_low = bf16[240,256]{1,0:T(8,128)(2,1)S(1)} collective-permute-done((bf16[240,256]{1,0:T(8,128)(2,1)S(1)}, bf16[240,256]{1,0:T(8,128)(2,1)S(1)}, u32[]{:S(2)}, u32[]{:S(2)}) %collective-permute-start.39) | collective-permute-done | bytes 122912 | tf_op jit(solution)/shard_map/ppermute | solution.py:334
  (177 shorter events, 79.0 us)
Async XLA Ops:
  0.6 37.6 %collective-permute-start.1 = (bf16[29,64,256]{2,1,0:T(8,128)(2,1)}, bf16[29,64,256]{2,1,0:T(8,128)(2,1)S(1)}, u32[]{:S(2)}, u32[]{:S(2)}) collective-permute-start(bf16[29,64,256]{2,1,0:T(8,128)(2,1)} %own.1), channel_id=1, source_target_pairs={{0,24},{8,0},{16,8},{24,16},{1,25},{9,1},{17,9},{25,17},{2,26},{10... | collective-permute-start | bytes 2850824 | tf_op jit(solution)/shard_map/ppermute | solution.py:334
  4.3 34.0 %collective-permute-start = (bf16[29,64,256]{2,1,0:T(8,128)(2,1)}, bf16[29,64,256]{2,1,0:T(8,128)(2,1)S(1)}, u32[]{:S(2)}, u32[]{:S(2)}) collective-permute-start(bf16[29,64,256]{2,1,0:T(8,128)(2,1)} %own.1), channel_id=1, source_target_pairs={{0,8},{8,16},{16,24},{24,0},{1,9},{9,17},{17,25},{25,1},{2,10},{10... | collective-permute-start | bytes 2850824 | tf_op jit(solution)/shard_map/ppermute | solution.py:334
  40.8 18.4 %collective-permute-start.4 = (bf16[29,64,256]{2,1,0:T(8,128)(2,1)S(1)}, bf16[29,64,256]{2,1,0:T(8,128)(2,1)S(1)}, u32[]{:S(2)}, u32[]{:S(2)}) collective-permute-start(bf16[29,64,256]{2,1,0:T(8,128)(2,1)S(1)} %copy-done.22), channel_id=1, source_target_pairs={{0,4},{4,0},{1,5},{5,1},{2,6},{6,2},{3,7},{7,3},{8,12},{12,8},{9,1... | collective-permute-start | bytes 2850824 | tf_op jit(solution)/shard_map/ppermute | solution.py:330
  43.4 17.0 %collective-permute-start.5 = (bf16[29,64,256]{2,1,0:T(8,128)(2,1)}, bf16[29,64,256]{2,1,0:T(8,128)(2,1)S(1)}, u32[]{:S(2)}, u32[]{:S(2)}) collective-permute-start(bf16[29,64,256]{2,1,0:T(8,128)(2,1)} %get-tuple-element.30.refs_1_), channel_id=1, source_target_pairs={{0,4},{4,0},{1,5},{5,1},{2,6},{6,2},{3,7},{7,3},{8,12},{12,8},{9,1... | collective-permute-start | bytes 2850824 | tf_op jit(solution)/shard_map/ppermute | solution.py:330
  43.5 16.9 %collective-permute-start.6 = (bf16[29,64,256]{2,1,0:T(8,128)(2,1)}, bf16[29,64,256]{2,1,0:T(8,128)(2,1)}, u32[]{:S(2)}, u32[]{:S(2)}) collective-permute-start(bf16[29,64,256]{2,1,0:T(8,128)(2,1)} %get-tuple-element.31.refs_2_), channel_id=1, source_target_pairs={{0,4},{4,0},{1,5},{5,1},{2,6},{6,2},{3,7},{7,3},{8,12},{12,8},{9,1... | collective-permute-start | bytes 2850824 | tf_op jit(solution)/shard_map/ppermute | solution.py:330
  45.0 12.9 %collective-permute-start.3 = (bf16[14,64,256]{2,1,0:T(8,128)(2,1)S(1)}, bf16[14,64,256]{2,1,0:T(8,128)(2,1)}, u32[]{:S(2)}, u32[]{:S(2)}) collective-permute-start(bf16[14,64,256]{2,1,0:T(8,128)(2,1)S(1)} %slice.55), channel_id=1, source_target_pairs={{0,24},{8,0},{16,8},{24,16},{1,25},{9,1},{17,9},{25,17},{2,26},{10... | collective-permute-start | bytes 1376264 | tf_op jit(solution)/shard_map/ppermute | solution.py:334
  70.7 18.3 %collective-permute-start.10 = (f32[136,1024]{1,0:T(8,128)}, f32[136,1024]{1,0:T(8,128)S(1)}, u32[]{:S(2)}, u32[]{:S(2)}) collective-permute-start(f32[136,1024]{1,0:T(8,128)} %get-tuple-element.34), channel_id=1, source_target_pairs={{0,96},{32,0},{64,32},{96,64},{1,97},{33,1},{65,33},{97,65},{2,98}... | collective-permute-start | bytes 1671176 | tf_op jit(solution)/shard_map/ppermute | solution.py:334
  71.3 19.6 %collective-permute-start.9 = (f32[136,1024]{1,0:T(8,128)}, f32[136,1024]{1,0:T(8,128)S(1)}, u32[]{:S(2)}, u32[]{:S(2)}) collective-permute-start(f32[136,1024]{1,0:T(8,128)} %get-tuple-element.33), channel_id=1, source_target_pairs={{0,32},{32,64},{64,96},{96,0},{1,33},{33,65},{65,97},{97,1},{2,34}... | collective-permute-start | bytes 1671176 | tf_op jit(solution)/shard_map/ppermute | solution.py:334
  72.2 19.4 %all-to-all-start.1 = ((bf16[16,128,128]{2,1,0:T(8,128)(2,1)}), bf16[16,128,128]{2,1,0:T(8,128)(2,1)S(1)}, u32[]{:S(2)}, u32[]{:S(2)}) async-start(bf16[16,128,128]{2,1,0:T(8,128)(2,1)} %shard_map.78), calls=%async_computation.1 | async-start | bytes 1048576 | tf_op jit(solution)/shard_map/all_to_all | solution.py:358
  115.6 17.3 %collective-permute-start.24 = (bf16[2,2,8,16,512]{4,3,1,2,0:T(8,128)(2,1)S(1)}, bf16[2,2,8,16,512]{4,3,1,2,0:T(8,128)(2,1)S(1)}, u32[]{:S(2)}, u32[]{:S(2)}) collective-permute-start(bf16[2,2,8,16,512]{4,3,1,2,0:T(8,128)(2,1)S(1)} %pad_maximum_fusion.2), channel_id=1, source_target_pairs={{0,4},{4,0},{1,5},{5,1},{2,6},{6,2},{3,7},{7,3},{8,12},{12,8},{9,1... | collective-permute-start | bytes 1572872 | tf_op jit(solution)/shard_map/ppermute | solution.py:330
  117.4 14.6 %collective-permute-start.20 = (bf16[2,2,8,16,512]{4,3,1,2,0:T(8,128)(2,1)S(1)}, bf16[2,2,8,16,512]{4,3,1,2,0:T(8,128)(2,1)S(1)}, u32[]{:S(2)}, u32[]{:S(2)}) collective-permute-start(bf16[2,2,8,16,512]{4,3,1,2,0:T(8,128)(2,1)S(1)} %pad_maximum_fusion.2), channel_id=1, source_target_pairs={{0,96},{4,28},{8,104},{12,4},{16,112},{20,12},{24,120},{28,20},{32... | collective-permute-start | bytes 1572872 | tf_op jit(solution)/shard_map/ppermute | solution.py:349
  120.1 16.1 %collective-permute-start.21 = (bf16[2,2,8,16,512]{4,3,2,1,0:T(8,128)(2,1)}, bf16[2,2,8,16,512]{4,3,2,1,0:T(8,128)(2,1)}, u32[]{:S(2)}, u32[]{:S(2)}) collective-permute-start(bf16[2,2,8,16,512]{4,3,2,1,0:T(8,128)(2,1)} %pad_maximum_fusion.3.refs_2_.refs_1_), channel_id=1, source_target_pairs={{0,96},{4,28},{8,104},{12,4},{16,112},{20,12},{24,120},{28,20},{32... | collective-permute-start | bytes 1572872 | tf_op jit(solution)/shard_map/ppermute | solution.py:349
  122.8 19.8 %all-to-all-start.2 = ((bf16[16,96,256]{2,1,0:T(8,128)(2,1)}), bf16[16,96,256]{2,1,0:T(8,128)(2,1)S(1)}, u32[]{:S(2)}, u32[]{:S(2)}) async-start(bf16[16,96,256]{2,1,0:T(8,128)(2,1)} %shard_map.81), calls=%async_computation.2 | async-start | bytes 1572864 | tf_op jit(solution)/shard_map/all_to_all | solution.py:358
  129.2 16.2 %collective-permute-start.19 = (bf16[2,2,8,16,512]{4,3,2,1,0:T(8,128)(2,1)}, bf16[2,2,8,16,512]{4,3,2,1,0:T(8,128)(2,1)}, u32[]{:S(2)}, u32[]{:S(2)}) collective-permute-start(bf16[2,2,8,16,512]{4,3,2,1,0:T(8,128)(2,1)} %pad_maximum_fusion.3.refs_2_.refs_1_), channel_id=1, source_target_pairs={{0,32},{4,12},{8,40},{12,20},{16,48},{20,28},{24,56},{28,4},{32,64... | collective-permute-start | bytes 1572872 | tf_op jit(solution)/shard_map/ppermute | solution.py:349
  130.8 19.4 %collective-permute-start.22 = (bf16[2,2,8,16,512]{4,3,1,2,0:T(8,128)(2,1)S(1)}, bf16[2,2,8,16,512]{4,3,1,2,0:T(8,128)(2,1)S(1)}, u32[]{:S(2)}, u32[]{:S(2)}) collective-permute-start(bf16[2,2,8,16,512]{4,3,1,2,0:T(8,128)(2,1)S(1)} %collective-permute-done.18), channel_id=1, source_target_pairs={{0,32},{4,12},{8,40},{12,20},{16,48},{20,28},{24,56},{28,4},{32,64... | collective-permute-start | bytes 1572872 | tf_op jit(solution)/shard_map/ppermute | solution.py:349
  132.0 19.2 %collective-permute-start.28 = (bf16[2,2,8,16,512]{4,3,1,2,0:T(8,128)(2,1)S(1)}, bf16[2,2,8,16,512]{4,3,1,2,0:T(8,128)(2,1)}, u32[]{:S(2)}, u32[]{:S(2)}) collective-permute-start(bf16[2,2,8,16,512]{4,3,1,2,0:T(8,128)(2,1)S(1)} %collective-permute-done.20), channel_id=1, source_target_pairs={{0,4},{4,0},{1,5},{5,1},{2,6},{6,2},{3,7},{7,3},{8,12},{12,8},{9,1... | collective-permute-start | bytes 1572872 | tf_op jit(solution)/shard_map/ppermute | solution.py:330
  132.9 18.3 %collective-permute-start.26 = (bf16[2,2,8,16,512]{4,3,1,2,0:T(8,128)(2,1)S(1)}, bf16[2,2,8,16,512]{4,3,1,2,0:T(8,128)(2,1)S(1)}, u32[]{:S(2)}, u32[]{:S(2)}) collective-permute-start(bf16[2,2,8,16,512]{4,3,1,2,0:T(8,128)(2,1)S(1)} %collective-permute-done.18), channel_id=1, source_target_pairs={{0,4},{4,0},{1,5},{5,1},{2,6},{6,2},{3,7},{7,3},{8,12},{12,8},{9,1... | collective-permute-start | bytes 1572872 | tf_op jit(solution)/shard_map/ppermute | solution.py:330
  136.3 15.4 %collective-permute-start.23 = (bf16[2,2,8,16,512]{4,3,2,1,0:T(8,128)(2,1)}, bf16[2,2,8,16,512]{4,3,2,1,0:T(8,128)(2,1)}, u32[]{:S(2)}, u32[]{:S(2)}) collective-permute-start(bf16[2,2,8,16,512]{4,3,2,1,0:T(8,128)(2,1)} %collective-permute-done.21.refs_5_), channel_id=1, source_target_pairs={{0,96},{4,28},{8,104},{12,4},{16,112},{20,12},{24,120},{28,20},{32... | collective-permute-start | bytes 1572872 | tf_op jit(solution)/shard_map/ppermute | solution.py:349
  147.0 13.1 %collective-permute-start.25 = (bf16[2,2,8,16,512]{4,3,2,1,0:T(8,128)(2,1)}, bf16[2,2,8,16,512]{4,3,2,1,0:T(8,128)(2,1)}, u32[]{:S(2)}, u32[]{:S(2)}) collective-permute-start(bf16[2,2,8,16,512]{4,3,2,1,0:T(8,128)(2,1)} %pad_maximum_fusion.3.refs_2_.refs_1_), channel_id=1, source_target_pairs={{0,4},{4,0},{1,5},{5,1},{2,6},{6,2},{3,7},{7,3},{8,12},{12,8},{9,1... | collective-permute-start | bytes 1572872 | tf_op jit(solution)/shard_map/ppermute | solution.py:330
  158.0 12.2 %collective-permute-start.42 = (f32[80,256]{1,0:T(8,128)S(1)}, f32[80,256]{1,0:T(8,128)S(1)}, u32[]{:S(2)}, u32[]{:S(2)}) collective-permute-start(f32[80,256]{1,0:T(8,128)S(1)} %pad_maximum_fusion.5), channel_id=1, source_target_pairs={{0,1},{1,0},{2,3},{3,2},{4,5},{5,4},{6,7},{7,6},{8,9},{9,8},{10,11... | collective-permute-start | bytes 245768 | tf_op jit(solution)/shard_map/ppermute | solution.py:338
  169.4 22.3 %collective-permute-start.32 = (bf16[29,64,256]{2,1,0:T(8,128)(2,1)}, bf16[29,64,256]{2,1,0:T(8,128)(2,1)S(1)}, u32[]{:S(2)}, u32[]{:S(2)}) collective-permute-start(bf16[29,64,256]{2,1,0:T(8,128)(2,1)} %get-tuple-element.47), channel_id=1, source_target_pairs={{0,4},{4,0},{1,5},{5,1},{2,6},{6,2},{3,7},{7,3},{8,12},{12,8},{9,1... | collective-permute-start | bytes 2850824 | tf_op jit(solution)/shard_map/ppermute | solution.py:330
  195.2 19.3 %collective-permute-start.34 = (bf16[464,256]{1,0:T(8,128)(2,1)}, bf16[464,256]{1,0:T(8,128)(2,1)S(1)}, u32[]{:S(2)}, u32[]{:S(2)}) collective-permute-start(bf16[464,256]{1,0:T(8,128)(2,1)} %get-tuple-element.49), channel_id=1, source_target_pairs={{0,1},{1,2},{2,3},{3,0},{4,5},{5,6},{6,7},{7,4},{8,9},{9,10},{10,1... | collective-permute-start | bytes 712712 | tf_op jit(solution)/shard_map/ppermute | solution.py:334
  195.5 19.0 %collective-permute-start.35 = (bf16[464,256]{1,0:T(8,128)(2,1)}, bf16[464,256]{1,0:T(8,128)(2,1)S(1)}, u32[]{:S(2)}, u32[]{:S(2)}) collective-permute-start(bf16[464,256]{1,0:T(8,128)(2,1)} %get-tuple-element.50), channel_id=1, source_target_pairs={{0,3},{1,0},{2,1},{3,2},{4,7},{5,4},{6,5},{7,6},{8,11},{9,8},{10,9... | collective-permute-start | bytes 712712 | tf_op jit(solution)/shard_map/ppermute | solution.py:334
  197.9 16.6 %collective-permute-start.36 = (bf16[464,256]{1,0:T(8,128)(2,1)}, bf16[464,256]{1,0:T(8,128)(2,1)S(1)}, u32[]{:S(2)}, u32[]{:S(2)}) collective-permute-start(bf16[464,256]{1,0:T(8,128)(2,1)} %get-tuple-element.51), channel_id=1, source_target_pairs={{0,2},{1,3},{2,0},{3,1},{4,6},{5,7},{6,4},{7,5},{8,10},{9,11},{10,... | collective-permute-start | bytes 712712 | tf_op jit(solution)/shard_map/ppermute | solution.py:334
  (48 other events, 262.5 us)

commit v3 on v2

--- a/solution.py
+++ b/solution.py
@@ -119,6 +119,20 @@
     plus_half[...] = rows(1, 0, 64)
     minus_half[0:64, :] = rows(-1, 64, 64)
     minus_half[64:72, :] = extra
+
+
+def pair_kernel(first_ref, second_ref, out_ref):
+    out_ref[0] = first_ref[...]
+    out_ref[1] = second_ref[...]
+
+
+def stack_kernel(first_ref, second_ref, out_ref, sums_ref):
+    total = jnp.zeros((16, 512), F32)
+    for k, ref in enumerate((first_ref, second_ref)):
+        for side in range(2):
+            out_ref[k, side] = ref[side, 0:8]
+            total = total + ref[side, 8].astype(F32)
+    sums_ref[...] = jnp.broadcast_to(jnp.sum(total, axis=0, keepdims=True), (8, 512))
 
 
 def turn_kernel(x_ref, xt_ref, colsum_ref):
@@ -283,17 +297,10 @@
         outs[k][...] = (own[rows, :].astype(F32) + other[rows, :].astype(F32)).astype(BF)
 
 
-def join_kernel(pos_ref, own, below, above, far_low, far_high, out_ref):
-    r = pos_ref[3]
-
-    def place(step, low, size):
-        return pl.ds(pl.multiple_of(wrap(r + step) * 464 + low, 8), size)
-
-    out_ref[place(0, 0, 464), :] = own[...].astype(F32)
-    out_ref[place(-1, 0, 464), :] = below[...].astype(F32)
-    out_ref[place(1, 0, 464), :] = above[...].astype(F32)
-    out_ref[place(2, 0, 240), :] = far_low[...].astype(F32)
-    out_ref[place(2, 240, 224), :] = far_high[...].astype(F32)
+def join_kernel(pos_ref, *refs):
+    for k, step in enumerate((0, -1, 1, 2)):
+        rows = pl.ds(pl.multiple_of(wrap(pos_ref[3] + step) * 464, 8), 464)
+        refs[4][rows, :] = refs[k][...].astype(F32)
 
 
 def call(kernel, out_shape, scratch, flops, *args, scalar=True, raw=0):
@@ -311,6 +318,7 @@
         scratch_shapes=scratch,
         compiler_params=pltpu.CompilerParams(vmem_limit_bytes=60 * 2**20),
         cost_estimate=pl.CostEstimate(flops=flops, bytes_accessed=moved, transcendentals=0),
+        name=kernel.__name__,
     )(*args)
 
 
@@ -390,38 +398,30 @@
         (shape((9, 16, 512), BF), shape((9, 16, 512), BF), shape((GROUPS, 96, BR), BF)),
         [], 2 * 10**8, pos, own, from_low, from_high, half_a, half_b, x, proj_weight, turned, raw=1,
     )
-    block = jnp.stack([keep, swap(give)])
+    block = call(pair_kernel, shape((2, 9, 16, 512), BF), [], 10**5, keep, swap(give), scalar=False)
     near = [block, cross(block, 1, False), cross(block, -1, False), cross(block, 2, False)]
-    low = jnp.stack([near[0][:, 0:8], near[1][:, 0:8]])
-    high = jnp.stack([near[2][:, 0:8], near[3][:, 0:8]])
+    stacked = (shape((2, 2, 8, 16, 512), BF), shape((8, 512), F32))
+    low, low_sums = call(stack_kernel, stacked, [], 10**5, near[0], near[1], scalar=False)
+    high, high_sums = call(stack_kernel, stacked, [], 10**5, near[2], near[3], scalar=False)
     low_below, high_above = cross(low, 1, True), cross(high, -1, True)
     high_below, low_above = cross(high, 1, True), cross(low, -1, True)
     every = [
         low, high, low_below, high_below, low_above, high_above, cross(low_below, 1, True), cross(high_above, -1, True)
     ]
     every = every + [swap(piece) for piece in every]
-    sums = jnp.sum(jnp.stack([piece[:, 8] for piece in near]).astype(F32), axis=(0, 1, 2))
-    sums = jnp.broadcast_to(sums[None], (8, 512))
+    sums = low_sums + high_sums
     sums = jnp.where(pos[2] == 0, sums, swap(sums))
     const, pool_grad, outer = call(
         pool_kernel, (shape((8, BR), F32), shape((8, BR), F32), shape((16, BR), F32)), [pltpu.VMEM((256, BR), F32)],
         10**7, pos, sums, proj_weight,
     )
     (pay,) = gate((pay,), (low, high))
-    part, head_out = call(
-        collect_kernel, (shape((64, BR), F32), shape((128, BR), BF)), [pltpu.VMEM((2, 128, 128), F32)],
-        10**6, pos, exchange(pay), const,
-    )
-    part = jnp.concatenate([part + swap(part), outer], axis=0)
-    part = part + pair(part, "rep", 1)
-    part = part + pair(part, "rep", 2)
-    part = exchange(jnp.broadcast_to(part.astype(BF)[None], (GROUPS, 80, BR))).astype(F32)
-    grad_proj = jnp.concatenate([part[:, 0:64].reshape(1024, BR), part[:, 64:80].reshape(256, BR)], axis=0)
+    pay = exchange(pay)
     dw, dw_other = call(
         weight_grad_kernel,
         (shape((29, 64, BR), BF), shape((29, 64, BR), BF)),
         [pltpu.VMEM((2 * GROUPS, 4, 16, 1024), BF), pltpu.VMEM((29, CH, BR), F32), pltpu.SemaphoreType.DMA((32,))],
-        4 * 10**9, pos, turned, colsum, pool_grad, *every, raw=16,
+        4 * 10**9, pos, turned, colsum, pool_grad, *every, pay, raw=17,
     )
     quarters = call(
         add_kernel, (shape((464, BR), BF),) * 4, [], 10**6, pos, dw.reshape(1856, BR), swap(dw_other).reshape(1856, BR)
@@ -437,11 +437,20 @@
     )
     terms = [quarters[0]] + [send(quarters[k], "rep", k) for k in (1, 3, 2)]
     dw = sum(term.astype(F32) for term in terms).astype(BF)
-    below, above = send(dw, "rep", 1), send(dw, "rep", -1)
-    far_low, far_high = send(below[0:240], "rep", 1), send(above[240:464], "rep", -1)
-    grad_branch = call(
-        join_kernel, shape((1856, BR), F32), [], 10**6, pos, dw, below, above, far_low, far_high
-    ).reshape(29, 64, BR)
+    dw = [dw] + [send(dw, "rep", step) for step in (1, -1, 2)]
+    grad_branch = call(join_kernel, shape((1856, BR), F32), [], 10**6, pos, *dw).reshape(29, 64, BR)
+    (pay,) = gate((pay,), (quarters[0],))
+    part, head_out = call(
+        collect_kernel, (shape((64, BR), F32), shape((128, BR), BF)), [pltpu.VMEM((2, 128, 128), F32)],
+        10**6, pos, pay, const,
+    )
+    part = jnp.concatenate([part + swap(part), outer], axis=0)
+    part = part + pair(part, "rep", 1)
+    part = part + pair(part, "rep", 2)
+    part = jnp.broadcast_to(part.astype(BF)[None], (GROUPS, 80, BR))
+    (part,) = gate((part,), (dw[0],))
+    part = exchange(part).astype(F32)
+    grad_proj = jnp.concatenate([part[:, 0:64].reshape(1024, BR), part[:, 64:80].reshape(256, BR)], axis=0)
     mine, theirs = dx[0], swap(dx[1])
     even = jnp.where(pos[2] == 0, mine, theirs).reshape(GROUPS, 1, 2, 64, 64)
     odd = jnp.where(pos[2] == 0, theirs, mine).reshape(GROUPS, 1, 2, 64, 64)

time: 234 us -> 224 us (0.957)
  blocking collectives: 47.3 us -> 31.7 us
  waiting for transfers between devices: 45.3 us -> 51.9 us
  Pallas kernels: 47.7 us -> 53.3 us
  local copies, waits for them, and re-layouts: 19.6 us -> 14.1 us
    all_to_all x2 -> x1, blocking collectives: 47.3 us -> 31.7 us  [exchange(): return lax.all_to_all(value, plane, split_axis=0, concat_axis=0, tiled=True)]
    all_to_all x2 -> x3, waiting for transfers between devices: 0.5 us -> 7.68 us  [exchange(): return lax.all_to_all(value, plane, split_axis=0, concat_axis=0, tiled=True)]
    ppermute x7 -> x0, local copies, waits for them, and re-layouts: 7.04 us -> none  [the longest x4 4.48 us: swap(): return lax.ppermute(value, 'core', [(0, 1), (1, 0)])]
    ppermute x9, waiting for transfers between devices: 9.75 us -> 16.3 us  [cross(): return lax.ppermute(value, ('z', 'y', 'core'), pairs)]
    ppermute x15 -> x14, waiting for transfers between devices: 27.6 us -> 21.8 us  [send(): return lax.ppermute(value, axis, [(k, (k + step) % 4) for k in range(4)])]
    pallas_call x10 -> x13, Pallas kernels: 47.7 us -> 53.3 us  [call(): pl.pallas_call(kernel, out_shape=out_shape, in_specs=specs, out_specs=jax...]
    ppermute x18, starting transfers between devices: 20.5 us -> 16.5 us  [swap(): return lax.ppermute(value, 'core', [(0, 1), (1, 0)])]
    all_to_all x2 -> x3, starting transfers between devices: 10.3 us -> 13.9 us  [exchange(): return lax.all_to_all(value, plane, split_axis=0, concat_axis=0, tiled=True)]
  transfers between devices with their start and end apart: 46 -> 46, of which waited for: 16 -> 19; matrix products, arithmetic and copies ran while one was open for 7% -> 3% of each run, Pallas kernels for 13% -> 11%
where the time goes in v3:
time: 224 us; the launch traced here: 220 us
  starting transfers between devices  63.2 us (28%)
  Pallas kernels  53.3 us (24%)
  waiting for transfers between devices  51.9 us (23%)
  blocking collectives  31.7 us (14%)
  local copies, waits for them, and re-layouts  14.1 us (6%)
  other arithmetic  4.54 us (2%)
    pallas_call x13, Pallas kernels, call(): pl.pallas_call(kernel, out_shape=out_shape, in_specs=specs, out_specs=jax...  53.3 us
    all_to_all x1, blocking collectives, exchange(): return lax.all_to_all(value, plane, split_axis=0, concat_axis=0, tiled=True)  31.7 us
    ppermute x14, waiting for transfers between devices, send(): return lax.ppermute(value, axis, [(k, (k + step) % 4) for k in range(4)])  21.8 us
    ppermute x14, starting transfers between devices, send(): return lax.ppermute(value, axis, [(k, (k + step) % 4) for k in range(4)])  18 us
    ppermute x18, starting transfers between devices, swap(): return lax.ppermute(value, 'core', [(0, 1), (1, 0)])  16.5 us
    ppermute x9, waiting for transfers between devices, cross(): return lax.ppermute(value, ('z', 'y', 'core'), pairs)  16.3 us
    all_to_all x3, starting transfers between devices, exchange(): return lax.all_to_all(value, plane, split_axis=0, concat_axis=0, tiled=True)  13.9 us
    ppermute x9, starting transfers between devices, cross(): return lax.ppermute(value, ('z', 'y', 'core'), pairs)  12.3 us
  transfers between devices with their start and end apart: 46, of which 19 were waited for; matrix products, arithmetic and copies ran while one was open for 3% of the time, Pallas kernels for 11%

profile of v3, /device:TPU:1, one launch (start us, length us, event | category | flops | bytes accessed | tf_op | source)
XLA Modules:
  0.0 219.9 jit_solution(8716084816667999198)
XLA Ops:
  0.6 3.6 %collective-permute-start.1 = (bf16[29,64,256]{2,1,0:T(8,128)(2,1)}, bf16[29,64,256]{2,1,0:T(8,128)(2,1)S(1)}, u32[]{:S(2)}, u32[]{:S(2)}) collective-permute-start(bf16[29,64,256]{2,1,0:T(8,128)(2,1)} %own.1), channel_id=1, source_target_pairs={{0,24},{8,0},{16,8},{24,16},{1,25},{9,1},{17,9},{25,17},{2,26},{10... | collective-permute-start | bytes 2850824 | tf_op jit(solution)/shard_map/ppermute | solution.py:342
  6.6 31.7 %all_to_all.20 = bf16[16,32,768]{2,1,0:T(8,128)(2,1)} all-to-all(bf16[16,32,768]{2,1,0:T(8,128)(2,1)} %get-tuple-element.33), channel_id=1, replica_groups=mesh['z'=4,'y'=4,'core'=2,'rep'=4] {'z','y'}, dimensions={0} | all-to-all | bytes 1572864 | tf_op jit(solution)/shard_map/all_to_all | solution.py:366
  45.0 2.9 %collective-permute-start.3 = (bf16[14,64,256]{2,1,0:T(8,128)(2,1)S(1)}, bf16[14,64,256]{2,1,0:T(8,128)(2,1)}, u32[]{:S(2)}, u32[]{:S(2)}) collective-permute-start(bf16[14,64,256]{2,1,0:T(8,128)(2,1)S(1)} %slice.25), channel_id=1, source_target_pairs={{0,24},{8,0},{16,8},{24,16},{1,25},{9,1},{17,9},{25,17},{2,26},{10... | collective-permute-start | bytes 1376264 | tf_op jit(solution)/shard_map/ppermute | solution.py:342
  47.9 4.2 %collective-permute-done.2.refs_3_ = bf16[15,64,256]{2,1,0:T(8,128)(2,1)S(1)} collective-permute-done((bf16[15,64,256]{2,1,0:T(8,128)(2,1)S(1)}, bf16[15,64,256]{2,1,0:T(8,128)(2,1)S(1)}, u32[]{:S(2)}, u32[]{:S(2)}) %collective-permute-start.2) | collective-permute-done | bytes 491552 | tf_op jit(solution)/shard_map/ppermute | solution.py:342
  52.1 3.5 %collective-permute-start.7 = (bf16[15,64,256]{2,1,0:T(8,128)(2,1)S(1)}, bf16[15,64,256]{2,1,0:T(8,128)(2,1)}, u32[]{:S(2)}, u32[]{:S(2)}) collective-permute-start(bf16[15,64,256]{2,1,0:T(8,128)(2,1)S(1)} %collective-permute-done.2.refs_3_), channel_id=1, source_target_pairs={{0,4},{4,0},{1,5},{5,1},{2,6},{6,2},{3,7},{7,3},{8,12},{12,8},{9,1... | collective-permute-start | bytes 1474568 | tf_op jit(solution)/shard_map/ppermute | solution.py:338
  61.3 9.3 %forward_kernel.1 = (f32[136,1024]{1,0:T(8,128)}, f32[136,1024]{1,0:T(8,128)}, f32[136,1024]{1,0:T(8,128)}, f32[64,1024]{1,0:T(8,128)}, f32[72,1024]{1,0:T(8,128)}) custom-call(s32[4]{0:T(128)} %pad_add_fusion.pos_ref, bf16[512,768]{1,0:T(8,128)(2,1)} %bitcast.26, bf16[128,256]{1,0:T(8,128)(2,1)} %bitcast.39, bf16[29,64,256]{2,1,0:T(8,128)(2,1)} %own.1, ...), custom_call_target="tpu_custom_call" | custom-call | flops 4000000000 | bytes 10682384 | tf_op jit(solution)/shard_map/forward_kernel/pallas_call | solution.py:313
  72.2 6.6 %all-to-all-start.1 = ((bf16[16,128,128]{2,1,0:T(8,128)(2,1)}), bf16[16,128,128]{2,1,0:T(8,128)(2,1)S(1)}, u32[]{:S(2)}, u32[]{:S(2)}) async-start(bf16[16,128,128]{2,1,0:T(8,128)(2,1)} %shard_map.76), calls=%async_computation.1 | async-start | bytes 1048576 | tf_op jit(solution)/shard_map/all_to_all | solution.py:366
  78.8 10.2 %collective-permute-done.10.from_high = f32[136,1024]{1,0:T(8,128)S(1)} collective-permute-done((f32[136,1024]{1,0:T(8,128)}, f32[136,1024]{1,0:T(8,128)S(1)}, u32[]{:S(2)}, u32[]{:S(2)}) %collective-permute-start.10) | collective-permute-done | bytes 557088 | tf_op jit(solution)/shard_map/ppermute | solution.py:342
  92.4 4.1 %turn_kernel.1 = (bf16[7,128,2048]{2,1,0:T(8,128)(2,1)}, f32[8,128]{1,0:T(8,128)}) custom-call(bf16[2048,128]{1,0:T(8,128)(2,1)} %bitcast.29), custom_call_target="tpu_custom_call" | custom-call | flops 100000000 | bytes 4198400 | tf_op jit(solution)/shard_map/turn_kernel/pallas_call | solution.py:313
  98.7 3.4 %middle_kernel.1 = (bf16[9,16,512]{2,1,0:T(8,128)(2,1)}, bf16[9,16,512]{2,1,0:T(8,128)(2,1)}, bf16[16,96,256]{2,1,0:T(8,128)(2,1)}) custom-call(s32[4]{0:T(128)} %pad_add_fusion.pos_ref, f32[136,1024]{1,0:T(8,128)} %get-tuple-element.36.refs_1_.own, f32[136,1024]{1,0:T(8,128)} %copy-done.6, f32[136,1024]{1,0:T(8,128)} %copy-done.5, f32[64,1024]{1,0:T(8,128)} %copy-done.16, ...), custom_call_target="tpu_custom_call" | custom-call | flops 200000000 | bytes 8421392 | tf_op jit(solution)/shard_map/middle_kernel/pallas_call | solution.py:313
  102.1 3.1 %collective-permute-start.13 = (bf16[9,16,512]{2,1,0:T(8,128)(2,1)}, bf16[9,16,512]{2,1,0:T(8,128)(2,1)S(1)}, u32[]{:S(2)}, u32[]{:S(2)}) collective-permute-start(bf16[9,16,512]{2,1,0:T(8,128)(2,1)} %get-tuple-element.45), channel_id=1, source_target_pairs={{0,4},{4,0},{1,5},{5,1},{2,6},{6,2},{3,7},{7,3},{8,12},{12,8},{9,1... | collective-permute-start | bytes 442376 | tf_op jit(solution)/shard_map/ppermute | solution.py:338
  111.5 7.8 %collective-permute-done.14.second_ref = bf16[2,9,16,512]{3,2,1,0:T(8,128)(2,1)S(1)} collective-permute-done((bf16[2,9,16,512]{3,2,1,0:T(8,128)(2,1)}, bf16[2,9,16,512]{3,2,1,0:T(8,128)(2,1)S(1)}, u32[]{:S(2)}, u32[]{:S(2)}) %collective-permute-start.14) | collective-permute-done | bytes 294944 | tf_op jit(solution)/shard_map/ppermute | solution.py:357
  121.9 3.5 %collective-permute-start.20 = (bf16[2,2,8,16,512]{4,3,2,1,0:T(8,128)(2,1)}, bf16[2,2,8,16,512]{4,3,2,1,0:T(8,128)(2,1)S(1)}, u32[]{:S(2)}, u32[]{:S(2)}) collective-permute-start(bf16[2,2,8,16,512]{4,3,2,1,0:T(8,128)(2,1)} %get-tuple-element.46.refs_1_.refs_0_), channel_id=1, source_target_pairs={{0,96},{4,28},{8,104},{12,4},{16,112},{20,12},{24,120},{28,20},{32... | collective-permute-start | bytes 1572872 | tf_op jit(solution)/shard_map/ppermute | solution.py:357
  128.7 2.7 %collective-permute-start.21 = (bf16[2,2,8,16,512]{4,3,2,1,0:T(8,128)(2,1)}, bf16[2,2,8,16,512]{4,3,2,1,0:T(8,128)(2,1)S(1)}, u32[]{:S(2)}, u32[]{:S(2)}) collective-permute-start(bf16[2,2,8,16,512]{4,3,2,1,0:T(8,128)(2,1)} %get-tuple-element.47.refs_2_.refs_1_), channel_id=1, source_target_pairs={{0,96},{4,28},{8,104},{12,4},{16,112},{20,12},{24,120},{28,20},{32... | collective-permute-start | bytes 1572872 | tf_op jit(solution)/shard_map/ppermute | solution.py:357
  134.9 3.0 %collective-permute-done.21.refs_5_ = bf16[2,2,8,16,512]{4,3,2,1,0:T(8,128)(2,1)S(1)} collective-permute-done((bf16[2,2,8,16,512]{4,3,2,1,0:T(8,128)(2,1)}, bf16[2,2,8,16,512]{4,3,2,1,0:T(8,128)(2,1)S(1)}, u32[]{:S(2)}, u32[]{:S(2)}) %collective-permute-start.21) | collective-permute-done | bytes 524320 | tf_op jit(solution)/shard_map/ppermute | solution.py:357
  137.9 3.4 %collective-permute-start.23 = (bf16[2,2,8,16,512]{4,3,2,1,0:T(8,128)(2,1)S(1)}, bf16[2,2,8,16,512]{4,3,2,1,0:T(8,128)(2,1)}, u32[]{:S(2)}, u32[]{:S(2)}) collective-permute-start(bf16[2,2,8,16,512]{4,3,2,1,0:T(8,128)(2,1)S(1)} %collective-permute-done.21.refs_5_), channel_id=1, source_target_pairs={{0,96},{4,28},{8,104},{12,4},{16,112},{20,12},{24,120},{28,20},{32... | collective-permute-start | bytes 1572872 | tf_op jit(solution)/shard_map/ppermute | solution.py:357
  141.3 3.6 %all-to-all-start.2 = ((bf16[16,96,256]{2,1,0:T(8,128)(2,1)}), bf16[16,96,256]{2,1,0:T(8,128)(2,1)S(1)}, u32[]{:S(2)}, u32[]{:S(2)}) async-start(bf16[16,96,256]{2,1,0:T(8,128)(2,1)} %shard_map.77), calls=%async_computation.2 | async-start | bytes 1572864 | tf_op jit(solution)/shard_map/all_to_all | solution.py:366
  145.6 3.3 %collective-permute-done.22.refs_6_ = bf16[2,2,8,16,512]{4,3,2,1,0:T(8,128)(2,1)} collective-permute-done((bf16[2,2,8,16,512]{4,3,2,1,0:T(8,128)(2,1)S(1)}, bf16[2,2,8,16,512]{4,3,2,1,0:T(8,128)(2,1)}, u32[]{:S(2)}, u32[]{:S(2)}) %collective-permute-start.22) | collective-permute-done | bytes 524320 | tf_op jit(solution)/shard_map/ppermute | solution.py:357
  155.2 5.0 %all-to-all-done.2.refs_16_.refs_0_ = bf16[16,96,256]{2,1,0:T(8,128)(2,1)S(1)} async-done(((bf16[16,96,256]{2,1,0:T(8,128)(2,1)}), bf16[16,96,256]{2,1,0:T(8,128)(2,1)S(1)}, u32[]{:S(2)}, u32[]{:S(2)}) %all-to-all-start.2) | async-done | bytes 786464 | tf_op jit(solution)/shard_map/all_to_all | solution.py:366
  161.5 9.2 %weight_grad_kernel.1 = (bf16[29,64,256]{2,1,0:T(8,128)(2,1)}, bf16[29,64,256]{2,1,0:T(8,128)(2,1)}) custom-call(s32[4]{0:T(128)} %pad_add_fusion.pos_ref, bf16[7,128,2048]{2,1,0:T(8,128)(2,1)} %get-tuple-element.42._.xt_ref, f32[8,128]{1,0:T(8,128)} %get-tuple-element.48.colsum_ref, f32[8,256]{1,0:T(8,128)} %get-tuple-element.51.grad_ref, ...), custom_call_target="tpu_custom_call" | custom-call | flops 4000000000 | bytes 14757904 | tf_op jit(solution)/shard_map/weight_grad_kernel/pallas_call | solution.py:313
  174.7 2.6 %add_kernel.1 = (bf16[464,256]{1,0:T(8,128)(2,1)}, bf16[464,256]{1,0:T(8,128)(2,1)}, bf16[464,256]{1,0:T(8,128)(2,1)}, bf16[464,256]{1,0:T(8,128)(2,1)}) custom-call(s32[4]{0:T(128)} %pad_add_fusion.pos_ref, bf16[1856,256]{1,0:T(8,128)(2,1)} %bitcast.35, bf16[1856,256]{1,0:T(8,128)(2,1)} %bitcast.36), custom_call_target="tpu_custom_call" | custom-call | flops 1000000 | bytes 2850832 | tf_op jit(solution)/shard_map/add_kernel/pallas_call | solution.py:313
  185.4 9.9 %field_grad_kernel.1 = bf16[2,2048,64]{2,1,0:T(8,128)(2,1)} custom-call(s32[4]{0:T(128)} %pad_add_fusion.pos_ref, f32[8,256]{1,0:T(8,128)} %get-tuple-element.51.grad_ref, bf16[29,64,256]{2,1,0:T(8,128)(2,1)} %own.1, bf16[29,64,256]{2,1,0:T(8,128)(2,1)} %copy-done.22, bf16[2,2,8,16,512]{4,3,2,1,0:T(8,128)(2,1)} %get-tuple-element.46.refs_1_.refs_0_, ...), custom_call_target="tpu_custom_call" | custom-call | flops 4000000000 | bytes 11059216 | tf_op jit(solution)/shard_map/field_grad_kernel/pallas_call | solution.py:313
  204.9 3.7 %all-to-all-start.3 = ((bf16[16,80,256]{2,1,0:T(8,128)(2,1)}), bf16[16,80,256]{2,1,0:T(8,128)(2,1)S(1)}, u32[]{:S(2)}, u32[]{:S(2)}) async-start(bf16[16,80,256]{2,1,0:T(8,128)(2,1)} %shard_map.79), calls=%async_computation.3 | async-start | bytes 1310720 | tf_op jit(solution)/shard_map/all_to_all | solution.py:366
  213.8 2.7 %join_kernel.1 = f32[1856,256]{1,0:T(8,128)} custom-call(s32[4]{0:T(128)} %pad_add_fusion.pos_ref, bf16[464,256]{1,0:T(8,128)(2,1)} %copy-done.2, bf16[464,256]{1,0:T(8,128)(2,1)} %collective-permute-done.37.refs_1_, bf16[464,256]{1,0:T(8,128)(2,1)} %copy-done.18, bf16[464,256]{1,0:T(8,128)(2,1)} %copy-done.17), custom_call_target="tpu_custom_call" | custom-call | flops 1000000 | bytes 2850832 | tf_op jit(solution)/shard_map/join_kernel/pallas_call | solution.py:313
  (177 shorter events, 75.6 us)
Async XLA Ops:
  0.6 37.6 %collective-permute-start.1 = (bf16[29,64,256]{2,1,0:T(8,128)(2,1)}, bf16[29,64,256]{2,1,0:T(8,128)(2,1)S(1)}, u32[]{:S(2)}, u32[]{:S(2)}) collective-permute-start(bf16[29,64,256]{2,1,0:T(8,128)(2,1)} %own.1), channel_id=1, source_target_pairs={{0,24},{8,0},{16,8},{24,16},{1,25},{9,1},{17,9},{25,17},{2,26},{10... | collective-permute-start | bytes 2850824 | tf_op jit(solution)/shard_map/ppermute | solution.py:342
  4.3 34.0 %collective-permute-start = (bf16[29,64,256]{2,1,0:T(8,128)(2,1)}, bf16[29,64,256]{2,1,0:T(8,128)(2,1)S(1)}, u32[]{:S(2)}, u32[]{:S(2)}) collective-permute-start(bf16[29,64,256]{2,1,0:T(8,128)(2,1)} %own.1), channel_id=1, source_target_pairs={{0,8},{8,16},{16,24},{24,0},{1,9},{9,17},{17,25},{25,1},{2,10},{10... | collective-permute-start | bytes 2850824 | tf_op jit(solution)/shard_map/ppermute | solution.py:342
  40.8 18.4 %collective-permute-start.4 = (bf16[29,64,256]{2,1,0:T(8,128)(2,1)S(1)}, bf16[29,64,256]{2,1,0:T(8,128)(2,1)S(1)}, u32[]{:S(2)}, u32[]{:S(2)}) collective-permute-start(bf16[29,64,256]{2,1,0:T(8,128)(2,1)S(1)} %copy-done.21), channel_id=1, source_target_pairs={{0,4},{4,0},{1,5},{5,1},{2,6},{6,2},{3,7},{7,3},{8,12},{12,8},{9,1... | collective-permute-start | bytes 2850824 | tf_op jit(solution)/shard_map/ppermute | solution.py:338
  43.4 17.0 %collective-permute-start.5 = (bf16[29,64,256]{2,1,0:T(8,128)(2,1)}, bf16[29,64,256]{2,1,0:T(8,128)(2,1)S(1)}, u32[]{:S(2)}, u32[]{:S(2)}) collective-permute-start(bf16[29,64,256]{2,1,0:T(8,128)(2,1)} %get-tuple-element.34.refs_1_), channel_id=1, source_target_pairs={{0,4},{4,0},{1,5},{5,1},{2,6},{6,2},{3,7},{7,3},{8,12},{12,8},{9,1... | collective-permute-start | bytes 2850824 | tf_op jit(solution)/shard_map/ppermute | solution.py:338
  43.5 16.9 %collective-permute-start.6 = (bf16[29,64,256]{2,1,0:T(8,128)(2,1)}, bf16[29,64,256]{2,1,0:T(8,128)(2,1)}, u32[]{:S(2)}, u32[]{:S(2)}) collective-permute-start(bf16[29,64,256]{2,1,0:T(8,128)(2,1)} %get-tuple-element.35.refs_2_), channel_id=1, source_target_pairs={{0,4},{4,0},{1,5},{5,1},{2,6},{6,2},{3,7},{7,3},{8,12},{12,8},{9,1... | collective-permute-start | bytes 2850824 | tf_op jit(solution)/shard_map/ppermute | solution.py:338
  45.0 12.9 %collective-permute-start.3 = (bf16[14,64,256]{2,1,0:T(8,128)(2,1)S(1)}, bf16[14,64,256]{2,1,0:T(8,128)(2,1)}, u32[]{:S(2)}, u32[]{:S(2)}) collective-permute-start(bf16[14,64,256]{2,1,0:T(8,128)(2,1)S(1)} %slice.25), channel_id=1, source_target_pairs={{0,24},{8,0},{16,8},{24,16},{1,25},{9,1},{17,9},{25,17},{2,26},{10... | collective-permute-start | bytes 1376264 | tf_op jit(solution)/shard_map/ppermute | solution.py:342
  70.7 18.3 %collective-permute-start.10 = (f32[136,1024]{1,0:T(8,128)}, f32[136,1024]{1,0:T(8,128)S(1)}, u32[]{:S(2)}, u32[]{:S(2)}) collective-permute-start(f32[136,1024]{1,0:T(8,128)} %get-tuple-element.38), channel_id=1, source_target_pairs={{0,96},{32,0},{64,32},{96,64},{1,97},{33,1},{65,33},{97,65},{2,98}... | collective-permute-start | bytes 1671176 | tf_op jit(solution)/shard_map/ppermute | solution.py:342
  71.4 19.6 %collective-permute-start.9 = (f32[136,1024]{1,0:T(8,128)}, f32[136,1024]{1,0:T(8,128)S(1)}, u32[]{:S(2)}, u32[]{:S(2)}) collective-permute-start(f32[136,1024]{1,0:T(8,128)} %get-tuple-element.37), channel_id=1, source_target_pairs={{0,32},{32,64},{64,96},{96,0},{1,33},{33,65},{65,97},{97,1},{2,34}... | collective-permute-start | bytes 1671176 | tf_op jit(solution)/shard_map/ppermute | solution.py:342
  72.2 19.4 %all-to-all-start.1 = ((bf16[16,128,128]{2,1,0:T(8,128)(2,1)}), bf16[16,128,128]{2,1,0:T(8,128)(2,1)S(1)}, u32[]{:S(2)}, u32[]{:S(2)}) async-start(bf16[16,128,128]{2,1,0:T(8,128)(2,1)} %shard_map.76), calls=%async_computation.1 | async-start | bytes 1048576 | tf_op jit(solution)/shard_map/all_to_all | solution.py:366
  108.8 16.6 %collective-permute-start.16 = (bf16[2,9,16,512]{3,2,1,0:T(8,128)(2,1)}, bf16[2,9,16,512]{3,2,1,0:T(8,128)(2,1)S(1)}, u32[]{:S(2)}, u32[]{:S(2)}) collective-permute-start(bf16[2,9,16,512]{3,2,1,0:T(8,128)(2,1)} %pair_kernel.1.first_ref), channel_id=1, source_target_pairs={{0,16},{4,68},{8,24},{12,76},{16,0},{20,84},{24,8},{28,92},{32,48}... | collective-permute-start | bytes 884744 | tf_op jit(solution)/shard_map/ppermute | solution.py:357
  110.5 14.9 %collective-permute-start.15 = (bf16[2,9,16,512]{3,2,1,0:T(8,128)(2,1)}, bf16[2,9,16,512]{3,2,1,0:T(8,128)(2,1)S(1)}, u32[]{:S(2)}, u32[]{:S(2)}) collective-permute-start(bf16[2,9,16,512]{3,2,1,0:T(8,128)(2,1)} %pair_kernel.1.first_ref), channel_id=1, source_target_pairs={{0,24},{4,100},{8,0},{12,108},{16,8},{20,116},{24,16},{28,124},{32... | collective-permute-start | bytes 884744 | tf_op jit(solution)/shard_map/ppermute | solution.py:357
  121.9 11.6 %collective-permute-start.24 = (bf16[2,2,8,16,512]{4,3,2,1,0:T(8,128)(2,1)}, bf16[2,2,8,16,512]{4,3,2,1,0:T(8,128)(2,1)S(1)}, u32[]{:S(2)}, u32[]{:S(2)}) collective-permute-start(bf16[2,2,8,16,512]{4,3,2,1,0:T(8,128)(2,1)} %get-tuple-element.46.refs_1_.refs_0_), channel_id=1, source_target_pairs={{0,4},{4,0},{1,5},{5,1},{2,6},{6,2},{3,7},{7,3},{8,12},{12,8},{9,1... | collective-permute-start | bytes 1572872 | tf_op jit(solution)/shard_map/ppermute | solution.py:338
  121.9 11.6 %collective-permute-start.20 = (bf16[2,2,8,16,512]{4,3,2,1,0:T(8,128)(2,1)}, bf16[2,2,8,16,512]{4,3,2,1,0:T(8,128)(2,1)S(1)}, u32[]{:S(2)}, u32[]{:S(2)}) collective-permute-start(bf16[2,2,8,16,512]{4,3,2,1,0:T(8,128)(2,1)} %get-tuple-element.46.refs_1_.refs_0_), channel_id=1, source_target_pairs={{0,96},{4,28},{8,104},{12,4},{16,112},{20,12},{24,120},{28,20},{32... | collective-permute-start | bytes 1572872 | tf_op jit(solution)/shard_map/ppermute | solution.py:357
  133.5 12.0 %collective-permute-start.28 = (bf16[2,2,8,16,512]{4,3,2,1,0:T(8,128)(2,1)S(1)}, bf16[2,2,8,16,512]{4,3,2,1,0:T(8,128)(2,1)}, u32[]{:S(2)}, u32[]{:S(2)}) collective-permute-start(bf16[2,2,8,16,512]{4,3,2,1,0:T(8,128)(2,1)S(1)} %collective-permute-done.20.refs_4_), channel_id=1, source_target_pairs={{0,4},{4,0},{1,5},{5,1},{2,6},{6,2},{3,7},{7,3},{8,12},{12,8},{9,1... | collective-permute-start | bytes 1572872 | tf_op jit(solution)/shard_map/ppermute | solution.py:338
  134.8 14.1 %collective-permute-start.22 = (bf16[2,2,8,16,512]{4,3,2,1,0:T(8,128)(2,1)S(1)}, bf16[2,2,8,16,512]{4,3,2,1,0:T(8,128)(2,1)}, u32[]{:S(2)}, u32[]{:S(2)}) collective-permute-start(bf16[2,2,8,16,512]{4,3,2,1,0:T(8,128)(2,1)S(1)} %collective-permute-done.18.refs_2_), channel_id=1, source_target_pairs={{0,32},{4,12},{8,40},{12,20},{16,48},{20,28},{24,56},{28,4},{32,64... | collective-permute-start | bytes 1572872 | tf_op jit(solution)/shard_map/ppermute | solution.py:357
  137.9 14.4 %collective-permute-start.23 = (bf16[2,2,8,16,512]{4,3,2,1,0:T(8,128)(2,1)S(1)}, bf16[2,2,8,16,512]{4,3,2,1,0:T(8,128)(2,1)}, u32[]{:S(2)}, u32[]{:S(2)}) collective-permute-start(bf16[2,2,8,16,512]{4,3,2,1,0:T(8,128)(2,1)S(1)} %collective-permute-done.21.refs_5_), channel_id=1, source_target_pairs={{0,96},{4,28},{8,104},{12,4},{16,112},{20,12},{24,120},{28,20},{32... | collective-permute-start | bytes 1572872 | tf_op jit(solution)/shard_map/ppermute | solution.py:357
  141.3 18.9 %all-to-all-start.2 = ((bf16[16,96,256]{2,1,0:T(8,128)(2,1)}), bf16[16,96,256]{2,1,0:T(8,128)(2,1)S(1)}, u32[]{:S(2)}, u32[]{:S(2)}) async-start(bf16[16,96,256]{2,1,0:T(8,128)(2,1)} %shard_map.77), calls=%async_computation.2 | async-start | bytes 1572864 | tf_op jit(solution)/shard_map/all_to_all | solution.py:366
  144.9 15.3 %collective-permute-start.26 = (bf16[2,2,8,16,512]{4,3,2,1,0:T(8,128)(2,1)S(1)}, bf16[2,2,8,16,512]{4,3,2,1,0:T(8,128)(2,1)S(1)}, u32[]{:S(2)}, u32[]{:S(2)}) collective-permute-start(bf16[2,2,8,16,512]{4,3,2,1,0:T(8,128)(2,1)S(1)} %collective-permute-done.18.refs_2_), channel_id=1, source_target_pairs={{0,4},{4,0},{1,5},{5,1},{2,6},{6,2},{3,7},{7,3},{8,12},{12,8},{9,1... | collective-permute-start | bytes 1572872 | tf_op jit(solution)/shard_map/ppermute | solution.py:338
  145.1 15.2 %collective-permute-start.29 = (bf16[2,2,8,16,512]{4,3,2,1,0:T(8,128)(2,1)S(1)}, bf16[2,2,8,16,512]{4,3,2,1,0:T(8,128)(2,1)}, u32[]{:S(2)}, u32[]{:S(2)}) collective-permute-start(bf16[2,2,8,16,512]{4,3,2,1,0:T(8,128)(2,1)S(1)} %collective-permute-done.21.refs_5_), channel_id=1, source_target_pairs={{0,4},{4,0},{1,5},{5,1},{2,6},{6,2},{3,7},{7,3},{8,12},{12,8},{9,1... | collective-permute-start | bytes 1572872 | tf_op jit(solution)/shard_map/ppermute | solution.py:338
  145.5 14.7 %collective-permute-start.27 = (bf16[2,2,8,16,512]{4,3,2,1,0:T(8,128)(2,1)}, bf16[2,2,8,16,512]{4,3,2,1,0:T(8,128)(2,1)S(1)}, u32[]{:S(2)}, u32[]{:S(2)}) collective-permute-start(bf16[2,2,8,16,512]{4,3,2,1,0:T(8,128)(2,1)} %collective-permute-done.19.refs_3_), channel_id=1, source_target_pairs={{0,4},{4,0},{1,5},{5,1},{2,6},{6,2},{3,7},{7,3},{8,12},{12,8},{9,1... | collective-permute-start | bytes 1572872 | tf_op jit(solution)/shard_map/ppermute | solution.py:338
  179.6 20.6 %collective-permute-start.34 = (bf16[464,256]{1,0:T(8,128)(2,1)S(1)}, bf16[464,256]{1,0:T(8,128)(2,1)S(1)}, u32[]{:S(2)}, u32[]{:S(2)}) collective-permute-start(bf16[464,256]{1,0:T(8,128)(2,1)S(1)} %copy-done.34), channel_id=1, source_target_pairs={{0,1},{1,2},{2,3},{3,0},{4,5},{5,6},{6,7},{7,4},{8,9},{9,10},{10,1... | collective-permute-start | bytes 712712 | tf_op jit(solution)/shard_map/ppermute | solution.py:342
  180.9 19.4 %collective-permute-start.35 = (bf16[464,256]{1,0:T(8,128)(2,1)S(1)}, bf16[464,256]{1,0:T(8,128)(2,1)S(1)}, u32[]{:S(2)}, u32[]{:S(2)}) collective-permute-start(bf16[464,256]{1,0:T(8,128)(2,1)S(1)} %copy-done.33), channel_id=1, source_target_pairs={{0,3},{1,0},{2,1},{3,2},{4,7},{5,4},{6,5},{7,6},{8,11},{9,8},{10,9... | collective-permute-start | bytes 712712 | tf_op jit(solution)/shard_map/ppermute | solution.py:342
  182.3 17.9 %collective-permute-start.36 = (bf16[464,256]{1,0:T(8,128)(2,1)S(1)}, bf16[464,256]{1,0:T(8,128)(2,1)S(1)}, u32[]{:S(2)}, u32[]{:S(2)}) collective-permute-start(bf16[464,256]{1,0:T(8,128)(2,1)S(1)} %copy-done.32), channel_id=1, source_target_pairs={{0,2},{1,3},{2,0},{3,1},{4,6},{5,7},{6,4},{7,5},{8,10},{9,11},{10,... | collective-permute-start | bytes 712712 | tf_op jit(solution)/shard_map/ppermute | solution.py:342
  204.9 13.7 %all-to-all-start.3 = ((bf16[16,80,256]{2,1,0:T(8,128)(2,1)}), bf16[16,80,256]{2,1,0:T(8,128)(2,1)S(1)}, u32[]{:S(2)}, u32[]{:S(2)}) async-start(bf16[16,80,256]{2,1,0:T(8,128)(2,1)} %shard_map.79), calls=%async_computation.3 | async-start | bytes 1310720 | tf_op jit(solution)/shard_map/all_to_all | solution.py:366
  (57 other events, 337.4 us)

commit v4 on v3

--- a/solution.py
+++ b/solution.py
@@ -37,7 +37,7 @@
     return lax.rem(value + 8, 4)
 
 
-def split_kernel(x_ref, hg_ref, first_ref, second_ref, wide):
+def split_kernel(x_ref, hg_ref, first_ref, wide):
     for t in range(GROUPS):
         wide[t] = x_ref[:, CH * t : CH * (t + 1)].astype(F32)
     for t in range(2):
@@ -46,8 +46,6 @@
         for t in range(GROUPS + 2):
             part = wide[t, pl.ds(v, 32, stride=4), :].astype(BF)
             if t < GROUPS:
-                second_ref[t, 16 * v : 16 * (v + 1), :] = part[0:16]
-                second_ref[t, 64 + 16 * v : 80 + 16 * v, :] = part[16:32]
                 place = CH * (t % 4)
                 first_ref[4 * (t // 4) + v, :, place : place + CH] = part
             else:
@@ -72,11 +70,12 @@
 
 
 def forward_kernel(pos_ref, x_ref, hg_ref, *refs):
-    blocks, outs, (w, xs, total, sem) = refs[:10], refs[10:15], refs[15:]
-    own_ref, plus_ref, minus_ref, plus_half, minus_half = outs
+    blocks, outs, pieces, (w, xs, total, sem) = refs[:10], refs[10:14], refs[14:18], refs[18:]
     copies = weight_copies(pos_ref, blocks, w, sem)
     for copy in copies:
         copy.start()
+    for step in range(4):
+        pieces[step][...] = x_ref[:, pl.ds(pl.multiple_of(wrap(pos_ref[1] + step) * CH, CH), CH)]
     wide = x_ref[:, 0:KCH].astype(F32)
     colsum = jnp.broadcast_to(jnp.sum(wide, axis=0, keepdims=True), (8, KCH))
     for slot, amount in enumerate(SHIFTS):
@@ -103,22 +102,10 @@
             else:
                 total[out_low:out_high, cols] += part
     extra = jnp.concatenate([pool, hsum, jnp.zeros((8, 512), F32)], axis=1)
-    z = pos_ref[0]
-
-    def rows(step, low, size):
-        return total[pl.ds(pl.multiple_of(wrap(z + step) * 128 + low, 64), size), :]
-
-    own_ref[0:128, :] = rows(0, 0, 128)
-    own_ref[128:136, :] = extra
-    plus_ref[0:64, :] = rows(2, 0, 64)
-    plus_ref[64:128, :] = rows(1, 64, 64)
-    plus_ref[128:136, :] = extra
-    minus_ref[0:64, :] = rows(2, 64, 64)
-    minus_ref[64:72, :] = extra
-    minus_ref[72:136, :] = rows(-1, 0, 64)
-    plus_half[...] = rows(1, 0, 64)
-    minus_half[0:64, :] = rows(-1, 64, 64)
-    minus_half[64:72, :] = extra
+    for step in range(4):
+        rows = pl.ds(pl.multiple_of(wrap(pos_ref[0] + step) * 128, 128), 128)
+        outs[step][0:128, :] = total[rows, :]
+        outs[step][128:136, :] = extra
 
 
 def pair_kernel(first_ref, second_ref, out_ref):
@@ -126,29 +113,33 @@
     out_ref[1] = second_ref[...]
 
 
-def stack_kernel(first_ref, second_ref, out_ref, sums_ref):
+def group_kernel(*refs):
+    parts, (out_ref, sums_ref) = refs[:4], refs[4:]
     total = jnp.zeros((16, 512), F32)
-    for k, ref in enumerate((first_ref, second_ref)):
+    for k in range(4):
         for side in range(2):
-            out_ref[k, side] = ref[side, 0:8]
-            total = total + ref[side, 8].astype(F32)
+            out_ref[k, side] = parts[k][side, 0:8]
+            total = total + parts[k][side, 8].astype(F32)
     sums_ref[...] = jnp.broadcast_to(jnp.sum(total, axis=0, keepdims=True), (8, 512))
 
 
-def turn_kernel(x_ref, xt_ref, colsum_ref):
+def turn_kernel(pos_ref, *refs):
+    pieces, (xt_ref, colsum_ref, joined) = refs[:4], refs[4:]
+    for k in range(4):
+        joined[:, wrap(pos_ref[1] - k)] = pieces[k][...].reshape(32, 16, CH)
     total = jnp.zeros((1, CH), F32)
     for m in range(4):
-        wide = x_ref[pl.ds(m * 512, 512), :].astype(F32)
+        wide = joined[8 * m : 8 * (m + 1)].reshape(512, CH).astype(F32)
         total = total + jnp.sum(wide, axis=0, keepdims=True)
         for slot, amount in enumerate(SHIFTS):
             xt_ref[slot, :, pl.ds(m * 512, 512)] = column_shift(wide, amount).T.astype(BF)
     colsum_ref[...] = jnp.broadcast_to(total, (8, CH))
 
 
-def middle_kernel(pos_ref, own, from_low, from_high, half_a, half_b, x_ref, pw_ref, _, keep_ref, give_ref, pay_ref):
-    top = own[0:64, :] + from_high[72:136, :] + half_a[...]
-    bottom = own[64:136, :] + from_low[64:136, :] + half_b[...]
-    pre = jnp.concatenate([top, bottom[0:64, :]], axis=0)
+def middle_kernel(pos_ref, *refs):
+    parts, (x_ref, pw_ref, _, keep_ref, give_ref, pay_ref) = refs[:4], refs[4:]
+    whole = parts[0][...] + parts[1][...] + parts[2][...] + parts[3][...]
+    pre = whole[0:128, :]
     act = jnp.maximum(pre, 0.0).astype(BF)
     low = pw_ref[0:1024, :]
     hg = x_ref[pl.ds(pl.multiple_of(pos_ref[0] * 128, 128), 128), KCH:]
@@ -157,7 +148,7 @@
     first = pos_ref[2] == 0
     keep_ref[0:8] = jnp.where(first, grads[:, 0:512], grads[:, 512:1024]).astype(BF).reshape(8, 16, 512)
     give_ref[0:8] = jnp.where(first, grads[:, 512:1024], grads[:, 0:512]).astype(BF).reshape(8, 16, 512)
-    sums = jnp.concatenate([bottom[64:72, 0:512]] * 2, axis=0)
+    sums = jnp.concatenate([whole[128:136, 0:512]] * 2, axis=0)
     one = sums.astype(BF).astype(F32)
     two = (sums - one).astype(BF).astype(F32)
     row = lax.broadcasted_iota(jnp.int32, sums.shape, 0)
@@ -186,11 +177,14 @@
     outer_ref[...] = whole[pl.ds(pl.multiple_of(chunk * 16, 16), 16), :]
 
 
-def collect_kernel(pos_ref, pay_ref, const_ref, part_ref, head_ref, wide):
+def collect_kernel(pay_ref, part_ref):
     total = pay_ref[0, 0:64, :].astype(F32)
     for t in range(1, GROUPS):
         total = total + pay_ref[t, 0:64, :].astype(F32)
     part_ref[...] = total
+
+
+def head_kernel(pos_ref, pay_ref, const_ref, head_ref, wide):
     for v in range(4):
         piece = pay_ref[4 * pos_ref[0] + v, 64:96, :].astype(F32) + const_ref[0:1, :]
         wide[0, pl.ds(v, 32, stride=4), :] = piece[:, 0:128]
@@ -206,7 +200,7 @@
         half = c if side == 0 else 1 - c
         for place, far in enumerate((0, -1, 1, 2)):
             for k, step in enumerate((0, -1, 1, 2)):
-                src = blocks[8 * side + 2 * place + k // 2].at[k % 2, side]
+                src = blocks[4 * side + place].at[k, side]
                 v = wrap(y + jnp.where(half == 0, step, far))
                 group = wrap(z + jnp.where(half == 0, far, step))
                 cols = pl.ds(pl.multiple_of(512 * half, 512), 512)
@@ -216,7 +210,7 @@
 
 
 def weight_grad_kernel(pos_ref, xt_ref, colsum_ref, grad_ref, *refs):
-    blocks, (own_ref, other_ref), (g, dw, sem) = refs[:16], refs[-5:-3], refs[-3:]
+    blocks, (own_ref, other_ref), (g, dw, sem) = refs[:8], refs[-5:-3], refs[-3:]
     copies = gather_copies(pos_ref, blocks, g, sem, 0)
     for copy in copies:
         copy.start()
@@ -246,7 +240,7 @@
 
 
 def field_grad_kernel(pos_ref, grad_ref, own, other, *refs):
-    blocks, dx_ref, (g, w, whole, sem) = refs[:16], refs[-5], refs[-4:]
+    blocks, dx_ref, (g, w, whole, sem) = refs[:8], refs[-5], refs[-4:]
     copies = gather_copies(pos_ref, blocks, g, sem, PAD)
     for copy in copies:
         copy.start()
@@ -365,9 +359,8 @@
     def exchange(value):
         return lax.all_to_all(value, plane, split_axis=0, concat_axis=0, tiled=True)
 
-    first, second = call(
-        split_kernel,
-        (shape((GROUPS, 32, KCH + BR), BF), shape((GROUPS, 128, CH), BF)),
+    first = call(
+        split_kernel, shape((GROUPS, 32, KCH + BR), BF),
         [pltpu.VMEM((GROUPS + 2, 128, CH), F32)], 10**6,
         features.reshape(128, 2048), head_grad.reshape(128, BR), scalar=False,
     )
@@ -376,52 +369,51 @@
     below, above = gate((below, above), (x,))
     blocks = [branch_weight, below, above, send(below[0:CUT], "y", 1), send(above[CUT:29], "y", -1)]
     blocks = blocks + [swap(b) for b in blocks]
-    own, plus, minus, plus_half, minus_half = call(
+    results = call(
         forward_kernel,
-        tuple(shape((n, 1024), F32) for n in (136, 136, 136, 64, 72)),
+        (shape((136, 1024), F32),) * 4 + (shape((512, CH), BF),) * 4,
         [
             pltpu.VMEM((29, KCH, BR), BF), pltpu.VMEM((7, 512, KCH), BF), pltpu.VMEM((512, 1024), F32),
             pltpu.SemaphoreType.DMA((10,)),
         ],
         4 * 10**9, pos, x, head_grad.reshape(128, BR), *blocks, raw=10,
     )
-    from_low, from_high = send(plus, "z", 1), send(minus, "z", -1)
-    half_a = send(plus_half + from_low[0:64], "z", 1)
-    half_b = send(minus_half + from_high[0:72], "z", -1)
-    (second,) = gate((second,), (own,))
+    sums = [results[0]] + [send(results[k], "z", k) for k in (1, 3, 2)]
+    pieces = [results[4]] + [send(results[4 + k], "y", k) for k in (1, 2, 3)]
     turned, colsum = call(
-        turn_kernel, (shape((7, CH, HALF), BF), shape((8, CH), F32)), [], 10**8,
-        exchange(second).reshape(HALF, CH), scalar=False,
+        turn_kernel, (shape((7, CH, HALF), BF), shape((8, CH), F32)), [pltpu.VMEM((32, 4, 16, CH), BF)], 10**8,
+        pos, *pieces,
     )
     keep, give, pay = call(
         middle_kernel,
         (shape((9, 16, 512), BF), shape((9, 16, 512), BF), shape((GROUPS, 96, BR), BF)),
-        [], 2 * 10**8, pos, own, from_low, from_high, half_a, half_b, x, proj_weight, turned, raw=1,
+        [], 2 * 10**8, pos, *sums, x, proj_weight, turned, raw=1,
     )
     block = call(pair_kernel, shape((2, 9, 16, 512), BF), [], 10**5, keep, swap(give), scalar=False)
     near = [block, cross(block, 1, False), cross(block, -1, False), cross(block, 2, False)]
-    stacked = (shape((2, 2, 8, 16, 512), BF), shape((8, 512), F32))
-    low, low_sums = call(stack_kernel, stacked, [], 10**5, near[0], near[1], scalar=False)
-    high, high_sums = call(stack_kernel, stacked, [], 10**5, near[2], near[3], scalar=False)
-    low_below, high_above = cross(low, 1, True), cross(high, -1, True)
-    high_below, low_above = cross(high, 1, True), cross(low, -1, True)
-    every = [
-        low, high, low_below, high_below, low_above, high_above, cross(low_below, 1, True), cross(high_above, -1, True)
-    ]
-    every = every + [swap(piece) for piece in every]
-    sums = low_sums + high_sums
+    group, sums = call(
+        group_kernel, (shape((4, 2, 8, 16, 512), BF), shape((8, 512), F32)), [], 10**5, *near, scalar=False
+    )
+    every = [group] + [cross(group, step, True) for step in (1, -1, 2)]
     sums = jnp.where(pos[2] == 0, sums, swap(sums))
     const, pool_grad, outer = call(
         pool_kernel, (shape((8, BR), F32), shape((8, BR), F32), shape((16, BR), F32)), [pltpu.VMEM((256, BR), F32)],
         10**7, pos, sums, proj_weight,
     )
-    (pay,) = gate((pay,), (low, high))
     pay = exchange(pay)
+    part = call(collect_kernel, shape((64, BR), F32), [], 10**6, pay, scalar=False)
+    part = jnp.concatenate([part + swap(part), outer], axis=0)
+    part = part + pair(part, "rep", 1)
+    part = part + pair(part, "rep", 2)
+    part = jnp.broadcast_to(part.astype(BF)[None], (GROUPS, 80, BR))
+    theirs = [swap(piece) for piece in every[0:3]]
+    (far,) = gate((every[3],), (part, theirs[1], theirs[2]))
+    every = every[0:3] + [far] + theirs + [swap(far)]
     dw, dw_other = call(
         weight_grad_kernel,
         (shape((29, 64, BR), BF), shape((29, 64, BR), BF)),
         [pltpu.VMEM((2 * GROUPS, 4, 16, 1024), BF), pltpu.VMEM((29, CH, BR), F32), pltpu.SemaphoreType.DMA((32,))],
-        4 * 10**9, pos, turned, colsum, pool_grad, *every, pay, raw=17,
+        4 * 10**9, pos, turned, colsum, pool_grad, *every, raw=8,
     )
     quarters = call(
         add_kernel, (shape((464, BR), BF),) * 4, [], 10**6, pos, dw.reshape(1856, BR), swap(dw_other).reshape(1856, BR)
@@ -433,24 +425,17 @@
             pltpu.VMEM((2 * (GROUPS + 2 * PAD), 4, 16, 1024), BF), pltpu.VMEM((29, CH, BR), BF),
             pltpu.VMEM((HALF, CH), F32), pltpu.SemaphoreType.DMA((32,)),
         ],
-        4 * 10**9, pos, pool_grad, branch_weight, blocks[5], *every, quarters[0], raw=17,
+        4 * 10**9, pos, pool_grad, branch_weight, blocks[5], *every, quarters[0], raw=9,
     )
     terms = [quarters[0]] + [send(quarters[k], "rep", k) for k in (1, 3, 2)]
     dw = sum(term.astype(F32) for term in terms).astype(BF)
     dw = [dw] + [send(dw, "rep", step) for step in (1, -1, 2)]
     grad_branch = call(join_kernel, shape((1856, BR), F32), [], 10**6, pos, *dw).reshape(29, 64, BR)
-    (pay,) = gate((pay,), (quarters[0],))
-    part, head_out = call(
-        collect_kernel, (shape((64, BR), F32), shape((128, BR), BF)), [pltpu.VMEM((2, 128, 128), F32)],
-        10**6, pos, pay, const,
-    )
-    part = jnp.concatenate([part + swap(part), outer], axis=0)
-    part = part + pair(part, "rep", 1)
-    part = part + pair(part, "rep", 2)
-    part = jnp.broadcast_to(part.astype(BF)[None], (GROUPS, 80, BR))
-    (part,) = gate((part,), (dw[0],))
-    part = exchange(part).astype(F32)
+    (part,) = gate((exchange(part),), (dw[0],))
+    part = part.astype(F32)
     grad_proj = jnp.concatenate([part[:, 0:64].reshape(1024, BR), part[:, 64:80].reshape(256, BR)], axis=0)
+    (const,) = gate((const,), (dw[0],))
+    head_out = call(head_kernel, shape((128, BR), BF), [pltpu.VMEM((2, 128, 128), F32)], 10**6, pos, pay, const)
     mine, theirs = dx[0], swap(dx[1])
     even = jnp.where(pos[2] == 0, mine, theirs).reshape(GROUPS, 1, 2, 64, 64)
     odd = jnp.where(pos[2] == 0, theirs, mine).reshape(GROUPS, 1, 2, 64, 64)

time: 224 us -> 239 us (1.067); the launches traced: 220 us -> 238 us
  starting transfers between devices: 63.2 us -> 79.7 us
  local copies, waits for them, and re-layouts: 14.1 us -> 18.1 us
  waiting for transfers between devices: 51.9 us -> 48.3 us
    ppermute x18 -> x14, starting transfers between devices: 16.5 us -> 33.9 us  [swap(): return lax.ppermute(value, 'core', [(0, 1), (1, 0)])]
    all_to_all x3 -> x2, waiting for transfers between devices: 7.68 us -> 0.01 us  [exchange(): return lax.all_to_all(value, plane, split_axis=0, concat_axis=0, tiled=True)]
    ppermute x14 -> x16, starting transfers between devices: 18 us -> 22.9 us  [send(): return lax.ppermute(value, axis, [(k, (k + step) % 4) for k in range(4)])]
    all_to_all x3 -> x2, starting transfers between devices: 13.9 us -> 9.53 us  [exchange(): return lax.all_to_all(value, plane, split_axis=0, concat_axis=0, tiled=True)]
    ppermute x2, waiting for transfers between devices: 0.32 us -> 3.85 us  [pair(): return lax.ppermute(value, axis, [(k, k ^ bit) for k in range(4)])]
    ppermute x9 -> x6, starting transfers between devices: 12.3 us -> 9.46 us  [cross(): return lax.ppermute(value, ('z', 'y', 'core'), pairs)]
    unnamed x70 -> x58, local copies, waits for them, and re-layouts: 8.81 us -> 10.7 us
    ppermute x18 -> x14, waiting for transfers between devices: 5.92 us -> 4.85 us  [swap(): return lax.ppermute(value, 'core', [(0, 1), (1, 0)])]
  transfers between devices with their start and end apart: 46 -> 40, of which waited for: 19 -> 16; matrix products, arithmetic and copies ran while one was open for 3% -> 5% of each run, Pallas kernels for 11% -> 10%
where the time goes in v4:
time: 239 us; the launch traced here: 238 us
  starting transfers between devices  79.7 us (33%)
  Pallas kernels  53.5 us (22%)
  waiting for transfers between devices  48.3 us (20%)
  blocking collectives  31.9 us (13%)
  local copies, waits for them, and re-layouts  18.1 us (8%)
  other arithmetic  5.17 us (2%)
    pallas_call x13, Pallas kernels, call(): pl.pallas_call(kernel, out_shape=out_shape, in_specs=specs, out_specs=jax...  53.5 us
    ppermute x14, starting transfers between devices, swap(): return lax.ppermute(value, 'core', [(0, 1), (1, 0)])  33.9 us
    all_to_all x1, blocking collectives, exchange(): return lax.all_to_all(value, plane, split_axis=0, concat_axis=0, tiled=True)  31.9 us
    ppermute x16, starting transfers between devices, send(): return lax.ppermute(value, axis, [(k, (k + step) % 4) for k in range(4)])  22.9 us
    ppermute x16, waiting for transfers between devices, send(): return lax.ppermute(value, axis, [(k, (k + step) % 4) for k in range(4)])  22.7 us
    ppermute x6, waiting for transfers between devices, cross(): return lax.ppermute(value, ('z', 'y', 'core'), pairs)  17 us
    unnamed x58, local copies, waits for them, and re-layouts  10.7 us
    all_to_all x2, starting transfers between devices, exchange(): return lax.all_to_all(value, plane, split_axis=0, concat_axis=0, tiled=True)  9.53 us
  transfers between devices with their start and end apart: 40, of which 16 were waited for; matrix products, arithmetic and copies ran while one was open for 5% of the time, Pallas kernels for 10%

profile of v4, /device:TPU:1, one launch (start us, length us, event | category | flops | bytes accessed | tf_op | source)
XLA Modules:
  0.0 237.6 jit_solution(11163131085561232012)
XLA Ops:
  0.6 3.6 %collective-permute-start.1 = (bf16[29,64,256]{2,1,0:T(8,128)(2,1)}, bf16[29,64,256]{2,1,0:T(8,128)(2,1)S(1)}, u32[]{:S(2)}, u32[]{:S(2)}) collective-permute-start(bf16[29,64,256]{2,1,0:T(8,128)(2,1)} %own.1), channel_id=1, source_target_pairs={{0,24},{8,0},{16,8},{24,16},{1,25},{9,1},{17,9},{25,17},{2,26},{10... | collective-permute-start | bytes 2850824 | tf_op jit(solution)/shard_map/ppermute | solution.py:336
  6.4 31.9 %all_to_all.15 = bf16[16,32,768]{2,1,0:T(8,128)(2,1)} all-to-all(bf16[16,32,768]{2,1,0:T(8,128)(2,1)} %split_kernel.1), channel_id=1, replica_groups=mesh['z'=4,'y'=4,'core'=2,'rep'=4] {'z','y'}, dimensions={0} | all-to-all | bytes 1572864 | tf_op jit(solution)/shard_map/all_to_all | solution.py:360
  45.0 2.9 %collective-permute-start.3 = (bf16[14,64,256]{2,1,0:T(8,128)(2,1)S(1)}, bf16[14,64,256]{2,1,0:T(8,128)(2,1)}, u32[]{:S(2)}, u32[]{:S(2)}) collective-permute-start(bf16[14,64,256]{2,1,0:T(8,128)(2,1)S(1)} %slice.19), channel_id=1, source_target_pairs={{0,24},{8,0},{16,8},{24,16},{1,25},{9,1},{17,9},{25,17},{2,26},{10... | collective-permute-start | bytes 1376264 | tf_op jit(solution)/shard_map/ppermute | solution.py:336
  47.9 4.2 %collective-permute-done.2.refs_3_ = bf16[15,64,256]{2,1,0:T(8,128)(2,1)S(1)} collective-permute-done((bf16[15,64,256]{2,1,0:T(8,128)(2,1)S(1)}, bf16[15,64,256]{2,1,0:T(8,128)(2,1)S(1)}, u32[]{:S(2)}, u32[]{:S(2)}) %collective-permute-start.2) | collective-permute-done | bytes 491552 | tf_op jit(solution)/shard_map/ppermute | solution.py:336
  52.1 3.5 %collective-permute-start.7 = (bf16[15,64,256]{2,1,0:T(8,128)(2,1)S(1)}, bf16[15,64,256]{2,1,0:T(8,128)(2,1)}, u32[]{:S(2)}, u32[]{:S(2)}) collective-permute-start(bf16[15,64,256]{2,1,0:T(8,128)(2,1)S(1)} %collective-permute-done.2.refs_3_), channel_id=1, source_target_pairs={{0,4},{4,0},{1,5},{5,1},{2,6},{6,2},{3,7},{7,3},{8,12},{12,8},{9,1... | collective-permute-start | bytes 1474568 | tf_op jit(solution)/shard_map/ppermute | solution.py:332
  61.3 9.3 %forward_kernel.1 = (f32[136,1024]{1,0:T(8,128)}, f32[136,1024]{1,0:T(8,128)}, f32[136,1024]{1,0:T(8,128)}, f32[136,1024]{1,0:T(8,128)}, bf16[512,128]{1,0:T(8,1...) custom-call(s32[4]{0:T(128)} %pad_add_fusion.pos_ref, ...), custom_call_target="tpu_custom_call" | custom-call | flops 4000000000 | bytes 11206672 | tf_op jit(solution)/shard_map/forward_kernel/pallas_call | solution.py:307
  73.5 4.7 %collective-permute-start.13 = (bf16[512,128]{1,0:T(8,128)(2,1)}, bf16[512,128]{1,0:T(8,128)(2,1)S(1)}, u32[]{:S(2)}, u32[]{:S(2)}) collective-permute-start(bf16[512,128]{1,0:T(8,128)(2,1)} %get-tuple-element.38), channel_id=1, source_target_pairs={{0,16},{8,24},{16,0},{24,8},{1,17},{9,25},{17,1},{25,9},{2,18},{10... | collective-permute-start | bytes 393224 | tf_op jit(solution)/shard_map/ppermute | solution.py:336
  84.9 4.2 %turn_kernel.1 = (bf16[7,128,2048]{2,1,0:T(8,128)(2,1)}, f32[8,128]{1,0:T(8,128)}) custom-call(s32[4]{0:T(128)} %pad_add_fusion.pos_ref, bf16[512,128]{1,0:T(8,128)(2,1)} %get-tuple-element.36.refs_0_, bf16[512,128]{1,0:T(8,128)(2,1)} %copy-done.19, bf16[512,128]{1,0:T(8,128)(2,1)} %copy-done.20, bf16[512,128]{1,0:T(8,128)(2,1)} %copy-done.21), custom_call_target="tpu_custom_call" | custom-call | flops 100000000 | bytes 4198416 | tf_op jit(solution)/shard_map/turn_kernel/pallas_call | solution.py:307
  89.1 7.9 %collective-permute-done.11.refs_3_ = f32[136,1024]{1,0:T(8,128)S(1)} collective-permute-done((f32[136,1024]{1,0:T(8,128)}, f32[136,1024]{1,0:T(8,128)S(1)}, u32[]{:S(2)}, u32[]{:S(2)}) %collective-permute-start.11) | collective-permute-done | bytes 557088 | tf_op jit(solution)/shard_map/ppermute | solution.py:336
  97.8 3.5 %middle_kernel.1 = (bf16[9,16,512]{2,1,0:T(8,128)(2,1)}, bf16[9,16,512]{2,1,0:T(8,128)(2,1)}, bf16[16,96,256]{2,1,0:T(8,128)(2,1)}) custom-call(s32[4]{0:T(128)} %pad_add_fusion.pos_ref, f32[136,1024]{1,0:T(8,128)} %get-tuple-element.32.refs_0_, f32[136,1024]{1,0:T(8,128)} %copy-done.9, f32[136,1024]{1,0:T(8,128)} %copy-done.10, f32[136,1024]{1,0:T(8,128)} %copy-done.11, ...), custom_call_target="tpu_custom_call" | custom-call | flops 200000000 | bytes 8421392 | tf_op jit(solution)/shard_map/middle_kernel/pallas_call | solution.py:307
  110.4 4.5 %collective-permute-done.18.refs_3_ = bf16[2,9,16,512]{3,2,1,0:T(8,128)(2,1)S(1)} collective-permute-done((bf16[2,9,16,512]{3,2,1,0:T(8,128)(2,1)}, bf16[2,9,16,512]{3,2,1,0:T(8,128)(2,1)S(1)}, u32[]{:S(2)}, u32[]{:S(2)}) %collective-permute-start.18) | collective-permute-done | bytes 294944 | tf_op jit(solution)/shard_map/ppermute | solution.py:351
  114.9 3.3 %collective-permute-done.17.refs_2_ = bf16[2,9,16,512]{3,2,1,0:T(8,128)(2,1)S(1)} collective-permute-done((bf16[2,9,16,512]{3,2,1,0:T(8,128)(2,1)}, bf16[2,9,16,512]{3,2,1,0:T(8,128)(2,1)S(1)}, u32[]{:S(2)}, u32[]{:S(2)}) %collective-permute-start.17) | collective-permute-done | bytes 294944 | tf_op jit(solution)/shard_map/ppermute | solution.py:351
  121.9 3.5 %collective-permute-start.21 = (bf16[4,2,8,16,512]{4,3,2,1,0:T(8,128)(2,1)}, bf16[4,2,8,16,512]{4,3,2,1,0:T(8,128)(2,1)}, u32[]{:S(2)}, u32[]{:S(2)}) collective-permute-start(bf16[4,2,8,16,512]{4,3,2,1,0:T(8,128)(2,1)} %get-tuple-element.48.refs_0_), channel_id=1, source_target_pairs={{0,96},{4,28},{8,104},{12,4},{16,112},{20,12},{24,120},{28,20},{32... | collective-permute-start | bytes 3145736 | tf_op jit(solution)/shard_map/ppermute | solution.py:351
  125.4 5.9 %all-to-all-start.1 = ((bf16[16,96,256]{2,1,0:T(8,128)(2,1)}), bf16[16,96,256]{2,1,0:T(8,128)(2,1)S(1)}, u32[]{:S(2)}, u32[]{:S(2)}) async-start(bf16[16,96,256]{2,1,0:T(8,128)(2,1)} %get-tuple-element.41), calls=%async_computation.1 | async-start | bytes 1572864 | tf_op jit(solution)/shard_map/all_to_all | solution.py:360
  131.4 2.9 %collective-permute-start.22 = (bf16[4,2,8,16,512]{4,3,2,1,0:T(8,128)(2,1)}, bf16[4,2,8,16,512]{4,3,2,1,0:T(8,128)(2,1)}, u32[]{:S(2)}, u32[]{:S(2)}) collective-permute-start(bf16[4,2,8,16,512]{4,3,2,1,0:T(8,128)(2,1)} %get-tuple-element.48.refs_0_), channel_id=1, source_target_pairs={{0,64},{4,20},{8,72},{12,28},{16,80},{20,4},{24,88},{28,12},{32,96... | collective-permute-start | bytes 3145736 | tf_op jit(solution)/shard_map/ppermute | solution.py:351
  134.2 9.1 %collective-permute-done.21.refs_2_ = bf16[4,2,8,16,512]{4,3,2,1,0:T(8,128)(2,1)} collective-permute-done((bf16[4,2,8,16,512]{4,3,2,1,0:T(8,128)(2,1)}, bf16[4,2,8,16,512]{4,3,2,1,0:T(8,128)(2,1)}, u32[]{:S(2)}, u32[]{:S(2)}) %collective-permute-start.21) | collective-permute-done | bytes 1048608 | tf_op jit(solution)/shard_map/ppermute | solution.py:351
  143.4 14.8 %collective-permute-start.27 = (bf16[4,2,8,16,512]{4,3,2,1,0:T(8,128)(2,1)}, bf16[4,2,8,16,512]{4,3,2,1,0:T(8,128)(2,1)S(1)}, u32[]{:S(2)}, u32[]{:S(2)}) collective-permute-start(bf16[4,2,8,16,512]{4,3,2,1,0:T(8,128)(2,1)} %collective-permute-done.21.refs_2_), channel_id=1, source_target_pairs={{0,4},{4,0},{1,5},{5,1},{2,6},{6,2},{3,7},{7,3},{8,12},{12,8},{9,1... | collective-permute-start | bytes 3145736 | tf_op jit(solution)/shard_map/ppermute | solution.py:332
  158.2 4.2 %collective-permute-start.26 = (bf16[4,2,8,16,512]{4,3,2,1,0:T(8,128)(2,1)}, bf16[4,2,8,16,512]{4,3,2,1,0:T(8,128)(2,1)S(1)}, u32[]{:S(2)}, u32[]{:S(2)}) collective-permute-start(bf16[4,2,8,16,512]{4,3,2,1,0:T(8,128)(2,1)} %collective-permute-done.20.refs_1_), channel_id=1, source_target_pairs={{0,4},{4,0},{1,5},{5,1},{2,6},{6,2},{3,7},{7,3},{8,12},{12,8},{9,1... | collective-permute-start | bytes 3145736 | tf_op jit(solution)/shard_map/ppermute | solution.py:332
  171.4 2.9 %collective-permute-done.24 = f32[80,256]{1,0:T(8,128)S(1)} collective-permute-done((f32[80,256]{1,0:T(8,128)S(1)}, f32[80,256]{1,0:T(8,128)S(1)}, u32[]{:S(2)}, u32[]{:S(2)}) %collective-permute-start.24) | collective-permute-done | bytes 81952 | tf_op jit(solution)/shard_map/ppermute | solution.py:340
  175.0 2.8 %collective-permute-start.25 = (f32[80,256]{1,0:T(8,128)S(1)}, f32[80,256]{1,0:T(8,128)S(1)}, u32[]{:S(2)}, u32[]{:S(2)}) collective-permute-start(f32[80,256]{1,0:T(8,128)S(1)} %fusion), channel_id=1, source_target_pairs={{0,2},{1,3},{2,0},{3,1},{4,6},{5,7},{6,4},{7,5},{8,10},{9,11},{10,... | collective-permute-start | bytes 245768 | tf_op jit(solution)/shard_map/ppermute | solution.py:340
  186.9 9.3 %weight_grad_kernel.1 = (bf16[29,64,256]{2,1,0:T(8,128)(2,1)}, bf16[29,64,256]{2,1,0:T(8,128)(2,1)}) custom-call(s32[4]{0:T(128)} %pad_add_fusion.pos_ref, bf16[7,128,2048]{2,1,0:T(8,128)(2,1)} %get-tuple-element.40.refs_6_.xt_ref, f32[8,128]{1,0:T(8,128)} %get-tuple-element.46.colsum_ref, f32[8,256]{1,0:T(8,128)} %get-tuple-element.47.grad_ref, ...), custom_call_target="tpu_custom_call" | custom-call | flops 4000000000 | bytes 13971472 | tf_op jit(solution)/shard_map/weight_grad_kernel/pallas_call | solution.py:307
  196.6 3.6 %all-to-all-start.2 = ((bf16[16,80,256]{2,1,0:T(8,128)(2,1)}), bf16[16,80,256]{2,1,0:T(8,128)(2,1)S(1)}, u32[]{:S(2)}, u32[]{:S(2)}) async-start(bf16[16,80,256]{2,1,0:T(8,128)(2,1)} %broadcast_in_dim.2.refs_1_), calls=%async_computation.2 | async-start | bytes 1310720 | tf_op jit(solution)/shard_map/all_to_all | solution.py:360
  208.0 10.0 %field_grad_kernel.1 = bf16[2,2048,64]{2,1,0:T(8,128)(2,1)} custom-call(s32[4]{0:T(128)} %pad_add_fusion.pos_ref, f32[8,256]{1,0:T(8,128)} %get-tuple-element.47.grad_ref, bf16[29,64,256]{2,1,0:T(8,128)(2,1)} %own.1, bf16[29,64,256]{2,1,0:T(8,128)(2,1)} %copy-done.26, bf16[4,2,8,16,512]{4,3,2,1,0:T(8,128)(2,1)} %get-tuple-element.48.refs_0_, ...), custom_call_target="tpu_custom_call" | custom-call | flops 4000000000 | bytes 11059216 | tf_op jit(solution)/shard_map/field_grad_kernel/pallas_call | solution.py:307
  235.0 2.7 %join_kernel.1 = f32[1856,256]{1,0:T(8,128)} custom-call(s32[4]{0:T(128)} %pad_add_fusion.pos_ref, bf16[464,256]{1,0:T(8,128)(2,1)} %copy-done.2, bf16[464,256]{1,0:T(8,128)(2,1)} %collective-permute-done.35.refs_1_, bf16[464,256]{1,0:T(8,128)(2,1)} %copy-done.17, bf16[464,256]{1,0:T(8,128)(2,1)} %copy-done.16), custom_call_target="tpu_custom_call" | custom-call | flops 1000000 | bytes 2850832 | tf_op jit(solution)/shard_map/join_kernel/pallas_call | solution.py:307
  (149 shorter events, 81.5 us)
Async XLA Ops:
  0.6 37.6 %collective-permute-start.1 = (bf16[29,64,256]{2,1,0:T(8,128)(2,1)}, bf16[29,64,256]{2,1,0:T(8,128)(2,1)S(1)}, u32[]{:S(2)}, u32[]{:S(2)}) collective-permute-start(bf16[29,64,256]{2,1,0:T(8,128)(2,1)} %own.1), channel_id=1, source_target_pairs={{0,24},{8,0},{16,8},{24,16},{1,25},{9,1},{17,9},{25,17},{2,26},{10... | collective-permute-start | bytes 2850824 | tf_op jit(solution)/shard_map/ppermute | solution.py:336
  4.3 34.0 %collective-permute-start = (bf16[29,64,256]{2,1,0:T(8,128)(2,1)}, bf16[29,64,256]{2,1,0:T(8,128)(2,1)S(1)}, u32[]{:S(2)}, u32[]{:S(2)}) collective-permute-start(bf16[29,64,256]{2,1,0:T(8,128)(2,1)} %own.1), channel_id=1, source_target_pairs={{0,8},{8,16},{16,24},{24,0},{1,9},{9,17},{17,25},{25,1},{2,10},{10... | collective-permute-start | bytes 2850824 | tf_op jit(solution)/shard_map/ppermute | solution.py:336
  40.7 11.4 %collective-permute-start.2 = (bf16[15,64,256]{2,1,0:T(8,128)(2,1)S(1)}, bf16[15,64,256]{2,1,0:T(8,128)(2,1)S(1)}, u32[]{:S(2)}, u32[]{:S(2)}) collective-permute-start(bf16[15,64,256]{2,1,0:T(8,128)(2,1)S(1)} %slice.18), channel_id=1, source_target_pairs={{0,8},{8,16},{16,24},{24,0},{1,9},{9,17},{17,25},{25,1},{2,10},{10... | collective-permute-start | bytes 1474568 | tf_op jit(solution)/shard_map/ppermute | solution.py:336
  40.8 18.4 %collective-permute-start.4 = (bf16[29,64,256]{2,1,0:T(8,128)(2,1)S(1)}, bf16[29,64,256]{2,1,0:T(8,128)(2,1)S(1)}, u32[]{:S(2)}, u32[]{:S(2)}) collective-permute-start(bf16[29,64,256]{2,1,0:T(8,128)(2,1)S(1)} %copy-done.25), channel_id=1, source_target_pairs={{0,4},{4,0},{1,5},{5,1},{2,6},{6,2},{3,7},{7,3},{8,12},{12,8},{9,1... | collective-permute-start | bytes 2850824 | tf_op jit(solution)/shard_map/ppermute | solution.py:332
  43.4 17.0 %collective-permute-start.5 = (bf16[29,64,256]{2,1,0:T(8,128)(2,1)}, bf16[29,64,256]{2,1,0:T(8,128)(2,1)S(1)}, u32[]{:S(2)}, u32[]{:S(2)}) collective-permute-start(bf16[29,64,256]{2,1,0:T(8,128)(2,1)} %get-tuple-element.30.refs_1_), channel_id=1, source_target_pairs={{0,4},{4,0},{1,5},{5,1},{2,6},{6,2},{3,7},{7,3},{8,12},{12,8},{9,1... | collective-permute-start | bytes 2850824 | tf_op jit(solution)/shard_map/ppermute | solution.py:332
  43.5 16.9 %collective-permute-start.6 = (bf16[29,64,256]{2,1,0:T(8,128)(2,1)}, bf16[29,64,256]{2,1,0:T(8,128)(2,1)}, u32[]{:S(2)}, u32[]{:S(2)}) collective-permute-start(bf16[29,64,256]{2,1,0:T(8,128)(2,1)} %get-tuple-element.31.refs_2_), channel_id=1, source_target_pairs={{0,4},{4,0},{1,5},{5,1},{2,6},{6,2},{3,7},{7,3},{8,12},{12,8},{9,1... | collective-permute-start | bytes 2850824 | tf_op jit(solution)/shard_map/ppermute | solution.py:332
  45.0 12.9 %collective-permute-start.3 = (bf16[14,64,256]{2,1,0:T(8,128)(2,1)S(1)}, bf16[14,64,256]{2,1,0:T(8,128)(2,1)}, u32[]{:S(2)}, u32[]{:S(2)}) collective-permute-start(bf16[14,64,256]{2,1,0:T(8,128)(2,1)S(1)} %slice.19), channel_id=1, source_target_pairs={{0,24},{8,0},{16,8},{24,16},{1,25},{9,1},{17,9},{25,17},{2,26},{10... | collective-permute-start | bytes 1376264 | tf_op jit(solution)/shard_map/ppermute | solution.py:336
  70.6 18.5 %collective-permute-start.9 = (f32[136,1024]{1,0:T(8,128)}, f32[136,1024]{1,0:T(8,128)S(1)}, u32[]{:S(2)}, u32[]{:S(2)}) collective-permute-start(f32[136,1024]{1,0:T(8,128)} %get-tuple-element.33), channel_id=1, source_target_pairs={{0,32},{32,64},{64,96},{96,0},{1,33},{33,65},{65,97},{97,1},{2,34}... | collective-permute-start | bytes 1671176 | tf_op jit(solution)/shard_map/ppermute | solution.py:336
  71.2 17.8 %collective-permute-start.10 = (f32[136,1024]{1,0:T(8,128)}, f32[136,1024]{1,0:T(8,128)S(1)}, u32[]{:S(2)}, u32[]{:S(2)}) collective-permute-start(f32[136,1024]{1,0:T(8,128)} %get-tuple-element.34), channel_id=1, source_target_pairs={{0,96},{32,0},{64,32},{96,64},{1,97},{33,1},{65,33},{97,65},{2,98}... | collective-permute-start | bytes 1671176 | tf_op jit(solution)/shard_map/ppermute | solution.py:336
  73.3 23.7 %collective-permute-start.11 = (f32[136,1024]{1,0:T(8,128)}, f32[136,1024]{1,0:T(8,128)S(1)}, u32[]{:S(2)}, u32[]{:S(2)}) collective-permute-start(f32[136,1024]{1,0:T(8,128)} %get-tuple-element.35), channel_id=1, source_target_pairs={{0,64},{32,96},{64,0},{96,32},{1,65},{33,97},{65,1},{97,33},{2,66}... | collective-permute-start | bytes 1671176 | tf_op jit(solution)/shard_map/ppermute | solution.py:336
  107.8 10.4 %collective-permute-start.17 = (bf16[2,9,16,512]{3,2,1,0:T(8,128)(2,1)}, bf16[2,9,16,512]{3,2,1,0:T(8,128)(2,1)S(1)}, u32[]{:S(2)}, u32[]{:S(2)}) collective-permute-start(bf16[2,9,16,512]{3,2,1,0:T(8,128)(2,1)} %pair_kernel.1.refs_0_), channel_id=1, source_target_pairs={{0,24},{4,100},{8,0},{12,108},{16,8},{20,116},{24,16},{28,124},{32... | collective-permute-start | bytes 884744 | tf_op jit(solution)/shard_map/ppermute | solution.py:351
  121.9 21.5 %collective-permute-start.21 = (bf16[4,2,8,16,512]{4,3,2,1,0:T(8,128)(2,1)}, bf16[4,2,8,16,512]{4,3,2,1,0:T(8,128)(2,1)}, u32[]{:S(2)}, u32[]{:S(2)}) collective-permute-start(bf16[4,2,8,16,512]{4,3,2,1,0:T(8,128)(2,1)} %get-tuple-element.48.refs_0_), channel_id=1, source_target_pairs={{0,96},{4,28},{8,104},{12,4},{16,112},{20,12},{24,120},{28,20},{32... | collective-permute-start | bytes 3145736 | tf_op jit(solution)/shard_map/ppermute | solution.py:351
  125.4 32.8 %collective-permute-start.20 = (bf16[4,2,8,16,512]{4,3,2,1,0:T(8,128)(2,1)}, bf16[4,2,8,16,512]{4,3,2,1,0:T(8,128)(2,1)}, u32[]{:S(2)}, u32[]{:S(2)}) collective-permute-start(bf16[4,2,8,16,512]{4,3,2,1,0:T(8,128)(2,1)} %get-tuple-element.48.refs_0_), channel_id=1, source_target_pairs={{0,32},{4,12},{8,40},{12,20},{16,48},{20,28},{24,56},{28,4},{32,64... | collective-permute-start | bytes 3145736 | tf_op jit(solution)/shard_map/ppermute | solution.py:351
  125.4 37.0 %all-to-all-start.1 = ((bf16[16,96,256]{2,1,0:T(8,128)(2,1)}), bf16[16,96,256]{2,1,0:T(8,128)(2,1)S(1)}, u32[]{:S(2)}, u32[]{:S(2)}) async-start(bf16[16,96,256]{2,1,0:T(8,128)(2,1)} %get-tuple-element.41), calls=%async_computation.1 | async-start | bytes 1572864 | tf_op jit(solution)/shard_map/all_to_all | solution.py:360
  131.4 48.5 %collective-permute-start.22 = (bf16[4,2,8,16,512]{4,3,2,1,0:T(8,128)(2,1)}, bf16[4,2,8,16,512]{4,3,2,1,0:T(8,128)(2,1)}, u32[]{:S(2)}, u32[]{:S(2)}) collective-permute-start(bf16[4,2,8,16,512]{4,3,2,1,0:T(8,128)(2,1)} %get-tuple-element.48.refs_0_), channel_id=1, source_target_pairs={{0,64},{4,20},{8,72},{12,28},{16,80},{20,4},{24,88},{28,12},{32,96... | collective-permute-start | bytes 3145736 | tf_op jit(solution)/shard_map/ppermute | solution.py:351
  143.4 36.5 %collective-permute-start.27 = (bf16[4,2,8,16,512]{4,3,2,1,0:T(8,128)(2,1)}, bf16[4,2,8,16,512]{4,3,2,1,0:T(8,128)(2,1)S(1)}, u32[]{:S(2)}, u32[]{:S(2)}) collective-permute-start(bf16[4,2,8,16,512]{4,3,2,1,0:T(8,128)(2,1)} %collective-permute-done.21.refs_2_), channel_id=1, source_target_pairs={{0,4},{4,0},{1,5},{5,1},{2,6},{6,2},{3,7},{7,3},{8,12},{12,8},{9,1... | collective-permute-start | bytes 3145736 | tf_op jit(solution)/shard_map/ppermute | solution.py:332
  158.2 21.7 %collective-permute-start.26 = (bf16[4,2,8,16,512]{4,3,2,1,0:T(8,128)(2,1)}, bf16[4,2,8,16,512]{4,3,2,1,0:T(8,128)(2,1)S(1)}, u32[]{:S(2)}, u32[]{:S(2)}) collective-permute-start(bf16[4,2,8,16,512]{4,3,2,1,0:T(8,128)(2,1)} %collective-permute-done.20.refs_1_), channel_id=1, source_target_pairs={{0,4},{4,0},{1,5},{5,1},{2,6},{6,2},{3,7},{7,3},{8,12},{12,8},{9,1... | collective-permute-start | bytes 3145736 | tf_op jit(solution)/shard_map/ppermute | solution.py:332
  196.6 26.8 %all-to-all-start.2 = ((bf16[16,80,256]{2,1,0:T(8,128)(2,1)}), bf16[16,80,256]{2,1,0:T(8,128)(2,1)S(1)}, u32[]{:S(2)}, u32[]{:S(2)}) async-start(bf16[16,80,256]{2,1,0:T(8,128)(2,1)} %broadcast_in_dim.2.refs_1_), calls=%async_computation.2 | async-start | bytes 1310720 | tf_op jit(solution)/shard_map/all_to_all | solution.py:360
  203.8 16.5 %collective-permute-start.31 = (bf16[464,256]{1,0:T(8,128)(2,1)}, bf16[464,256]{1,0:T(8,128)(2,1)S(1)}, u32[]{:S(2)}, u32[]{:S(2)}) collective-permute-start(bf16[464,256]{1,0:T(8,128)(2,1)} %get-tuple-element.53), channel_id=1, source_target_pairs={{0,1},{1,2},{2,3},{3,0},{4,5},{5,6},{6,7},{7,4},{8,9},{9,10},{10,1... | collective-permute-start | bytes 712712 | tf_op jit(solution)/shard_map/ppermute | solution.py:336
  205.0 15.3 %collective-permute-start.32 = (bf16[464,256]{1,0:T(8,128)(2,1)}, bf16[464,256]{1,0:T(8,128)(2,1)S(1)}, u32[]{:S(2)}, u32[]{:S(2)}) collective-permute-start(bf16[464,256]{1,0:T(8,128)(2,1)} %get-tuple-element.54), channel_id=1, source_target_pairs={{0,3},{1,0},{2,1},{3,2},{4,7},{5,4},{6,5},{7,6},{8,11},{9,8},{10,9... | collective-permute-start | bytes 712712 | tf_op jit(solution)/shard_map/ppermute | solution.py:336
  206.5 13.8 %collective-permute-start.33 = (bf16[464,256]{1,0:T(8,128)(2,1)}, bf16[464,256]{1,0:T(8,128)(2,1)S(1)}, u32[]{:S(2)}, u32[]{:S(2)}) collective-permute-start(bf16[464,256]{1,0:T(8,128)(2,1)} %get-tuple-element.55), channel_id=1, source_target_pairs={{0,2},{1,3},{2,0},{3,1},{4,6},{5,7},{6,4},{7,5},{8,10},{9,11},{10,... | collective-permute-start | bytes 712712 | tf_op jit(solution)/shard_map/ppermute | solution.py:336
  220.5 10.8 %collective-permute-start.37 = (bf16[464,256]{1,0:T(8,128)(2,1)S(1)}, bf16[464,256]{1,0:T(8,128)(2,1)S(1)}, u32[]{:S(2)}, u32[]{:S(2)}) collective-permute-start(bf16[464,256]{1,0:T(8,128)(2,1)S(1)} %add_convert_fusion.refs_1_.refs_0_), channel_id=1, source_target_pairs={{0,2},{1,3},{2,0},{3,1},{4,6},{5,7},{6,4},{7,5},{8,10},{9,11},{10,... | collective-permute-start | bytes 712712 | tf_op jit(solution)/shard_map/ppermute | solution.py:336
  222.0 11.2 %collective-permute-start.36 = (bf16[464,256]{1,0:T(8,128)(2,1)S(1)}, bf16[464,256]{1,0:T(8,128)(2,1)S(1)}, u32[]{:S(2)}, u32[]{:S(2)}) collective-permute-start(bf16[464,256]{1,0:T(8,128)(2,1)S(1)} %add_convert_fusion.refs_1_.refs_0_), channel_id=1, source_target_pairs={{0,3},{1,0},{2,1},{3,2},{4,7},{5,4},{6,5},{7,6},{8,11},{9,8},{10,9... | collective-permute-start | bytes 712712 | tf_op jit(solution)/shard_map/ppermute | solution.py:336
  223.2 11.7 %collective-permute-start.35 = (bf16[464,256]{1,0:T(8,128)(2,1)S(1)}, bf16[464,256]{1,0:T(8,128)(2,1)}, u32[]{:S(2)}, u32[]{:S(2)}) collective-permute-start(bf16[464,256]{1,0:T(8,128)(2,1)S(1)} %add_convert_fusion.refs_1_.refs_0_), channel_id=1, source_target_pairs={{0,1},{1,2},{2,3},{3,0},{4,5},{5,6},{6,7},{7,4},{8,9},{9,10},{10,1... | collective-permute-start | bytes 712712 | tf_op jit(solution)/shard_map/ppermute | solution.py:336
  (45 other events, 204.7 us)

commit v5 on v4

--- a/solution.py
+++ b/solution.py
@@ -297,6 +297,9 @@
         refs[4][rows, :] = refs[k][...].astype(F32)
 
 
+ROOM = {"forward_kernel": 28, "weight_grad_kernel": 26, "field_grad_kernel": 28, "turn_kernel": 16, "middle_kernel": 16}
+
+
 def call(kernel, out_shape, scratch, flops, *args, scalar=True, raw=0):
     specs = [pl.BlockSpec(memory_space=pltpu.VMEM) for _ in args]
     if scalar:
@@ -310,7 +313,7 @@
         in_specs=specs,
         out_specs=jax.tree.map(lambda _: pl.BlockSpec(memory_space=pltpu.VMEM), out_shape),
         scratch_shapes=scratch,
-        compiler_params=pltpu.CompilerParams(vmem_limit_bytes=60 * 2**20),
+        compiler_params=pltpu.CompilerParams(vmem_limit_bytes=ROOM.get(kernel.__name__, 12) * 2**20),
         cost_estimate=pl.CostEstimate(flops=flops, bytes_accessed=moved, transcendentals=0),
         name=kernel.__name__,
     )(*args)
@@ -406,9 +409,9 @@
     part = part + pair(part, "rep", 1)
     part = part + pair(part, "rep", 2)
     part = jnp.broadcast_to(part.astype(BF)[None], (GROUPS, 80, BR))
-    theirs = [swap(piece) for piece in every[0:3]]
-    (far,) = gate((every[3],), (part, theirs[1], theirs[2]))
-    every = every[0:3] + [far] + theirs + [swap(far)]
+    below, = gate((every[1],), (part,))
+    every = [every[0], below] + every[2:4]
+    every = every + [swap(piece) for piece in every]
     dw, dw_other = call(
         weight_grad_kernel,
         (shape((29, 64, BR), BF), shape((29, 64, BR), BF)),

time: 239 us -> 209 us (0.87)
  Pallas kernels: 53.5 us -> 33.3 us
  starting transfers between devices: 79.7 us -> 65 us
  waiting for transfers between devices: 48.3 us -> 51.9 us
  local copies, waits for them, and re-layouts: 18.1 us -> 20.5 us
    pallas_call x13, Pallas kernels: 53.5 us -> 33.3 us  [call(): pl.pallas_call(kernel, out_shape=out_shape, in_specs=specs, out_specs=jax...]
    ppermute x14, starting transfers between devices: 33.9 us -> 18.6 us  [swap(): return lax.ppermute(value, 'core', [(0, 1), (1, 0)])]
    ppermute x6, waiting for transfers between devices: 17 us -> 19.5 us  [cross(): return lax.ppermute(value, ('z', 'y', 'core'), pairs)]
    unnamed x58 -> x46, local copies, waits for them, and re-layouts: 10.7 us -> 12.3 us
  transfers between devices with their start and end apart: 40 -> 40, of which waited for: 16 -> 19; matrix products, arithmetic and copies ran while one was open for 5% -> 5% of each run, Pallas kernels for 10% -> 8%
where the time goes in v5:
time: 209 us; the launch traced here: 208 us
  starting transfers between devices  65 us (31%)
  waiting for transfers between devices  51.9 us (25%)
  Pallas kernels  33.3 us (16%)
  blocking collectives  31.9 us (15%)
  local copies, waits for them, and re-layouts  20.5 us (10%)
  other arithmetic  3.97 us (2%)
    pallas_call x13, Pallas kernels, call(): pl.pallas_call(kernel, out_shape=out_shape, in_specs=specs, out_specs=jax...  33.3 us
    all_to_all x1, blocking collectives, exchange(): return lax.all_to_all(value, plane, split_axis=0, concat_axis=0, tiled=True)  31.9 us
    ppermute x16, waiting for transfers between devices, send(): return lax.ppermute(value, axis, [(k, (k + step) % 4) for k in range(4)])  23.4 us
    ppermute x16, starting transfers between devices, send(): return lax.ppermute(value, axis, [(k, (k + step) % 4) for k in range(4)])  23 us
    ppermute x6, waiting for transfers between devices, cross(): return lax.ppermute(value, ('z', 'y', 'core'), pairs)  19.5 us
    ppermute x14, starting transfers between devices, swap(): return lax.ppermute(value, 'core', [(0, 1), (1, 0)])  18.6 us
    unnamed x46, local copies, waits for them, and re-layouts  12.3 us
    all_to_all x2, starting transfers between devices, exchange(): return lax.all_to_all(value, plane, split_axis=0, concat_axis=0, tiled=True)  11.5 us
  transfers between devices with their start and end apart: 40, of which 19 were waited for; matrix products, arithmetic and copies ran while one was open for 5% of the time, Pallas kernels for 8%

profile of v5, /device:TPU:1, one launch (start us, length us, event | category | flops | bytes accessed | tf_op | source)
XLA Modules:
  0.0 207.5 jit_solution(18006915805638732447)
XLA Ops:
  0.6 3.6 %collective-permute-start.1 = (bf16[29,64,256]{2,1,0:T(8,128)(2,1)}, bf16[29,64,256]{2,1,0:T(8,128)(2,1)S(1)}, u32[]{:S(2)}, u32[]{:S(2)}) collective-permute-start(bf16[29,64,256]{2,1,0:T(8,128)(2,1)} %own.1), channel_id=1, source_target_pairs={{0,24},{8,0},{16,8},{24,16},{1,25},{9,1},{17,9},{25,17},{2,26},{10... | collective-permute-start | bytes 2850824 | tf_op jit(solution)/shard_map/ppermute | solution.py:339
  6.3 31.9 %all_to_all.15 = bf16[16,32,768]{2,1,0:T(8,128)(2,1)} all-to-all(bf16[16,32,768]{2,1,0:T(8,128)(2,1)S(1)} %split_kernel.1), channel_id=1, replica_groups=mesh['z'=4,'y'=4,'core'=2,'rep'=4] {'z','y'}, dimensions={0} | all-to-all | bytes 1572864 | tf_op jit(solution)/shard_map/all_to_all | solution.py:363
  40.8 2.6 %collective-permute-start.4 = (bf16[29,64,256]{2,1,0:T(8,128)(2,1)}, bf16[29,64,256]{2,1,0:T(8,128)(2,1)}, u32[]{:S(2)}, u32[]{:S(2)}) collective-permute-start(bf16[29,64,256]{2,1,0:T(8,128)(2,1)} %own.1), channel_id=1, source_target_pairs={{0,4},{4,0},{1,5},{5,1},{2,6},{6,2},{3,7},{7,3},{8,12},{12,8},{9,1... | collective-permute-start | bytes 2850824 | tf_op jit(solution)/shard_map/ppermute | solution.py:335
  45.0 2.9 %collective-permute-start.3 = (bf16[14,64,256]{2,1,0:T(8,128)(2,1)S(1)}, bf16[14,64,256]{2,1,0:T(8,128)(2,1)}, u32[]{:S(2)}, u32[]{:S(2)}) collective-permute-start(bf16[14,64,256]{2,1,0:T(8,128)(2,1)S(1)} %slice.19), channel_id=1, source_target_pairs={{0,24},{8,0},{16,8},{24,16},{1,25},{9,1},{17,9},{25,17},{2,26},{10... | collective-permute-start | bytes 1376264 | tf_op jit(solution)/shard_map/ppermute | solution.py:339
  47.9 4.2 %collective-permute-done.2.refs_3_ = bf16[15,64,256]{2,1,0:T(8,128)(2,1)S(1)} collective-permute-done((bf16[15,64,256]{2,1,0:T(8,128)(2,1)S(1)}, bf16[15,64,256]{2,1,0:T(8,128)(2,1)S(1)}, u32[]{:S(2)}, u32[]{:S(2)}) %collective-permute-start.2) | collective-permute-done | bytes 491552 | tf_op jit(solution)/shard_map/ppermute | solution.py:339
  52.2 3.5 %collective-permute-start.7 = (bf16[15,64,256]{2,1,0:T(8,128)(2,1)S(1)}, bf16[15,64,256]{2,1,0:T(8,128)(2,1)}, u32[]{:S(2)}, u32[]{:S(2)}) collective-permute-start(bf16[15,64,256]{2,1,0:T(8,128)(2,1)S(1)} %collective-permute-done.2.refs_3_), channel_id=1, source_target_pairs={{0,4},{4,0},{1,5},{5,1},{2,6},{6,2},{3,7},{7,3},{8,12},{12,8},{9,1... | collective-permute-start | bytes 1474568 | tf_op jit(solution)/shard_map/ppermute | solution.py:335
  55.6 2.2 %collective-permute-done.3.refs_4_ = bf16[14,64,256]{2,1,0:T(8,128)(2,1)} collective-permute-done((bf16[14,64,256]{2,1,0:T(8,128)(2,1)S(1)}, bf16[14,64,256]{2,1,0:T(8,128)(2,1)}, u32[]{:S(2)}, u32[]{:S(2)}) %collective-permute-start.3) | collective-permute-done | bytes 458784 | tf_op jit(solution)/shard_map/ppermute | solution.py:339
  61.7 6.6 %forward_kernel.1 = (f32[136,1024]{1,0:T(8,128)S(1)}, f32[136,1024]{1,0:T(8,128)S(1)}, f32[136,1024]{1,0:T(8,128)S(1)}, f32[136,1024]{1,0:T(8,128)S(1)}, bf16[51...) custom-call(s32[4]{0:T(128)S(1)} %pad_add_fusion.pos_ref, ...), custom_call_target="tpu_custom_call" | custom-call | flops 4000000000 | bytes 11206672 | tf_op jit(solution)/shard_map/forward_kernel/pallas_call | solution.py:310
  71.2 4.7 %collective-permute-start.13 = (bf16[512,128]{1,0:T(8,128)(2,1)S(1)}, bf16[512,128]{1,0:T(8,128)(2,1)S(1)}, u32[]{:S(2)}, u32[]{:S(2)}) collective-permute-start(bf16[512,128]{1,0:T(8,128)(2,1)S(1)} %get-tuple-element.38), channel_id=1, source_target_pairs={{0,16},{8,24},{16,0},{24,8},{1,17},{9,25},{17,1},{25,9},{2,18},{10... | collective-permute-start | bytes 393224 | tf_op jit(solution)/shard_map/ppermute | solution.py:339
  84.2 10.3 %collective-permute-done.11.refs_3_ = f32[136,1024]{1,0:T(8,128)S(1)} collective-permute-done((f32[136,1024]{1,0:T(8,128)S(1)}, f32[136,1024]{1,0:T(8,128)S(1)}, u32[]{:S(2)}, u32[]{:S(2)}) %collective-permute-start.11) | collective-permute-done | bytes 557088 | tf_op jit(solution)/shard_map/ppermute | solution.py:339
  96.5 6.9 %all-to-all-start.1 = ((bf16[16,96,256]{2,1,0:T(8,128)(2,1)}), bf16[16,96,256]{2,1,0:T(8,128)(2,1)S(1)}, u32[]{:S(2)}, u32[]{:S(2)}) async-start(bf16[16,96,256]{2,1,0:T(8,128)(2,1)} %get-tuple-element.41), calls=%async_computation.1 | async-start | bytes 1572864 | tf_op jit(solution)/shard_map/all_to_all | solution.py:363
  103.5 2.8 %collective-permute-start.15 = (bf16[9,16,512]{2,1,0:T(8,128)(2,1)S(1)}, bf16[9,16,512]{2,1,0:T(8,128)(2,1)S(1)}, u32[]{:S(2)}, u32[]{:S(2)}) collective-permute-start(bf16[9,16,512]{2,1,0:T(8,128)(2,1)S(1)} %get-tuple-element.43), channel_id=1, source_target_pairs={{0,4},{4,0},{1,5},{5,1},{2,6},{6,2},{3,7},{7,3},{8,12},{12,8},{9,1... | collective-permute-start | bytes 442376 | tf_op jit(solution)/shard_map/ppermute | solution.py:335
  107.3 3.2 %collective-permute-start.18 = (bf16[2,9,16,512]{3,2,1,0:T(8,128)(2,1)S(1)}, bf16[2,9,16,512]{3,2,1,0:T(8,128)(2,1)S(1)}, u32[]{:S(2)}, u32[]{:S(2)}) collective-permute-start(bf16[2,9,16,512]{3,2,1,0:T(8,128)(2,1)S(1)} %pair_kernel.1.refs_0_), channel_id=1, source_target_pairs={{0,16},{4,68},{8,24},{12,76},{16,0},{20,84},{24,8},{28,92},{32,48}... | collective-permute-start | bytes 884744 | tf_op jit(solution)/shard_map/ppermute | solution.py:354
  111.9 8.3 %collective-permute-done.18.refs_3_ = bf16[2,9,16,512]{3,2,1,0:T(8,128)(2,1)S(1)} collective-permute-done((bf16[2,9,16,512]{3,2,1,0:T(8,128)(2,1)S(1)}, bf16[2,9,16,512]{3,2,1,0:T(8,128)(2,1)S(1)}, u32[]{:S(2)}, u32[]{:S(2)}) %collective-permute-start.18) | collective-permute-done | bytes 294944 | tf_op jit(solution)/shard_map/ppermute | solution.py:354
  120.2 2.3 %collective-permute-done.17.refs_2_ = bf16[2,9,16,512]{3,2,1,0:T(8,128)(2,1)S(1)} collective-permute-done((bf16[2,9,16,512]{3,2,1,0:T(8,128)(2,1)S(1)}, bf16[2,9,16,512]{3,2,1,0:T(8,128)(2,1)S(1)}, u32[]{:S(2)}, u32[]{:S(2)}) %collective-permute-start.17) | collective-permute-done | bytes 294944 | tf_op jit(solution)/shard_map/ppermute | solution.py:354
  132.4 2.6 %collective-permute-done.22 = f32[80,256]{1,0:T(8,128)S(1)} collective-permute-done((f32[80,256]{1,0:T(8,128)S(1)}, f32[80,256]{1,0:T(8,128)S(1)}, u32[]{:S(2)}, u32[]{:S(2)}) %collective-permute-start.22) | collective-permute-done | bytes 81952 | tf_op jit(solution)/shard_map/ppermute | solution.py:343
  135.0 2.8 %collective-permute-start.23 = (f32[80,256]{1,0:T(8,128)S(1)}, f32[80,256]{1,0:T(8,128)S(1)}, u32[]{:S(2)}, u32[]{:S(2)}) collective-permute-start(f32[80,256]{1,0:T(8,128)S(1)} %fusion), channel_id=1, source_target_pairs={{0,2},{1,3},{2,0},{3,1},{4,6},{5,7},{6,4},{7,5},{8,10},{9,11},{10,... | collective-permute-start | bytes 245768 | tf_op jit(solution)/shard_map/ppermute | solution.py:343
  142.2 8.2 %collective-permute-done.24.refs_2_ = bf16[4,2,8,16,512]{4,3,2,1,0:T(8,128)(2,1)} collective-permute-done((bf16[4,2,8,16,512]{4,3,2,1,0:T(8,128)(2,1)}, bf16[4,2,8,16,512]{4,3,2,1,0:T(8,128)(2,1)}, u32[]{:S(2)}, u32[]{:S(2)}) %collective-permute-start.24) | collective-permute-done | bytes 1048608 | tf_op jit(solution)/shard_map/ppermute | solution.py:354
  156.1 2.4 %copy-done.4 = bf16[7,128,2048]{2,1,0:T(8,128)(2,1)S(1)} copy-done((bf16[7,128,2048]{2,1,0:T(8,128)(2,1)S(1)}, bf16[7,128,2048]{2,1,0:T(8,128)(2,1)}, u32[]{:S(2)}) %copy-start.4) | copy-done | bytes 3670040
  160.9 7.2 %weight_grad_kernel.1 = (bf16[29,64,256]{2,1,0:T(8,128)(2,1)S(1)}, bf16[29,64,256]{2,1,0:T(8,128)(2,1)}) custom-call(s32[4]{0:T(128)S(1)} %pad_add_fusion.pos_ref, bf16[7,128,2048]{2,1,0:T(8,128)(2,1)S(1)} %copy-done.4, f32[8,128]{1,0:T(8,128)S(1)} %get-tuple-element.46.colsum_ref, f32[8,256]{1,0:T(8,128)S(1)} %get-tuple-element.47.grad_ref, ...), custom_call_target="tpu_custom_call" | custom-call | flops 4000000000 | bytes 13971472 | tf_op jit(solution)/shard_map/weight_grad_kernel/pallas_call | solution.py:310
  168.6 4.6 %all-to-all-start.2 = ((bf16[16,80,256]{2,1,0:T(8,128)(2,1)}), bf16[16,80,256]{2,1,0:T(8,128)(2,1)}, u32[]{:S(2)}, u32[]{:S(2)}) async-start(bf16[16,80,256]{2,1,0:T(8,128)(2,1)} %broadcast_in_dim.2.refs_1_), calls=%async_computation.2 | async-start | bytes 1310720 | tf_op jit(solution)/shard_map/all_to_all | solution.py:363
  180.2 8.6 %field_grad_kernel.1 = bf16[2,2048,64]{2,1,0:T(8,128)(2,1)S(1)} custom-call(s32[4]{0:T(128)S(1)} %pad_add_fusion.pos_ref, f32[8,256]{1,0:T(8,128)S(1)} %get-tuple-element.47.grad_ref, bf16[29,64,256]{2,1,0:T(8,128)(2,1)} %own.1, bf16[29,64,256]{2,1,0:T(8,128)(2,1)} %collective-permute-done.4.refs_5_.other, ...), custom_call_target="tpu_custom_call" | custom-call | flops 4000000000 | bytes 11059216 | tf_op jit(solution)/shard_map/field_grad_kernel/pallas_call | solution.py:310
  195.1 2.1 %slice.26 = f32[16,64,256]{2,1,0:T(8,128)} slice(bf16[16,80,256]{2,1,0:T(8,128)(2,1)} %shard_map.78), slice={[0:16], [0:64], [0:256]} | slice | bytes 2097152 | tf_op jit(solution)/shard_map/slice | solution.py:439
  199.2 2.4 %pad_maximum_fusion = f32[1280,256]{1,0:T(8,128)} fusion(f32[256,256]{1,0:T(8,128)S(1)} %bitcast.35, f32[1024,256]{1,0:T(8,128)} %bitcast.31), kind=kLoop, calls=%fused_computation | loop fusion | flops 327680 | bytes 2621440 | tf_op jit(solution)/shard_map/concatenate | solution.py:439
  (137 shorter events, 69.6 us)
Async XLA Ops:
  0.6 37.6 %collective-permute-start.1 = (bf16[29,64,256]{2,1,0:T(8,128)(2,1)}, bf16[29,64,256]{2,1,0:T(8,128)(2,1)S(1)}, u32[]{:S(2)}, u32[]{:S(2)}) collective-permute-start(bf16[29,64,256]{2,1,0:T(8,128)(2,1)} %own.1), channel_id=1, source_target_pairs={{0,24},{8,0},{16,8},{24,16},{1,25},{9,1},{17,9},{25,17},{2,26},{10... | collective-permute-start | bytes 2850824 | tf_op jit(solution)/shard_map/ppermute | solution.py:339
  4.3 34.0 %collective-permute-start = (bf16[29,64,256]{2,1,0:T(8,128)(2,1)}, bf16[29,64,256]{2,1,0:T(8,128)(2,1)S(1)}, u32[]{:S(2)}, u32[]{:S(2)}) collective-permute-start(bf16[29,64,256]{2,1,0:T(8,128)(2,1)} %own.1), channel_id=1, source_target_pairs={{0,8},{8,16},{16,24},{24,0},{1,9},{9,17},{17,25},{25,1},{2,10},{10... | collective-permute-start | bytes 2850824 | tf_op jit(solution)/shard_map/ppermute | solution.py:339
  40.8 17.9 %collective-permute-start.4 = (bf16[29,64,256]{2,1,0:T(8,128)(2,1)}, bf16[29,64,256]{2,1,0:T(8,128)(2,1)}, u32[]{:S(2)}, u32[]{:S(2)}) collective-permute-start(bf16[29,64,256]{2,1,0:T(8,128)(2,1)} %own.1), channel_id=1, source_target_pairs={{0,4},{4,0},{1,5},{5,1},{2,6},{6,2},{3,7},{7,3},{8,12},{12,8},{9,1... | collective-permute-start | bytes 2850824 | tf_op jit(solution)/shard_map/ppermute | solution.py:335
  43.4 17.0 %collective-permute-start.5 = (bf16[29,64,256]{2,1,0:T(8,128)(2,1)}, bf16[29,64,256]{2,1,0:T(8,128)(2,1)}, u32[]{:S(2)}, u32[]{:S(2)}) collective-permute-start(bf16[29,64,256]{2,1,0:T(8,128)(2,1)} %get-tuple-element.30.refs_1_), channel_id=1, source_target_pairs={{0,4},{4,0},{1,5},{5,1},{2,6},{6,2},{3,7},{7,3},{8,12},{12,8},{9,1... | collective-permute-start | bytes 2850824 | tf_op jit(solution)/shard_map/ppermute | solution.py:335
  43.5 16.9 %collective-permute-start.6 = (bf16[29,64,256]{2,1,0:T(8,128)(2,1)}, bf16[29,64,256]{2,1,0:T(8,128)(2,1)}, u32[]{:S(2)}, u32[]{:S(2)}) collective-permute-start(bf16[29,64,256]{2,1,0:T(8,128)(2,1)} %get-tuple-element.31.refs_2_), channel_id=1, source_target_pairs={{0,4},{4,0},{1,5},{5,1},{2,6},{6,2},{3,7},{7,3},{8,12},{12,8},{9,1... | collective-permute-start | bytes 2850824 | tf_op jit(solution)/shard_map/ppermute | solution.py:335
  45.0 12.9 %collective-permute-start.3 = (bf16[14,64,256]{2,1,0:T(8,128)(2,1)S(1)}, bf16[14,64,256]{2,1,0:T(8,128)(2,1)}, u32[]{:S(2)}, u32[]{:S(2)}) collective-permute-start(bf16[14,64,256]{2,1,0:T(8,128)(2,1)S(1)} %slice.19), channel_id=1, source_target_pairs={{0,24},{8,0},{16,8},{24,16},{1,25},{9,1},{17,9},{25,17},{2,26},{10... | collective-permute-start | bytes 1376264 | tf_op jit(solution)/shard_map/ppermute | solution.py:339
  68.3 15.9 %collective-permute-start.9 = (f32[136,1024]{1,0:T(8,128)S(1)}, f32[136,1024]{1,0:T(8,128)S(1)}, u32[]{:S(2)}, u32[]{:S(2)}) collective-permute-start(f32[136,1024]{1,0:T(8,128)S(1)} %get-tuple-element.33), channel_id=1, source_target_pairs={{0,32},{32,64},{64,96},{96,0},{1,33},{33,65},{65,97},{97,1},{2,34}... | collective-permute-start | bytes 1671176 | tf_op jit(solution)/shard_map/ppermute | solution.py:339
  69.0 15.3 %collective-permute-start.10 = (f32[136,1024]{1,0:T(8,128)S(1)}, f32[136,1024]{1,0:T(8,128)S(1)}, u32[]{:S(2)}, u32[]{:S(2)}) collective-permute-start(f32[136,1024]{1,0:T(8,128)S(1)} %get-tuple-element.34), channel_id=1, source_target_pairs={{0,96},{32,0},{64,32},{96,64},{1,97},{33,1},{65,33},{97,65},{2,98}... | collective-permute-start | bytes 1671176 | tf_op jit(solution)/shard_map/ppermute | solution.py:339
  71.1 23.5 %collective-permute-start.11 = (f32[136,1024]{1,0:T(8,128)S(1)}, f32[136,1024]{1,0:T(8,128)S(1)}, u32[]{:S(2)}, u32[]{:S(2)}) collective-permute-start(f32[136,1024]{1,0:T(8,128)S(1)} %get-tuple-element.35), channel_id=1, source_target_pairs={{0,64},{32,96},{64,0},{96,32},{1,65},{33,97},{65,1},{97,33},{2,66}... | collective-permute-start | bytes 1671176 | tf_op jit(solution)/shard_map/ppermute | solution.py:339
  96.5 32.5 %all-to-all-start.1 = ((bf16[16,96,256]{2,1,0:T(8,128)(2,1)}), bf16[16,96,256]{2,1,0:T(8,128)(2,1)S(1)}, u32[]{:S(2)}, u32[]{:S(2)}) async-start(bf16[16,96,256]{2,1,0:T(8,128)(2,1)} %get-tuple-element.41), calls=%async_computation.1 | async-start | bytes 1572864 | tf_op jit(solution)/shard_map/all_to_all | solution.py:363
  107.3 12.9 %collective-permute-start.18 = (bf16[2,9,16,512]{3,2,1,0:T(8,128)(2,1)S(1)}, bf16[2,9,16,512]{3,2,1,0:T(8,128)(2,1)S(1)}, u32[]{:S(2)}, u32[]{:S(2)}) collective-permute-start(bf16[2,9,16,512]{3,2,1,0:T(8,128)(2,1)S(1)} %pair_kernel.1.refs_0_), channel_id=1, source_target_pairs={{0,16},{4,68},{8,24},{12,76},{16,0},{20,84},{24,8},{28,92},{32,48}... | collective-permute-start | bytes 884744 | tf_op jit(solution)/shard_map/ppermute | solution.py:354
  110.4 12.1 %collective-permute-start.17 = (bf16[2,9,16,512]{3,2,1,0:T(8,128)(2,1)S(1)}, bf16[2,9,16,512]{3,2,1,0:T(8,128)(2,1)S(1)}, u32[]{:S(2)}, u32[]{:S(2)}) collective-permute-start(bf16[2,9,16,512]{3,2,1,0:T(8,128)(2,1)S(1)} %pair_kernel.1.refs_0_), channel_id=1, source_target_pairs={{0,24},{4,100},{8,0},{12,108},{16,8},{20,116},{24,16},{28,124},{32... | collective-permute-start | bytes 884744 | tf_op jit(solution)/shard_map/ppermute | solution.py:354
  111.3 11.9 %collective-permute-start.16 = (bf16[2,9,16,512]{3,2,1,0:T(8,128)(2,1)S(1)}, bf16[2,9,16,512]{3,2,1,0:T(8,128)(2,1)S(1)}, u32[]{:S(2)}, u32[]{:S(2)}) collective-permute-start(bf16[2,9,16,512]{3,2,1,0:T(8,128)(2,1)S(1)} %pair_kernel.1.refs_0_), channel_id=1, source_target_pairs={{0,8},{4,36},{8,16},{12,44},{16,24},{20,52},{24,0},{28,60},{32,40}... | collective-permute-start | bytes 884744 | tf_op jit(solution)/shard_map/ppermute | solution.py:354
  124.2 16.0 %collective-permute-start.25 = (bf16[4,2,8,16,512]{4,3,2,1,0:T(8,128)(2,1)}, bf16[4,2,8,16,512]{4,3,2,1,0:T(8,128)(2,1)}, u32[]{:S(2)}, u32[]{:S(2)}) collective-permute-start(bf16[4,2,8,16,512]{4,3,2,1,0:T(8,128)(2,1)} %get-tuple-element.48.refs_0_), channel_id=1, source_target_pairs={{0,64},{4,20},{8,72},{12,28},{16,80},{20,4},{24,88},{28,12},{32,96... | collective-permute-start | bytes 3145736 | tf_op jit(solution)/shard_map/ppermute | solution.py:354
  126.0 24.4 %collective-permute-start.24 = (bf16[4,2,8,16,512]{4,3,2,1,0:T(8,128)(2,1)}, bf16[4,2,8,16,512]{4,3,2,1,0:T(8,128)(2,1)}, u32[]{:S(2)}, u32[]{:S(2)}) collective-permute-start(bf16[4,2,8,16,512]{4,3,2,1,0:T(8,128)(2,1)} %get-tuple-element.48.refs_0_), channel_id=1, source_target_pairs={{0,96},{4,28},{8,104},{12,4},{16,112},{20,12},{24,120},{28,20},{32... | collective-permute-start | bytes 3145736 | tf_op jit(solution)/shard_map/ppermute | solution.py:354
  126.9 25.2 %collective-permute-start.20 = (bf16[4,2,8,16,512]{4,3,2,1,0:T(8,128)(2,1)}, bf16[4,2,8,16,512]{4,3,2,1,0:T(8,128)(2,1)S(1)}, u32[]{:S(2)}, u32[]{:S(2)}) collective-permute-start(bf16[4,2,8,16,512]{4,3,2,1,0:T(8,128)(2,1)} %get-tuple-element.48.refs_0_), channel_id=1, source_target_pairs={{0,32},{4,12},{8,40},{12,20},{16,48},{20,28},{24,56},{28,4},{32,64... | collective-permute-start | bytes 3145736 | tf_op jit(solution)/shard_map/ppermute | solution.py:354
  137.8 15.4 %collective-permute-start.26 = (bf16[4,2,8,16,512]{4,3,2,1,0:T(8,128)(2,1)}, bf16[4,2,8,16,512]{4,3,2,1,0:T(8,128)(2,1)S(1)}, u32[]{:S(2)}, u32[]{:S(2)}) collective-permute-start(bf16[4,2,8,16,512]{4,3,2,1,0:T(8,128)(2,1)} %get-tuple-element.48.refs_0_), channel_id=1, source_target_pairs={{0,4},{4,0},{1,5},{5,1},{2,6},{6,2},{3,7},{7,3},{8,12},{12,8},{9,1... | collective-permute-start | bytes 3145736 | tf_op jit(solution)/shard_map/ppermute | solution.py:335
  140.3 13.9 %collective-permute-start.29 = (bf16[4,2,8,16,512]{4,3,2,1,0:T(8,128)(2,1)}, bf16[4,2,8,16,512]{4,3,2,1,0:T(8,128)(2,1)}, u32[]{:S(2)}, u32[]{:S(2)}) collective-permute-start(bf16[4,2,8,16,512]{4,3,2,1,0:T(8,128)(2,1)} %collective-permute-done.25.refs_3_), channel_id=1, source_target_pairs={{0,4},{4,0},{1,5},{5,1},{2,6},{6,2},{3,7},{7,3},{8,12},{12,8},{9,1... | collective-permute-start | bytes 3145736 | tf_op jit(solution)/shard_map/ppermute | solution.py:335
  168.6 25.6 %all-to-all-start.2 = ((bf16[16,80,256]{2,1,0:T(8,128)(2,1)}), bf16[16,80,256]{2,1,0:T(8,128)(2,1)}, u32[]{:S(2)}, u32[]{:S(2)}) async-start(bf16[16,80,256]{2,1,0:T(8,128)(2,1)} %broadcast_in_dim.2.refs_1_), calls=%async_computation.2 | async-start | bytes 1310720 | tf_op jit(solution)/shard_map/all_to_all | solution.py:363
  174.7 16.4 %collective-permute-start.31 = (bf16[464,256]{1,0:T(8,128)(2,1)S(1)}, bf16[464,256]{1,0:T(8,128)(2,1)S(1)}, u32[]{:S(2)}, u32[]{:S(2)}) collective-permute-start(bf16[464,256]{1,0:T(8,128)(2,1)S(1)} %get-tuple-element.53), channel_id=1, source_target_pairs={{0,1},{1,2},{2,3},{3,0},{4,5},{5,6},{6,7},{7,4},{8,9},{9,10},{10,1... | collective-permute-start | bytes 712712 | tf_op jit(solution)/shard_map/ppermute | solution.py:339
  176.0 15.1 %collective-permute-start.32 = (bf16[464,256]{1,0:T(8,128)(2,1)S(1)}, bf16[464,256]{1,0:T(8,128)(2,1)S(1)}, u32[]{:S(2)}, u32[]{:S(2)}) collective-permute-start(bf16[464,256]{1,0:T(8,128)(2,1)S(1)} %get-tuple-element.54), channel_id=1, source_target_pairs={{0,3},{1,0},{2,1},{3,2},{4,7},{5,4},{6,5},{7,6},{8,11},{9,8},{10,9... | collective-permute-start | bytes 712712 | tf_op jit(solution)/shard_map/ppermute | solution.py:339
  177.4 13.6 %collective-permute-start.33 = (bf16[464,256]{1,0:T(8,128)(2,1)S(1)}, bf16[464,256]{1,0:T(8,128)(2,1)S(1)}, u32[]{:S(2)}, u32[]{:S(2)}) collective-permute-start(bf16[464,256]{1,0:T(8,128)(2,1)S(1)} %get-tuple-element.55), channel_id=1, source_target_pairs={{0,2},{1,3},{2,0},{3,1},{4,6},{5,7},{6,4},{7,5},{8,10},{9,11},{10,... | collective-permute-start | bytes 712712 | tf_op jit(solution)/shard_map/ppermute | solution.py:339
  189.6 11.9 %collective-permute-start.34 = (bf16[2048,64]{1,0:T(8,128)(2,1)}, bf16[2048,64]{1,0:T(8,128)(2,1)}, u32[]{:S(2)}, u32[]{:S(2)}) collective-permute-start(bf16[2048,64]{1,0:T(8,128)(2,1)} %slice_bitcast_fusion), channel_id=1, source_target_pairs={{0,4},{4,0},{1,5},{5,1},{2,6},{6,2},{3,7},{7,3},{8,12},{12,8},{9,1... | collective-permute-start | bytes 786440 | tf_op jit(solution)/shard_map/ppermute | solution.py:335
  191.2 12.7 %collective-permute-start.37 = (bf16[464,256]{1,0:T(8,128)(2,1)S(1)}, bf16[464,256]{1,0:T(8,128)(2,1)S(1)}, u32[]{:S(2)}, u32[]{:S(2)}) collective-permute-start(bf16[464,256]{1,0:T(8,128)(2,1)S(1)} %add_convert_fusion.refs_1_.refs_0_), channel_id=1, source_target_pairs={{0,2},{1,3},{2,0},{3,1},{4,6},{5,7},{6,4},{7,5},{8,10},{9,11},{10,... | collective-permute-start | bytes 712712 | tf_op jit(solution)/shard_map/ppermute | solution.py:339
  (39 other events, 274.1 us)

commit v6 on v5

--- a/solution.py
+++ b/solution.py
@@ -70,7 +70,8 @@
 
 
 def forward_kernel(pos_ref, x_ref, hg_ref, *refs):
-    blocks, outs, pieces, (w, xs, total, sem) = refs[:10], refs[10:14], refs[14:18], refs[18:]
+    blocks, outs, pieces, (w, xs, total, sem) = refs[:10], refs[10:15], refs[15:19], refs[19:]
+    own_ref, plus_ref, minus_ref, plus_half, minus_half = outs
     copies = weight_copies(pos_ref, blocks, w, sem)
     for copy in copies:
         copy.start()
@@ -102,10 +103,27 @@
             else:
                 total[out_low:out_high, cols] += part
     extra = jnp.concatenate([pool, hsum, jnp.zeros((8, 512), F32)], axis=1)
-    for step in range(4):
-        rows = pl.ds(pl.multiple_of(wrap(pos_ref[0] + step) * 128, 128), 128)
-        outs[step][0:128, :] = total[rows, :]
-        outs[step][128:136, :] = extra
+    z = pos_ref[0]
+
+    def rows(step, low, size):
+        return total[pl.ds(pl.multiple_of(wrap(z + step) * 128 + low, 64), size), :]
+
+    own_ref[0:128, :] = rows(0, 0, 128)
+    own_ref[128:136, :] = extra
+    plus_ref[0:64, :] = rows(2, 0, 64)
+    plus_ref[64:128, :] = rows(1, 64, 64)
+    plus_ref[128:136, :] = extra
+    minus_ref[0:64, :] = rows(2, 64, 64)
+    minus_ref[64:72, :] = extra
+    minus_ref[72:136, :] = rows(-1, 0, 64)
+    plus_half[...] = rows(1, 0, 64)
+    minus_half[0:64, :] = rows(-1, 64, 64)
+    minus_half[64:72, :] = extra
+
+
+def bridge_kernel(plus_half, from_low, minus_half, from_high, *refs):
+    refs[3][...] = plus_half[...] + from_low[0:64, :]
+    refs[4][...] = minus_half[...] + from_high[0:72, :]
 
 
 def pair_kernel(first_ref, second_ref, out_ref):
@@ -136,10 +154,10 @@
     colsum_ref[...] = jnp.broadcast_to(total, (8, CH))
 
 
-def middle_kernel(pos_ref, *refs):
-    parts, (x_ref, pw_ref, _, keep_ref, give_ref, pay_ref) = refs[:4], refs[4:]
-    whole = parts[0][...] + parts[1][...] + parts[2][...] + parts[3][...]
-    pre = whole[0:128, :]
+def middle_kernel(pos_ref, own, from_low, from_high, half_a, half_b, x_ref, pw_ref, _, keep_ref, give_ref, pay_ref):
+    top = own[0:64, :] + from_high[72:136, :] + half_a[...]
+    bottom = own[64:136, :] + from_low[64:136, :] + half_b[...]
+    pre = jnp.concatenate([top, bottom[0:64, :]], axis=0)
     act = jnp.maximum(pre, 0.0).astype(BF)
     low = pw_ref[0:1024, :]
     hg = x_ref[pl.ds(pl.multiple_of(pos_ref[0] * 128, 128), 128), KCH:]
@@ -148,7 +166,7 @@
     first = pos_ref[2] == 0
     keep_ref[0:8] = jnp.where(first, grads[:, 0:512], grads[:, 512:1024]).astype(BF).reshape(8, 16, 512)
     give_ref[0:8] = jnp.where(first, grads[:, 512:1024], grads[:, 0:512]).astype(BF).reshape(8, 16, 512)
-    sums = jnp.concatenate([whole[128:136, 0:512]] * 2, axis=0)
+    sums = jnp.concatenate([bottom[64:72, 0:512]] * 2, axis=0)
     one = sums.astype(BF).astype(F32)
     two = (sums - one).astype(BF).astype(F32)
     row = lax.broadcasted_iota(jnp.int32, sums.shape, 0)
@@ -372,17 +390,22 @@
     below, above = gate((below, above), (x,))
     blocks = [branch_weight, below, above, send(below[0:CUT], "y", 1), send(above[CUT:29], "y", -1)]
     blocks = blocks + [swap(b) for b in blocks]
-    results = call(
+    own, plus, minus, plus_half, minus_half, *pieces = call(
         forward_kernel,
-        (shape((136, 1024), F32),) * 4 + (shape((512, CH), BF),) * 4,
+        tuple(shape((n, 1024), F32) for n in (136, 136, 136, 64, 72)) + (shape((512, CH), BF),) * 4,
         [
             pltpu.VMEM((29, KCH, BR), BF), pltpu.VMEM((7, 512, KCH), BF), pltpu.VMEM((512, 1024), F32),
             pltpu.SemaphoreType.DMA((10,)),
         ],
         4 * 10**9, pos, x, head_grad.reshape(128, BR), *blocks, raw=10,
     )
-    sums = [results[0]] + [send(results[k], "z", k) for k in (1, 3, 2)]
-    pieces = [results[4]] + [send(results[4 + k], "y", k) for k in (1, 2, 3)]
+    from_low, from_high = send(plus, "z", 1), send(minus, "z", -1)
+    pieces = [pieces[0]] + [send(pieces[k], "y", k) for k in (1, 2, 3)]
+    half_a, half_b = call(
+        bridge_kernel, (shape((64, 1024), F32), shape((72, 1024), F32)), [], 10**5,
+        plus_half, from_low, minus_half, from_high, *pieces[1:], scalar=False,
+    )
+    half_a, half_b = send(half_a, "z", 1), send(half_b, "z", -1)
     turned, colsum = call(
         turn_kernel, (shape((7, CH, HALF), BF), shape((8, CH), F32)), [pltpu.VMEM((32, 4, 16, CH), BF)], 10**8,
         pos, *pieces,
@@ -390,7 +413,7 @@
     keep, give, pay = call(
         middle_kernel,
         (shape((9, 16, 512), BF), shape((9, 16, 512), BF), shape((GROUPS, 96, BR), BF)),
-        [], 2 * 10**8, pos, *sums, x, proj_weight, turned, raw=1,
+        [], 2 * 10**8, pos, own, from_low, from_high, half_a, half_b, x, proj_weight, colsum,
     )
     block = call(pair_kernel, shape((2, 9, 16, 512), BF), [], 10**5, keep, swap(give), scalar=False)
     near = [block, cross(block, 1, False), cross(block, -1, False), cross(block, 2, False)]

time: 209 us -> 205 us (0.981)
  waiting for transfers between devices: 51.9 us -> 48.7 us
    ppermute x16 -> x17, waiting for transfers between devices: 23.4 us -> 19.4 us  [send(): return lax.ppermute(value, axis, [(k, (k + step) % 4) for k in range(4)])]
    ppermute x16 -> x17, starting transfers between devices: 23 us -> 24 us  [send(): return lax.ppermute(value, axis, [(k, (k + step) % 4) for k in range(4)])]
    unnamed x46 -> x44, local copies, waits for them, and re-layouts: 12.3 us -> 11.9 us
    pallas_call x13 -> x14, Pallas kernels: 33.3 us -> 33.4 us  [call(): pl.pallas_call(kernel, out_shape=out_shape, in_specs=specs, out_specs=jax...]
  transfers between devices with their start and end apart: 40 -> 41, of which waited for: 19 -> 18; matrix products, arithmetic and copies ran while one was open for 5% -> 5% of each run, Pallas kernels for 8% -> 8%
where the time goes in v6:
time: 205 us; the launch traced here: 204 us
  starting transfers between devices  64.8 us (32%)
  waiting for transfers between devices  48.7 us (24%)
  Pallas kernels  33.4 us (16%)
  blocking collectives  31.9 us (16%)
  local copies, waits for them, and re-layouts  20.1 us (10%)
  other arithmetic  3.97 us (2%)
    pallas_call x14, Pallas kernels, call(): pl.pallas_call(kernel, out_shape=out_shape, in_specs=specs, out_specs=jax...  33.4 us
    all_to_all x1, blocking collectives, exchange(): return lax.all_to_all(value, plane, split_axis=0, concat_axis=0, tiled=True)  31.9 us
    ppermute x17, starting transfers between devices, send(): return lax.ppermute(value, axis, [(k, (k + step) % 4) for k in range(4)])  24 us
    ppermute x6, waiting for transfers between devices, cross(): return lax.ppermute(value, ('z', 'y', 'core'), pairs)  19.4 us
    ppermute x17, waiting for transfers between devices, send(): return lax.ppermute(value, axis, [(k, (k + step) % 4) for k in range(4)])  19.4 us
    ppermute x14, starting transfers between devices, swap(): return lax.ppermute(value, 'core', [(0, 1), (1, 0)])  18.7 us
    unnamed x44, local copies, waits for them, and re-layouts  11.9 us
    all_to_all x2, starting transfers between devices, exchange(): return lax.all_to_all(value, plane, split_axis=0, concat_axis=0, tiled=True)  10.1 us
  transfers between devices with their start and end apart: 41, of which 18 were waited for; matrix products, arithmetic and copies ran while one was open for 5% of the time, Pallas kernels for 8%

profile of v6, /device:TPU:1, one launch (start us, length us, event | category | flops | bytes accessed | tf_op | source)
XLA Modules:
  0.0 203.8 jit_solution(8419801595053838669)
XLA Ops:
  0.6 3.6 %collective-permute-start.1 = (bf16[29,64,256]{2,1,0:T(8,128)(2,1)}, bf16[29,64,256]{2,1,0:T(8,128)(2,1)S(1)}, u32[]{:S(2)}, u32[]{:S(2)}) collective-permute-start(bf16[29,64,256]{2,1,0:T(8,128)(2,1)} %own.1), channel_id=1, source_target_pairs={{0,24},{8,0},{16,8},{24,16},{1,25},{9,1},{17,9},{25,17},{2,26},{10... | collective-permute-start | bytes 2850824 | tf_op jit(solution)/shard_map/ppermute | solution.py:357
  6.3 31.9 %all_to_all.15 = bf16[16,32,768]{2,1,0:T(8,128)(2,1)} all-to-all(bf16[16,32,768]{2,1,0:T(8,128)(2,1)S(1)} %split_kernel.1), channel_id=1, replica_groups=mesh['z'=4,'y'=4,'core'=2,'rep'=4] {'z','y'}, dimensions={0} | all-to-all | bytes 1572864 | tf_op jit(solution)/shard_map/all_to_all | solution.py:381
  40.8 2.6 %collective-permute-start.4 = (bf16[29,64,256]{2,1,0:T(8,128)(2,1)S(1)}, bf16[29,64,256]{2,1,0:T(8,128)(2,1)}, u32[]{:S(2)}, u32[]{:S(2)}) collective-permute-start(bf16[29,64,256]{2,1,0:T(8,128)(2,1)S(1)} %copy-done.20), channel_id=1, source_target_pairs={{0,4},{4,0},{1,5},{5,1},{2,6},{6,2},{3,7},{7,3},{8,12},{12,8},{9,1... | collective-permute-start | bytes 2850824 | tf_op jit(solution)/shard_map/ppermute | solution.py:353
  45.0 2.9 %collective-permute-start.3 = (bf16[14,64,256]{2,1,0:T(8,128)(2,1)S(1)}, bf16[14,64,256]{2,1,0:T(8,128)(2,1)}, u32[]{:S(2)}, u32[]{:S(2)}) collective-permute-start(bf16[14,64,256]{2,1,0:T(8,128)(2,1)S(1)} %slice.19), channel_id=1, source_target_pairs={{0,24},{8,0},{16,8},{24,16},{1,25},{9,1},{17,9},{25,17},{2,26},{10... | collective-permute-start | bytes 1376264 | tf_op jit(solution)/shard_map/ppermute | solution.py:357
  47.9 4.3 %collective-permute-done.2.refs_3_ = bf16[15,64,256]{2,1,0:T(8,128)(2,1)} collective-permute-done((bf16[15,64,256]{2,1,0:T(8,128)(2,1)S(1)}, bf16[15,64,256]{2,1,0:T(8,128)(2,1)}, u32[]{:S(2)}, u32[]{:S(2)}) %collective-permute-start.2) | collective-permute-done | bytes 491552 | tf_op jit(solution)/shard_map/ppermute | solution.py:357
  52.3 3.5 %collective-permute-start.7 = (bf16[15,64,256]{2,1,0:T(8,128)(2,1)}, bf16[15,64,256]{2,1,0:T(8,128)(2,1)}, u32[]{:S(2)}, u32[]{:S(2)}) collective-permute-start(bf16[15,64,256]{2,1,0:T(8,128)(2,1)} %collective-permute-done.2.refs_3_), channel_id=1, source_target_pairs={{0,4},{4,0},{1,5},{5,1},{2,6},{6,2},{3,7},{7,3},{8,12},{12,8},{9,1... | collective-permute-start | bytes 1474568 | tf_op jit(solution)/shard_map/ppermute | solution.py:353
  61.7 6.7 %forward_kernel.1 = (f32[136,1024]{1,0:T(8,128)S(1)}, f32[136,1024]{1,0:T(8,128)S(1)}, f32[136,1024]{1,0:T(8,128)S(1)}, f32[64,1024]{1,0:T(8,128)S(1)}, f32[72,1...) custom-call(s32[4]{0:T(128)S(1)} %pad_add_fusion.pos_ref, ...), custom_call_target="tpu_custom_call" | custom-call | flops 4000000000 | bytes 11206672 | tf_op jit(solution)/shard_map/forward_kernel/pallas_call | solution.py:328
  71.2 4.7 %collective-permute-start.12 = (bf16[512,128]{1,0:T(8,128)(2,1)S(1)}, bf16[512,128]{1,0:T(8,128)(2,1)S(1)}, u32[]{:S(2)}, u32[]{:S(2)}) collective-permute-start(bf16[512,128]{1,0:T(8,128)(2,1)S(1)} %get-tuple-element.41), channel_id=1, source_target_pairs={{0,16},{8,24},{16,0},{24,8},{1,17},{9,25},{17,1},{25,9},{2,18},{10... | collective-permute-start | bytes 393224 | tf_op jit(solution)/shard_map/ppermute | solution.py:357
  77.6 3.4 %collective-permute-done.12.refs_1_.refs_2_ = bf16[512,128]{1,0:T(8,128)(2,1)S(1)} collective-permute-done((bf16[512,128]{1,0:T(8,128)(2,1)S(1)}, bf16[512,128]{1,0:T(8,128)(2,1)S(1)}, u32[]{:S(2)}, u32[]{:S(2)}) %collective-permute-start.12) | collective-permute-done | bytes 131104 | tf_op jit(solution)/shard_map/ppermute | solution.py:357
  81.0 2.6 %collective-permute-done.9.from_low = f32[136,1024]{1,0:T(8,128)S(1)} collective-permute-done((f32[136,1024]{1,0:T(8,128)S(1)}, f32[136,1024]{1,0:T(8,128)S(1)}, u32[]{:S(2)}, u32[]{:S(2)}) %collective-permute-start.9) | collective-permute-done | bytes 557088 | tf_op jit(solution)/shard_map/ppermute | solution.py:357
  83.6 2.4 %collective-permute-start.15 = (f32[72,1024]{1,0:T(8,128)S(1)}, f32[72,1024]{1,0:T(8,128)S(1)}, u32[]{:S(2)}, u32[]{:S(2)}) collective-permute-start(f32[72,1024]{1,0:T(8,128)S(1)} %get-tuple-element.44), channel_id=1, source_target_pairs={{0,96},{32,0},{64,32},{96,64},{1,97},{33,1},{65,33},{97,65},{2,98}... | collective-permute-start | bytes 884744 | tf_op jit(solution)/shard_map/ppermute | solution.py:357
  89.7 3.5 %collective-permute-done.14.half_a = f32[64,1024]{1,0:T(8,128)S(1)} collective-permute-done((f32[64,1024]{1,0:T(8,128)S(1)}, f32[64,1024]{1,0:T(8,128)S(1)}, u32[]{:S(2)}, u32[]{:S(2)}) %collective-permute-start.14) | collective-permute-done | bytes 262176 | tf_op jit(solution)/shard_map/ppermute | solution.py:357
  95.2 5.6 %all-to-all-start.1 = ((bf16[16,96,256]{2,1,0:T(8,128)(2,1)}), bf16[16,96,256]{2,1,0:T(8,128)(2,1)S(1)}, u32[]{:S(2)}, u32[]{:S(2)}) async-start(bf16[16,96,256]{2,1,0:T(8,128)(2,1)} %get-tuple-element.47), calls=%async_computation.1 | async-start | bytes 1572864 | tf_op jit(solution)/shard_map/all_to_all | solution.py:381
  100.8 2.8 %collective-permute-start.16 = (bf16[9,16,512]{2,1,0:T(8,128)(2,1)S(1)}, bf16[9,16,512]{2,1,0:T(8,128)(2,1)S(1)}, u32[]{:S(2)}, u32[]{:S(2)}) collective-permute-start(bf16[9,16,512]{2,1,0:T(8,128)(2,1)S(1)} %get-tuple-element.49), channel_id=1, source_target_pairs={{0,4},{4,0},{1,5},{5,1},{2,6},{6,2},{3,7},{7,3},{8,12},{12,8},{9,1... | collective-permute-start | bytes 442376 | tf_op jit(solution)/shard_map/ppermute | solution.py:353
  104.6 3.2 %collective-permute-start.19 = (bf16[2,9,16,512]{3,2,1,0:T(8,128)(2,1)S(1)}, bf16[2,9,16,512]{3,2,1,0:T(8,128)(2,1)S(1)}, u32[]{:S(2)}, u32[]{:S(2)}) collective-permute-start(bf16[2,9,16,512]{3,2,1,0:T(8,128)(2,1)S(1)} %pair_kernel.1.refs_0_), channel_id=1, source_target_pairs={{0,16},{4,68},{8,24},{12,76},{16,0},{20,84},{24,8},{28,92},{32,48}... | collective-permute-start | bytes 884744 | tf_op jit(solution)/shard_map/ppermute | solution.py:372
  109.3 8.3 %collective-permute-done.19.refs_3_ = bf16[2,9,16,512]{3,2,1,0:T(8,128)(2,1)S(1)} collective-permute-done((bf16[2,9,16,512]{3,2,1,0:T(8,128)(2,1)S(1)}, bf16[2,9,16,512]{3,2,1,0:T(8,128)(2,1)S(1)}, u32[]{:S(2)}, u32[]{:S(2)}) %collective-permute-start.19) | collective-permute-done | bytes 294944 | tf_op jit(solution)/shard_map/ppermute | solution.py:372
  117.5 2.3 %collective-permute-done.18.refs_2_ = bf16[2,9,16,512]{3,2,1,0:T(8,128)(2,1)S(1)} collective-permute-done((bf16[2,9,16,512]{3,2,1,0:T(8,128)(2,1)S(1)}, bf16[2,9,16,512]{3,2,1,0:T(8,128)(2,1)S(1)}, u32[]{:S(2)}, u32[]{:S(2)}) %collective-permute-start.18) | collective-permute-done | bytes 294944 | tf_op jit(solution)/shard_map/ppermute | solution.py:372
  129.7 2.6 %collective-permute-done.23 = f32[80,256]{1,0:T(8,128)S(1)} collective-permute-done((f32[80,256]{1,0:T(8,128)S(1)}, f32[80,256]{1,0:T(8,128)S(1)}, u32[]{:S(2)}, u32[]{:S(2)}) %collective-permute-start.23) | collective-permute-done | bytes 81952 | tf_op jit(solution)/shard_map/ppermute | solution.py:361
  132.3 2.8 %collective-permute-start.24 = (f32[80,256]{1,0:T(8,128)S(1)}, f32[80,256]{1,0:T(8,128)S(1)}, u32[]{:S(2)}, u32[]{:S(2)}) collective-permute-start(f32[80,256]{1,0:T(8,128)S(1)} %fusion), channel_id=1, source_target_pairs={{0,2},{1,3},{2,0},{3,1},{4,6},{5,7},{6,4},{7,5},{8,10},{9,11},{10,... | collective-permute-start | bytes 245768 | tf_op jit(solution)/shard_map/ppermute | solution.py:361
  139.5 8.2 %collective-permute-done.25.refs_2_ = bf16[4,2,8,16,512]{4,3,2,1,0:T(8,128)(2,1)} collective-permute-done((bf16[4,2,8,16,512]{4,3,2,1,0:T(8,128)(2,1)}, bf16[4,2,8,16,512]{4,3,2,1,0:T(8,128)(2,1)}, u32[]{:S(2)}, u32[]{:S(2)}) %collective-permute-start.25) | collective-permute-done | bytes 1048608 | tf_op jit(solution)/shard_map/ppermute | solution.py:372
  157.0 7.3 %weight_grad_kernel.1 = (bf16[29,64,256]{2,1,0:T(8,128)(2,1)S(1)}, bf16[29,64,256]{2,1,0:T(8,128)(2,1)}) custom-call(s32[4]{0:T(128)S(1)} %pad_add_fusion.pos_ref, bf16[7,128,2048]{2,1,0:T(8,128)(2,1)S(1)} %copy-done.17, f32[8,128]{1,0:T(8,128)S(1)} %get-tuple-element.46._.colsum_ref, f32[8,256]{1,0:T(8,128)S(1)} %get-tuple-element.53.grad_ref, ...), custom_call_target="tpu_custom_call" | custom-call | flops 4000000000 | bytes 13971472 | tf_op jit(solution)/shard_map/weight_grad_kernel/pallas_call | solution.py:328
  164.8 4.6 %all-to-all-start.2 = ((bf16[16,80,256]{2,1,0:T(8,128)(2,1)}), bf16[16,80,256]{2,1,0:T(8,128)(2,1)}, u32[]{:S(2)}, u32[]{:S(2)}) async-start(bf16[16,80,256]{2,1,0:T(8,128)(2,1)} %broadcast_in_dim.2.refs_1_), calls=%async_computation.2 | async-start | bytes 1310720 | tf_op jit(solution)/shard_map/all_to_all | solution.py:381
  176.6 8.4 %field_grad_kernel.1 = bf16[2,2048,64]{2,1,0:T(8,128)(2,1)S(1)} custom-call(s32[4]{0:T(128)S(1)} %pad_add_fusion.pos_ref, f32[8,256]{1,0:T(8,128)S(1)} %get-tuple-element.53.grad_ref, bf16[29,64,256]{2,1,0:T(8,128)(2,1)S(1)} %copy-done.21, bf16[29,64,256]{2,1,0:T(8,128)(2,1)} %collective-permute-done.4.refs_5_.other, ...), custom_call_target="tpu_custom_call" | custom-call | flops 4000000000 | bytes 11059216 | tf_op jit(solution)/shard_map/field_grad_kernel/pallas_call | solution.py:328
  195.4 2.4 %pad_maximum_fusion = f32[1280,256]{1,0:T(8,128)} fusion(f32[256,256]{1,0:T(8,128)S(1)} %bitcast.35, f32[1024,256]{1,0:T(8,128)} %bitcast.31), kind=kLoop, calls=%fused_computation | loop fusion | flops 327680 | bytes 2621440 | tf_op jit(solution)/shard_map/concatenate | solution.py:462
  (138 shorter events, 72.3 us)
Async XLA Ops:
  0.6 37.6 %collective-permute-start.1 = (bf16[29,64,256]{2,1,0:T(8,128)(2,1)}, bf16[29,64,256]{2,1,0:T(8,128)(2,1)S(1)}, u32[]{:S(2)}, u32[]{:S(2)}) collective-permute-start(bf16[29,64,256]{2,1,0:T(8,128)(2,1)} %own.1), channel_id=1, source_target_pairs={{0,24},{8,0},{16,8},{24,16},{1,25},{9,1},{17,9},{25,17},{2,26},{10... | collective-permute-start | bytes 2850824 | tf_op jit(solution)/shard_map/ppermute | solution.py:357
  4.3 34.0 %collective-permute-start = (bf16[29,64,256]{2,1,0:T(8,128)(2,1)}, bf16[29,64,256]{2,1,0:T(8,128)(2,1)S(1)}, u32[]{:S(2)}, u32[]{:S(2)}) collective-permute-start(bf16[29,64,256]{2,1,0:T(8,128)(2,1)} %own.1), channel_id=1, source_target_pairs={{0,8},{8,16},{16,24},{24,0},{1,9},{9,17},{17,25},{25,1},{2,10},{10... | collective-permute-start | bytes 2850824 | tf_op jit(solution)/shard_map/ppermute | solution.py:357
  40.8 17.9 %collective-permute-start.4 = (bf16[29,64,256]{2,1,0:T(8,128)(2,1)S(1)}, bf16[29,64,256]{2,1,0:T(8,128)(2,1)}, u32[]{:S(2)}, u32[]{:S(2)}) collective-permute-start(bf16[29,64,256]{2,1,0:T(8,128)(2,1)S(1)} %copy-done.20), channel_id=1, source_target_pairs={{0,4},{4,0},{1,5},{5,1},{2,6},{6,2},{3,7},{7,3},{8,12},{12,8},{9,1... | collective-permute-start | bytes 2850824 | tf_op jit(solution)/shard_map/ppermute | solution.py:353
  43.5 17.0 %collective-permute-start.5 = (bf16[29,64,256]{2,1,0:T(8,128)(2,1)}, bf16[29,64,256]{2,1,0:T(8,128)(2,1)}, u32[]{:S(2)}, u32[]{:S(2)}) collective-permute-start(bf16[29,64,256]{2,1,0:T(8,128)(2,1)} %get-tuple-element.33.refs_1_), channel_id=1, source_target_pairs={{0,4},{4,0},{1,5},{5,1},{2,6},{6,2},{3,7},{7,3},{8,12},{12,8},{9,1... | collective-permute-start | bytes 2850824 | tf_op jit(solution)/shard_map/ppermute | solution.py:353
  43.6 16.9 %collective-permute-start.6 = (bf16[29,64,256]{2,1,0:T(8,128)(2,1)}, bf16[29,64,256]{2,1,0:T(8,128)(2,1)}, u32[]{:S(2)}, u32[]{:S(2)}) collective-permute-start(bf16[29,64,256]{2,1,0:T(8,128)(2,1)} %get-tuple-element.34.refs_2_), channel_id=1, source_target_pairs={{0,4},{4,0},{1,5},{5,1},{2,6},{6,2},{3,7},{7,3},{8,12},{12,8},{9,1... | collective-permute-start | bytes 2850824 | tf_op jit(solution)/shard_map/ppermute | solution.py:353
  45.0 12.9 %collective-permute-start.3 = (bf16[14,64,256]{2,1,0:T(8,128)(2,1)S(1)}, bf16[14,64,256]{2,1,0:T(8,128)(2,1)}, u32[]{:S(2)}, u32[]{:S(2)}) collective-permute-start(bf16[14,64,256]{2,1,0:T(8,128)(2,1)S(1)} %slice.19), channel_id=1, source_target_pairs={{0,24},{8,0},{16,8},{24,16},{1,25},{9,1},{17,9},{25,17},{2,26},{10... | collective-permute-start | bytes 1376264 | tf_op jit(solution)/shard_map/ppermute | solution.py:357
  68.4 15.1 %collective-permute-start.9 = (f32[136,1024]{1,0:T(8,128)S(1)}, f32[136,1024]{1,0:T(8,128)S(1)}, u32[]{:S(2)}, u32[]{:S(2)}) collective-permute-start(f32[136,1024]{1,0:T(8,128)S(1)} %get-tuple-element.36), channel_id=1, source_target_pairs={{0,32},{32,64},{64,96},{96,0},{1,33},{33,65},{65,97},{97,1},{2,34}... | collective-permute-start | bytes 1671176 | tf_op jit(solution)/shard_map/ppermute | solution.py:357
  69.1 14.5 %collective-permute-start.10 = (f32[136,1024]{1,0:T(8,128)S(1)}, f32[136,1024]{1,0:T(8,128)S(1)}, u32[]{:S(2)}, u32[]{:S(2)}) collective-permute-start(f32[136,1024]{1,0:T(8,128)S(1)} %get-tuple-element.37), channel_id=1, source_target_pairs={{0,96},{32,0},{64,32},{96,64},{1,97},{33,1},{65,33},{97,65},{2,98}... | collective-permute-start | bytes 1671176 | tf_op jit(solution)/shard_map/ppermute | solution.py:357
  95.2 31.2 %all-to-all-start.1 = ((bf16[16,96,256]{2,1,0:T(8,128)(2,1)}), bf16[16,96,256]{2,1,0:T(8,128)(2,1)S(1)}, u32[]{:S(2)}, u32[]{:S(2)}) async-start(bf16[16,96,256]{2,1,0:T(8,128)(2,1)} %get-tuple-element.47), calls=%async_computation.1 | async-start | bytes 1572864 | tf_op jit(solution)/shard_map/all_to_all | solution.py:381
  104.6 12.9 %collective-permute-start.19 = (bf16[2,9,16,512]{3,2,1,0:T(8,128)(2,1)S(1)}, bf16[2,9,16,512]{3,2,1,0:T(8,128)(2,1)S(1)}, u32[]{:S(2)}, u32[]{:S(2)}) collective-permute-start(bf16[2,9,16,512]{3,2,1,0:T(8,128)(2,1)S(1)} %pair_kernel.1.refs_0_), channel_id=1, source_target_pairs={{0,16},{4,68},{8,24},{12,76},{16,0},{20,84},{24,8},{28,92},{32,48}... | collective-permute-start | bytes 884744 | tf_op jit(solution)/shard_map/ppermute | solution.py:372
  107.8 12.0 %collective-permute-start.18 = (bf16[2,9,16,512]{3,2,1,0:T(8,128)(2,1)S(1)}, bf16[2,9,16,512]{3,2,1,0:T(8,128)(2,1)S(1)}, u32[]{:S(2)}, u32[]{:S(2)}) collective-permute-start(bf16[2,9,16,512]{3,2,1,0:T(8,128)(2,1)S(1)} %pair_kernel.1.refs_0_), channel_id=1, source_target_pairs={{0,24},{4,100},{8,0},{12,108},{16,8},{20,116},{24,16},{28,124},{32... | collective-permute-start | bytes 884744 | tf_op jit(solution)/shard_map/ppermute | solution.py:372
  108.7 11.9 %collective-permute-start.17 = (bf16[2,9,16,512]{3,2,1,0:T(8,128)(2,1)S(1)}, bf16[2,9,16,512]{3,2,1,0:T(8,128)(2,1)S(1)}, u32[]{:S(2)}, u32[]{:S(2)}) collective-permute-start(bf16[2,9,16,512]{3,2,1,0:T(8,128)(2,1)S(1)} %pair_kernel.1.refs_0_), channel_id=1, source_target_pairs={{0,8},{4,36},{8,16},{12,44},{16,24},{20,52},{24,0},{28,60},{32,40}... | collective-permute-start | bytes 884744 | tf_op jit(solution)/shard_map/ppermute | solution.py:372
  121.6 16.0 %collective-permute-start.26 = (bf16[4,2,8,16,512]{4,3,2,1,0:T(8,128)(2,1)}, bf16[4,2,8,16,512]{4,3,2,1,0:T(8,128)(2,1)}, u32[]{:S(2)}, u32[]{:S(2)}) collective-permute-start(bf16[4,2,8,16,512]{4,3,2,1,0:T(8,128)(2,1)} %get-tuple-element.54.refs_0_), channel_id=1, source_target_pairs={{0,64},{4,20},{8,72},{12,28},{16,80},{20,4},{24,88},{28,12},{32,96... | collective-permute-start | bytes 3145736 | tf_op jit(solution)/shard_map/ppermute | solution.py:372
  123.3 24.4 %collective-permute-start.25 = (bf16[4,2,8,16,512]{4,3,2,1,0:T(8,128)(2,1)}, bf16[4,2,8,16,512]{4,3,2,1,0:T(8,128)(2,1)}, u32[]{:S(2)}, u32[]{:S(2)}) collective-permute-start(bf16[4,2,8,16,512]{4,3,2,1,0:T(8,128)(2,1)} %get-tuple-element.54.refs_0_), channel_id=1, source_target_pairs={{0,96},{4,28},{8,104},{12,4},{16,112},{20,12},{24,120},{28,20},{32... | collective-permute-start | bytes 3145736 | tf_op jit(solution)/shard_map/ppermute | solution.py:372
  124.2 25.2 %collective-permute-start.21 = (bf16[4,2,8,16,512]{4,3,2,1,0:T(8,128)(2,1)}, bf16[4,2,8,16,512]{4,3,2,1,0:T(8,128)(2,1)S(1)}, u32[]{:S(2)}, u32[]{:S(2)}) collective-permute-start(bf16[4,2,8,16,512]{4,3,2,1,0:T(8,128)(2,1)} %get-tuple-element.54.refs_0_), channel_id=1, source_target_pairs={{0,32},{4,12},{8,40},{12,20},{16,48},{20,28},{24,56},{28,4},{32,64... | collective-permute-start | bytes 3145736 | tf_op jit(solution)/shard_map/ppermute | solution.py:372
  135.1 15.4 %collective-permute-start.27 = (bf16[4,2,8,16,512]{4,3,2,1,0:T(8,128)(2,1)}, bf16[4,2,8,16,512]{4,3,2,1,0:T(8,128)(2,1)}, u32[]{:S(2)}, u32[]{:S(2)}) collective-permute-start(bf16[4,2,8,16,512]{4,3,2,1,0:T(8,128)(2,1)} %get-tuple-element.54.refs_0_), channel_id=1, source_target_pairs={{0,4},{4,0},{1,5},{5,1},{2,6},{6,2},{3,7},{7,3},{8,12},{12,8},{9,1... | collective-permute-start | bytes 3145736 | tf_op jit(solution)/shard_map/ppermute | solution.py:353
  137.6 12.9 %collective-permute-start.30 = (bf16[4,2,8,16,512]{4,3,2,1,0:T(8,128)(2,1)}, bf16[4,2,8,16,512]{4,3,2,1,0:T(8,128)(2,1)}, u32[]{:S(2)}, u32[]{:S(2)}) collective-permute-start(bf16[4,2,8,16,512]{4,3,2,1,0:T(8,128)(2,1)} %collective-permute-done.26.refs_3_), channel_id=1, source_target_pairs={{0,4},{4,0},{1,5},{5,1},{2,6},{6,2},{3,7},{7,3},{8,12},{12,8},{9,1... | collective-permute-start | bytes 3145736 | tf_op jit(solution)/shard_map/ppermute | solution.py:353
  164.8 25.7 %all-to-all-start.2 = ((bf16[16,80,256]{2,1,0:T(8,128)(2,1)}), bf16[16,80,256]{2,1,0:T(8,128)(2,1)}, u32[]{:S(2)}, u32[]{:S(2)}) async-start(bf16[16,80,256]{2,1,0:T(8,128)(2,1)} %broadcast_in_dim.2.refs_1_), calls=%async_computation.2 | async-start | bytes 1310720 | tf_op jit(solution)/shard_map/all_to_all | solution.py:381
  170.9 16.5 %collective-permute-start.32 = (bf16[464,256]{1,0:T(8,128)(2,1)S(1)}, bf16[464,256]{1,0:T(8,128)(2,1)S(1)}, u32[]{:S(2)}, u32[]{:S(2)}) collective-permute-start(bf16[464,256]{1,0:T(8,128)(2,1)S(1)} %get-tuple-element.59), channel_id=1, source_target_pairs={{0,1},{1,2},{2,3},{3,0},{4,5},{5,6},{6,7},{7,4},{8,9},{9,10},{10,1... | collective-permute-start | bytes 712712 | tf_op jit(solution)/shard_map/ppermute | solution.py:357
  172.4 14.9 %collective-permute-start.33 = (bf16[464,256]{1,0:T(8,128)(2,1)S(1)}, bf16[464,256]{1,0:T(8,128)(2,1)S(1)}, u32[]{:S(2)}, u32[]{:S(2)}) collective-permute-start(bf16[464,256]{1,0:T(8,128)(2,1)S(1)} %get-tuple-element.60), channel_id=1, source_target_pairs={{0,3},{1,0},{2,1},{3,2},{4,7},{5,4},{6,5},{7,6},{8,11},{9,8},{10,9... | collective-permute-start | bytes 712712 | tf_op jit(solution)/shard_map/ppermute | solution.py:357
  173.9 13.5 %collective-permute-start.34 = (bf16[464,256]{1,0:T(8,128)(2,1)S(1)}, bf16[464,256]{1,0:T(8,128)(2,1)S(1)}, u32[]{:S(2)}, u32[]{:S(2)}) collective-permute-start(bf16[464,256]{1,0:T(8,128)(2,1)S(1)} %get-tuple-element.61), channel_id=1, source_target_pairs={{0,2},{1,3},{2,0},{3,1},{4,6},{5,7},{6,4},{7,5},{8,10},{9,11},{10,... | collective-permute-start | bytes 712712 | tf_op jit(solution)/shard_map/ppermute | solution.py:357
  185.9 11.9 %collective-permute-start.35 = (bf16[2048,64]{1,0:T(8,128)(2,1)}, bf16[2048,64]{1,0:T(8,128)(2,1)}, u32[]{:S(2)}, u32[]{:S(2)}) collective-permute-start(bf16[2048,64]{1,0:T(8,128)(2,1)} %slice_bitcast_fusion), channel_id=1, source_target_pairs={{0,4},{4,0},{1,5},{5,1},{2,6},{6,2},{3,7},{7,3},{8,12},{12,8},{9,1... | collective-permute-start | bytes 786440 | tf_op jit(solution)/shard_map/ppermute | solution.py:353
  187.5 12.7 %collective-permute-start.38 = (bf16[464,256]{1,0:T(8,128)(2,1)S(1)}, bf16[464,256]{1,0:T(8,128)(2,1)S(1)}, u32[]{:S(2)}, u32[]{:S(2)}) collective-permute-start(bf16[464,256]{1,0:T(8,128)(2,1)S(1)} %add_convert_fusion.refs_1_.refs_0_), channel_id=1, source_target_pairs={{0,2},{1,3},{2,0},{3,1},{4,6},{5,7},{6,4},{7,5},{8,10},{9,11},{10,... | collective-permute-start | bytes 712712 | tf_op jit(solution)/shard_map/ppermute | solution.py:357
  190.3 11.6 %collective-permute-start.36 = (bf16[464,256]{1,0:T(8,128)(2,1)S(1)}, bf16[464,256]{1,0:T(8,128)(2,1)S(1)}, u32[]{:S(2)}, u32[]{:S(2)}) collective-permute-start(bf16[464,256]{1,0:T(8,128)(2,1)S(1)} %add_convert_fusion.refs_1_.refs_0_), channel_id=1, source_target_pairs={{0,1},{1,2},{2,3},{3,0},{4,5},{5,6},{6,7},{7,4},{8,9},{9,10},{10,1... | collective-permute-start | bytes 712712 | tf_op jit(solution)/shard_map/ppermute | solution.py:357
  (39 other events, 257.2 us)

commit v7 on v6

--- a/solution.py
+++ b/solution.py
@@ -418,7 +418,7 @@
     block = call(pair_kernel, shape((2, 9, 16, 512), BF), [], 10**5, keep, swap(give), scalar=False)
     near = [block, cross(block, 1, False), cross(block, -1, False), cross(block, 2, False)]
     group, sums = call(
-        group_kernel, (shape((4, 2, 8, 16, 512), BF), shape((8, 512), F32)), [], 10**5, *near, scalar=False
+        group_kernel, (shape((4, 2, 8, 16, 512), BF), shape((8, 512), F32)), [], 10**10, *near, scalar=False
     )
     every = [group] + [cross(group, step, True) for step in (1, -1, 2)]
     sums = jnp.where(pos[2] == 0, sums, swap(sums))

time: 205 us -> 204 us (level)
  waiting for transfers between devices: 48.7 us -> 34.9 us
  starting transfers between devices: 64.8 us -> 77.3 us
    ppermute x6, waiting for transfers between devices: 19.4 us -> 1.47 us  [cross(): return lax.ppermute(value, ('z', 'y', 'core'), pairs)]
    ppermute x14, starting transfers between devices: 18.7 us -> 28.9 us  [swap(): return lax.ppermute(value, 'core', [(0, 1), (1, 0)])]
    all_to_all x2, starting transfers between devices: 10.1 us -> 14.5 us  [exchange(): return lax.all_to_all(value, plane, split_axis=0, concat_axis=0, tiled=True)]
    all_to_all x2, waiting for transfers between devices: 0.01 us -> 3.97 us  [exchange(): return lax.all_to_all(value, plane, split_axis=0, concat_axis=0, tiled=True)]
    ppermute x6, starting transfers between devices: 7.81 us -> 5.71 us  [cross(): return lax.ppermute(value, ('z', 'y', 'core'), pairs)]
  transfers between devices with their start and end apart: 41 -> 41, of which waited for: 18 -> 16; matrix products, arithmetic and copies ran while one was open for 5% -> 5% of each run, Pallas kernels for 8% -> 8%
where the time goes in v7:
time: 204 us; the launch traced here: 203 us
  starting transfers between devices  77.3 us (38%)
  waiting for transfers between devices  34.9 us (17%)
  Pallas kernels  33.4 us (16%)
  blocking collectives  31.9 us (16%)
  local copies, waits for them, and re-layouts  20.1 us (10%)
  other arithmetic  3.97 us (2%)
    pallas_call x14, Pallas kernels, call(): pl.pallas_call(kernel, out_shape=out_shape, in_specs=specs, out_specs=jax...  33.4 us
    all_to_all x1, blocking collectives, exchange(): return lax.all_to_all(value, plane, split_axis=0, concat_axis=0, tiled=True)  31.9 us
    ppermute x14, starting transfers between devices, swap(): return lax.ppermute(value, 'core', [(0, 1), (1, 0)])  28.9 us
    ppermute x17, starting transfers between devices, send(): return lax.ppermute(value, axis, [(k, (k + step) % 4) for k in range(4)])  24 us
    ppermute x17, waiting for transfers between devices, send(): return lax.ppermute(value, axis, [(k, (k + step) % 4) for k in range(4)])  19.3 us
    all_to_all x2, starting transfers between devices, exchange(): return lax.all_to_all(value, plane, split_axis=0, concat_axis=0, tiled=True)  14.5 us
    unnamed x44, local copies, waits for them, and re-layouts  11.9 us
    ppermute x14, waiting for transfers between devices, swap(): return lax.ppermute(value, 'core', [(0, 1), (1, 0)])  6.24 us
  transfers between devices with their start and end apart: 41, of which 16 were waited for; matrix products, arithmetic and copies ran while one was open for 5% of the time, Pallas kernels for 8%

profile of v7, /device:TPU:1, one launch (start us, length us, event | category | flops | bytes accessed | tf_op | source)
XLA Modules:
  0.0 202.5 jit_solution(14788313437535515088)
XLA Ops:
  0.6 3.6 %collective-permute-start.1 = (bf16[29,64,256]{2,1,0:T(8,128)(2,1)}, bf16[29,64,256]{2,1,0:T(8,128)(2,1)S(1)}, u32[]{:S(2)}, u32[]{:S(2)}) collective-permute-start(bf16[29,64,256]{2,1,0:T(8,128)(2,1)} %own.1), channel_id=1, source_target_pairs={{0,24},{8,0},{16,8},{24,16},{1,25},{9,1},{17,9},{25,17},{2,26},{10... | collective-permute-start | bytes 2850824 | tf_op jit(solution)/shard_map/ppermute | solution.py:357
  6.3 31.9 %all_to_all.15 = bf16[16,32,768]{2,1,0:T(8,128)(2,1)} all-to-all(bf16[16,32,768]{2,1,0:T(8,128)(2,1)S(1)} %split_kernel.1), channel_id=1, replica_groups=mesh['z'=4,'y'=4,'core'=2,'rep'=4] {'z','y'}, dimensions={0} | all-to-all | bytes 1572864 | tf_op jit(solution)/shard_map/all_to_all | solution.py:381
  40.8 2.6 %collective-permute-start.4 = (bf16[29,64,256]{2,1,0:T(8,128)(2,1)S(1)}, bf16[29,64,256]{2,1,0:T(8,128)(2,1)}, u32[]{:S(2)}, u32[]{:S(2)}) collective-permute-start(bf16[29,64,256]{2,1,0:T(8,128)(2,1)S(1)} %copy-done.20), channel_id=1, source_target_pairs={{0,4},{4,0},{1,5},{5,1},{2,6},{6,2},{3,7},{7,3},{8,12},{12,8},{9,1... | collective-permute-start | bytes 2850824 | tf_op jit(solution)/shard_map/ppermute | solution.py:353
  45.0 2.9 %collective-permute-start.3 = (bf16[14,64,256]{2,1,0:T(8,128)(2,1)S(1)}, bf16[14,64,256]{2,1,0:T(8,128)(2,1)}, u32[]{:S(2)}, u32[]{:S(2)}) collective-permute-start(bf16[14,64,256]{2,1,0:T(8,128)(2,1)S(1)} %slice.19), channel_id=1, source_target_pairs={{0,24},{8,0},{16,8},{24,16},{1,25},{9,1},{17,9},{25,17},{2,26},{10... | collective-permute-start | bytes 1376264 | tf_op jit(solution)/shard_map/ppermute | solution.py:357
  47.9 4.3 %collective-permute-done.2.refs_3_ = bf16[15,64,256]{2,1,0:T(8,128)(2,1)} collective-permute-done((bf16[15,64,256]{2,1,0:T(8,128)(2,1)S(1)}, bf16[15,64,256]{2,1,0:T(8,128)(2,1)}, u32[]{:S(2)}, u32[]{:S(2)}) %collective-permute-start.2) | collective-permute-done | bytes 491552 | tf_op jit(solution)/shard_map/ppermute | solution.py:357
  52.3 3.5 %collective-permute-start.7 = (bf16[15,64,256]{2,1,0:T(8,128)(2,1)}, bf16[15,64,256]{2,1,0:T(8,128)(2,1)}, u32[]{:S(2)}, u32[]{:S(2)}) collective-permute-start(bf16[15,64,256]{2,1,0:T(8,128)(2,1)} %collective-permute-done.2.refs_3_), channel_id=1, source_target_pairs={{0,4},{4,0},{1,5},{5,1},{2,6},{6,2},{3,7},{7,3},{8,12},{12,8},{9,1... | collective-permute-start | bytes 1474568 | tf_op jit(solution)/shard_map/ppermute | solution.py:353
  55.8 2.1 %collective-permute-done.3.refs_4_ = bf16[14,64,256]{2,1,0:T(8,128)(2,1)} collective-permute-done((bf16[14,64,256]{2,1,0:T(8,128)(2,1)S(1)}, bf16[14,64,256]{2,1,0:T(8,128)(2,1)}, u32[]{:S(2)}, u32[]{:S(2)}) %collective-permute-start.3) | collective-permute-done | bytes 458784 | tf_op jit(solution)/shard_map/ppermute | solution.py:357
  61.7 6.7 %forward_kernel.1 = (f32[136,1024]{1,0:T(8,128)S(1)}, f32[136,1024]{1,0:T(8,128)S(1)}, f32[136,1024]{1,0:T(8,128)S(1)}, f32[64,1024]{1,0:T(8,128)S(1)}, f32[72,1...) custom-call(s32[4]{0:T(128)S(1)} %pad_add_fusion.pos_ref, ...), custom_call_target="tpu_custom_call" | custom-call | flops 4000000000 | bytes 11206672 | tf_op jit(solution)/shard_map/forward_kernel/pallas_call | solution.py:328
  71.2 4.7 %collective-permute-start.12 = (bf16[512,128]{1,0:T(8,128)(2,1)S(1)}, bf16[512,128]{1,0:T(8,128)(2,1)S(1)}, u32[]{:S(2)}, u32[]{:S(2)}) collective-permute-start(bf16[512,128]{1,0:T(8,128)(2,1)S(1)} %get-tuple-element.41), channel_id=1, source_target_pairs={{0,16},{8,24},{16,0},{24,8},{1,17},{9,25},{17,1},{25,9},{2,18},{10... | collective-permute-start | bytes 393224 | tf_op jit(solution)/shard_map/ppermute | solution.py:357
  77.6 3.4 %collective-permute-done.12.refs_1_.refs_2_ = bf16[512,128]{1,0:T(8,128)(2,1)S(1)} collective-permute-done((bf16[512,128]{1,0:T(8,128)(2,1)S(1)}, bf16[512,128]{1,0:T(8,128)(2,1)S(1)}, u32[]{:S(2)}, u32[]{:S(2)}) %collective-permute-start.12) | collective-permute-done | bytes 131104 | tf_op jit(solution)/shard_map/ppermute | solution.py:357
  81.0 2.6 %collective-permute-done.9.from_low = f32[136,1024]{1,0:T(8,128)S(1)} collective-permute-done((f32[136,1024]{1,0:T(8,128)S(1)}, f32[136,1024]{1,0:T(8,128)S(1)}, u32[]{:S(2)}, u32[]{:S(2)}) %collective-permute-start.9) | collective-permute-done | bytes 557088 | tf_op jit(solution)/shard_map/ppermute | solution.py:357
  83.6 2.4 %collective-permute-start.15 = (f32[72,1024]{1,0:T(8,128)S(1)}, f32[72,1024]{1,0:T(8,128)S(1)}, u32[]{:S(2)}, u32[]{:S(2)}) collective-permute-start(f32[72,1024]{1,0:T(8,128)S(1)} %get-tuple-element.44), channel_id=1, source_target_pairs={{0,96},{32,0},{64,32},{96,64},{1,97},{33,1},{65,33},{97,65},{2,98}... | collective-permute-start | bytes 884744 | tf_op jit(solution)/shard_map/ppermute | solution.py:357
  89.7 3.5 %collective-permute-done.14.half_a = f32[64,1024]{1,0:T(8,128)S(1)} collective-permute-done((f32[64,1024]{1,0:T(8,128)S(1)}, f32[64,1024]{1,0:T(8,128)S(1)}, u32[]{:S(2)}, u32[]{:S(2)}) %collective-permute-start.14) | collective-permute-done | bytes 262176 | tf_op jit(solution)/shard_map/ppermute | solution.py:357
  95.2 2.7 %collective-permute-start.16 = (bf16[9,16,512]{2,1,0:T(8,128)(2,1)S(1)}, bf16[9,16,512]{2,1,0:T(8,128)(2,1)S(1)}, u32[]{:S(2)}, u32[]{:S(2)}) collective-permute-start(bf16[9,16,512]{2,1,0:T(8,128)(2,1)S(1)} %get-tuple-element.49), channel_id=1, source_target_pairs={{0,4},{4,0},{1,5},{5,1},{2,6},{6,2},{3,7},{7,3},{8,12},{12,8},{9,1... | collective-permute-start | bytes 442376 | tf_op jit(solution)/shard_map/ppermute | solution.py:353
  100.6 7.5 %all-to-all-start.1 = ((bf16[16,96,256]{2,1,0:T(8,128)(2,1)}), bf16[16,96,256]{2,1,0:T(8,128)(2,1)S(1)}, u32[]{:S(2)}, u32[]{:S(2)}) async-start(bf16[16,96,256]{2,1,0:T(8,128)(2,1)} %get-tuple-element.47), calls=%async_computation.1 | async-start | bytes 1572864 | tf_op jit(solution)/shard_map/all_to_all | solution.py:381
  114.7 3.5 %collective-permute-start.20 = (f32[8,512]{1,0:T(8,128)S(1)}, f32[8,512]{1,0:T(8,128)S(1)}, u32[]{:S(2)}, u32[]{:S(2)}) collective-permute-start(f32[8,512]{1,0:T(8,128)S(1)} %get-tuple-element.50), channel_id=1, source_target_pairs={{0,4},{4,0},{1,5},{5,1},{2,6},{6,2},{3,7},{7,3},{8,12},{12,8},{9,1... | collective-permute-start | bytes 49160 | tf_op jit(solution)/shard_map/ppermute | solution.py:353
  118.2 4.0 %all-to-all-done.1.pay_ref = bf16[16,96,256]{2,1,0:T(8,128)(2,1)S(1)} async-done(((bf16[16,96,256]{2,1,0:T(8,128)(2,1)}), bf16[16,96,256]{2,1,0:T(8,128)(2,1)S(1)}, u32[]{:S(2)}, u32[]{:S(2)}) %all-to-all-start.1) | async-done | bytes 786464 | tf_op jit(solution)/shard_map/all_to_all | solution.py:381
  122.3 9.6 %collective-permute-start.22 = (f32[64,256]{1,0:T(8,128)S(1)}, f32[64,256]{1,0:T(8,128)S(1)}, u32[]{:S(2)}, u32[]{:S(2)}) collective-permute-start(f32[64,256]{1,0:T(8,128)S(1)} %collect_kernel.1), channel_id=1, source_target_pairs={{0,4},{4,0},{1,5},{5,1},{2,6},{6,2},{3,7},{7,3},{8,12},{12,8},{9,1... | collective-permute-start | bytes 196616 | tf_op jit(solution)/shard_map/ppermute | solution.py:353
  134.4 2.9 %collective-permute-done.23 = f32[80,256]{1,0:T(8,128)S(1)} collective-permute-done((f32[80,256]{1,0:T(8,128)S(1)}, f32[80,256]{1,0:T(8,128)S(1)}, u32[]{:S(2)}, u32[]{:S(2)}) %collective-permute-start.23) | collective-permute-done | bytes 81952 | tf_op jit(solution)/shard_map/ppermute | solution.py:361
  137.3 2.8 %collective-permute-start.24 = (f32[80,256]{1,0:T(8,128)S(1)}, f32[80,256]{1,0:T(8,128)S(1)}, u32[]{:S(2)}, u32[]{:S(2)}) collective-permute-start(f32[80,256]{1,0:T(8,128)S(1)} %fusion), channel_id=1, source_target_pairs={{0,2},{1,3},{2,0},{3,1},{4,6},{5,7},{6,4},{7,5},{8,10},{9,11},{10,... | collective-permute-start | bytes 245768 | tf_op jit(solution)/shard_map/ppermute | solution.py:361
  153.4 7.3 %weight_grad_kernel.1 = (bf16[29,64,256]{2,1,0:T(8,128)(2,1)S(1)}, bf16[29,64,256]{2,1,0:T(8,128)(2,1)}) custom-call(s32[4]{0:T(128)S(1)} %pad_add_fusion.pos_ref, bf16[7,128,2048]{2,1,0:T(8,128)(2,1)S(1)} %copy-done.17, f32[8,128]{1,0:T(8,128)S(1)} %get-tuple-element.46._.colsum_ref, f32[8,256]{1,0:T(8,128)S(1)} %get-tuple-element.53.grad_ref, ...), custom_call_target="tpu_custom_call" | custom-call | flops 4000000000 | bytes 13971472 | tf_op jit(solution)/shard_map/weight_grad_kernel/pallas_call | solution.py:328
  161.2 7.0 %all-to-all-start.2 = ((bf16[16,80,256]{2,1,0:T(8,128)(2,1)}), bf16[16,80,256]{2,1,0:T(8,128)(2,1)}, u32[]{:S(2)}, u32[]{:S(2)}) async-start(bf16[16,80,256]{2,1,0:T(8,128)(2,1)} %broadcast_in_dim.2.refs_1_), calls=%async_computation.2 | async-start | bytes 1310720 | tf_op jit(solution)/shard_map/all_to_all | solution.py:381
  175.4 8.4 %field_grad_kernel.1 = bf16[2,2048,64]{2,1,0:T(8,128)(2,1)S(1)} custom-call(s32[4]{0:T(128)S(1)} %pad_add_fusion.pos_ref, f32[8,256]{1,0:T(8,128)S(1)} %get-tuple-element.53.grad_ref, bf16[29,64,256]{2,1,0:T(8,128)(2,1)S(1)} %copy-done.21, bf16[29,64,256]{2,1,0:T(8,128)(2,1)} %collective-permute-done.4.refs_5_.other, ...), custom_call_target="tpu_custom_call" | custom-call | flops 4000000000 | bytes 11059216 | tf_op jit(solution)/shard_map/field_grad_kernel/pallas_call | solution.py:328
  194.2 2.4 %pad_maximum_fusion = f32[1280,256]{1,0:T(8,128)} fusion(f32[256,256]{1,0:T(8,128)S(1)} %bitcast.35, f32[1024,256]{1,0:T(8,128)} %bitcast.31), kind=kLoop, calls=%fused_computation | loop fusion | flops 327680 | bytes 2621440 | tf_op jit(solution)/shard_map/concatenate | solution.py:462
  (138 shorter events, 69.1 us)
Async XLA Ops:
  0.6 37.6 %collective-permute-start.1 = (bf16[29,64,256]{2,1,0:T(8,128)(2,1)}, bf16[29,64,256]{2,1,0:T(8,128)(2,1)S(1)}, u32[]{:S(2)}, u32[]{:S(2)}) collective-permute-start(bf16[29,64,256]{2,1,0:T(8,128)(2,1)} %own.1), channel_id=1, source_target_pairs={{0,24},{8,0},{16,8},{24,16},{1,25},{9,1},{17,9},{25,17},{2,26},{10... | collective-permute-start | bytes 2850824 | tf_op jit(solution)/shard_map/ppermute | solution.py:357
  4.3 34.0 %collective-permute-start = (bf16[29,64,256]{2,1,0:T(8,128)(2,1)}, bf16[29,64,256]{2,1,0:T(8,128)(2,1)S(1)}, u32[]{:S(2)}, u32[]{:S(2)}) collective-permute-start(bf16[29,64,256]{2,1,0:T(8,128)(2,1)} %own.1), channel_id=1, source_target_pairs={{0,8},{8,16},{16,24},{24,0},{1,9},{9,17},{17,25},{25,1},{2,10},{10... | collective-permute-start | bytes 2850824 | tf_op jit(solution)/shard_map/ppermute | solution.py:357
  40.7 11.6 %collective-permute-start.2 = (bf16[15,64,256]{2,1,0:T(8,128)(2,1)S(1)}, bf16[15,64,256]{2,1,0:T(8,128)(2,1)}, u32[]{:S(2)}, u32[]{:S(2)}) collective-permute-start(bf16[15,64,256]{2,1,0:T(8,128)(2,1)S(1)} %slice.18), channel_id=1, source_target_pairs={{0,8},{8,16},{16,24},{24,0},{1,9},{9,17},{17,25},{25,1},{2,10},{10... | collective-permute-start | bytes 1474568 | tf_op jit(solution)/shard_map/ppermute | solution.py:357
  40.8 17.9 %collective-permute-start.4 = (bf16[29,64,256]{2,1,0:T(8,128)(2,1)S(1)}, bf16[29,64,256]{2,1,0:T(8,128)(2,1)}, u32[]{:S(2)}, u32[]{:S(2)}) collective-permute-start(bf16[29,64,256]{2,1,0:T(8,128)(2,1)S(1)} %copy-done.20), channel_id=1, source_target_pairs={{0,4},{4,0},{1,5},{5,1},{2,6},{6,2},{3,7},{7,3},{8,12},{12,8},{9,1... | collective-permute-start | bytes 2850824 | tf_op jit(solution)/shard_map/ppermute | solution.py:353
  43.5 17.0 %collective-permute-start.5 = (bf16[29,64,256]{2,1,0:T(8,128)(2,1)}, bf16[29,64,256]{2,1,0:T(8,128)(2,1)}, u32[]{:S(2)}, u32[]{:S(2)}) collective-permute-start(bf16[29,64,256]{2,1,0:T(8,128)(2,1)} %get-tuple-element.33.refs_1_), channel_id=1, source_target_pairs={{0,4},{4,0},{1,5},{5,1},{2,6},{6,2},{3,7},{7,3},{8,12},{12,8},{9,1... | collective-permute-start | bytes 2850824 | tf_op jit(solution)/shard_map/ppermute | solution.py:353
  43.6 16.9 %collective-permute-start.6 = (bf16[29,64,256]{2,1,0:T(8,128)(2,1)}, bf16[29,64,256]{2,1,0:T(8,128)(2,1)}, u32[]{:S(2)}, u32[]{:S(2)}) collective-permute-start(bf16[29,64,256]{2,1,0:T(8,128)(2,1)} %get-tuple-element.34.refs_2_), channel_id=1, source_target_pairs={{0,4},{4,0},{1,5},{5,1},{2,6},{6,2},{3,7},{7,3},{8,12},{12,8},{9,1... | collective-permute-start | bytes 2850824 | tf_op jit(solution)/shard_map/ppermute | solution.py:353
  45.0 12.9 %collective-permute-start.3 = (bf16[14,64,256]{2,1,0:T(8,128)(2,1)S(1)}, bf16[14,64,256]{2,1,0:T(8,128)(2,1)}, u32[]{:S(2)}, u32[]{:S(2)}) collective-permute-start(bf16[14,64,256]{2,1,0:T(8,128)(2,1)S(1)} %slice.19), channel_id=1, source_target_pairs={{0,24},{8,0},{16,8},{24,16},{1,25},{9,1},{17,9},{25,17},{2,26},{10... | collective-permute-start | bytes 1376264 | tf_op jit(solution)/shard_map/ppermute | solution.py:357
  68.4 15.1 %collective-permute-start.9 = (f32[136,1024]{1,0:T(8,128)S(1)}, f32[136,1024]{1,0:T(8,128)S(1)}, u32[]{:S(2)}, u32[]{:S(2)}) collective-permute-start(f32[136,1024]{1,0:T(8,128)S(1)} %get-tuple-element.36), channel_id=1, source_target_pairs={{0,32},{32,64},{64,96},{96,0},{1,33},{33,65},{65,97},{97,1},{2,34}... | collective-permute-start | bytes 1671176 | tf_op jit(solution)/shard_map/ppermute | solution.py:357
  69.1 14.5 %collective-permute-start.10 = (f32[136,1024]{1,0:T(8,128)S(1)}, f32[136,1024]{1,0:T(8,128)S(1)}, u32[]{:S(2)}, u32[]{:S(2)}) collective-permute-start(f32[136,1024]{1,0:T(8,128)S(1)} %get-tuple-element.37), channel_id=1, source_target_pairs={{0,96},{32,0},{64,32},{96,64},{1,97},{33,1},{65,33},{97,65},{2,98}... | collective-permute-start | bytes 1671176 | tf_op jit(solution)/shard_map/ppermute | solution.py:357
  71.2 9.8 %collective-permute-start.12 = (bf16[512,128]{1,0:T(8,128)(2,1)S(1)}, bf16[512,128]{1,0:T(8,128)(2,1)S(1)}, u32[]{:S(2)}, u32[]{:S(2)}) collective-permute-start(bf16[512,128]{1,0:T(8,128)(2,1)S(1)} %get-tuple-element.41), channel_id=1, source_target_pairs={{0,16},{8,24},{16,0},{24,8},{1,17},{9,25},{17,1},{25,9},{2,18},{10... | collective-permute-start | bytes 393224 | tf_op jit(solution)/shard_map/ppermute | solution.py:357
  100.6 21.6 %all-to-all-start.1 = ((bf16[16,96,256]{2,1,0:T(8,128)(2,1)}), bf16[16,96,256]{2,1,0:T(8,128)(2,1)S(1)}, u32[]{:S(2)}, u32[]{:S(2)}) async-start(bf16[16,96,256]{2,1,0:T(8,128)(2,1)} %get-tuple-element.47), calls=%async_computation.1 | async-start | bytes 1572864 | tf_op jit(solution)/shard_map/all_to_all | solution.py:381
  110.6 31.6 %collective-permute-start.26 = (bf16[4,2,8,16,512]{4,3,2,1,0:T(8,128)(2,1)}, bf16[4,2,8,16,512]{4,3,2,1,0:T(8,128)(2,1)}, u32[]{:S(2)}, u32[]{:S(2)}) collective-permute-start(bf16[4,2,8,16,512]{4,3,2,1,0:T(8,128)(2,1)} %get-tuple-element.54.refs_0_), channel_id=1, source_target_pairs={{0,64},{4,20},{8,72},{12,28},{16,80},{20,4},{24,88},{28,12},{32,96... | collective-permute-start | bytes 3145736 | tf_op jit(solution)/shard_map/ppermute | solution.py:372
  112.3 31.9 %collective-permute-start.25 = (bf16[4,2,8,16,512]{4,3,2,1,0:T(8,128)(2,1)}, bf16[4,2,8,16,512]{4,3,2,1,0:T(8,128)(2,1)}, u32[]{:S(2)}, u32[]{:S(2)}) collective-permute-start(bf16[4,2,8,16,512]{4,3,2,1,0:T(8,128)(2,1)} %get-tuple-element.54.refs_0_), channel_id=1, source_target_pairs={{0,96},{4,28},{8,104},{12,4},{16,112},{20,12},{24,120},{28,20},{32... | collective-permute-start | bytes 3145736 | tf_op jit(solution)/shard_map/ppermute | solution.py:372
  114.1 30.2 %collective-permute-start.21 = (bf16[4,2,8,16,512]{4,3,2,1,0:T(8,128)(2,1)}, bf16[4,2,8,16,512]{4,3,2,1,0:T(8,128)(2,1)S(1)}, u32[]{:S(2)}, u32[]{:S(2)}) collective-permute-start(bf16[4,2,8,16,512]{4,3,2,1,0:T(8,128)(2,1)} %get-tuple-element.54.refs_0_), channel_id=1, source_target_pairs={{0,32},{4,12},{8,40},{12,20},{16,48},{20,28},{24,56},{28,4},{32,64... | collective-permute-start | bytes 3145736 | tf_op jit(solution)/shard_map/ppermute | solution.py:372
  114.7 17.2 %collective-permute-start.20 = (f32[8,512]{1,0:T(8,128)S(1)}, f32[8,512]{1,0:T(8,128)S(1)}, u32[]{:S(2)}, u32[]{:S(2)}) collective-permute-start(f32[8,512]{1,0:T(8,128)S(1)} %get-tuple-element.50), channel_id=1, source_target_pairs={{0,4},{4,0},{1,5},{5,1},{2,6},{6,2},{3,7},{7,3},{8,12},{12,8},{9,1... | collective-permute-start | bytes 49160 | tf_op jit(solution)/shard_map/ppermute | solution.py:353
  122.3 10.8 %collective-permute-start.22 = (f32[64,256]{1,0:T(8,128)S(1)}, f32[64,256]{1,0:T(8,128)S(1)}, u32[]{:S(2)}, u32[]{:S(2)}) collective-permute-start(f32[64,256]{1,0:T(8,128)S(1)} %collect_kernel.1), channel_id=1, source_target_pairs={{0,4},{4,0},{1,5},{5,1},{2,6},{6,2},{3,7},{7,3},{8,12},{12,8},{9,1... | collective-permute-start | bytes 196616 | tf_op jit(solution)/shard_map/ppermute | solution.py:353
  161.2 28.0 %all-to-all-start.2 = ((bf16[16,80,256]{2,1,0:T(8,128)(2,1)}), bf16[16,80,256]{2,1,0:T(8,128)(2,1)}, u32[]{:S(2)}, u32[]{:S(2)}) async-start(bf16[16,80,256]{2,1,0:T(8,128)(2,1)} %broadcast_in_dim.2.refs_1_), calls=%async_computation.2 | async-start | bytes 1310720 | tf_op jit(solution)/shard_map/all_to_all | solution.py:381
  169.7 16.4 %collective-permute-start.32 = (bf16[464,256]{1,0:T(8,128)(2,1)S(1)}, bf16[464,256]{1,0:T(8,128)(2,1)S(1)}, u32[]{:S(2)}, u32[]{:S(2)}) collective-permute-start(bf16[464,256]{1,0:T(8,128)(2,1)S(1)} %get-tuple-element.59), channel_id=1, source_target_pairs={{0,1},{1,2},{2,3},{3,0},{4,5},{5,6},{6,7},{7,4},{8,9},{9,10},{10,1... | collective-permute-start | bytes 712712 | tf_op jit(solution)/shard_map/ppermute | solution.py:357
  171.2 14.9 %collective-permute-start.33 = (bf16[464,256]{1,0:T(8,128)(2,1)S(1)}, bf16[464,256]{1,0:T(8,128)(2,1)S(1)}, u32[]{:S(2)}, u32[]{:S(2)}) collective-permute-start(bf16[464,256]{1,0:T(8,128)(2,1)S(1)} %get-tuple-element.60), channel_id=1, source_target_pairs={{0,3},{1,0},{2,1},{3,2},{4,7},{5,4},{6,5},{7,6},{8,11},{9,8},{10,9... | collective-permute-start | bytes 712712 | tf_op jit(solution)/shard_map/ppermute | solution.py:357
  172.7 13.4 %collective-permute-start.34 = (bf16[464,256]{1,0:T(8,128)(2,1)S(1)}, bf16[464,256]{1,0:T(8,128)(2,1)S(1)}, u32[]{:S(2)}, u32[]{:S(2)}) collective-permute-start(bf16[464,256]{1,0:T(8,128)(2,1)S(1)} %get-tuple-element.61), channel_id=1, source_target_pairs={{0,2},{1,3},{2,0},{3,1},{4,6},{5,7},{6,4},{7,5},{8,10},{9,11},{10,... | collective-permute-start | bytes 712712 | tf_op jit(solution)/shard_map/ppermute | solution.py:357
  184.7 11.9 %collective-permute-start.35 = (bf16[2048,64]{1,0:T(8,128)(2,1)}, bf16[2048,64]{1,0:T(8,128)(2,1)}, u32[]{:S(2)}, u32[]{:S(2)}) collective-permute-start(bf16[2048,64]{1,0:T(8,128)(2,1)} %slice_bitcast_fusion), channel_id=1, source_target_pairs={{0,4},{4,0},{1,5},{5,1},{2,6},{6,2},{3,7},{7,3},{8,12},{12,8},{9,1... | collective-permute-start | bytes 786440 | tf_op jit(solution)/shard_map/ppermute | solution.py:353
  186.2 12.7 %collective-permute-start.38 = (bf16[464,256]{1,0:T(8,128)(2,1)S(1)}, bf16[464,256]{1,0:T(8,128)(2,1)S(1)}, u32[]{:S(2)}, u32[]{:S(2)}) collective-permute-start(bf16[464,256]{1,0:T(8,128)(2,1)S(1)} %add_convert_fusion.refs_1_.refs_0_), channel_id=1, source_target_pairs={{0,2},{1,3},{2,0},{3,1},{4,6},{5,7},{6,4},{7,5},{8,10},{9,11},{10,... | collective-permute-start | bytes 712712 | tf_op jit(solution)/shard_map/ppermute | solution.py:357
  187.8 11.2 %collective-permute-start.37 = (bf16[464,256]{1,0:T(8,128)(2,1)S(1)}, bf16[464,256]{1,0:T(8,128)(2,1)S(1)}, u32[]{:S(2)}, u32[]{:S(2)}) collective-permute-start(bf16[464,256]{1,0:T(8,128)(2,1)S(1)} %add_convert_fusion.refs_1_.refs_0_), channel_id=1, source_target_pairs={{0,3},{1,0},{2,1},{3,2},{4,7},{5,4},{6,5},{7,6},{8,11},{9,8},{10,9... | collective-permute-start | bytes 712712 | tf_op jit(solution)/shard_map/ppermute | solution.py:357
  189.0 11.6 %collective-permute-start.36 = (bf16[464,256]{1,0:T(8,128)(2,1)S(1)}, bf16[464,256]{1,0:T(8,128)(2,1)S(1)}, u32[]{:S(2)}, u32[]{:S(2)}) collective-permute-start(bf16[464,256]{1,0:T(8,128)(2,1)S(1)} %add_convert_fusion.refs_1_.refs_0_), channel_id=1, source_target_pairs={{0,1},{1,2},{2,3},{3,0},{4,5},{5,6},{6,7},{7,4},{8,9},{9,10},{10,1... | collective-permute-start | bytes 712712 | tf_op jit(solution)/shard_map/ppermute | solution.py:357
  (39 other events, 256.2 us)

commit v8 on v7

--- a/solution.py
+++ b/solution.py
@@ -195,7 +195,7 @@
     outer_ref[...] = whole[pl.ds(pl.multiple_of(chunk * 16, 16), 16), :]
 
 
-def collect_kernel(pay_ref, part_ref):
+def collect_kernel(pay_ref, _, part_ref):
     total = pay_ref[0, 0:64, :].astype(F32)
     for t in range(1, GROUPS):
         total = total + pay_ref[t, 0:64, :].astype(F32)
@@ -315,7 +315,7 @@
         refs[4][rows, :] = refs[k][...].astype(F32)
 
 
-ROOM = {"forward_kernel": 28, "weight_grad_kernel": 26, "field_grad_kernel": 28, "turn_kernel": 16, "middle_kernel": 16}
+ROOM = {"forward_kernel": 28, "weight_grad_kernel": 18, "field_grad_kernel": 22, "turn_kernel": 16, "middle_kernel": 16}
 
 
 def call(kernel, out_shape, scratch, flops, *args, scalar=True, raw=0):
@@ -427,7 +427,7 @@
         10**7, pos, sums, proj_weight,
     )
     pay = exchange(pay)
-    part = call(collect_kernel, shape((64, BR), F32), [], 10**6, pay, scalar=False)
+    part = call(collect_kernel, shape((64, BR), F32), [], 10**6, pay, outer, scalar=False)
     part = jnp.concatenate([part + swap(part), outer], axis=0)
     part = part + pair(part, "rep", 1)
     part = part + pair(part, "rep", 2)

time: 204 us -> 203 us (level)
    all_to_all x2, waiting for transfers between devices: 3.97 us -> 1.4 us  [exchange(): return lax.all_to_all(value, plane, split_axis=0, concat_axis=0, tiled=True)]
  transfers between devices with their start and end apart: 41 -> 41, of which waited for: 16 -> 18; matrix products, arithmetic and copies ran while one was open for 5% -> 5% of each run, Pallas kernels for 8% -> 8%
where the time goes in v8:
time: 203 us; the launch traced here: 202 us
  starting transfers between devices  78.2 us (39%)
  Pallas kernels  33.4 us (16%)
  waiting for transfers between devices  33.1 us (16%)
  blocking collectives  31.9 us (16%)
  local copies, waits for them, and re-layouts  20.7 us (10%)
  other arithmetic  3.97 us (2%)
    pallas_call x14, Pallas kernels, call(): pl.pallas_call(kernel, out_shape=out_shape, in_specs=specs, out_specs=jax...  33.4 us
    all_to_all x1, blocking collectives, exchange(): return lax.all_to_all(value, plane, split_axis=0, concat_axis=0, tiled=True)  31.9 us
    ppermute x14, starting transfers between devices, swap(): return lax.ppermute(value, 'core', [(0, 1), (1, 0)])  29.8 us
    ppermute x17, starting transfers between devices, send(): return lax.ppermute(value, axis, [(k, (k + step) % 4) for k in range(4)])  24 us
    ppermute x17, waiting for transfers between devices, send(): return lax.ppermute(value, axis, [(k, (k + step) % 4) for k in range(4)])  19.3 us
    all_to_all x2, starting transfers between devices, exchange(): return lax.all_to_all(value, plane, split_axis=0, concat_axis=0, tiled=True)  14.5 us
    unnamed x44, local copies, waits for them, and re-layouts  12.5 us
    ppermute x14, waiting for transfers between devices, swap(): return lax.ppermute(value, 'core', [(0, 1), (1, 0)])  7.7 us
  transfers between devices with their start and end apart: 41, of which 18 were waited for; matrix products, arithmetic and copies ran while one was open for 5% of the time, Pallas kernels for 8%

profile of v8, /device:TPU:1, one launch (start us, length us, event | category | flops | bytes accessed | tf_op | source)
XLA Modules:
  0.0 202.3 jit_solution(13149436948798636626)
XLA Ops:
  0.6 3.6 %collective-permute-start.1 = (bf16[29,64,256]{2,1,0:T(8,128)(2,1)}, bf16[29,64,256]{2,1,0:T(8,128)(2,1)S(1)}, u32[]{:S(2)}, u32[]{:S(2)}) collective-permute-start(bf16[29,64,256]{2,1,0:T(8,128)(2,1)} %own.1), channel_id=1, source_target_pairs={{0,24},{8,0},{16,8},{24,16},{1,25},{9,1},{17,9},{25,17},{2,26},{10... | collective-permute-start | bytes 2850824 | tf_op jit(solution)/shard_map/ppermute | solution.py:357
  6.3 31.9 %all_to_all.15 = bf16[16,32,768]{2,1,0:T(8,128)(2,1)} all-to-all(bf16[16,32,768]{2,1,0:T(8,128)(2,1)S(1)} %split_kernel.1), channel_id=1, replica_groups=mesh['z'=4,'y'=4,'core'=2,'rep'=4] {'z','y'}, dimensions={0} | all-to-all | bytes 1572864 | tf_op jit(solution)/shard_map/all_to_all | solution.py:381
  40.8 2.6 %collective-permute-start.4 = (bf16[29,64,256]{2,1,0:T(8,128)(2,1)S(1)}, bf16[29,64,256]{2,1,0:T(8,128)(2,1)}, u32[]{:S(2)}, u32[]{:S(2)}) collective-permute-start(bf16[29,64,256]{2,1,0:T(8,128)(2,1)S(1)} %copy-done.20), channel_id=1, source_target_pairs={{0,4},{4,0},{1,5},{5,1},{2,6},{6,2},{3,7},{7,3},{8,12},{12,8},{9,1... | collective-permute-start | bytes 2850824 | tf_op jit(solution)/shard_map/ppermute | solution.py:353
  45.0 2.9 %collective-permute-start.3 = (bf16[14,64,256]{2,1,0:T(8,128)(2,1)S(1)}, bf16[14,64,256]{2,1,0:T(8,128)(2,1)}, u32[]{:S(2)}, u32[]{:S(2)}) collective-permute-start(bf16[14,64,256]{2,1,0:T(8,128)(2,1)S(1)} %slice.19), channel_id=1, source_target_pairs={{0,24},{8,0},{16,8},{24,16},{1,25},{9,1},{17,9},{25,17},{2,26},{10... | collective-permute-start | bytes 1376264 | tf_op jit(solution)/shard_map/ppermute | solution.py:357
  47.9 4.3 %collective-permute-done.2.refs_3_ = bf16[15,64,256]{2,1,0:T(8,128)(2,1)} collective-permute-done((bf16[15,64,256]{2,1,0:T(8,128)(2,1)S(1)}, bf16[15,64,256]{2,1,0:T(8,128)(2,1)}, u32[]{:S(2)}, u32[]{:S(2)}) %collective-permute-start.2) | collective-permute-done | bytes 491552 | tf_op jit(solution)/shard_map/ppermute | solution.py:357
  52.3 3.5 %collective-permute-start.7 = (bf16[15,64,256]{2,1,0:T(8,128)(2,1)}, bf16[15,64,256]{2,1,0:T(8,128)(2,1)}, u32[]{:S(2)}, u32[]{:S(2)}) collective-permute-start(bf16[15,64,256]{2,1,0:T(8,128)(2,1)} %collective-permute-done.2.refs_3_), channel_id=1, source_target_pairs={{0,4},{4,0},{1,5},{5,1},{2,6},{6,2},{3,7},{7,3},{8,12},{12,8},{9,1... | collective-permute-start | bytes 1474568 | tf_op jit(solution)/shard_map/ppermute | solution.py:353
  55.8 2.1 %collective-permute-done.3.refs_4_ = bf16[14,64,256]{2,1,0:T(8,128)(2,1)} collective-permute-done((bf16[14,64,256]{2,1,0:T(8,128)(2,1)S(1)}, bf16[14,64,256]{2,1,0:T(8,128)(2,1)}, u32[]{:S(2)}, u32[]{:S(2)}) %collective-permute-start.3) | collective-permute-done | bytes 458784 | tf_op jit(solution)/shard_map/ppermute | solution.py:357
  61.7 6.7 %forward_kernel.1 = (f32[136,1024]{1,0:T(8,128)S(1)}, f32[136,1024]{1,0:T(8,128)S(1)}, f32[136,1024]{1,0:T(8,128)S(1)}, f32[64,1024]{1,0:T(8,128)S(1)}, f32[72,1...) custom-call(s32[4]{0:T(128)S(1)} %pad_add_fusion.pos_ref, ...), custom_call_target="tpu_custom_call" | custom-call | flops 4000000000 | bytes 11206672 | tf_op jit(solution)/shard_map/forward_kernel/pallas_call | solution.py:328
  71.2 4.7 %collective-permute-start.12 = (bf16[512,128]{1,0:T(8,128)(2,1)S(1)}, bf16[512,128]{1,0:T(8,128)(2,1)S(1)}, u32[]{:S(2)}, u32[]{:S(2)}) collective-permute-start(bf16[512,128]{1,0:T(8,128)(2,1)S(1)} %get-tuple-element.41), channel_id=1, source_target_pairs={{0,16},{8,24},{16,0},{24,8},{1,17},{9,25},{17,1},{25,9},{2,18},{10... | collective-permute-start | bytes 393224 | tf_op jit(solution)/shard_map/ppermute | solution.py:357
  77.6 3.4 %collective-permute-done.12.refs_1_.refs_2_ = bf16[512,128]{1,0:T(8,128)(2,1)S(1)} collective-permute-done((bf16[512,128]{1,0:T(8,128)(2,1)S(1)}, bf16[512,128]{1,0:T(8,128)(2,1)S(1)}, u32[]{:S(2)}, u32[]{:S(2)}) %collective-permute-start.12) | collective-permute-done | bytes 131104 | tf_op jit(solution)/shard_map/ppermute | solution.py:357
  81.0 2.6 %collective-permute-done.9.from_low = f32[136,1024]{1,0:T(8,128)S(1)} collective-permute-done((f32[136,1024]{1,0:T(8,128)S(1)}, f32[136,1024]{1,0:T(8,128)S(1)}, u32[]{:S(2)}, u32[]{:S(2)}) %collective-permute-start.9) | collective-permute-done | bytes 557088 | tf_op jit(solution)/shard_map/ppermute | solution.py:357
  83.6 2.4 %collective-permute-start.15 = (f32[72,1024]{1,0:T(8,128)S(1)}, f32[72,1024]{1,0:T(8,128)S(1)}, u32[]{:S(2)}, u32[]{:S(2)}) collective-permute-start(f32[72,1024]{1,0:T(8,128)S(1)} %get-tuple-element.44), channel_id=1, source_target_pairs={{0,96},{32,0},{64,32},{96,64},{1,97},{33,1},{65,33},{97,65},{2,98}... | collective-permute-start | bytes 884744 | tf_op jit(solution)/shard_map/ppermute | solution.py:357
  89.7 3.5 %collective-permute-done.14.half_a = f32[64,1024]{1,0:T(8,128)S(1)} collective-permute-done((f32[64,1024]{1,0:T(8,128)S(1)}, f32[64,1024]{1,0:T(8,128)S(1)}, u32[]{:S(2)}, u32[]{:S(2)}) %collective-permute-start.14) | collective-permute-done | bytes 262176 | tf_op jit(solution)/shard_map/ppermute | solution.py:357
  95.2 2.7 %collective-permute-start.16 = (bf16[9,16,512]{2,1,0:T(8,128)(2,1)S(1)}, bf16[9,16,512]{2,1,0:T(8,128)(2,1)S(1)}, u32[]{:S(2)}, u32[]{:S(2)}) collective-permute-start(bf16[9,16,512]{2,1,0:T(8,128)(2,1)S(1)} %get-tuple-element.49), channel_id=1, source_target_pairs={{0,4},{4,0},{1,5},{5,1},{2,6},{6,2},{3,7},{7,3},{8,12},{12,8},{9,1... | collective-permute-start | bytes 442376 | tf_op jit(solution)/shard_map/ppermute | solution.py:353
  100.6 7.5 %all-to-all-start.1 = ((bf16[16,96,256]{2,1,0:T(8,128)(2,1)}), bf16[16,96,256]{2,1,0:T(8,128)(2,1)S(1)}, u32[]{:S(2)}, u32[]{:S(2)}) async-start(bf16[16,96,256]{2,1,0:T(8,128)(2,1)} %get-tuple-element.47), calls=%async_computation.1 | async-start | bytes 1572864 | tf_op jit(solution)/shard_map/all_to_all | solution.py:381
  114.7 3.5 %collective-permute-start.20 = (f32[8,512]{1,0:T(8,128)S(1)}, f32[8,512]{1,0:T(8,128)S(1)}, u32[]{:S(2)}, u32[]{:S(2)}) collective-permute-start(f32[8,512]{1,0:T(8,128)S(1)} %get-tuple-element.50), channel_id=1, source_target_pairs={{0,4},{4,0},{1,5},{5,1},{2,6},{6,2},{3,7},{7,3},{8,12},{12,8},{9,1... | collective-permute-start | bytes 49160 | tf_op jit(solution)/shard_map/ppermute | solution.py:353
  122.3 9.6 %collective-permute-start.22 = (f32[64,256]{1,0:T(8,128)S(1)}, f32[64,256]{1,0:T(8,128)S(1)}, u32[]{:S(2)}, u32[]{:S(2)}) collective-permute-start(f32[64,256]{1,0:T(8,128)S(1)} %collect_kernel.1), channel_id=1, source_target_pairs={{0,4},{4,0},{1,5},{5,1},{2,6},{6,2},{3,7},{7,3},{8,12},{12,8},{9,1... | collective-permute-start | bytes 196616 | tf_op jit(solution)/shard_map/ppermute | solution.py:353
  134.2 2.6 %collective-permute-done.23 = f32[80,256]{1,0:T(8,128)S(1)} collective-permute-done((f32[80,256]{1,0:T(8,128)S(1)}, f32[80,256]{1,0:T(8,128)S(1)}, u32[]{:S(2)}, u32[]{:S(2)}) %collective-permute-start.23) | collective-permute-done | bytes 81952 | tf_op jit(solution)/shard_map/ppermute | solution.py:361
  136.7 2.8 %collective-permute-start.24 = (f32[80,256]{1,0:T(8,128)S(1)}, f32[80,256]{1,0:T(8,128)S(1)}, u32[]{:S(2)}, u32[]{:S(2)}) collective-permute-start(f32[80,256]{1,0:T(8,128)S(1)} %fusion), channel_id=1, source_target_pairs={{0,2},{1,3},{2,0},{3,1},{4,6},{5,7},{6,4},{7,5},{8,10},{9,11},{10,... | collective-permute-start | bytes 245768 | tf_op jit(solution)/shard_map/ppermute | solution.py:361
  141.6 2.3 %collective-permute-start.30 = (bf16[4,2,8,16,512]{4,3,2,1,0:T(8,128)(2,1)}, bf16[4,2,8,16,512]{4,3,2,1,0:T(8,128)(2,1)}, u32[]{:S(2)}, u32[]{:S(2)}) collective-permute-start(bf16[4,2,8,16,512]{4,3,2,1,0:T(8,128)(2,1)} %collective-permute-done.26.refs_3_), channel_id=1, source_target_pairs={{0,4},{4,0},{1,5},{5,1},{2,6},{6,2},{3,7},{7,3},{8,12},{12,8},{9,1... | collective-permute-start | bytes 3145736 | tf_op jit(solution)/shard_map/ppermute | solution.py:353
  153.1 7.3 %weight_grad_kernel.1 = (bf16[29,64,256]{2,1,0:T(8,128)(2,1)S(1)}, bf16[29,64,256]{2,1,0:T(8,128)(2,1)}) custom-call(s32[4]{0:T(128)S(1)} %pad_add_fusion.pos_ref, bf16[7,128,2048]{2,1,0:T(8,128)(2,1)S(1)} %copy-done.17, f32[8,128]{1,0:T(8,128)S(1)} %get-tuple-element.46._.colsum_ref, f32[8,256]{1,0:T(8,128)S(1)} %get-tuple-element.53.grad_ref, ...), custom_call_target="tpu_custom_call" | custom-call | flops 4000000000 | bytes 13971472 | tf_op jit(solution)/shard_map/weight_grad_kernel/pallas_call | solution.py:328
  160.9 7.0 %all-to-all-start.2 = ((bf16[16,80,256]{2,1,0:T(8,128)(2,1)}), bf16[16,80,256]{2,1,0:T(8,128)(2,1)}, u32[]{:S(2)}, u32[]{:S(2)}) async-start(bf16[16,80,256]{2,1,0:T(8,128)(2,1)} %broadcast_in_dim.2.refs_1_), calls=%async_computation.2 | async-start | bytes 1310720 | tf_op jit(solution)/shard_map/all_to_all | solution.py:381
  175.2 8.4 %field_grad_kernel.1 = bf16[2,2048,64]{2,1,0:T(8,128)(2,1)S(1)} custom-call(s32[4]{0:T(128)S(1)} %pad_add_fusion.pos_ref, f32[8,256]{1,0:T(8,128)S(1)} %get-tuple-element.53.grad_ref, bf16[29,64,256]{2,1,0:T(8,128)(2,1)S(1)} %copy-done.21, bf16[29,64,256]{2,1,0:T(8,128)(2,1)} %collective-permute-done.4.refs_5_.other, ...), custom_call_target="tpu_custom_call" | custom-call | flops 4000000000 | bytes 11059216 | tf_op jit(solution)/shard_map/field_grad_kernel/pallas_call | solution.py:328
  193.9 2.4 %pad_maximum_fusion = f32[1280,256]{1,0:T(8,128)} fusion(f32[256,256]{1,0:T(8,128)S(1)} %bitcast.35, f32[1024,256]{1,0:T(8,128)} %bitcast.31), kind=kLoop, calls=%fused_computation | loop fusion | flops 327680 | bytes 2621440 | tf_op jit(solution)/shard_map/concatenate | solution.py:462
  (138 shorter events, 70.8 us)
Async XLA Ops:
  0.6 37.6 %collective-permute-start.1 = (bf16[29,64,256]{2,1,0:T(8,128)(2,1)}, bf16[29,64,256]{2,1,0:T(8,128)(2,1)S(1)}, u32[]{:S(2)}, u32[]{:S(2)}) collective-permute-start(bf16[29,64,256]{2,1,0:T(8,128)(2,1)} %own.1), channel_id=1, source_target_pairs={{0,24},{8,0},{16,8},{24,16},{1,25},{9,1},{17,9},{25,17},{2,26},{10... | collective-permute-start | bytes 2850824 | tf_op jit(solution)/shard_map/ppermute | solution.py:357
  4.3 34.0 %collective-permute-start = (bf16[29,64,256]{2,1,0:T(8,128)(2,1)}, bf16[29,64,256]{2,1,0:T(8,128)(2,1)S(1)}, u32[]{:S(2)}, u32[]{:S(2)}) collective-permute-start(bf16[29,64,256]{2,1,0:T(8,128)(2,1)} %own.1), channel_id=1, source_target_pairs={{0,8},{8,16},{16,24},{24,0},{1,9},{9,17},{17,25},{25,1},{2,10},{10... | collective-permute-start | bytes 2850824 | tf_op jit(solution)/shard_map/ppermute | solution.py:357
  40.7 11.6 %collective-permute-start.2 = (bf16[15,64,256]{2,1,0:T(8,128)(2,1)S(1)}, bf16[15,64,256]{2,1,0:T(8,128)(2,1)}, u32[]{:S(2)}, u32[]{:S(2)}) collective-permute-start(bf16[15,64,256]{2,1,0:T(8,128)(2,1)S(1)} %slice.18), channel_id=1, source_target_pairs={{0,8},{8,16},{16,24},{24,0},{1,9},{9,17},{17,25},{25,1},{2,10},{10... | collective-permute-start | bytes 1474568 | tf_op jit(solution)/shard_map/ppermute | solution.py:357
  40.8 17.9 %collective-permute-start.4 = (bf16[29,64,256]{2,1,0:T(8,128)(2,1)S(1)}, bf16[29,64,256]{2,1,0:T(8,128)(2,1)}, u32[]{:S(2)}, u32[]{:S(2)}) collective-permute-start(bf16[29,64,256]{2,1,0:T(8,128)(2,1)S(1)} %copy-done.20), channel_id=1, source_target_pairs={{0,4},{4,0},{1,5},{5,1},{2,6},{6,2},{3,7},{7,3},{8,12},{12,8},{9,1... | collective-permute-start | bytes 2850824 | tf_op jit(solution)/shard_map/ppermute | solution.py:353
  43.5 17.0 %collective-permute-start.5 = (bf16[29,64,256]{2,1,0:T(8,128)(2,1)}, bf16[29,64,256]{2,1,0:T(8,128)(2,1)}, u32[]{:S(2)}, u32[]{:S(2)}) collective-permute-start(bf16[29,64,256]{2,1,0:T(8,128)(2,1)} %get-tuple-element.33.refs_1_), channel_id=1, source_target_pairs={{0,4},{4,0},{1,5},{5,1},{2,6},{6,2},{3,7},{7,3},{8,12},{12,8},{9,1... | collective-permute-start | bytes 2850824 | tf_op jit(solution)/shard_map/ppermute | solution.py:353
  43.6 16.9 %collective-permute-start.6 = (bf16[29,64,256]{2,1,0:T(8,128)(2,1)}, bf16[29,64,256]{2,1,0:T(8,128)(2,1)}, u32[]{:S(2)}, u32[]{:S(2)}) collective-permute-start(bf16[29,64,256]{2,1,0:T(8,128)(2,1)} %get-tuple-element.34.refs_2_), channel_id=1, source_target_pairs={{0,4},{4,0},{1,5},{5,1},{2,6},{6,2},{3,7},{7,3},{8,12},{12,8},{9,1... | collective-permute-start | bytes 2850824 | tf_op jit(solution)/shard_map/ppermute | solution.py:353
  45.0 12.9 %collective-permute-start.3 = (bf16[14,64,256]{2,1,0:T(8,128)(2,1)S(1)}, bf16[14,64,256]{2,1,0:T(8,128)(2,1)}, u32[]{:S(2)}, u32[]{:S(2)}) collective-permute-start(bf16[14,64,256]{2,1,0:T(8,128)(2,1)S(1)} %slice.19), channel_id=1, source_target_pairs={{0,24},{8,0},{16,8},{24,16},{1,25},{9,1},{17,9},{25,17},{2,26},{10... | collective-permute-start | bytes 1376264 | tf_op jit(solution)/shard_map/ppermute | solution.py:357
  68.4 15.1 %collective-permute-start.9 = (f32[136,1024]{1,0:T(8,128)S(1)}, f32[136,1024]{1,0:T(8,128)S(1)}, u32[]{:S(2)}, u32[]{:S(2)}) collective-permute-start(f32[136,1024]{1,0:T(8,128)S(1)} %get-tuple-element.36), channel_id=1, source_target_pairs={{0,32},{32,64},{64,96},{96,0},{1,33},{33,65},{65,97},{97,1},{2,34}... | collective-permute-start | bytes 1671176 | tf_op jit(solution)/shard_map/ppermute | solution.py:357
  69.1 14.5 %collective-permute-start.10 = (f32[136,1024]{1,0:T(8,128)S(1)}, f32[136,1024]{1,0:T(8,128)S(1)}, u32[]{:S(2)}, u32[]{:S(2)}) collective-permute-start(f32[136,1024]{1,0:T(8,128)S(1)} %get-tuple-element.37), channel_id=1, source_target_pairs={{0,96},{32,0},{64,32},{96,64},{1,97},{33,1},{65,33},{97,65},{2,98}... | collective-permute-start | bytes 1671176 | tf_op jit(solution)/shard_map/ppermute | solution.py:357
  71.2 9.8 %collective-permute-start.12 = (bf16[512,128]{1,0:T(8,128)(2,1)S(1)}, bf16[512,128]{1,0:T(8,128)(2,1)S(1)}, u32[]{:S(2)}, u32[]{:S(2)}) collective-permute-start(bf16[512,128]{1,0:T(8,128)(2,1)S(1)} %get-tuple-element.41), channel_id=1, source_target_pairs={{0,16},{8,24},{16,0},{24,8},{1,17},{9,25},{17,1},{25,9},{2,18},{10... | collective-permute-start | bytes 393224 | tf_op jit(solution)/shard_map/ppermute | solution.py:357
  83.6 9.6 %collective-permute-start.15 = (f32[72,1024]{1,0:T(8,128)S(1)}, f32[72,1024]{1,0:T(8,128)S(1)}, u32[]{:S(2)}, u32[]{:S(2)}) collective-permute-start(f32[72,1024]{1,0:T(8,128)S(1)} %get-tuple-element.44), channel_id=1, source_target_pairs={{0,96},{32,0},{64,32},{96,64},{1,97},{33,1},{65,33},{97,65},{2,98}... | collective-permute-start | bytes 884744 | tf_op jit(solution)/shard_map/ppermute | solution.py:357
  100.6 21.6 %all-to-all-start.1 = ((bf16[16,96,256]{2,1,0:T(8,128)(2,1)}), bf16[16,96,256]{2,1,0:T(8,128)(2,1)S(1)}, u32[]{:S(2)}, u32[]{:S(2)}) async-start(bf16[16,96,256]{2,1,0:T(8,128)(2,1)} %get-tuple-element.47), calls=%async_computation.1 | async-start | bytes 1572864 | tf_op jit(solution)/shard_map/all_to_all | solution.py:381
  110.6 31.0 %collective-permute-start.26 = (bf16[4,2,8,16,512]{4,3,2,1,0:T(8,128)(2,1)}, bf16[4,2,8,16,512]{4,3,2,1,0:T(8,128)(2,1)}, u32[]{:S(2)}, u32[]{:S(2)}) collective-permute-start(bf16[4,2,8,16,512]{4,3,2,1,0:T(8,128)(2,1)} %get-tuple-element.54.refs_0_), channel_id=1, source_target_pairs={{0,64},{4,20},{8,72},{12,28},{16,80},{20,4},{24,88},{28,12},{32,96... | collective-permute-start | bytes 3145736 | tf_op jit(solution)/shard_map/ppermute | solution.py:372
  112.3 31.6 %collective-permute-start.25 = (bf16[4,2,8,16,512]{4,3,2,1,0:T(8,128)(2,1)}, bf16[4,2,8,16,512]{4,3,2,1,0:T(8,128)(2,1)}, u32[]{:S(2)}, u32[]{:S(2)}) collective-permute-start(bf16[4,2,8,16,512]{4,3,2,1,0:T(8,128)(2,1)} %get-tuple-element.54.refs_0_), channel_id=1, source_target_pairs={{0,96},{4,28},{8,104},{12,4},{16,112},{20,12},{24,120},{28,20},{32... | collective-permute-start | bytes 3145736 | tf_op jit(solution)/shard_map/ppermute | solution.py:372
  114.1 29.9 %collective-permute-start.21 = (bf16[4,2,8,16,512]{4,3,2,1,0:T(8,128)(2,1)}, bf16[4,2,8,16,512]{4,3,2,1,0:T(8,128)(2,1)S(1)}, u32[]{:S(2)}, u32[]{:S(2)}) collective-permute-start(bf16[4,2,8,16,512]{4,3,2,1,0:T(8,128)(2,1)} %get-tuple-element.54.refs_0_), channel_id=1, source_target_pairs={{0,32},{4,12},{8,40},{12,20},{16,48},{20,28},{24,56},{28,4},{32,64... | collective-permute-start | bytes 3145736 | tf_op jit(solution)/shard_map/ppermute | solution.py:372
  122.3 10.5 %collective-permute-start.22 = (f32[64,256]{1,0:T(8,128)S(1)}, f32[64,256]{1,0:T(8,128)S(1)}, u32[]{:S(2)}, u32[]{:S(2)}) collective-permute-start(f32[64,256]{1,0:T(8,128)S(1)} %collect_kernel.1), channel_id=1, source_target_pairs={{0,4},{4,0},{1,5},{5,1},{2,6},{6,2},{3,7},{7,3},{8,12},{12,8},{9,1... | collective-permute-start | bytes 196616 | tf_op jit(solution)/shard_map/ppermute | solution.py:353
  160.9 28.0 %all-to-all-start.2 = ((bf16[16,80,256]{2,1,0:T(8,128)(2,1)}), bf16[16,80,256]{2,1,0:T(8,128)(2,1)}, u32[]{:S(2)}, u32[]{:S(2)}) async-start(bf16[16,80,256]{2,1,0:T(8,128)(2,1)} %broadcast_in_dim.2.refs_1_), calls=%async_computation.2 | async-start | bytes 1310720 | tf_op jit(solution)/shard_map/all_to_all | solution.py:381
  169.4 16.4 %collective-permute-start.32 = (bf16[464,256]{1,0:T(8,128)(2,1)S(1)}, bf16[464,256]{1,0:T(8,128)(2,1)S(1)}, u32[]{:S(2)}, u32[]{:S(2)}) collective-permute-start(bf16[464,256]{1,0:T(8,128)(2,1)S(1)} %get-tuple-element.59), channel_id=1, source_target_pairs={{0,1},{1,2},{2,3},{3,0},{4,5},{5,6},{6,7},{7,4},{8,9},{9,10},{10,1... | collective-permute-start | bytes 712712 | tf_op jit(solution)/shard_map/ppermute | solution.py:357
  170.9 14.9 %collective-permute-start.33 = (bf16[464,256]{1,0:T(8,128)(2,1)S(1)}, bf16[464,256]{1,0:T(8,128)(2,1)S(1)}, u32[]{:S(2)}, u32[]{:S(2)}) collective-permute-start(bf16[464,256]{1,0:T(8,128)(2,1)S(1)} %get-tuple-element.60), channel_id=1, source_target_pairs={{0,3},{1,0},{2,1},{3,2},{4,7},{5,4},{6,5},{7,6},{8,11},{9,8},{10,9... | collective-permute-start | bytes 712712 | tf_op jit(solution)/shard_map/ppermute | solution.py:357
  172.4 13.4 %collective-permute-start.34 = (bf16[464,256]{1,0:T(8,128)(2,1)S(1)}, bf16[464,256]{1,0:T(8,128)(2,1)S(1)}, u32[]{:S(2)}, u32[]{:S(2)}) collective-permute-start(bf16[464,256]{1,0:T(8,128)(2,1)S(1)} %get-tuple-element.61), channel_id=1, source_target_pairs={{0,2},{1,3},{2,0},{3,1},{4,6},{5,7},{6,4},{7,5},{8,10},{9,11},{10,... | collective-permute-start | bytes 712712 | tf_op jit(solution)/shard_map/ppermute | solution.py:357
  184.4 11.9 %collective-permute-start.35 = (bf16[2048,64]{1,0:T(8,128)(2,1)}, bf16[2048,64]{1,0:T(8,128)(2,1)}, u32[]{:S(2)}, u32[]{:S(2)}) collective-permute-start(bf16[2048,64]{1,0:T(8,128)(2,1)} %slice_bitcast_fusion), channel_id=1, source_target_pairs={{0,4},{4,0},{1,5},{5,1},{2,6},{6,2},{3,7},{7,3},{8,12},{12,8},{9,1... | collective-permute-start | bytes 786440 | tf_op jit(solution)/shard_map/ppermute | solution.py:353
  186.0 12.7 %collective-permute-start.38 = (bf16[464,256]{1,0:T(8,128)(2,1)S(1)}, bf16[464,256]{1,0:T(8,128)(2,1)S(1)}, u32[]{:S(2)}, u32[]{:S(2)}) collective-permute-start(bf16[464,256]{1,0:T(8,128)(2,1)S(1)} %add_convert_fusion.refs_1_.refs_0_), channel_id=1, source_target_pairs={{0,2},{1,3},{2,0},{3,1},{4,6},{5,7},{6,4},{7,5},{8,10},{9,11},{10,... | collective-permute-start | bytes 712712 | tf_op jit(solution)/shard_map/ppermute | solution.py:357
  187.5 11.2 %collective-permute-start.37 = (bf16[464,256]{1,0:T(8,128)(2,1)S(1)}, bf16[464,256]{1,0:T(8,128)(2,1)S(1)}, u32[]{:S(2)}, u32[]{:S(2)}) collective-permute-start(bf16[464,256]{1,0:T(8,128)(2,1)S(1)} %add_convert_fusion.refs_1_.refs_0_), channel_id=1, source_target_pairs={{0,3},{1,0},{2,1},{3,2},{4,7},{5,4},{6,5},{7,6},{8,11},{9,8},{10,9... | collective-permute-start | bytes 712712 | tf_op jit(solution)/shard_map/ppermute | solution.py:357
  188.7 11.6 %collective-permute-start.36 = (bf16[464,256]{1,0:T(8,128)(2,1)S(1)}, bf16[464,256]{1,0:T(8,128)(2,1)S(1)}, u32[]{:S(2)}, u32[]{:S(2)}) collective-permute-start(bf16[464,256]{1,0:T(8,128)(2,1)S(1)} %add_convert_fusion.refs_1_.refs_0_), channel_id=1, source_target_pairs={{0,1},{1,2},{2,3},{3,0},{4,5},{5,6},{6,7},{7,4},{8,9},{9,10},{10,1... | collective-permute-start | bytes 712712 | tf_op jit(solution)/shard_map/ppermute | solution.py:357
  (39 other events, 241.0 us)

commit v9 on v8

--- a/solution.py
+++ b/solution.py
@@ -429,8 +429,7 @@
     pay = exchange(pay)
     part = call(collect_kernel, shape((64, BR), F32), [], 10**6, pay, outer, scalar=False)
     part = jnp.concatenate([part + swap(part), outer], axis=0)
-    part = part + pair(part, "rep", 1)
-    part = part + pair(part, "rep", 2)
+    part = (part + pair(part, "rep", 1)) + (pair(part, "rep", 2) + pair(part, "rep", 3))
     part = jnp.broadcast_to(part.astype(BF)[None], (GROUPS, 80, BR))
     below, = gate((every[1],), (part,))
     every = [every[0], below] + every[2:4]

time: 203 us -> 203 us (level)
    ppermute x2 -> x3, starting transfers between devices: 4.13 us -> 4.91 us  [pair(): return lax.ppermute(value, axis, [(k, k ^ bit) for k in range(4)])]
  transfers between devices with their start and end apart: 41 -> 42, of which waited for: 18 -> 18; matrix products, arithmetic and copies ran while one was open for 5% -> 5% of each run, Pallas kernels for 8% -> 8%
where the time goes in v9:
time: 203 us; the launch traced here: 202 us
  starting transfers between devices  78.5 us (39%)
  Pallas kernels  33.4 us (16%)
  waiting for transfers between devices  32.7 us (16%)
  blocking collectives  31.9 us (16%)
  local copies, waits for them, and re-layouts  20.7 us (10%)
  other arithmetic  3.97 us (2%)
    pallas_call x14, Pallas kernels, call(): pl.pallas_call(kernel, out_shape=out_shape, in_specs=specs, out_specs=jax...  33.4 us
    all_to_all x1, blocking collectives, exchange(): return lax.all_to_all(value, plane, split_axis=0, concat_axis=0, tiled=True)  31.9 us
    ppermute x14, starting transfers between devices, swap(): return lax.ppermute(value, 'core', [(0, 1), (1, 0)])  29.6 us
    ppermute x17, starting transfers between devices, send(): return lax.ppermute(value, axis, [(k, (k + step) % 4) for k in range(4)])  23.8 us
    ppermute x17, waiting for transfers between devices, send(): return lax.ppermute(value, axis, [(k, (k + step) % 4) for k in range(4)])  19.4 us
    all_to_all x2, starting transfers between devices, exchange(): return lax.all_to_all(value, plane, split_axis=0, concat_axis=0, tiled=True)  14.5 us
    unnamed x44, local copies, waits for them, and re-layouts  12.5 us
    ppermute x14, waiting for transfers between devices, swap(): return lax.ppermute(value, 'core', [(0, 1), (1, 0)])  7.62 us
  transfers between devices with their start and end apart: 42, of which 18 were waited for; matrix products, arithmetic and copies ran while one was open for 5% of the time, Pallas kernels for 8%

profile of v9, /device:TPU:1, one launch (start us, length us, event | category | flops | bytes accessed | tf_op | source)
XLA Modules:
  0.0 202.1 jit_solution(6380359527234826303)
XLA Ops:
  0.6 3.6 %collective-permute-start.1 = (bf16[29,64,256]{2,1,0:T(8,128)(2,1)}, bf16[29,64,256]{2,1,0:T(8,128)(2,1)S(1)}, u32[]{:S(2)}, u32[]{:S(2)}) collective-permute-start(bf16[29,64,256]{2,1,0:T(8,128)(2,1)} %own.1), channel_id=1, source_target_pairs={{0,24},{8,0},{16,8},{24,16},{1,25},{9,1},{17,9},{25,17},{2,26},{10... | collective-permute-start | bytes 2850824 | tf_op jit(solution)/shard_map/ppermute | solution.py:357
  6.3 31.9 %all_to_all.15 = bf16[16,32,768]{2,1,0:T(8,128)(2,1)} all-to-all(bf16[16,32,768]{2,1,0:T(8,128)(2,1)S(1)} %split_kernel.1), channel_id=1, replica_groups=mesh['z'=4,'y'=4,'core'=2,'rep'=4] {'z','y'}, dimensions={0} | all-to-all | bytes 1572864 | tf_op jit(solution)/shard_map/all_to_all | solution.py:381
  40.8 2.6 %collective-permute-start.4 = (bf16[29,64,256]{2,1,0:T(8,128)(2,1)S(1)}, bf16[29,64,256]{2,1,0:T(8,128)(2,1)}, u32[]{:S(2)}, u32[]{:S(2)}) collective-permute-start(bf16[29,64,256]{2,1,0:T(8,128)(2,1)S(1)} %copy-done.20), channel_id=1, source_target_pairs={{0,4},{4,0},{1,5},{5,1},{2,6},{6,2},{3,7},{7,3},{8,12},{12,8},{9,1... | collective-permute-start | bytes 2850824 | tf_op jit(solution)/shard_map/ppermute | solution.py:353
  45.0 2.9 %collective-permute-start.3 = (bf16[14,64,256]{2,1,0:T(8,128)(2,1)S(1)}, bf16[14,64,256]{2,1,0:T(8,128)(2,1)}, u32[]{:S(2)}, u32[]{:S(2)}) collective-permute-start(bf16[14,64,256]{2,1,0:T(8,128)(2,1)S(1)} %slice.19), channel_id=1, source_target_pairs={{0,24},{8,0},{16,8},{24,16},{1,25},{9,1},{17,9},{25,17},{2,26},{10... | collective-permute-start | bytes 1376264 | tf_op jit(solution)/shard_map/ppermute | solution.py:357
  47.9 4.3 %collective-permute-done.2.refs_3_ = bf16[15,64,256]{2,1,0:T(8,128)(2,1)} collective-permute-done((bf16[15,64,256]{2,1,0:T(8,128)(2,1)S(1)}, bf16[15,64,256]{2,1,0:T(8,128)(2,1)}, u32[]{:S(2)}, u32[]{:S(2)}) %collective-permute-start.2) | collective-permute-done | bytes 491552 | tf_op jit(solution)/shard_map/ppermute | solution.py:357
  52.3 3.5 %collective-permute-start.7 = (bf16[15,64,256]{2,1,0:T(8,128)(2,1)}, bf16[15,64,256]{2,1,0:T(8,128)(2,1)}, u32[]{:S(2)}, u32[]{:S(2)}) collective-permute-start(bf16[15,64,256]{2,1,0:T(8,128)(2,1)} %collective-permute-done.2.refs_3_), channel_id=1, source_target_pairs={{0,4},{4,0},{1,5},{5,1},{2,6},{6,2},{3,7},{7,3},{8,12},{12,8},{9,1... | collective-permute-start | bytes 1474568 | tf_op jit(solution)/shard_map/ppermute | solution.py:353
  55.8 2.1 %collective-permute-done.3.refs_4_ = bf16[14,64,256]{2,1,0:T(8,128)(2,1)} collective-permute-done((bf16[14,64,256]{2,1,0:T(8,128)(2,1)S(1)}, bf16[14,64,256]{2,1,0:T(8,128)(2,1)}, u32[]{:S(2)}, u32[]{:S(2)}) %collective-permute-start.3) | collective-permute-done | bytes 458784 | tf_op jit(solution)/shard_map/ppermute | solution.py:357
  61.7 6.7 %forward_kernel.1 = (f32[136,1024]{1,0:T(8,128)S(1)}, f32[136,1024]{1,0:T(8,128)S(1)}, f32[136,1024]{1,0:T(8,128)S(1)}, f32[64,1024]{1,0:T(8,128)S(1)}, f32[72,1...) custom-call(s32[4]{0:T(128)S(1)} %pad_add_fusion.pos_ref, ...), custom_call_target="tpu_custom_call" | custom-call | flops 4000000000 | bytes 11206672 | tf_op jit(solution)/shard_map/forward_kernel/pallas_call | solution.py:328
  69.1 2.1 %collective-permute-start.10 = (f32[136,1024]{1,0:T(8,128)S(1)}, f32[136,1024]{1,0:T(8,128)S(1)}, u32[]{:S(2)}, u32[]{:S(2)}) collective-permute-start(f32[136,1024]{1,0:T(8,128)S(1)} %get-tuple-element.37), channel_id=1, source_target_pairs={{0,96},{32,0},{64,32},{96,64},{1,97},{33,1},{65,33},{97,65},{2,98}... | collective-permute-start | bytes 1671176 | tf_op jit(solution)/shard_map/ppermute | solution.py:357
  71.2 4.7 %collective-permute-start.12 = (bf16[512,128]{1,0:T(8,128)(2,1)S(1)}, bf16[512,128]{1,0:T(8,128)(2,1)S(1)}, u32[]{:S(2)}, u32[]{:S(2)}) collective-permute-start(bf16[512,128]{1,0:T(8,128)(2,1)S(1)} %get-tuple-element.41), channel_id=1, source_target_pairs={{0,16},{8,24},{16,0},{24,8},{1,17},{9,25},{17,1},{25,9},{2,18},{10... | collective-permute-start | bytes 393224 | tf_op jit(solution)/shard_map/ppermute | solution.py:357
  77.6 3.4 %collective-permute-done.12.refs_1_.refs_2_ = bf16[512,128]{1,0:T(8,128)(2,1)S(1)} collective-permute-done((bf16[512,128]{1,0:T(8,128)(2,1)S(1)}, bf16[512,128]{1,0:T(8,128)(2,1)S(1)}, u32[]{:S(2)}, u32[]{:S(2)}) %collective-permute-start.12) | collective-permute-done | bytes 131104 | tf_op jit(solution)/shard_map/ppermute | solution.py:357
  81.0 2.6 %collective-permute-done.9.from_low = f32[136,1024]{1,0:T(8,128)S(1)} collective-permute-done((f32[136,1024]{1,0:T(8,128)S(1)}, f32[136,1024]{1,0:T(8,128)S(1)}, u32[]{:S(2)}, u32[]{:S(2)}) %collective-permute-start.9) | collective-permute-done | bytes 557088 | tf_op jit(solution)/shard_map/ppermute | solution.py:357
  83.6 2.4 %collective-permute-start.15 = (f32[72,1024]{1,0:T(8,128)S(1)}, f32[72,1024]{1,0:T(8,128)S(1)}, u32[]{:S(2)}, u32[]{:S(2)}) collective-permute-start(f32[72,1024]{1,0:T(8,128)S(1)} %get-tuple-element.44), channel_id=1, source_target_pairs={{0,96},{32,0},{64,32},{96,64},{1,97},{33,1},{65,33},{97,65},{2,98}... | collective-permute-start | bytes 884744 | tf_op jit(solution)/shard_map/ppermute | solution.py:357
  89.7 3.5 %collective-permute-done.14.half_a = f32[64,1024]{1,0:T(8,128)S(1)} collective-permute-done((f32[64,1024]{1,0:T(8,128)S(1)}, f32[64,1024]{1,0:T(8,128)S(1)}, u32[]{:S(2)}, u32[]{:S(2)}) %collective-permute-start.14) | collective-permute-done | bytes 262176 | tf_op jit(solution)/shard_map/ppermute | solution.py:357
  95.2 2.7 %collective-permute-start.16 = (bf16[9,16,512]{2,1,0:T(8,128)(2,1)S(1)}, bf16[9,16,512]{2,1,0:T(8,128)(2,1)S(1)}, u32[]{:S(2)}, u32[]{:S(2)}) collective-permute-start(bf16[9,16,512]{2,1,0:T(8,128)(2,1)S(1)} %get-tuple-element.49), channel_id=1, source_target_pairs={{0,4},{4,0},{1,5},{5,1},{2,6},{6,2},{3,7},{7,3},{8,12},{12,8},{9,1... | collective-permute-start | bytes 442376 | tf_op jit(solution)/shard_map/ppermute | solution.py:353
  100.6 7.5 %all-to-all-start.1 = ((bf16[16,96,256]{2,1,0:T(8,128)(2,1)}), bf16[16,96,256]{2,1,0:T(8,128)(2,1)S(1)}, u32[]{:S(2)}, u32[]{:S(2)}) async-start(bf16[16,96,256]{2,1,0:T(8,128)(2,1)} %get-tuple-element.47), calls=%async_computation.1 | async-start | bytes 1572864 | tf_op jit(solution)/shard_map/all_to_all | solution.py:381
  114.7 3.5 %collective-permute-start.20 = (f32[8,512]{1,0:T(8,128)S(1)}, f32[8,512]{1,0:T(8,128)S(1)}, u32[]{:S(2)}, u32[]{:S(2)}) collective-permute-start(f32[8,512]{1,0:T(8,128)S(1)} %get-tuple-element.50), channel_id=1, source_target_pairs={{0,4},{4,0},{1,5},{5,1},{2,6},{6,2},{3,7},{7,3},{8,12},{12,8},{9,1... | collective-permute-start | bytes 49160 | tf_op jit(solution)/shard_map/ppermute | solution.py:353
  122.3 9.6 %collective-permute-start.22 = (f32[64,256]{1,0:T(8,128)S(1)}, f32[64,256]{1,0:T(8,128)S(1)}, u32[]{:S(2)}, u32[]{:S(2)}) collective-permute-start(f32[64,256]{1,0:T(8,128)S(1)} %collect_kernel.1), channel_id=1, source_target_pairs={{0,4},{4,0},{1,5},{5,1},{2,6},{6,2},{3,7},{7,3},{8,12},{12,8},{9,1... | collective-permute-start | bytes 196616 | tf_op jit(solution)/shard_map/ppermute | solution.py:353
  132.9 2.8 %collective-permute-start.24 = (f32[80,256]{1,0:T(8,128)S(1)}, f32[80,256]{1,0:T(8,128)S(1)}, u32[]{:S(2)}, u32[]{:S(2)}) collective-permute-start(f32[80,256]{1,0:T(8,128)S(1)} %pad_maximum_fusion.2), channel_id=1, source_target_pairs={{0,2},{1,3},{2,0},{3,1},{4,6},{5,7},{6,4},{7,5},{8,10},{9,11},{10,... | collective-permute-start | bytes 245768 | tf_op jit(solution)/shard_map/ppermute | solution.py:361
  153.0 7.3 %weight_grad_kernel.1 = (bf16[29,64,256]{2,1,0:T(8,128)(2,1)S(1)}, bf16[29,64,256]{2,1,0:T(8,128)(2,1)}) custom-call(s32[4]{0:T(128)S(1)} %pad_add_fusion.pos_ref, bf16[7,128,2048]{2,1,0:T(8,128)(2,1)S(1)} %copy-done.17, f32[8,128]{1,0:T(8,128)S(1)} %get-tuple-element.46._.colsum_ref, f32[8,256]{1,0:T(8,128)S(1)} %get-tuple-element.53.grad_ref, ...), custom_call_target="tpu_custom_call" | custom-call | flops 4000000000 | bytes 13971472 | tf_op jit(solution)/shard_map/weight_grad_kernel/pallas_call | solution.py:328
  160.8 7.0 %all-to-all-start.2 = ((bf16[16,80,256]{2,1,0:T(8,128)(2,1)}), bf16[16,80,256]{2,1,0:T(8,128)(2,1)}, u32[]{:S(2)}, u32[]{:S(2)}) async-start(bf16[16,80,256]{2,1,0:T(8,128)(2,1)} %broadcast_in_dim.2.refs_1_), calls=%async_computation.2 | async-start | bytes 1310720 | tf_op jit(solution)/shard_map/all_to_all | solution.py:381
  175.0 8.4 %field_grad_kernel.1 = bf16[2,2048,64]{2,1,0:T(8,128)(2,1)S(1)} custom-call(s32[4]{0:T(128)S(1)} %pad_add_fusion.pos_ref, f32[8,256]{1,0:T(8,128)S(1)} %get-tuple-element.53.grad_ref, bf16[29,64,256]{2,1,0:T(8,128)(2,1)S(1)} %copy-done.21, bf16[29,64,256]{2,1,0:T(8,128)(2,1)} %collective-permute-done.4.refs_5_.other, ...), custom_call_target="tpu_custom_call" | custom-call | flops 4000000000 | bytes 11059216 | tf_op jit(solution)/shard_map/field_grad_kernel/pallas_call | solution.py:328
  189.6 2.1 %slice.26 = f32[16,64,256]{2,1,0:T(8,128)} slice(bf16[16,80,256]{2,1,0:T(8,128)(2,1)} %shard_map.78), slice={[0:16], [0:64], [0:256]} | slice | bytes 2097152 | tf_op jit(solution)/shard_map/slice | solution.py:461
  193.6 2.4 %pad_maximum_fusion = f32[1280,256]{1,0:T(8,128)} fusion(f32[256,256]{1,0:T(8,128)S(1)} %bitcast.35, f32[1024,256]{1,0:T(8,128)} %bitcast.31), kind=kLoop, calls=%fused_computation | loop fusion | flops 327680 | bytes 2621440 | tf_op jit(solution)/shard_map/concatenate | solution.py:461
  (139 shorter events, 71.2 us)
Async XLA Ops:
  0.6 37.6 %collective-permute-start.1 = (bf16[29,64,256]{2,1,0:T(8,128)(2,1)}, bf16[29,64,256]{2,1,0:T(8,128)(2,1)S(1)}, u32[]{:S(2)}, u32[]{:S(2)}) collective-permute-start(bf16[29,64,256]{2,1,0:T(8,128)(2,1)} %own.1), channel_id=1, source_target_pairs={{0,24},{8,0},{16,8},{24,16},{1,25},{9,1},{17,9},{25,17},{2,26},{10... | collective-permute-start | bytes 2850824 | tf_op jit(solution)/shard_map/ppermute | solution.py:357
  4.3 34.0 %collective-permute-start = (bf16[29,64,256]{2,1,0:T(8,128)(2,1)}, bf16[29,64,256]{2,1,0:T(8,128)(2,1)S(1)}, u32[]{:S(2)}, u32[]{:S(2)}) collective-permute-start(bf16[29,64,256]{2,1,0:T(8,128)(2,1)} %own.1), channel_id=1, source_target_pairs={{0,8},{8,16},{16,24},{24,0},{1,9},{9,17},{17,25},{25,1},{2,10},{10... | collective-permute-start | bytes 2850824 | tf_op jit(solution)/shard_map/ppermute | solution.py:357
  40.7 11.6 %collective-permute-start.2 = (bf16[15,64,256]{2,1,0:T(8,128)(2,1)S(1)}, bf16[15,64,256]{2,1,0:T(8,128)(2,1)}, u32[]{:S(2)}, u32[]{:S(2)}) collective-permute-start(bf16[15,64,256]{2,1,0:T(8,128)(2,1)S(1)} %slice.18), channel_id=1, source_target_pairs={{0,8},{8,16},{16,24},{24,0},{1,9},{9,17},{17,25},{25,1},{2,10},{10... | collective-permute-start | bytes 1474568 | tf_op jit(solution)/shard_map/ppermute | solution.py:357
  40.8 17.9 %collective-permute-start.4 = (bf16[29,64,256]{2,1,0:T(8,128)(2,1)S(1)}, bf16[29,64,256]{2,1,0:T(8,128)(2,1)}, u32[]{:S(2)}, u32[]{:S(2)}) collective-permute-start(bf16[29,64,256]{2,1,0:T(8,128)(2,1)S(1)} %copy-done.20), channel_id=1, source_target_pairs={{0,4},{4,0},{1,5},{5,1},{2,6},{6,2},{3,7},{7,3},{8,12},{12,8},{9,1... | collective-permute-start | bytes 2850824 | tf_op jit(solution)/shard_map/ppermute | solution.py:353
  43.5 17.0 %collective-permute-start.5 = (bf16[29,64,256]{2,1,0:T(8,128)(2,1)}, bf16[29,64,256]{2,1,0:T(8,128)(2,1)}, u32[]{:S(2)}, u32[]{:S(2)}) collective-permute-start(bf16[29,64,256]{2,1,0:T(8,128)(2,1)} %get-tuple-element.33.refs_1_), channel_id=1, source_target_pairs={{0,4},{4,0},{1,5},{5,1},{2,6},{6,2},{3,7},{7,3},{8,12},{12,8},{9,1... | collective-permute-start | bytes 2850824 | tf_op jit(solution)/shard_map/ppermute | solution.py:353
  43.6 16.9 %collective-permute-start.6 = (bf16[29,64,256]{2,1,0:T(8,128)(2,1)}, bf16[29,64,256]{2,1,0:T(8,128)(2,1)}, u32[]{:S(2)}, u32[]{:S(2)}) collective-permute-start(bf16[29,64,256]{2,1,0:T(8,128)(2,1)} %get-tuple-element.34.refs_2_), channel_id=1, source_target_pairs={{0,4},{4,0},{1,5},{5,1},{2,6},{6,2},{3,7},{7,3},{8,12},{12,8},{9,1... | collective-permute-start | bytes 2850824 | tf_op jit(solution)/shard_map/ppermute | solution.py:353
  45.0 12.9 %collective-permute-start.3 = (bf16[14,64,256]{2,1,0:T(8,128)(2,1)S(1)}, bf16[14,64,256]{2,1,0:T(8,128)(2,1)}, u32[]{:S(2)}, u32[]{:S(2)}) collective-permute-start(bf16[14,64,256]{2,1,0:T(8,128)(2,1)S(1)} %slice.19), channel_id=1, source_target_pairs={{0,24},{8,0},{16,8},{24,16},{1,25},{9,1},{17,9},{25,17},{2,26},{10... | collective-permute-start | bytes 1376264 | tf_op jit(solution)/shard_map/ppermute | solution.py:357
  68.4 15.1 %collective-permute-start.9 = (f32[136,1024]{1,0:T(8,128)S(1)}, f32[136,1024]{1,0:T(8,128)S(1)}, u32[]{:S(2)}, u32[]{:S(2)}) collective-permute-start(f32[136,1024]{1,0:T(8,128)S(1)} %get-tuple-element.36), channel_id=1, source_target_pairs={{0,32},{32,64},{64,96},{96,0},{1,33},{33,65},{65,97},{97,1},{2,34}... | collective-permute-start | bytes 1671176 | tf_op jit(solution)/shard_map/ppermute | solution.py:357
  69.1 14.5 %collective-permute-start.10 = (f32[136,1024]{1,0:T(8,128)S(1)}, f32[136,1024]{1,0:T(8,128)S(1)}, u32[]{:S(2)}, u32[]{:S(2)}) collective-permute-start(f32[136,1024]{1,0:T(8,128)S(1)} %get-tuple-element.37), channel_id=1, source_target_pairs={{0,96},{32,0},{64,32},{96,64},{1,97},{33,1},{65,33},{97,65},{2,98}... | collective-permute-start | bytes 1671176 | tf_op jit(solution)/shard_map/ppermute | solution.py:357
  71.2 9.8 %collective-permute-start.12 = (bf16[512,128]{1,0:T(8,128)(2,1)S(1)}, bf16[512,128]{1,0:T(8,128)(2,1)S(1)}, u32[]{:S(2)}, u32[]{:S(2)}) collective-permute-start(bf16[512,128]{1,0:T(8,128)(2,1)S(1)} %get-tuple-element.41), channel_id=1, source_target_pairs={{0,16},{8,24},{16,0},{24,8},{1,17},{9,25},{17,1},{25,9},{2,18},{10... | collective-permute-start | bytes 393224 | tf_op jit(solution)/shard_map/ppermute | solution.py:357
  83.6 9.6 %collective-permute-start.15 = (f32[72,1024]{1,0:T(8,128)S(1)}, f32[72,1024]{1,0:T(8,128)S(1)}, u32[]{:S(2)}, u32[]{:S(2)}) collective-permute-start(f32[72,1024]{1,0:T(8,128)S(1)} %get-tuple-element.44), channel_id=1, source_target_pairs={{0,96},{32,0},{64,32},{96,64},{1,97},{33,1},{65,33},{97,65},{2,98}... | collective-permute-start | bytes 884744 | tf_op jit(solution)/shard_map/ppermute | solution.py:357
  100.6 21.6 %all-to-all-start.1 = ((bf16[16,96,256]{2,1,0:T(8,128)(2,1)}), bf16[16,96,256]{2,1,0:T(8,128)(2,1)S(1)}, u32[]{:S(2)}, u32[]{:S(2)}) async-start(bf16[16,96,256]{2,1,0:T(8,128)(2,1)} %get-tuple-element.47), calls=%async_computation.1 | async-start | bytes 1572864 | tf_op jit(solution)/shard_map/all_to_all | solution.py:381
  110.6 31.4 %collective-permute-start.27 = (bf16[4,2,8,16,512]{4,3,2,1,0:T(8,128)(2,1)}, bf16[4,2,8,16,512]{4,3,2,1,0:T(8,128)(2,1)}, u32[]{:S(2)}, u32[]{:S(2)}) collective-permute-start(bf16[4,2,8,16,512]{4,3,2,1,0:T(8,128)(2,1)} %get-tuple-element.54.refs_0_), channel_id=1, source_target_pairs={{0,64},{4,20},{8,72},{12,28},{16,80},{20,4},{24,88},{28,12},{32,96... | collective-permute-start | bytes 3145736 | tf_op jit(solution)/shard_map/ppermute | solution.py:372
  112.3 31.5 %collective-permute-start.26 = (bf16[4,2,8,16,512]{4,3,2,1,0:T(8,128)(2,1)}, bf16[4,2,8,16,512]{4,3,2,1,0:T(8,128)(2,1)}, u32[]{:S(2)}, u32[]{:S(2)}) collective-permute-start(bf16[4,2,8,16,512]{4,3,2,1,0:T(8,128)(2,1)} %get-tuple-element.54.refs_0_), channel_id=1, source_target_pairs={{0,96},{4,28},{8,104},{12,4},{16,112},{20,12},{24,120},{28,20},{32... | collective-permute-start | bytes 3145736 | tf_op jit(solution)/shard_map/ppermute | solution.py:372
  114.1 29.8 %collective-permute-start.21 = (bf16[4,2,8,16,512]{4,3,2,1,0:T(8,128)(2,1)}, bf16[4,2,8,16,512]{4,3,2,1,0:T(8,128)(2,1)S(1)}, u32[]{:S(2)}, u32[]{:S(2)}) collective-permute-start(bf16[4,2,8,16,512]{4,3,2,1,0:T(8,128)(2,1)} %get-tuple-element.54.refs_0_), channel_id=1, source_target_pairs={{0,32},{4,12},{8,40},{12,20},{16,48},{20,28},{24,56},{28,4},{32,64... | collective-permute-start | bytes 3145736 | tf_op jit(solution)/shard_map/ppermute | solution.py:372
  122.3 10.5 %collective-permute-start.22 = (f32[64,256]{1,0:T(8,128)S(1)}, f32[64,256]{1,0:T(8,128)S(1)}, u32[]{:S(2)}, u32[]{:S(2)}) collective-permute-start(f32[64,256]{1,0:T(8,128)S(1)} %collect_kernel.1), channel_id=1, source_target_pairs={{0,4},{4,0},{1,5},{5,1},{2,6},{6,2},{3,7},{7,3},{8,12},{12,8},{9,1... | collective-permute-start | bytes 196616 | tf_op jit(solution)/shard_map/ppermute | solution.py:353
  160.8 27.8 %all-to-all-start.2 = ((bf16[16,80,256]{2,1,0:T(8,128)(2,1)}), bf16[16,80,256]{2,1,0:T(8,128)(2,1)}, u32[]{:S(2)}, u32[]{:S(2)}) async-start(bf16[16,80,256]{2,1,0:T(8,128)(2,1)} %broadcast_in_dim.2.refs_1_), calls=%async_computation.2 | async-start | bytes 1310720 | tf_op jit(solution)/shard_map/all_to_all | solution.py:381
  169.4 16.3 %collective-permute-start.33 = (bf16[464,256]{1,0:T(8,128)(2,1)S(1)}, bf16[464,256]{1,0:T(8,128)(2,1)S(1)}, u32[]{:S(2)}, u32[]{:S(2)}) collective-permute-start(bf16[464,256]{1,0:T(8,128)(2,1)S(1)} %get-tuple-element.59), channel_id=1, source_target_pairs={{0,1},{1,2},{2,3},{3,0},{4,5},{5,6},{6,7},{7,4},{8,9},{9,10},{10,1... | collective-permute-start | bytes 712712 | tf_op jit(solution)/shard_map/ppermute | solution.py:357
  170.8 14.9 %collective-permute-start.34 = (bf16[464,256]{1,0:T(8,128)(2,1)S(1)}, bf16[464,256]{1,0:T(8,128)(2,1)S(1)}, u32[]{:S(2)}, u32[]{:S(2)}) collective-permute-start(bf16[464,256]{1,0:T(8,128)(2,1)S(1)} %get-tuple-element.60), channel_id=1, source_target_pairs={{0,3},{1,0},{2,1},{3,2},{4,7},{5,4},{6,5},{7,6},{8,11},{9,8},{10,9... | collective-permute-start | bytes 712712 | tf_op jit(solution)/shard_map/ppermute | solution.py:357
  172.1 13.5 %collective-permute-start.35 = (bf16[464,256]{1,0:T(8,128)(2,1)S(1)}, bf16[464,256]{1,0:T(8,128)(2,1)S(1)}, u32[]{:S(2)}, u32[]{:S(2)}) collective-permute-start(bf16[464,256]{1,0:T(8,128)(2,1)S(1)} %get-tuple-element.61), channel_id=1, source_target_pairs={{0,2},{1,3},{2,0},{3,1},{4,6},{5,7},{6,4},{7,5},{8,10},{9,11},{10,... | collective-permute-start | bytes 712712 | tf_op jit(solution)/shard_map/ppermute | solution.py:357
  184.2 11.7 %collective-permute-start.36 = (bf16[2048,64]{1,0:T(8,128)(2,1)}, bf16[2048,64]{1,0:T(8,128)(2,1)}, u32[]{:S(2)}, u32[]{:S(2)}) collective-permute-start(bf16[2048,64]{1,0:T(8,128)(2,1)} %slice_bitcast_fusion), channel_id=1, source_target_pairs={{0,4},{4,0},{1,5},{5,1},{2,6},{6,2},{3,7},{7,3},{8,12},{12,8},{9,1... | collective-permute-start | bytes 786440 | tf_op jit(solution)/shard_map/ppermute | solution.py:353
  185.8 12.6 %collective-permute-start.39 = (bf16[464,256]{1,0:T(8,128)(2,1)S(1)}, bf16[464,256]{1,0:T(8,128)(2,1)S(1)}, u32[]{:S(2)}, u32[]{:S(2)}) collective-permute-start(bf16[464,256]{1,0:T(8,128)(2,1)S(1)} %add_convert_fusion.refs_1_.refs_0_), channel_id=1, source_target_pairs={{0,2},{1,3},{2,0},{3,1},{4,6},{5,7},{6,4},{7,5},{8,10},{9,11},{10,... | collective-permute-start | bytes 712712 | tf_op jit(solution)/shard_map/ppermute | solution.py:357
  187.2 11.2 %collective-permute-start.38 = (bf16[464,256]{1,0:T(8,128)(2,1)S(1)}, bf16[464,256]{1,0:T(8,128)(2,1)S(1)}, u32[]{:S(2)}, u32[]{:S(2)}) collective-permute-start(bf16[464,256]{1,0:T(8,128)(2,1)S(1)} %add_convert_fusion.refs_1_.refs_0_), channel_id=1, source_target_pairs={{0,3},{1,0},{2,1},{3,2},{4,7},{5,4},{6,5},{7,6},{8,11},{9,8},{10,9... | collective-permute-start | bytes 712712 | tf_op jit(solution)/shard_map/ppermute | solution.py:357
  188.5 11.6 %collective-permute-start.37 = (bf16[464,256]{1,0:T(8,128)(2,1)S(1)}, bf16[464,256]{1,0:T(8,128)(2,1)S(1)}, u32[]{:S(2)}, u32[]{:S(2)}) collective-permute-start(bf16[464,256]{1,0:T(8,128)(2,1)S(1)} %add_convert_fusion.refs_1_.refs_0_), channel_id=1, source_target_pairs={{0,1},{1,2},{2,3},{3,0},{4,5},{5,6},{6,7},{7,4},{8,9},{9,10},{10,1... | collective-permute-start | bytes 712712 | tf_op jit(solution)/shard_map/ppermute | solution.py:357
  (40 other events, 244.6 us)

commit v10 on v9

--- a/solution.py
+++ b/solution.py
@@ -315,7 +315,7 @@
         refs[4][rows, :] = refs[k][...].astype(F32)
 
 
-ROOM = {"forward_kernel": 28, "weight_grad_kernel": 18, "field_grad_kernel": 22, "turn_kernel": 16, "middle_kernel": 16}
+ROOM = {"forward_kernel": 28, "weight_grad_kernel": 44, "field_grad_kernel": 22, "turn_kernel": 16, "middle_kernel": 16}
 
 
 def call(kernel, out_shape, scratch, flops, *args, scalar=True, raw=0):

time: 203 us -> 202 us (level)
  local copies, waits for them, and re-layouts: 20.7 us -> 18.6 us
    unnamed x44 -> x42, local copies, waits for them, and re-layouts: 12.5 us -> 10.5 us
where the time goes in v10:
time: 202 us
  starting transfers between devices  78.5 us (39%)
  Pallas kernels  34.9 us (17%)
  waiting for transfers between devices  32.7 us (16%)
  blocking collectives  31.9 us (16%)
  local copies, waits for them, and re-layouts  18.6 us (9%)
  other arithmetic  3.97 us (2%)
    pallas_call x14, Pallas kernels, call(): pl.pallas_call(kernel, out_shape=out_shape, in_specs=specs, out_specs=jax...  34.9 us
    all_to_all x1, blocking collectives, exchange(): return lax.all_to_all(value, plane, split_axis=0, concat_axis=0, tiled=True)  31.9 us
    ppermute x14, starting transfers between devices, swap(): return lax.ppermute(value, 'core', [(0, 1), (1, 0)])  29.6 us
    ppermute x17, starting transfers between devices, send(): return lax.ppermute(value, axis, [(k, (k + step) % 4) for k in range(4)])  23.8 us
    ppermute x17, waiting for transfers between devices, send(): return lax.ppermute(value, axis, [(k, (k + step) % 4) for k in range(4)])  19.4 us
    all_to_all x2, starting transfers between devices, exchange(): return lax.all_to_all(value, plane, split_axis=0, concat_axis=0, tiled=True)  14.5 us
    unnamed x42, local copies, waits for them, and re-layouts  10.5 us
    ppermute x14, waiting for transfers between devices, swap(): return lax.ppermute(value, 'core', [(0, 1), (1, 0)])  7.62 us
  transfers between devices with their start and end apart: 42, of which 18 were waited for; matrix products, arithmetic and copies ran while one was open for 5% of the time, Pallas kernels for 8%

profile of v10, /device:TPU:1, one launch (start us, length us, event | category | flops | bytes accessed | tf_op | source)
XLA Modules:
  0.0 201.5 jit_solution(5311102249842636970)
XLA Ops:
  0.6 3.6 %collective-permute-start.1 = (bf16[29,64,256]{2,1,0:T(8,128)(2,1)}, bf16[29,64,256]{2,1,0:T(8,128)(2,1)S(1)}, u32[]{:S(2)}, u32[]{:S(2)}) collective-permute-start(bf16[29,64,256]{2,1,0:T(8,128)(2,1)} %own.1), channel_id=1, source_target_pairs={{0,24},{8,0},{16,8},{24,16},{1,25},{9,1},{17,9},{25,17},{2,26},{10... | collective-permute-start | bytes 2850824 | tf_op jit(solution)/shard_map/ppermute | solution.py:357
  6.3 31.9 %all_to_all.15 = bf16[16,32,768]{2,1,0:T(8,128)(2,1)} all-to-all(bf16[16,32,768]{2,1,0:T(8,128)(2,1)S(1)} %split_kernel.1), channel_id=1, replica_groups=mesh['z'=4,'y'=4,'core'=2,'rep'=4] {'z','y'}, dimensions={0} | all-to-all | bytes 1572864 | tf_op jit(solution)/shard_map/all_to_all | solution.py:381
  40.8 2.6 %collective-permute-start.4 = (bf16[29,64,256]{2,1,0:T(8,128)(2,1)S(1)}, bf16[29,64,256]{2,1,0:T(8,128)(2,1)}, u32[]{:S(2)}, u32[]{:S(2)}) collective-permute-start(bf16[29,64,256]{2,1,0:T(8,128)(2,1)S(1)} %copy-done.19), channel_id=1, source_target_pairs={{0,4},{4,0},{1,5},{5,1},{2,6},{6,2},{3,7},{7,3},{8,12},{12,8},{9,1... | collective-permute-start | bytes 2850824 | tf_op jit(solution)/shard_map/ppermute | solution.py:353
  45.0 2.9 %collective-permute-start.3 = (bf16[14,64,256]{2,1,0:T(8,128)(2,1)S(1)}, bf16[14,64,256]{2,1,0:T(8,128)(2,1)}, u32[]{:S(2)}, u32[]{:S(2)}) collective-permute-start(bf16[14,64,256]{2,1,0:T(8,128)(2,1)S(1)} %slice.19), channel_id=1, source_target_pairs={{0,24},{8,0},{16,8},{24,16},{1,25},{9,1},{17,9},{25,17},{2,26},{10... | collective-permute-start | bytes 1376264 | tf_op jit(solution)/shard_map/ppermute | solution.py:357
  47.9 4.3 %collective-permute-done.2.refs_3_ = bf16[15,64,256]{2,1,0:T(8,128)(2,1)} collective-permute-done((bf16[15,64,256]{2,1,0:T(8,128)(2,1)S(1)}, bf16[15,64,256]{2,1,0:T(8,128)(2,1)}, u32[]{:S(2)}, u32[]{:S(2)}) %collective-permute-start.2) | collective-permute-done | bytes 491552 | tf_op jit(solution)/shard_map/ppermute | solution.py:357
  52.3 3.5 %collective-permute-start.7 = (bf16[15,64,256]{2,1,0:T(8,128)(2,1)}, bf16[15,64,256]{2,1,0:T(8,128)(2,1)}, u32[]{:S(2)}, u32[]{:S(2)}) collective-permute-start(bf16[15,64,256]{2,1,0:T(8,128)(2,1)} %collective-permute-done.2.refs_3_), channel_id=1, source_target_pairs={{0,4},{4,0},{1,5},{5,1},{2,6},{6,2},{3,7},{7,3},{8,12},{12,8},{9,1... | collective-permute-start | bytes 1474568 | tf_op jit(solution)/shard_map/ppermute | solution.py:353
  55.8 2.1 %collective-permute-done.3.refs_4_ = bf16[14,64,256]{2,1,0:T(8,128)(2,1)} collective-permute-done((bf16[14,64,256]{2,1,0:T(8,128)(2,1)S(1)}, bf16[14,64,256]{2,1,0:T(8,128)(2,1)}, u32[]{:S(2)}, u32[]{:S(2)}) %collective-permute-start.3) | collective-permute-done | bytes 458784 | tf_op jit(solution)/shard_map/ppermute | solution.py:357
  61.7 6.7 %forward_kernel.1 = (f32[136,1024]{1,0:T(8,128)S(1)}, f32[136,1024]{1,0:T(8,128)S(1)}, f32[136,1024]{1,0:T(8,128)S(1)}, f32[64,1024]{1,0:T(8,128)S(1)}, f32[72,1...) custom-call(s32[4]{0:T(128)S(1)} %pad_add_fusion.pos_ref, ...), custom_call_target="tpu_custom_call" | custom-call | flops 4000000000 | bytes 11206672 | tf_op jit(solution)/shard_map/forward_kernel/pallas_call | solution.py:328
  69.1 2.1 %collective-permute-start.10 = (f32[136,1024]{1,0:T(8,128)S(1)}, f32[136,1024]{1,0:T(8,128)S(1)}, u32[]{:S(2)}, u32[]{:S(2)}) collective-permute-start(f32[136,1024]{1,0:T(8,128)S(1)} %get-tuple-element.37), channel_id=1, source_target_pairs={{0,96},{32,0},{64,32},{96,64},{1,97},{33,1},{65,33},{97,65},{2,98}... | collective-permute-start | bytes 1671176 | tf_op jit(solution)/shard_map/ppermute | solution.py:357
  71.2 4.7 %collective-permute-start.12 = (bf16[512,128]{1,0:T(8,128)(2,1)S(1)}, bf16[512,128]{1,0:T(8,128)(2,1)S(1)}, u32[]{:S(2)}, u32[]{:S(2)}) collective-permute-start(bf16[512,128]{1,0:T(8,128)(2,1)S(1)} %get-tuple-element.41), channel_id=1, source_target_pairs={{0,16},{8,24},{16,0},{24,8},{1,17},{9,25},{17,1},{25,9},{2,18},{10... | collective-permute-start | bytes 393224 | tf_op jit(solution)/shard_map/ppermute | solution.py:357
  77.6 3.4 %collective-permute-done.12.refs_1_.refs_2_ = bf16[512,128]{1,0:T(8,128)(2,1)S(1)} collective-permute-done((bf16[512,128]{1,0:T(8,128)(2,1)S(1)}, bf16[512,128]{1,0:T(8,128)(2,1)S(1)}, u32[]{:S(2)}, u32[]{:S(2)}) %collective-permute-start.12) | collective-permute-done | bytes 131104 | tf_op jit(solution)/shard_map/ppermute | solution.py:357
  81.0 2.6 %collective-permute-done.9.from_low = f32[136,1024]{1,0:T(8,128)S(1)} collective-permute-done((f32[136,1024]{1,0:T(8,128)S(1)}, f32[136,1024]{1,0:T(8,128)S(1)}, u32[]{:S(2)}, u32[]{:S(2)}) %collective-permute-start.9) | collective-permute-done | bytes 557088 | tf_op jit(solution)/shard_map/ppermute | solution.py:357
  83.6 2.4 %collective-permute-start.15 = (f32[72,1024]{1,0:T(8,128)S(1)}, f32[72,1024]{1,0:T(8,128)S(1)}, u32[]{:S(2)}, u32[]{:S(2)}) collective-permute-start(f32[72,1024]{1,0:T(8,128)S(1)} %get-tuple-element.44), channel_id=1, source_target_pairs={{0,96},{32,0},{64,32},{96,64},{1,97},{33,1},{65,33},{97,65},{2,98}... | collective-permute-start | bytes 884744 | tf_op jit(solution)/shard_map/ppermute | solution.py:357
  89.7 3.5 %collective-permute-done.14.half_a = f32[64,1024]{1,0:T(8,128)S(1)} collective-permute-done((f32[64,1024]{1,0:T(8,128)S(1)}, f32[64,1024]{1,0:T(8,128)S(1)}, u32[]{:S(2)}, u32[]{:S(2)}) %collective-permute-start.14) | collective-permute-done | bytes 262176 | tf_op jit(solution)/shard_map/ppermute | solution.py:357
  95.2 2.7 %collective-permute-start.16 = (bf16[9,16,512]{2,1,0:T(8,128)(2,1)S(1)}, bf16[9,16,512]{2,1,0:T(8,128)(2,1)S(1)}, u32[]{:S(2)}, u32[]{:S(2)}) collective-permute-start(bf16[9,16,512]{2,1,0:T(8,128)(2,1)S(1)} %get-tuple-element.49), channel_id=1, source_target_pairs={{0,4},{4,0},{1,5},{5,1},{2,6},{6,2},{3,7},{7,3},{8,12},{12,8},{9,1... | collective-permute-start | bytes 442376 | tf_op jit(solution)/shard_map/ppermute | solution.py:353
  100.6 7.5 %all-to-all-start.1 = ((bf16[16,96,256]{2,1,0:T(8,128)(2,1)}), bf16[16,96,256]{2,1,0:T(8,128)(2,1)S(1)}, u32[]{:S(2)}, u32[]{:S(2)}) async-start(bf16[16,96,256]{2,1,0:T(8,128)(2,1)} %get-tuple-element.47), calls=%async_computation.1 | async-start | bytes 1572864 | tf_op jit(solution)/shard_map/all_to_all | solution.py:381
  114.7 3.5 %collective-permute-start.20 = (f32[8,512]{1,0:T(8,128)S(1)}, f32[8,512]{1,0:T(8,128)S(1)}, u32[]{:S(2)}, u32[]{:S(2)}) collective-permute-start(f32[8,512]{1,0:T(8,128)S(1)} %get-tuple-element.50), channel_id=1, source_target_pairs={{0,4},{4,0},{1,5},{5,1},{2,6},{6,2},{3,7},{7,3},{8,12},{12,8},{9,1... | collective-permute-start | bytes 49160 | tf_op jit(solution)/shard_map/ppermute | solution.py:353
  122.3 9.6 %collective-permute-start.22 = (f32[64,256]{1,0:T(8,128)S(1)}, f32[64,256]{1,0:T(8,128)S(1)}, u32[]{:S(2)}, u32[]{:S(2)}) collective-permute-start(f32[64,256]{1,0:T(8,128)S(1)} %collect_kernel.1), channel_id=1, source_target_pairs={{0,4},{4,0},{1,5},{5,1},{2,6},{6,2},{3,7},{7,3},{8,12},{12,8},{9,1... | collective-permute-start | bytes 196616 | tf_op jit(solution)/shard_map/ppermute | solution.py:353
  132.9 2.8 %collective-permute-start.24 = (f32[80,256]{1,0:T(8,128)S(1)}, f32[80,256]{1,0:T(8,128)S(1)}, u32[]{:S(2)}, u32[]{:S(2)}) collective-permute-start(f32[80,256]{1,0:T(8,128)S(1)} %pad_maximum_fusion.2), channel_id=1, source_target_pairs={{0,2},{1,3},{2,0},{3,1},{4,6},{5,7},{6,4},{7,5},{8,10},{9,11},{10,... | collective-permute-start | bytes 245768 | tf_op jit(solution)/shard_map/ppermute | solution.py:361
  151.0 8.8 %weight_grad_kernel.1 = (bf16[29,64,256]{2,1,0:T(8,128)(2,1)S(1)}, bf16[29,64,256]{2,1,0:T(8,128)(2,1)}) custom-call(s32[4]{0:T(128)S(1)} %pad_add_fusion.pos_ref, bf16[7,128,2048]{2,1,0:T(8,128)(2,1)} %copy-done.16, f32[8,128]{1,0:T(8,128)S(1)} %get-tuple-element.46._.colsum_ref, f32[8,256]{1,0:T(8,128)S(1)} %get-tuple-element.53.grad_ref, ...), custom_call_target="tpu_custom_call" | custom-call | flops 4000000000 | bytes 13971472 | tf_op jit(solution)/shard_map/weight_grad_kernel/pallas_call | solution.py:328
  160.3 7.0 %all-to-all-start.2 = ((bf16[16,80,256]{2,1,0:T(8,128)(2,1)}), bf16[16,80,256]{2,1,0:T(8,128)(2,1)}, u32[]{:S(2)}, u32[]{:S(2)}) async-start(bf16[16,80,256]{2,1,0:T(8,128)(2,1)} %broadcast_in_dim.2.refs_1_), calls=%async_computation.2 | async-start | bytes 1310720 | tf_op jit(solution)/shard_map/all_to_all | solution.py:381
  174.4 8.4 %field_grad_kernel.1 = bf16[2,2048,64]{2,1,0:T(8,128)(2,1)S(1)} custom-call(s32[4]{0:T(128)S(1)} %pad_add_fusion.pos_ref, f32[8,256]{1,0:T(8,128)S(1)} %get-tuple-element.53.grad_ref, bf16[29,64,256]{2,1,0:T(8,128)(2,1)S(1)} %copy-done.20, bf16[29,64,256]{2,1,0:T(8,128)(2,1)} %collective-permute-done.4.refs_5_.other, ...), custom_call_target="tpu_custom_call" | custom-call | flops 4000000000 | bytes 11059216 | tf_op jit(solution)/shard_map/field_grad_kernel/pallas_call | solution.py:328
  189.0 2.1 %slice.26 = f32[16,64,256]{2,1,0:T(8,128)} slice(bf16[16,80,256]{2,1,0:T(8,128)(2,1)} %shard_map.78), slice={[0:16], [0:64], [0:256]} | slice | bytes 2097152 | tf_op jit(solution)/shard_map/slice | solution.py:461
  193.0 2.4 %pad_maximum_fusion = f32[1280,256]{1,0:T(8,128)} fusion(f32[256,256]{1,0:T(8,128)S(1)} %bitcast.35, f32[1024,256]{1,0:T(8,128)} %bitcast.31), kind=kLoop, calls=%fused_computation | loop fusion | flops 327680 | bytes 2621440 | tf_op jit(solution)/shard_map/concatenate | solution.py:461
  (137 shorter events, 69.2 us)
Async XLA Ops:
  0.6 37.6 %collective-permute-start.1 = (bf16[29,64,256]{2,1,0:T(8,128)(2,1)}, bf16[29,64,256]{2,1,0:T(8,128)(2,1)S(1)}, u32[]{:S(2)}, u32[]{:S(2)}) collective-permute-start(bf16[29,64,256]{2,1,0:T(8,128)(2,1)} %own.1), channel_id=1, source_target_pairs={{0,24},{8,0},{16,8},{24,16},{1,25},{9,1},{17,9},{25,17},{2,26},{10... | collective-permute-start | bytes 2850824 | tf_op jit(solution)/shard_map/ppermute | solution.py:357
  4.3 34.0 %collective-permute-start = (bf16[29,64,256]{2,1,0:T(8,128)(2,1)}, bf16[29,64,256]{2,1,0:T(8,128)(2,1)S(1)}, u32[]{:S(2)}, u32[]{:S(2)}) collective-permute-start(bf16[29,64,256]{2,1,0:T(8,128)(2,1)} %own.1), channel_id=1, source_target_pairs={{0,8},{8,16},{16,24},{24,0},{1,9},{9,17},{17,25},{25,1},{2,10},{10... | collective-permute-start | bytes 2850824 | tf_op jit(solution)/shard_map/ppermute | solution.py:357
  40.7 11.6 %collective-permute-start.2 = (bf16[15,64,256]{2,1,0:T(8,128)(2,1)S(1)}, bf16[15,64,256]{2,1,0:T(8,128)(2,1)}, u32[]{:S(2)}, u32[]{:S(2)}) collective-permute-start(bf16[15,64,256]{2,1,0:T(8,128)(2,1)S(1)} %slice.18), channel_id=1, source_target_pairs={{0,8},{8,16},{16,24},{24,0},{1,9},{9,17},{17,25},{25,1},{2,10},{10... | collective-permute-start | bytes 1474568 | tf_op jit(solution)/shard_map/ppermute | solution.py:357
  40.8 17.9 %collective-permute-start.4 = (bf16[29,64,256]{2,1,0:T(8,128)(2,1)S(1)}, bf16[29,64,256]{2,1,0:T(8,128)(2,1)}, u32[]{:S(2)}, u32[]{:S(2)}) collective-permute-start(bf16[29,64,256]{2,1,0:T(8,128)(2,1)S(1)} %copy-done.19), channel_id=1, source_target_pairs={{0,4},{4,0},{1,5},{5,1},{2,6},{6,2},{3,7},{7,3},{8,12},{12,8},{9,1... | collective-permute-start | bytes 2850824 | tf_op jit(solution)/shard_map/ppermute | solution.py:353
  43.5 17.0 %collective-permute-start.5 = (bf16[29,64,256]{2,1,0:T(8,128)(2,1)}, bf16[29,64,256]{2,1,0:T(8,128)(2,1)}, u32[]{:S(2)}, u32[]{:S(2)}) collective-permute-start(bf16[29,64,256]{2,1,0:T(8,128)(2,1)} %get-tuple-element.33.refs_1_), channel_id=1, source_target_pairs={{0,4},{4,0},{1,5},{5,1},{2,6},{6,2},{3,7},{7,3},{8,12},{12,8},{9,1... | collective-permute-start | bytes 2850824 | tf_op jit(solution)/shard_map/ppermute | solution.py:353
  43.6 16.9 %collective-permute-start.6 = (bf16[29,64,256]{2,1,0:T(8,128)(2,1)}, bf16[29,64,256]{2,1,0:T(8,128)(2,1)}, u32[]{:S(2)}, u32[]{:S(2)}) collective-permute-start(bf16[29,64,256]{2,1,0:T(8,128)(2,1)} %get-tuple-element.34.refs_2_), channel_id=1, source_target_pairs={{0,4},{4,0},{1,5},{5,1},{2,6},{6,2},{3,7},{7,3},{8,12},{12,8},{9,1... | collective-permute-start | bytes 2850824 | tf_op jit(solution)/shard_map/ppermute | solution.py:353
  45.0 12.9 %collective-permute-start.3 = (bf16[14,64,256]{2,1,0:T(8,128)(2,1)S(1)}, bf16[14,64,256]{2,1,0:T(8,128)(2,1)}, u32[]{:S(2)}, u32[]{:S(2)}) collective-permute-start(bf16[14,64,256]{2,1,0:T(8,128)(2,1)S(1)} %slice.19), channel_id=1, source_target_pairs={{0,24},{8,0},{16,8},{24,16},{1,25},{9,1},{17,9},{25,17},{2,26},{10... | collective-permute-start | bytes 1376264 | tf_op jit(solution)/shard_map/ppermute | solution.py:357
  68.4 15.1 %collective-permute-start.9 = (f32[136,1024]{1,0:T(8,128)S(1)}, f32[136,1024]{1,0:T(8,128)S(1)}, u32[]{:S(2)}, u32[]{:S(2)}) collective-permute-start(f32[136,1024]{1,0:T(8,128)S(1)} %get-tuple-element.36), channel_id=1, source_target_pairs={{0,32},{32,64},{64,96},{96,0},{1,33},{33,65},{65,97},{97,1},{2,34}... | collective-permute-start | bytes 1671176 | tf_op jit(solution)/shard_map/ppermute | solution.py:357
  69.1 14.5 %collective-permute-start.10 = (f32[136,1024]{1,0:T(8,128)S(1)}, f32[136,1024]{1,0:T(8,128)S(1)}, u32[]{:S(2)}, u32[]{:S(2)}) collective-permute-start(f32[136,1024]{1,0:T(8,128)S(1)} %get-tuple-element.37), channel_id=1, source_target_pairs={{0,96},{32,0},{64,32},{96,64},{1,97},{33,1},{65,33},{97,65},{2,98}... | collective-permute-start | bytes 1671176 | tf_op jit(solution)/shard_map/ppermute | solution.py:357
  71.2 9.8 %collective-permute-start.12 = (bf16[512,128]{1,0:T(8,128)(2,1)S(1)}, bf16[512,128]{1,0:T(8,128)(2,1)S(1)}, u32[]{:S(2)}, u32[]{:S(2)}) collective-permute-start(bf16[512,128]{1,0:T(8,128)(2,1)S(1)} %get-tuple-element.41), channel_id=1, source_target_pairs={{0,16},{8,24},{16,0},{24,8},{1,17},{9,25},{17,1},{25,9},{2,18},{10... | collective-permute-start | bytes 393224 | tf_op jit(solution)/shard_map/ppermute | solution.py:357
  83.6 9.6 %collective-permute-start.15 = (f32[72,1024]{1,0:T(8,128)S(1)}, f32[72,1024]{1,0:T(8,128)S(1)}, u32[]{:S(2)}, u32[]{:S(2)}) collective-permute-start(f32[72,1024]{1,0:T(8,128)S(1)} %get-tuple-element.44), channel_id=1, source_target_pairs={{0,96},{32,0},{64,32},{96,64},{1,97},{33,1},{65,33},{97,65},{2,98}... | collective-permute-start | bytes 884744 | tf_op jit(solution)/shard_map/ppermute | solution.py:357
  100.6 21.6 %all-to-all-start.1 = ((bf16[16,96,256]{2,1,0:T(8,128)(2,1)}), bf16[16,96,256]{2,1,0:T(8,128)(2,1)S(1)}, u32[]{:S(2)}, u32[]{:S(2)}) async-start(bf16[16,96,256]{2,1,0:T(8,128)(2,1)} %get-tuple-element.47), calls=%async_computation.1 | async-start | bytes 1572864 | tf_op jit(solution)/shard_map/all_to_all | solution.py:381
  110.6 31.4 %collective-permute-start.27 = (bf16[4,2,8,16,512]{4,3,2,1,0:T(8,128)(2,1)}, bf16[4,2,8,16,512]{4,3,2,1,0:T(8,128)(2,1)}, u32[]{:S(2)}, u32[]{:S(2)}) collective-permute-start(bf16[4,2,8,16,512]{4,3,2,1,0:T(8,128)(2,1)} %get-tuple-element.54.refs_0_), channel_id=1, source_target_pairs={{0,64},{4,20},{8,72},{12,28},{16,80},{20,4},{24,88},{28,12},{32,96... | collective-permute-start | bytes 3145736 | tf_op jit(solution)/shard_map/ppermute | solution.py:372
  112.3 31.5 %collective-permute-start.26 = (bf16[4,2,8,16,512]{4,3,2,1,0:T(8,128)(2,1)}, bf16[4,2,8,16,512]{4,3,2,1,0:T(8,128)(2,1)}, u32[]{:S(2)}, u32[]{:S(2)}) collective-permute-start(bf16[4,2,8,16,512]{4,3,2,1,0:T(8,128)(2,1)} %get-tuple-element.54.refs_0_), channel_id=1, source_target_pairs={{0,96},{4,28},{8,104},{12,4},{16,112},{20,12},{24,120},{28,20},{32... | collective-permute-start | bytes 3145736 | tf_op jit(solution)/shard_map/ppermute | solution.py:372
  114.1 29.8 %collective-permute-start.21 = (bf16[4,2,8,16,512]{4,3,2,1,0:T(8,128)(2,1)}, bf16[4,2,8,16,512]{4,3,2,1,0:T(8,128)(2,1)S(1)}, u32[]{:S(2)}, u32[]{:S(2)}) collective-permute-start(bf16[4,2,8,16,512]{4,3,2,1,0:T(8,128)(2,1)} %get-tuple-element.54.refs_0_), channel_id=1, source_target_pairs={{0,32},{4,12},{8,40},{12,20},{16,48},{20,28},{24,56},{28,4},{32,64... | collective-permute-start | bytes 3145736 | tf_op jit(solution)/shard_map/ppermute | solution.py:372
  122.3 10.5 %collective-permute-start.22 = (f32[64,256]{1,0:T(8,128)S(1)}, f32[64,256]{1,0:T(8,128)S(1)}, u32[]{:S(2)}, u32[]{:S(2)}) collective-permute-start(f32[64,256]{1,0:T(8,128)S(1)} %collect_kernel.1), channel_id=1, source_target_pairs={{0,4},{4,0},{1,5},{5,1},{2,6},{6,2},{3,7},{7,3},{8,12},{12,8},{9,1... | collective-permute-start | bytes 196616 | tf_op jit(solution)/shard_map/ppermute | solution.py:353
  160.3 27.8 %all-to-all-start.2 = ((bf16[16,80,256]{2,1,0:T(8,128)(2,1)}), bf16[16,80,256]{2,1,0:T(8,128)(2,1)}, u32[]{:S(2)}, u32[]{:S(2)}) async-start(bf16[16,80,256]{2,1,0:T(8,128)(2,1)} %broadcast_in_dim.2.refs_1_), calls=%async_computation.2 | async-start | bytes 1310720 | tf_op jit(solution)/shard_map/all_to_all | solution.py:381
  168.8 16.3 %collective-permute-start.33 = (bf16[464,256]{1,0:T(8,128)(2,1)S(1)}, bf16[464,256]{1,0:T(8,128)(2,1)S(1)}, u32[]{:S(2)}, u32[]{:S(2)}) collective-permute-start(bf16[464,256]{1,0:T(8,128)(2,1)S(1)} %get-tuple-element.59), channel_id=1, source_target_pairs={{0,1},{1,2},{2,3},{3,0},{4,5},{5,6},{6,7},{7,4},{8,9},{9,10},{10,1... | collective-permute-start | bytes 712712 | tf_op jit(solution)/shard_map/ppermute | solution.py:357
  170.2 14.9 %collective-permute-start.34 = (bf16[464,256]{1,0:T(8,128)(2,1)S(1)}, bf16[464,256]{1,0:T(8,128)(2,1)S(1)}, u32[]{:S(2)}, u32[]{:S(2)}) collective-permute-start(bf16[464,256]{1,0:T(8,128)(2,1)S(1)} %get-tuple-element.60), channel_id=1, source_target_pairs={{0,3},{1,0},{2,1},{3,2},{4,7},{5,4},{6,5},{7,6},{8,11},{9,8},{10,9... | collective-permute-start | bytes 712712 | tf_op jit(solution)/shard_map/ppermute | solution.py:357
  171.6 13.5 %collective-permute-start.35 = (bf16[464,256]{1,0:T(8,128)(2,1)S(1)}, bf16[464,256]{1,0:T(8,128)(2,1)S(1)}, u32[]{:S(2)}, u32[]{:S(2)}) collective-permute-start(bf16[464,256]{1,0:T(8,128)(2,1)S(1)} %get-tuple-element.61), channel_id=1, source_target_pairs={{0,2},{1,3},{2,0},{3,1},{4,6},{5,7},{6,4},{7,5},{8,10},{9,11},{10,... | collective-permute-start | bytes 712712 | tf_op jit(solution)/shard_map/ppermute | solution.py:357
  183.7 11.7 %collective-permute-start.36 = (bf16[2048,64]{1,0:T(8,128)(2,1)}, bf16[2048,64]{1,0:T(8,128)(2,1)}, u32[]{:S(2)}, u32[]{:S(2)}) collective-permute-start(bf16[2048,64]{1,0:T(8,128)(2,1)} %slice_bitcast_fusion), channel_id=1, source_target_pairs={{0,4},{4,0},{1,5},{5,1},{2,6},{6,2},{3,7},{7,3},{8,12},{12,8},{9,1... | collective-permute-start | bytes 786440 | tf_op jit(solution)/shard_map/ppermute | solution.py:353
  185.2 12.6 %collective-permute-start.39 = (bf16[464,256]{1,0:T(8,128)(2,1)S(1)}, bf16[464,256]{1,0:T(8,128)(2,1)S(1)}, u32[]{:S(2)}, u32[]{:S(2)}) collective-permute-start(bf16[464,256]{1,0:T(8,128)(2,1)S(1)} %add_convert_fusion.refs_1_.refs_0_), channel_id=1, source_target_pairs={{0,2},{1,3},{2,0},{3,1},{4,6},{5,7},{6,4},{7,5},{8,10},{9,11},{10,... | collective-permute-start | bytes 712712 | tf_op jit(solution)/shard_map/ppermute | solution.py:357
  186.6 11.2 %collective-permute-start.38 = (bf16[464,256]{1,0:T(8,128)(2,1)S(1)}, bf16[464,256]{1,0:T(8,128)(2,1)S(1)}, u32[]{:S(2)}, u32[]{:S(2)}) collective-permute-start(bf16[464,256]{1,0:T(8,128)(2,1)S(1)} %add_convert_fusion.refs_1_.refs_0_), channel_id=1, source_target_pairs={{0,3},{1,0},{2,1},{3,2},{4,7},{5,4},{6,5},{7,6},{8,11},{9,8},{10,9... | collective-permute-start | bytes 712712 | tf_op jit(solution)/shard_map/ppermute | solution.py:357
  188.0 11.6 %collective-permute-start.37 = (bf16[464,256]{1,0:T(8,128)(2,1)S(1)}, bf16[464,256]{1,0:T(8,128)(2,1)S(1)}, u32[]{:S(2)}, u32[]{:S(2)}) collective-permute-start(bf16[464,256]{1,0:T(8,128)(2,1)S(1)} %add_convert_fusion.refs_1_.refs_0_), channel_id=1, source_target_pairs={{0,1},{1,2},{2,3},{3,0},{4,5},{5,6},{6,7},{7,4},{8,9},{9,10},{10,1... | collective-permute-start | bytes 712712 | tf_op jit(solution)/shard_map/ppermute | solution.py:357
  (39 other events, 242.0 us)
